TPU v7x, 32 devices: a whole 2x2x4 slice. The times are simulated.
32 devices in a mesh: row: 4 (over x, core), col: 8 (over z, y).
Axes of the slice: x: 2, y: 2, z: 4, core: 2. Of those that a mesh axis runs over, the one named last changes fastest.
Arguments:
- inputs: bfloat16 [512, 6144], P(('row', 'col')), may hold values from -6 to 6
- cotangent: bfloat16 [512, 6144], P(('row', 'col')), may hold values from -0.41992188 to 0.41992188
- w_in: bfloat16 [1536, 24576], P('row', 'col'), may hold values from -0.15625 to 0.15625
- w_out: bfloat16 [1536, 24576], P('row', 'col'), may hold values from -0.078125 to 0.078125
- keep_in: int32 [192, 12], replicated, may hold values from 0 to 47, all different within a row
- keep_out: int32 [192, 12], replicated, may hold values from 0 to 47, all different within a row
Outputs:
- grad_in: bfloat16 [1536, 24576], P('row', 'col')
- grad_out: bfloat16 [1536, 24576], P('row', 'col')
Inputs may be any that keep to these rules, and one draw needn't show every extreme that they name: `keep_in`: each row names 12 different input blocks, and every block is named by some row. `keep_out`: each row names 12 different output blocks, and every block is named by some row.
All inputs are finite; a program needn't handle non-finite values.
Results may differ from a plain program's by a relative error of at most 0.022.
Values may be sent and summed in bfloat16 or wider, within the bound.
No kernel may reach another device: no remote copies, remote signals or barrier semaphores. Data moves between devices by JAX's collectives and lax.ppermute only.
A program may use at most 128 MiB of HBM per device.

v0:
```python
import jax
import jax.numpy as jnp
from jax import lax
from jax.sharding import PartitionSpec as P

D = 6144
BLK = 128
KEEP = 12


def gelu_tanh(values):
    return jax.nn.gelu(values, approximate=True)


def pick_one(matrix, chosen):
    return jnp.take(matrix, chosen, axis=1)


def per_device(inputs, cotangent, w_in, w_out, keep_in, keep_out):
    width = w_in.shape[1]
    blocks_here = width // BLK
    kept_rows = w_in.shape[0]
    column = lax.axis_index("col")
    own_in = lax.dynamic_slice_in_dim(keep_in, column * blocks_here, blocks_here, 0)
    own_out = lax.dynamic_slice_in_dim(keep_out, column * blocks_here, blocks_here, 0)
    tables = jnp.stack((own_in, own_out), 0)
    stacked = jnp.stack((inputs, cotangent), 0)
    whole = lax.all_gather(stacked, "col", axis=1, tiled=True)
    tokens_here = whole.shape[1]
    blocks = whole.reshape(2, tokens_here, D // BLK, BLK)
    picked = jax.vmap(pick_one)(blocks, tables).reshape(2, tokens_here, blocks_here, KEEP * BLK)
    weights = jnp.stack((w_in, w_out), 1)
    full = lax.all_gather(weights, "row", axis=0, tiled=True)
    panel = full.reshape(KEEP * BLK, 2, blocks_here, BLK)
    mixed = jnp.einsum("ptck,kpcq->ptcq", picked, panel, preferred_element_type=jnp.float32)
    hidden = mixed[0].reshape(tokens_here, width)
    d_act = mixed[1].reshape(tokens_here, width)
    act, pullback = jax.vjp(gelu_tanh, hidden)
    d_hidden = pullback(d_act)[0].astype(jnp.bfloat16)
    act = act.astype(jnp.bfloat16)
    paired = jnp.stack((d_hidden, act), 0).reshape(2, tokens_here, blocks_here, BLK)
    term = jnp.einsum("ptck,ptcq->kpcq", picked, paired, preferred_element_type=jnp.float32)
    summed = (
        lax.psum_scatter(
            term.reshape(lax.axis_size("row") * kept_rows, 2 * width).astype(jnp.bfloat16),
            "row",
            scatter_dimension=0,
            tiled=True,
        )
        .astype(jnp.float32)
        .reshape(kept_rows, 2, width)
    )
    return (summed[:, 0].astype(jnp.bfloat16), summed[:, 1].astype(jnp.bfloat16))


def solution(mesh):
    in_specs = (
        P(("row", "col"), None),
        P(("row", "col"), None),
        P("row", "col"),
        P("row", "col"),
        P(),
        P(),
    )
    out_specs = (P("row", "col"), P("row", "col"))
    return jax.shard_map(
        per_device, mesh=mesh, in_specs=in_specs, out_specs=out_specs, check_vma=False
    )
```

profile of v0, /device:TPU:0, one launch (start us, length us, event | category | flops | bytes accessed | tf_op | source)
XLA Modules:
  0.0 437.3 jit_solution(6549816080089969860)
XLA Ops:
  7.2 0.0 all-gather.5.cloned.1.call-start
  7.2 1.1 pad_maximum_fusion.1
  8.3 1.2 copy.36
  9.4 0.0 all-gather.5.cloned.1.call-update
  9.4 0.0 all-gather.3.cloned.1.call-start
  9.5 5.0 %pad_maximum_fusion = bf16[384,2,3072]{2,0,1:T(8,128)(2,1)} fusion(bf16[384,1,3072]{2,0,1:T(8,128)(2,1)} %bitcast.42, bf16[384,1,3072]{2,0,1:T(8,128)(2,1)} %bitcast.43), kind=kLoop, calls=%fused_computation.3 | loop fusion | flops 2359296 | bytes 9437184 | tf_op jit(solution)/shard_map/stack | solution.py:32
  14.5 0.0 all-gather.3.cloned.1.call-update
  14.5 0.0 reduce-scatter.4.cloned.1.call-start
  14.5 0.6 copy-done
  15.2 0.1 dynamic-slice_bitcast_fusion.1
  15.3 0.1 copy.38
  15.4 0.1 reshape.127
  15.5 0.1 copy.35
  15.6 0.2 broadcast_in_dim.14
  15.8 0.1 broadcast_in_dim.15
  15.9 58.0 %all-gather.5.cloned.1.call-done = bf16[2,128,6144]{2,0,1:T(2,128)(2,1)} async-done(((bf16[2,16,6144]{2,0,1:T(2,128)(2,1)}), bf16[2,128,6144]{2,0,1:T(2,128)(2,1)}) %all-gather.5.cloned.1.call-update) | async-done | bytes 3145744 | tf_op jit(solution)/shard_map/all_gather | solution.py:28
  73.9 8.8 %copy.37 = bf16[2,128,6144]{1,2,0:T(8,128)(2,1)} copy(bf16[2,128,6144]{2,0,1:T(2,128)(2,1)} %all-gather.5.cloned.1.call-done) | data formatting | bytes 6291456 | tf_op jit(solution)/shard_map/all_gather | solution.py:28
  82.7 3.8 copy.39
  86.6 25.4 %gather_fusion = bf16[576,128,128]{2,1,0:T(8,128)(2,1)} fusion(bf16[2,128,48,128]{3,1,2,0:T(8,128)(2,1)S(1)} %copy.39, s32[576]{0:T(1024)S(1)} %reshape.127), kind=kCustom, calls=%fused_computation | custom fusion | bytes 37753344 | tf_op jit(solution)/shard_map/vmap(jit(_take))/gather | solution.py:16
  112.0 24.7 %copy.40 = bf16[2,128,24,12,128]{1,4,3,2,0:T(8,128)(2,1)} copy(bf16[2,128,24,12,128]{4,1,3,2,0:T(8,128)(2,1)} %bitcast.37) | data formatting | bytes 37748736 | tf_op jit(solution)/shard_map/vmap(jit(_take))/gather | solution.py:16
  136.6 19.8 %bitcast_select_fusion = bf16[2,128,24,1536]{1,3,2,0:T(8,128)(2,1)} fusion(bf16[2,128,24,12,128]{1,4,3,2,0:T(8,128)(2,1)} %copy.40, pred[2,24,1536]{2,1,0:T(8,128)(4,1)S(1)} %broadcast_in_dim.15), kind=kLoop, calls=%fused_computation.1 | loop fusion | flops 9437184 | bytes 37822464 | tf_op jit(solution)/shard_map/vmap(jit(_take))/select_n | solution.py:16
  156.4 35.8 %all-gather.3.cloned.1.call-done = bf16[1536,2,3072]{2,0,1:T(8,128)(2,1)} async-done(((bf16[384,2,3072]{2,0,1:T(8,128)(2,1)}), bf16[1536,2,3072]{2,0,1:T(8,128)(2,1)}) %all-gather.3.cloned.1.call-update) | async-done | bytes 18874384 | tf_op jit(solution)/shard_map/all_gather | solution.py:33
  192.2 24.6 %copy.34 = bf16[1536,2,3072]{0,2,1:T(8,128)(2,1)} copy(bf16[1536,2,3072]{2,0,1:T(8,128)(2,1)} %all-gather.3.cloned.1.call-done) | data formatting | bytes 37748736 | tf_op jit(solution)/shard_map/all_gather | solution.py:33
  216.8 14.4 %convolution_bitcast_fusion = f32[2,128,24,128]{1,3,2,0:T(8,128)S(1)} fusion(bf16[1536,2,24,128]{0,3,2,1:T(8,128)(2,1)} %bitcast.39, bf16[2,128,24,1536]{1,3,2,0:T(8,128)(2,1)} %bitcast_select_fusion), kind=kOutput, calls=%fused_computation.8 | convolution fusion | flops 2415919104 | bytes 40894464 | tf_op jit(solution)/shard_map/ptck,kpcq->ptcq/dot_general | solution.py:35
  231.2 1.2 fusion.6
  232.4 16.1 %convolution_convert_fusion = bf16[2,24,128,1536]{3,2,1,0:T(8,128)(2,1)} fusion(bf16[2,128,24,1536]{1,3,2,0:T(8,128)(2,1)} %bitcast_select_fusion, bf16[1,128,24,128]{1,3,2,0:T(8,128)(2,1)S(1)} %get-tuple-element.11, bf16[1,128,24,128]{1,3,2,0:T(8,128)(2,1)S(1)} %get-tuple-element.10), kind=kOutput, calls=%fused_computation.2 | convolution fusion | flops 2426142720 | bytes 39321600 | tf_op jit(solution)/shard_map/ptck,ptcq->kpcq/dot_general | solution.py:42
  248.5 24.7 %copy.47 = bf16[1536,6144]{1,0:T(8,128)(2,1)} copy(bf16[1536,6144]{0,1:T(8,128)(2,1)} %bitcast.38) | data formatting | bytes 37748736
  273.3 139.6 %reduce-scatter.4.cloned.1.call-done = bf16[384,6144]{1,0:T(8,128)(2,1)} async-done(((bf16[1536,6144]{1,0:T(8,128)(2,1)}), bf16[384,6144]{1,0:T(8,128)(2,1)}) %reduce-scatter.4.cloned.1.call-update) | async-done | bytes 4718608
  412.9 6.7 %copy.48 = bf16[384,6144]{0,1:T(8,128)(2,1)} copy(bf16[384,6144]{1,0:T(8,128)(2,1)} %reduce-scatter.4.cloned.1.call-done) | data formatting | bytes 9437184
  419.6 4.3 slice_bitcast_fusion
  423.9 4.3 copy.43
  428.1 2.6 copy.44
  (6 shorter events, 0.1 us)
Async XLA Ops:
  7.2 66.8 %all-gather.5.cloned.1.call-start = ((), (), s32[]{:S(2)}) async-start(), calls=%async_computation.2 | async-start | bytes 3538944 | tf_op jit(solution)/shard_map/all_gather | solution.py:28
  9.4 182.7 %all-gather.3.cloned.1.call-start = ((), (), s32[]{:S(2)}) async-start(), calls=%async_computation.1 | async-start | bytes 23592960 | tf_op jit(solution)/shard_map/all_gather | solution.py:33
  14.5 0.7 copy-start
  14.5 0.7 copy-start.1
  14.5 398.4 %reduce-scatter.4.cloned.1.call-start = ((), (), s32[]{:S(2)}) async-start(), calls=%async_computation.3 | async-start | bytes 23592960
Sparse Core Ops, SparseCore 0:
  10.8 63.1 all-gather.4
  75.5 116.6 all-gather.2
  273.4 139.4 reduce-scatter.3
where the time goes:
time: 440 us; the launch traced here: 437 us
  waiting for transfers between devices  233 us (53%)
  local copies, waits for them, and re-layouts  132 us (30%)
  matrix products  30.5 us (7%)
  other arithmetic  27 us (6%)
  between operations  13.8 us (3%)
    unnamed x4, waiting for transfers between devices  140 us
    all_gather x1, waiting for transfers between devices, per_device(): whole = lax.all_gather(stacked, 'col', axis=1, tiled=True)  58 us
    gather x4, local copies, waits for them, and re-layouts, pick_one(): return jnp.take(matrix, chosen, axis=1)  50.3 us
    unnamed x8, local copies, waits for them, and re-layouts  39 us
    all_gather x1, waiting for transfers between devices, per_device(): full = lax.all_gather(weights, 'row', axis=0, tiled=True)  35.8 us
    all_gather x1, local copies, waits for them, and re-layouts, per_device(): full = lax.all_gather(weights, 'row', axis=0, tiled=True)  24.6 us
    select_n x1, other arithmetic, pick_one(): return jnp.take(matrix, chosen, axis=1)  19.8 us
    dot_general x1, matrix products, per_device(): jnp.einsum('ptck,ptcq->kpcq', picked, paired, preferred_element_type=jnp....  16.1 us
  transfers between devices with their start and end apart: 3, of which 3 were waited for; matrix products, arithmetic and copies ran while one was open for 20% of the time, Pallas kernels for 0%

commit v1 on v0

--- a/solution.py
+++ b/solution.py
@@ -1,11 +1,21 @@
+import functools
+
 import jax
 import jax.numpy as jnp
 from jax import lax
+from jax.experimental import pallas as pl
+from jax.experimental.pallas import tpu as pltpu
 from jax.sharding import PartitionSpec as P
 
 D = 6144
 BLK = 128
 KEEP = 12
+ROWS = 4
+COLS = 8
+LANES = 4
+SCALE = 0.7978845608028654
+CUBIC = 0.044715
+VMEM_LIMIT = 56 * 1024 * 1024
 
 
 def gelu_tanh(values):
@@ -16,7 +26,7 @@
     return jnp.take(matrix, chosen, axis=1)
 
 
-def per_device(inputs, cotangent, w_in, w_out, keep_in, keep_out):
+def general(inputs, cotangent, w_in, w_out, keep_in, keep_out):
     width = w_in.shape[1]
     blocks_here = width // BLK
     kept_rows = w_in.shape[0]
@@ -53,7 +63,245 @@
     return (summed[:, 0].astype(jnp.bfloat16), summed[:, 1].astype(jnp.bfloat16))
 
 
+def picked_rows(table, buffers, side, block, slots):
+    columns = []
+    for slot in range(slots):
+        start = pl.multiple_of(table[(block * 2 + side) * slots + slot] * BLK, BLK)
+        columns.append(jnp.concatenate([buf[side, :, pl.ds(start, BLK)] for buf in buffers], axis=0))
+    return jnp.concatenate(columns, axis=1)
+
+
+def partial_kernel(n_buf, slots, table, *refs):
+    buffers = refs[:n_buf]
+    own = refs[n_buf : n_buf + 2]
+    sib = refs[n_buf + 2 : n_buf + 4]
+    keep_ref, send_ref = refs[n_buf + 4 :]
+    step = pl.program_id(0)
+    for lane in range(LANES):
+        at = slice(lane * BLK, (lane + 1) * BLK)
+        for side in range(2):
+            left = picked_rows(table, buffers, side, step * LANES + lane, slots)
+            right = jnp.concatenate((own[side][:, at], sib[side][:, at]), axis=0)
+            total = jnp.dot(left, right, preferred_element_type=jnp.float32)
+            keep_ref[side, :, at] = total
+            send_ref[side, :, at] = total.astype(jnp.bfloat16)
+
+
+def partial(table, buffers, w_in, w_out, s_in, s_out, core):
+    tokens = sum(b.shape[1] for b in buffers)
+    half = s_in.shape[1]
+    kept = w_in.shape[0]
+    wide = LANES * BLK
+    steps = half // wide
+    slots = 2 * kept // BLK
+    core_at = table.shape[0] - 1
+    whole = [pl.BlockSpec(b.shape, lambda g, t: (0, 0, 0)) for b in buffers]
+    own = pl.BlockSpec((kept, wide), lambda g, t: (0, t[core_at] * steps + g))
+    sib = pl.BlockSpec((kept, wide), lambda g, t: (0, g))
+    out = pl.BlockSpec((2, tokens, wide), lambda g, t: (0, 0, g))
+    return pl.pallas_call(
+        functools.partial(partial_kernel, len(buffers), slots),
+        grid_spec=pltpu.PrefetchScalarGridSpec(
+            num_scalar_prefetch=1,
+            grid=(steps,),
+            in_specs=whole + [own, own, sib, sib],
+            out_specs=[out, out],
+        ),
+        out_shape=[
+            jax.ShapeDtypeStruct((2, tokens, half), jnp.float32),
+            jax.ShapeDtypeStruct((2, tokens, half), jnp.bfloat16),
+        ],
+        compiler_params=pltpu.CompilerParams(vmem_limit_bytes=VMEM_LIMIT),
+        cost_estimate=pl.CostEstimate(flops=1000, bytes_accessed=1000, transcendentals=0),
+        name="partial",
+    )(table, *buffers, w_in, w_out, s_in, s_out)
+
+
+def grad_kernel(n_buf, slots, first, last, table, *refs):
+    buffers = refs[:n_buf]
+    keep_ref, got_ref = refs[n_buf : n_buf + 2]
+    refs = refs[n_buf + 2 :]
+    acc_ref = None
+    if not first:
+        acc_ref, refs = refs[0], refs[1:]
+    step = pl.program_id(0)
+    kept = slots * BLK // 2
+    for lane in range(LANES):
+        at = slice(lane * BLK, (lane + 1) * BLK)
+        hidden = keep_ref[0, :, at] + got_ref[0, :, at].astype(jnp.float32)
+        d_act = keep_ref[1, :, at] + got_ref[1, :, at].astype(jnp.float32)
+        square = hidden * hidden
+        tanh = jnp.tanh(SCALE * (hidden + CUBIC * square * hidden))
+        half_up = 0.5 * (1.0 + tanh)
+        act = hidden * half_up
+        slope = half_up + (0.5 * hidden) * (1.0 - tanh * tanh) * (SCALE + (3.0 * CUBIC * SCALE) * square)
+        rights = ((d_act * slope).astype(jnp.bfloat16), act.astype(jnp.bfloat16))
+        for side in range(2):
+            left = picked_rows(table, buffers, side, step * LANES + lane, slots)
+            total = lax.dot_general(
+                left, rights[side], (((0,), (0,)), ((), ())), preferred_element_type=jnp.float32
+            )
+            if not first:
+                total = total + acc_ref[side, :, at]
+            if last:
+                refs[side][:, at] = total[:kept].astype(jnp.bfloat16)
+                refs[2][side, :, at] = total[kept:].astype(jnp.bfloat16)
+            else:
+                refs[0][side, :, at] = total
+
+
+def grad(table, buffers, keep, got, acc, last):
+    tokens, half = keep.shape[1:]
+    wide = LANES * BLK
+    steps = half // wide
+    core_at = table.shape[0] - 1
+    slots = core_at // (half // BLK) // 2
+    kept = slots * BLK // 2
+    whole = [pl.BlockSpec(b.shape, lambda g, t: (0, 0, 0)) for b in buffers]
+    mixed = pl.BlockSpec((2, tokens, wide), lambda g, t: (0, 0, g))
+    sums = pl.BlockSpec((2, 2 * kept, wide), lambda g, t: (0, 0, g))
+    if last:
+        own = pl.BlockSpec((kept, wide), lambda g, t: (0, t[core_at] * steps + g))
+        out_specs = [own, own, pl.BlockSpec((2, kept, wide), lambda g, t: (0, 0, g))]
+        out_shape = [jax.ShapeDtypeStruct((kept, 2 * half), jnp.bfloat16)] * 2 + [
+            jax.ShapeDtypeStruct((2, kept, half), jnp.bfloat16)
+        ]
+    else:
+        out_specs = [sums]
+        out_shape = [jax.ShapeDtypeStruct((2, 2 * kept, half), jnp.float32)]
+    first = acc is None
+    return pl.pallas_call(
+        functools.partial(grad_kernel, len(buffers), slots, first, last),
+        grid_spec=pltpu.PrefetchScalarGridSpec(
+            num_scalar_prefetch=1,
+            grid=(steps,),
+            in_specs=whole + [mixed, mixed] + ([] if first else [sums]),
+            out_specs=out_specs,
+        ),
+        out_shape=out_shape,
+        compiler_params=pltpu.CompilerParams(vmem_limit_bytes=VMEM_LIMIT),
+        cost_estimate=pl.CostEstimate(flops=1000, bytes_accessed=1000, transcendentals=0),
+        name="grad_last" if last else "grad",
+    )(table, *buffers, keep, got, *(() if first else (acc,)))
+
+
+def place_kernel(core, got_ref, in_ref, out_ref, in_out, out_out):
+    in_out[...] = got_ref[0]
+    out_out[...] = got_ref[1]
+
+
+def place(core, got, g_in, g_out):
+    kept, half = got.shape[1:]
+    steps = half // (LANES * BLK)
+    anywhere = pl.BlockSpec(memory_space=pl.ANY)
+    theirs = pl.BlockSpec((kept, LANES * BLK), lambda g, c: (0, (1 - c[0]) * steps + g))
+    return pl.pallas_call(
+        place_kernel,
+        grid_spec=pltpu.PrefetchScalarGridSpec(
+            num_scalar_prefetch=1,
+            grid=(steps,),
+            in_specs=[pl.BlockSpec((2, kept, LANES * BLK), lambda g, c: (0, 0, g)), anywhere, anywhere],
+            out_specs=[theirs, theirs],
+        ),
+        out_shape=[jax.ShapeDtypeStruct(g_in.shape, g_in.dtype)] * 2,
+        input_output_aliases={2: 0, 3: 1},
+        name="place",
+    )(core, got, g_in, g_out)
+
+
+def fast(inputs, cotangent, w_in, w_out, keep_in, keep_out):
+    kept, width = w_in.shape
+    half = width // 2
+    here = half // BLK
+    mine = kept // BLK
+    row = lax.axis_index("row")
+    col = lax.axis_index("col")
+    core, x = row % 2, row // 2
+    z = col // 2
+    low = z < 2
+
+    over_x = [(r, r ^ 2) for r in range(ROWS)]
+    over_core = [(r, r ^ 1) for r in range(ROWS)]
+    over_y = [(c, c ^ 1) for c in range(COLS)]
+
+    def swap_x(v):
+        return lax.ppermute(v, "row", over_x)
+
+    def swap_core(v):
+        return lax.ppermute(v, "row", over_core)
+
+    def swap_y(v):
+        return lax.ppermute(v, "col", over_y)
+
+    def up(v, start):
+        return lax.ppermute(v, "col", [(c, c + 2) for c in range(2 * start, COLS - 2)])
+
+    def down(v, start):
+        return lax.ppermute(v, "col", [(c + 2, c) for c in range(COLS - 2 - 2 * start)])
+
+    gate = lax.optimization_barrier
+    own = jnp.stack((inputs, cotangent), 0)
+    other = swap_x(own)
+
+    first = col * 2 * here + core * here
+    pieces = []
+    for keep in (keep_in, keep_out):
+        rows = lax.dynamic_slice_in_dim(keep, first, here, 0)
+        pieces.append(
+            jnp.concatenate(
+                [lax.dynamic_slice_in_dim(rows, r * mine, mine, 1) for r in (row, row ^ 1)], axis=1
+            )
+        )
+    table = jnp.concatenate((jnp.stack(pieces, 1).reshape(-1), core.reshape(1).astype(jnp.int32)))
+
+    s_in, s_out = (
+        swap_core(lax.dynamic_slice_in_dim(w, (1 - core) * half, half, 1)) for w in (w_in, w_out)
+    )
+    other, table, s_in, s_out = gate((other, table, s_in, s_out))
+
+    lead = x == 0
+    m0 = jnp.concatenate((jnp.where(lead, own, other), jnp.where(lead, other, own)), axis=1)
+
+    def work(tokens):
+        return partial(table, tokens, w_in, w_out, s_in, s_out, core)
+
+    u1, d1, y0, c0 = up(m0, 0), down(m0, 0), swap_y(m0), swap_core(m0)
+    u1, d1, y0, c0, m0 = gate((u1, d1, y0, c0, m0))
+    m1 = jnp.where(low, d1, u1)
+    u2, d2, y1, c1, cy0 = up(u1, 1), down(d1, 1), swap_y(m1), swap_core(m1), swap_core(y0)
+    tok0 = (m0, y0, c0, cy0)
+    keep0, send0 = work(tok0)
+    u2, d2, y1, c1, m1, keep0, send0 = gate((u2, d2, y1, c1, m1, keep0, send0))
+    m2 = jnp.where(low, d2, u2)
+    u3, d3, y2, c2, cy1, got0 = up(u2, 2), down(d2, 2), swap_y(m2), swap_core(m2), swap_core(y1), swap_x(send0)
+    tok1 = (m1, y1, c1, cy1)
+    keep1, send1 = work(tok1)
+    u3, d3, y2, c2, m2, keep1, send1, got0 = gate((u3, d3, y2, c2, m2, keep1, send1, got0))
+    m3 = jnp.where(z == 0, d3, jnp.where(z == 1, u1, jnp.where(z == 2, d1, u3)))
+    y3, c3, cy2, got1 = swap_y(m3), swap_core(m3), swap_core(y2), swap_x(send1)
+    tok2 = (m2, y2, c2, cy2)
+    keep2, send2 = work(tok2)
+    (acc,) = grad(table, tok0, keep0, got0, None, False)
+    y3, c3, m3, keep2, send2, got1, acc = gate((y3, c3, m3, keep2, send2, got1, acc))
+    got2, cy3 = swap_x(send2), swap_core(y3)
+    tok3 = (m3, y3, c3, cy3)
+    keep3, send3 = work(tok3)
+    (acc,) = grad(table, tok1, keep1, got1, acc, False)
+    got2, keep3, send3, acc = gate((got2, keep3, send3, acc))
+    got3 = swap_x(send3)
+    (acc,) = grad(table, tok2, keep2, got2, acc, False)
+    got3, acc = gate((got3, acc))
+    g_in, g_out, away = grad(table, tok3, keep3, got3, acc, True)
+    return tuple(place(core.reshape(1).astype(jnp.int32), swap_core(away), g_in, g_out))
+
+
 def solution(mesh):
+    def per_device(inputs, cotangent, w_in, w_out, keep_in, keep_out):
+        kept, width = w_in.shape
+        fits = kept % BLK == 0 and width % (2 * LANES * BLK) == 0 and inputs.shape[0] % 16 == 0
+        chosen = fast if fits and mesh.shape["row"] == ROWS and mesh.shape["col"] == COLS else general
+        return chosen(inputs, cotangent, w_in, w_out, keep_in, keep_out)
+
     in_specs = (
         P(("row", "col"), None),
         P(("row", "col"), None),

time: 440 us -> 185 us (0.42)
  waiting for transfers between devices: 233 us -> 64.2 us
  local copies, waits for them, and re-layouts: 132 us -> 10.6 us
  Pallas kernels: 0 us -> 74.3 us
  matrix products: 30.5 us -> 0 us
  starting transfers between devices: 0.12 us -> 26.9 us
  other arithmetic: 27 us -> 6.2 us
  between operations: 13.8 us -> 1 us
    unnamed x4 -> x0, waiting for transfers between devices: 140 us -> none
    all_gather x2 -> x0, waiting for transfers between devices: 93.8 us -> none  [the longest x1 58 us: per_device(): whole = lax.all_gather(stacked, 'col', axis=1, tiled=True)]
    pallas_call x0 -> x9, Pallas kernels: none -> 74.3 us  [the longest x4 41.5 us: grad(): pl.pallas_call(functools.partial(grad_kernel, len(buffers), slots, first,...]
    ppermute x0 -> x26, waiting for transfers between devices: none -> 64.2 us  [the longest x5 16.6 us: swap_x(): return lax.ppermute(v, 'row', over_x)]
    gather x4 -> x0, local copies, waits for them, and re-layouts: 50.3 us -> none  [pick_one(): return jnp.take(matrix, chosen, axis=1)]
    all_gather x2 -> x0, local copies, waits for them, and re-layouts: 33.4 us -> none  [the longest x1 24.6 us: per_device(): full = lax.all_gather(weights, 'row', axis=0, tiled=True)]
    unnamed x8 -> x48, local copies, waits for them, and re-layouts: 39 us -> 5.95 us
    dot_general x2 -> x0, matrix products: 30.5 us -> none  [the longest x1 16.1 us: per_device(): jnp.einsum('ptck,ptcq->kpcq', picked, paired, preferred_element_type=jnp....]
  transfers between devices with their start and end apart: 3 -> 26, of which waited for: 3 -> 12; matrix products, arithmetic and copies ran while one was open for 20% -> 4% of each run, Pallas kernels for 0% -> 33%
where the time goes in v1:
time: 185 us; the launch traced here: 183 us
  Pallas kernels  74.3 us (40%)
  waiting for transfers between devices  64.2 us (35%)
  starting transfers between devices  26.9 us (15%)
  local copies, waits for them, and re-layouts  10.6 us (6%)
  other arithmetic  6.2 us (3%)
    pallas_call x4, Pallas kernels, grad(): pl.pallas_call(functools.partial(grad_kernel, len(buffers), slots, first,...  41.5 us
    pallas_call x4, Pallas kernels, partial(): pl.pallas_call(functools.partial(partial_kernel, len(buffers), slots), gr...  28.9 us
    ppermute x5, waiting for transfers between devices, swap_x(): return lax.ppermute(v, 'row', over_x)  16.6 us
    ppermute x3, waiting for transfers between devices, down(): lax.ppermute(v, 'col', [(c + 2, c) for c in range(COLS - 2 - 2 * start)])  16.1 us
    ppermute x4, waiting for transfers between devices, swap_y(): return lax.ppermute(v, 'col', over_y)  14.4 us
    ppermute x3, waiting for transfers between devices, up(): lax.ppermute(v, 'col', [(c, c + 2) for c in range(2 * start, COLS - 2)])  12.3 us
    ppermute x5, starting transfers between devices, swap_x(): return lax.ppermute(v, 'row', over_x)  8.36 us
    ppermute x3, starting transfers between devices, up(): lax.ppermute(v, 'col', [(c, c + 2) for c in range(2 * start, COLS - 2)])  7.84 us
  transfers between devices with their start and end apart: 26, of which 12 were waited for; matrix products, arithmetic and copies ran while one was open for 4% of the time, Pallas kernels for 33%

profile of v1, /device:TPU:0, one launch (start us, length us, event | category | flops | bytes accessed | tf_op | source)
XLA Modules:
  0.0 183.2 jit_solution(12229487398461306980)
XLA Ops:
  0.7 2.5 %constant_dynamic-slice_fusion.1 = bf16[384,1536]{1,0:T(8,128)(2,1)} fusion(bf16[384,3072]{1,0:T(8,128)(2,1)} %refs_4_.7, s32[]{:T(128)S(6)} %select_n.85), kind=kLoop, calls=%fused_computation.12 | loop fusion | bytes 2359300 | tf_op jit(solution)/shard_map/dynamic_slice | solution.py:258
  4.9 3.0 %collective-permute-start = (bf16[2,16,6144]{2,1,0:T(8,128)(2,1)S(1)}, bf16[2,16,6144]{2,1,0:T(8,128)(2,1)S(1)}, u32[]{:S(2)}, u32[]{:S(2)}) collective-permute-start(bf16[2,16,6144]{2,1,0:T(8,128)(2,1)S(1)} %pad_maximum_fusion.1), channel_id=1, source_target_pairs={{0,16},{8,24},{16,0},{24,8},{1,17},{9,25},{17,1},{25,9},{2,18},{10... | collective-permute-start | bytes 1179656 | tf_op jit(solution)/shard_map/ppermute | solution.py:228
  9.6 7.6 %collective-permute-done = bf16[2,16,6144]{2,1,0:T(8,128)(2,1)S(1)} collective-permute-done((bf16[2,16,6144]{2,1,0:T(8,128)(2,1)S(1)}, bf16[2,16,6144]{2,1,0:T(8,128)(2,1)S(1)}, u32[]{:S(2)}, u32[]{:S(2)}) %collective-permute-start) | collective-permute-done | bytes 393248 | tf_op jit(solution)/shard_map/ppermute | solution.py:228
  17.2 1.5 broadcast_select_fusion.3
  18.8 4.6 %collective-permute-start.3 = (bf16[2,32,6144]{2,1,0:T(8,128)(2,1)S(1)}, bf16[2,32,6144]{2,1,0:T(8,128)(2,1)}, u32[]{:S(2)}, u32[]{:S(2)}) collective-permute-start(bf16[2,32,6144]{2,1,0:T(8,128)(2,1)S(1)} %pad_maximum_fusion.refs_0_), channel_id=1, source_target_pairs={{0,2},{1,3},{2,4},{3,5},{4,6},{5,7},{8,10},{9,11},{10,12},{11,13},... | collective-permute-start | bytes 2359304 | tf_op jit(solution)/shard_map/ppermute | solution.py:237
  24.7 1.6 collective-permute-start.5
  26.3 12.3 %collective-permute-done.3 = bf16[2,32,6144]{2,1,0:T(8,128)(2,1)} collective-permute-done((bf16[2,32,6144]{2,1,0:T(8,128)(2,1)S(1)}, bf16[2,32,6144]{2,1,0:T(8,128)(2,1)}, u32[]{:S(2)}, u32[]{:S(2)}) %collective-permute-start.3) | collective-permute-done | bytes 786464 | tf_op jit(solution)/shard_map/ppermute | solution.py:237
  38.6 5.1 %collective-permute-done.4 = bf16[2,32,6144]{2,1,0:T(8,128)(2,1)} collective-permute-done((bf16[2,32,6144]{2,1,0:T(8,128)(2,1)S(1)}, bf16[2,32,6144]{2,1,0:T(8,128)(2,1)}, u32[]{:S(2)}, u32[]{:S(2)}) %collective-permute-start.4) | collective-permute-done | bytes 786464 | tf_op jit(solution)/shard_map/ppermute | solution.py:240
  45.6 1.5 collective-permute-start.9
  47.2 1.6 collective-permute-start.7
  50.9 7.2 %partial.4 = (f32[2,128,1536]{2,1,0:T(8,128)}, bf16[2,128,1536]{2,1,0:T(8,128)(2,1)}) custom-call(s32[145]{0:T(256)} %pad_add_fusion.1.table, bf16[2,32,6144]{2,1,0:T(8,128)(2,1)} %copy-done.5, bf16[2,32,6144]{2,1,0:T(8,128)(2,1)} %collective-permute-done.5.refs_1_, bf16[2,32,6144]{2,1,0:T(8,128)(2,1)} %collective-permute-done.6.refs_2_, ...), custom_call_target="tpu_custom_call" | custom-call | flops 1000 | bytes 1000 | tf_op jit(solution)/shard_map/partial/pallas_call | solution.py:102
  58.2 7.0 %collective-permute-done.9.refs_1_ = bf16[2,32,6144]{2,1,0:T(8,128)(2,1)S(1)} collective-permute-done((bf16[2,32,6144]{2,1,0:T(8,128)(2,1)S(1)}, bf16[2,32,6144]{2,1,0:T(8,128)(2,1)S(1)}, u32[]{:S(2)}, u32[]{:S(2)}) %collective-permute-start.9) | collective-permute-done | bytes 786464 | tf_op jit(solution)/shard_map/ppermute | solution.py:234
  65.2 6.7 %collective-permute-done.8 = bf16[2,32,6144]{2,1,0:T(8,128)(2,1)} collective-permute-done((bf16[2,32,6144]{2,1,0:T(8,128)(2,1)}, bf16[2,32,6144]{2,1,0:T(8,128)(2,1)}, u32[]{:S(2)}, u32[]{:S(2)}) %collective-permute-start.8) | collective-permute-done | bytes 786464 | tf_op jit(solution)/shard_map/ppermute | solution.py:240
  73.9 1.6 collective-permute-start.12
  77.7 1.5 collective-permute-start.17
  79.2 7.2 %partial.5 = (f32[2,128,1536]{2,1,0:T(8,128)}, bf16[2,128,1536]{2,1,0:T(8,128)(2,1)}) custom-call(s32[145]{0:T(256)} %pad_add_fusion.1.table, bf16[2,32,6144]{2,1,0:T(8,128)(2,1)} %copy-done.3, bf16[2,32,6144]{2,1,0:T(8,128)(2,1)} %copy-done.8, bf16[2,32,6144]{2,1,0:T(8,128)(2,1)} %copy-done.7, bf16[2,32,6144]{2,1,0:T(8,128)(2,1)} %copy-done.11, ...), custom_call_target="tpu_custom_call" | custom-call | flops 1000 | bytes 1000 | tf_op jit(solution)/shard_map/partial/pallas_call | solution.py:102
  86.5 6.6 %collective-permute-done.14.refs_1_ = bf16[2,32,6144]{2,1,0:T(8,128)(2,1)S(1)} collective-permute-done((bf16[2,32,6144]{2,1,0:T(8,128)(2,1)S(1)}, bf16[2,32,6144]{2,1,0:T(8,128)(2,1)S(1)}, u32[]{:S(2)}, u32[]{:S(2)}) %collective-permute-start.14) | collective-permute-done | bytes 786464 | tf_op jit(solution)/shard_map/ppermute | solution.py:234
  93.1 4.3 %collective-permute-done.13 = bf16[2,32,6144]{2,1,0:T(8,128)(2,1)} collective-permute-done((bf16[2,32,6144]{2,1,0:T(8,128)(2,1)}, bf16[2,32,6144]{2,1,0:T(8,128)(2,1)}, u32[]{:S(2)}, u32[]{:S(2)}) %collective-permute-start.13) | collective-permute-done | bytes 786464 | tf_op jit(solution)/shard_map/ppermute | solution.py:240
  97.8 1.5 select_select_fusion.refs_0_
  99.3 1.6 collective-permute-start.18
  101.1 1.5 collective-permute-start.21
  102.6 7.8 %grad.3.refs_6_ = f32[2,768,1536]{2,1,0:T(8,128)} custom-call(s32[145]{0:T(256)} %pad_add_fusion.1.table, bf16[2,32,6144]{2,1,0:T(8,128)(2,1)} %copy-done.5, bf16[2,32,6144]{2,1,0:T(8,128)(2,1)} %collective-permute-done.5.refs_1_, bf16[2,32,6144]{2,1,0:T(8,128)(2,1)} %collective-permute-done.6.refs_2_, bf16[2,32,6144]{2,1,0:T(8,128)(2,1)} %copy-done.13, ...), custom_call_target="tpu_custom_call" | custom-call | flops 1000 | bytes 1000 | tf_op jit(solution)/shard_map/grad/pallas_call | solution.py:173
  111.4 7.2 %partial.6 = (f32[2,128,1536]{2,1,0:T(8,128)}, bf16[2,128,1536]{2,1,0:T(8,128)(2,1)}) custom-call(s32[145]{0:T(256)} %pad_add_fusion.1.table, bf16[2,32,6144]{2,1,0:T(8,128)(2,1)} %copy-done.4, bf16[2,32,6144]{2,1,0:T(8,128)(2,1)} %copy-done.9, bf16[2,32,6144]{2,1,0:T(8,128)(2,1)} %copy-done.10, bf16[2,32,6144]{2,1,0:T(8,128)(2,1)} %copy-done.12, ...), custom_call_target="tpu_custom_call" | custom-call | flops 1000 | bytes 1000 | tf_op jit(solution)/shard_map/partial/pallas_call | solution.py:102
  119.3 1.5 collective-permute-done.21.refs_5_
  120.8 1.5 collective-permute-start.23
  122.3 11.9 %grad.4.refs_6_ = f32[2,768,1536]{2,1,0:T(8,128)} custom-call(s32[145]{0:T(256)} %pad_add_fusion.1.table, bf16[2,32,6144]{2,1,0:T(8,128)(2,1)} %copy-done.3, bf16[2,32,6144]{2,1,0:T(8,128)(2,1)} %copy-done.8, bf16[2,32,6144]{2,1,0:T(8,128)(2,1)} %copy-done.7, bf16[2,32,6144]{2,1,0:T(8,128)(2,1)} %copy-done.11, f32[2,128,1536]{2,1,0:T(8,128)} %get-tuple-element.85.refs_4_, ...), custom_call_target="tpu_custom_call" | custom-call | flops 1000 | bytes 1000 | tf_op jit(solution)/shard_map/grad/pallas_call | solution.py:173
  135.2 7.2 %partial.7 = (f32[2,128,1536]{2,1,0:T(8,128)}, bf16[2,128,1536]{2,1,0:T(8,128)(2,1)}) custom-call(s32[145]{0:T(256)} %pad_add_fusion.1.table, bf16[2,32,6144]{2,1,0:T(8,128)(2,1)} %copy-done.6, bf16[2,32,6144]{2,1,0:T(8,128)(2,1)} %copy-done.14, bf16[2,32,6144]{2,1,0:T(8,128)(2,1)} %copy-done.15, bf16[2,32,6144]{2,1,0:T(8,128)(2,1)} %copy-done.16, ...), custom_call_target="tpu_custom_call" | custom-call | flops 1000 | bytes 1000 | tf_op jit(solution)/shard_map/partial/pallas_call | solution.py:102
  143.3 11.8 %grad.5.refs_6_ = f32[2,768,1536]{2,1,0:T(8,128)} custom-call(s32[145]{0:T(256)} %pad_add_fusion.1.table, bf16[2,32,6144]{2,1,0:T(8,128)(2,1)} %copy-done.4, bf16[2,32,6144]{2,1,0:T(8,128)(2,1)} %copy-done.9, bf16[2,32,6144]{2,1,0:T(8,128)(2,1)} %copy-done.10, bf16[2,32,6144]{2,1,0:T(8,128)(2,1)} %copy-done.12, f32[2,128,1536]{2,1,0:T(8,128)} %get-tuple-element.90.refs_4_, ...), custom_call_target="tpu_custom_call" | custom-call | flops 1000 | bytes 1000 | tf_op jit(solution)/shard_map/grad/pallas_call | solution.py:173
  155.1 7.2 %collective-permute-done.24.refs_5_ = bf16[2,128,1536]{2,1,0:T(8,128)(2,1)S(1)} collective-permute-done((bf16[2,128,1536]{2,1,0:T(8,128)(2,1)}, bf16[2,128,1536]{2,1,0:T(8,128)(2,1)S(1)}, u32[]{:S(2)}, u32[]{:S(2)}) %collective-permute-start.24) | collective-permute-done | bytes 786464 | tf_op jit(solution)/shard_map/ppermute | solution.py:228
  163.1 10.0 %grad_last.1 = (bf16[384,3072]{1,0:T(8,128)(2,1)}, bf16[384,3072]{1,0:T(8,128)(2,1)}, bf16[2,384,1536]{2,1,0:T(8,128)(2,1)}) custom-call(s32[145]{0:T(256)} %pad_add_fusion.1.table, bf16[2,32,6144]{2,1,0:T(8,128)(2,1)} %copy-done.6, bf16[2,32,6144]{2,1,0:T(8,128)(2,1)} %copy-done.14, bf16[2,32,6144]{2,1,0:T(8,128)(2,1)} %copy-done.15, ...), custom_call_target="tpu_custom_call" | custom-call | flops 1000 | bytes 1000 | tf_op jit(solution)/shard_map/grad_last/pallas_call | solution.py:173
  173.2 4.7 %collective-permute-done.25.got_ref = bf16[2,384,1536]{2,1,0:T(8,128)(2,1)S(1)} collective-permute-done((bf16[2,384,1536]{2,1,0:T(8,128)(2,1)}, bf16[2,384,1536]{2,1,0:T(8,128)(2,1)S(1)}, u32[]{:S(2)}, u32[]{:S(2)}) %collective-permute-start.25) | collective-permute-done | bytes 2359328 | tf_op jit(solution)/shard_map/ppermute | solution.py:231
  179.3 3.9 %place.1 = (bf16[384,3072]{1,0:T(8,128)(2,1)}, bf16[384,3072]{1,0:T(8,128)(2,1)}) custom-call(s32[1]{0:T(128)} %bitcast.core, bf16[2,384,1536]{2,1,0:T(8,128)(2,1)} %copy-done.17, bf16[384,3072]{1,0:T(8,128)(2,1)} %get-tuple-element.96.in_ref, bf16[384,3072]{1,0:T(8,128)(2,1)} %get-tuple-element.97.out_ref), custom_call_target="tpu_custom_call", output_to_operand_aliasing={{0}: (2, {}), {1}: (3, {})} | custom-call | tf_op jit(solution)/shard_map/place/pallas_call | solution.py:198
  (92 shorter events, 19.2 us)
Async XLA Ops:
  3.2 13.9 %collective-permute-start.1 = (bf16[384,1536]{1,0:T(8,128)(2,1)}, bf16[384,1536]{1,0:T(8,128)(2,1)S(1)}, u32[]{:S(2)}, u32[]{:S(2)}) collective-permute-start(bf16[384,1536]{1,0:T(8,128)(2,1)} %constant_dynamic-slice_fusion.1), channel_id=1, source_target_pairs={{0,8},{8,0},{16,24},{24,16},{1,9},{9,1},{17,25},{25,17},{2,10},{10... | collective-permute-start | bytes 3538952 | tf_op jit(solution)/shard_map/ppermute | solution.py:231
  4.7 12.4 %collective-permute-start.2 = (bf16[384,1536]{1,0:T(8,128)(2,1)}, bf16[384,1536]{1,0:T(8,128)(2,1)S(1)}, u32[]{:S(2)}, u32[]{:S(2)}) collective-permute-start(bf16[384,1536]{1,0:T(8,128)(2,1)} %constant_dynamic-slice_fusion), channel_id=1, source_target_pairs={{0,8},{8,0},{16,24},{24,16},{1,9},{9,1},{17,25},{25,17},{2,10},{10... | collective-permute-start | bytes 3538952 | tf_op jit(solution)/shard_map/ppermute | solution.py:231
  4.9 12.3 %collective-permute-start = (bf16[2,16,6144]{2,1,0:T(8,128)(2,1)S(1)}, bf16[2,16,6144]{2,1,0:T(8,128)(2,1)S(1)}, u32[]{:S(2)}, u32[]{:S(2)}) collective-permute-start(bf16[2,16,6144]{2,1,0:T(8,128)(2,1)S(1)} %pad_maximum_fusion.1), channel_id=1, source_target_pairs={{0,16},{8,24},{16,0},{24,8},{1,17},{9,25},{17,1},{25,9},{2,18},{10... | collective-permute-start | bytes 1179656 | tf_op jit(solution)/shard_map/ppermute | solution.py:228
  17.2 27.9 %copy-start.1 = (bf16[384,1536]{1,0:T(8,128)(2,1)}, bf16[384,1536]{1,0:T(8,128)(2,1)S(1)}, u32[]{:S(2)}) copy-start(bf16[384,1536]{1,0:T(8,128)(2,1)S(1)} %collective-permute-done.1.refs_6_) | copy-start | bytes 3538948
  17.2 27.9 %copy-start.2 = (bf16[384,1536]{1,0:T(8,128)(2,1)}, bf16[384,1536]{1,0:T(8,128)(2,1)S(1)}, u32[]{:S(2)}) copy-start(bf16[384,1536]{1,0:T(8,128)(2,1)S(1)} %collective-permute-done.2.refs_7_) | copy-start | bytes 3538948
  18.8 25.0 %copy-start.5 = (bf16[2,32,6144]{2,1,0:T(8,128)(2,1)}, bf16[2,32,6144]{2,1,0:T(8,128)(2,1)S(1)}, u32[]{:S(2)}) copy-start(bf16[2,32,6144]{2,1,0:T(8,128)(2,1)S(1)} %pad_maximum_fusion.refs_0_) | copy-start | bytes 2359300
  18.8 19.8 %collective-permute-start.3 = (bf16[2,32,6144]{2,1,0:T(8,128)(2,1)S(1)}, bf16[2,32,6144]{2,1,0:T(8,128)(2,1)}, u32[]{:S(2)}, u32[]{:S(2)}) collective-permute-start(bf16[2,32,6144]{2,1,0:T(8,128)(2,1)S(1)} %pad_maximum_fusion.refs_0_), channel_id=1, source_target_pairs={{0,2},{1,3},{2,4},{3,5},{4,6},{5,7},{8,10},{9,11},{10,12},{11,13},... | collective-permute-start | bytes 2359304 | tf_op jit(solution)/shard_map/ppermute | solution.py:237
  23.4 20.3 %collective-permute-start.4 = (bf16[2,32,6144]{2,1,0:T(8,128)(2,1)S(1)}, bf16[2,32,6144]{2,1,0:T(8,128)(2,1)}, u32[]{:S(2)}, u32[]{:S(2)}) collective-permute-start(bf16[2,32,6144]{2,1,0:T(8,128)(2,1)S(1)} %pad_maximum_fusion.refs_0_), channel_id=1, source_target_pairs={{2,0},{3,1},{4,2},{5,3},{6,4},{7,5},{10,8},{11,9},{12,10},{13,11},... | collective-permute-start | bytes 2359304 | tf_op jit(solution)/shard_map/ppermute | solution.py:240
  24.7 19.0 %collective-permute-start.5 = (bf16[2,32,6144]{2,1,0:T(8,128)(2,1)S(1)}, bf16[2,32,6144]{2,1,0:T(8,128)(2,1)}, u32[]{:S(2)}, u32[]{:S(2)}) collective-permute-start(bf16[2,32,6144]{2,1,0:T(8,128)(2,1)S(1)} %pad_maximum_fusion.refs_0_), channel_id=1, source_target_pairs={{0,1},{1,0},{2,3},{3,2},{4,5},{5,4},{6,7},{7,6},{8,9},{9,8},{10,11... | collective-permute-start | bytes 2359304 | tf_op jit(solution)/shard_map/ppermute | solution.py:234
  26.3 17.4 %collective-permute-start.6 = (bf16[2,32,6144]{2,1,0:T(8,128)(2,1)S(1)}, bf16[2,32,6144]{2,1,0:T(8,128)(2,1)}, u32[]{:S(2)}, u32[]{:S(2)}) collective-permute-start(bf16[2,32,6144]{2,1,0:T(8,128)(2,1)S(1)} %pad_maximum_fusion.refs_0_), channel_id=1, source_target_pairs={{0,8},{8,0},{16,24},{24,16},{1,9},{9,1},{17,25},{25,17},{2,10},{10... | collective-permute-start | bytes 2359304 | tf_op jit(solution)/shard_map/ppermute | solution.py:231
  43.7 6.3 %collective-permute-start.11 = (bf16[2,32,6144]{2,1,0:T(8,128)(2,1)}, bf16[2,32,6144]{2,1,0:T(8,128)(2,1)S(1)}, u32[]{:S(2)}, u32[]{:S(2)}) collective-permute-start(bf16[2,32,6144]{2,1,0:T(8,128)(2,1)} %collective-permute-done.5.refs_1_), channel_id=1, source_target_pairs={{0,8},{8,0},{16,24},{24,16},{1,9},{9,1},{17,25},{25,17},{2,10},{10... | collective-permute-start | bytes 2359304 | tf_op jit(solution)/shard_map/ppermute | solution.py:231
  45.1 13.0 %collective-permute-start.10 = (bf16[2,32,6144]{2,1,0:T(8,128)(2,1)S(1)}, bf16[2,32,6144]{2,1,0:T(8,128)(2,1)S(1)}, u32[]{:S(2)}, u32[]{:S(2)}) collective-permute-start(bf16[2,32,6144]{2,1,0:T(8,128)(2,1)S(1)} %broadcast_select_fusion.1.refs_0_), channel_id=1, source_target_pairs={{0,8},{8,0},{16,24},{24,16},{1,9},{9,1},{17,25},{25,17},{2,10},{10... | collective-permute-start | bytes 2359304 | tf_op jit(solution)/shard_map/ppermute | solution.py:231
  45.6 19.5 %collective-permute-start.9 = (bf16[2,32,6144]{2,1,0:T(8,128)(2,1)S(1)}, bf16[2,32,6144]{2,1,0:T(8,128)(2,1)S(1)}, u32[]{:S(2)}, u32[]{:S(2)}) collective-permute-start(bf16[2,32,6144]{2,1,0:T(8,128)(2,1)S(1)} %broadcast_select_fusion.1.refs_0_), channel_id=1, source_target_pairs={{0,1},{1,0},{2,3},{3,2},{4,5},{5,4},{6,7},{7,6},{8,9},{9,8},{10,11... | collective-permute-start | bytes 2359304 | tf_op jit(solution)/shard_map/ppermute | solution.py:234
  47.2 18.0 %collective-permute-start.7 = (bf16[2,32,6144]{2,1,0:T(8,128)(2,1)}, bf16[2,32,6144]{2,1,0:T(8,128)(2,1)}, u32[]{:S(2)}, u32[]{:S(2)}) collective-permute-start(bf16[2,32,6144]{2,1,0:T(8,128)(2,1)} %collective-permute-done.3), channel_id=1, source_target_pairs={{2,4},{3,5},{4,6},{5,7},{10,12},{11,13},{12,14},{13,15},{18,20},{1... | collective-permute-start | bytes 2359304 | tf_op jit(solution)/shard_map/ppermute | solution.py:237
  48.7 23.1 %collective-permute-start.8 = (bf16[2,32,6144]{2,1,0:T(8,128)(2,1)}, bf16[2,32,6144]{2,1,0:T(8,128)(2,1)}, u32[]{:S(2)}, u32[]{:S(2)}) collective-permute-start(bf16[2,32,6144]{2,1,0:T(8,128)(2,1)} %collective-permute-done.4), channel_id=1, source_target_pairs={{2,0},{3,1},{4,2},{5,3},{10,8},{11,9},{12,10},{13,11},{18,16},{19,... | collective-permute-start | bytes 2359304 | tf_op jit(solution)/shard_map/ppermute | solution.py:240
  71.8 5.0 %collective-permute-start.16 = (bf16[2,32,6144]{2,1,0:T(8,128)(2,1)S(1)}, bf16[2,32,6144]{2,1,0:T(8,128)(2,1)S(1)}, u32[]{:S(2)}, u32[]{:S(2)}) collective-permute-start(bf16[2,32,6144]{2,1,0:T(8,128)(2,1)S(1)} %collective-permute-done.9.refs_1_), channel_id=1, source_target_pairs={{0,8},{8,0},{16,24},{24,16},{1,9},{9,1},{17,25},{25,17},{2,10},{10... | collective-permute-start | bytes 2359304 | tf_op jit(solution)/shard_map/ppermute | solution.py:231
  73.1 20.0 %collective-permute-start.14 = (bf16[2,32,6144]{2,1,0:T(8,128)(2,1)S(1)}, bf16[2,32,6144]{2,1,0:T(8,128)(2,1)S(1)}, u32[]{:S(2)}, u32[]{:S(2)}) collective-permute-start(bf16[2,32,6144]{2,1,0:T(8,128)(2,1)S(1)} %broadcast_select_fusion.refs_0_), channel_id=1, source_target_pairs={{0,1},{1,0},{2,3},{3,2},{4,5},{5,4},{6,7},{7,6},{8,9},{9,8},{10,11... | collective-permute-start | bytes 2359304 | tf_op jit(solution)/shard_map/ppermute | solution.py:234
  73.7 19.5 %collective-permute-start.15 = (bf16[2,32,6144]{2,1,0:T(8,128)(2,1)S(1)}, bf16[2,32,6144]{2,1,0:T(8,128)(2,1)S(1)}, u32[]{:S(2)}, u32[]{:S(2)}) collective-permute-start(bf16[2,32,6144]{2,1,0:T(8,128)(2,1)S(1)} %broadcast_select_fusion.refs_0_), channel_id=1, source_target_pairs={{0,8},{8,0},{16,24},{24,16},{1,9},{9,1},{17,25},{25,17},{2,10},{10... | collective-permute-start | bytes 2359304 | tf_op jit(solution)/shard_map/ppermute | solution.py:231
  73.9 19.2 %collective-permute-start.12 = (bf16[2,32,6144]{2,1,0:T(8,128)(2,1)}, bf16[2,32,6144]{2,1,0:T(8,128)(2,1)}, u32[]{:S(2)}, u32[]{:S(2)}) collective-permute-start(bf16[2,32,6144]{2,1,0:T(8,128)(2,1)} %collective-permute-done.7), channel_id=1, source_target_pairs={{4,6},{5,7},{12,14},{13,15},{20,22},{21,23},{28,30},{29,31}} | collective-permute-start | bytes 2359304 | tf_op jit(solution)/shard_map/ppermute | solution.py:237
  75.5 21.9 %collective-permute-start.13 = (bf16[2,32,6144]{2,1,0:T(8,128)(2,1)}, bf16[2,32,6144]{2,1,0:T(8,128)(2,1)}, u32[]{:S(2)}, u32[]{:S(2)}) collective-permute-start(bf16[2,32,6144]{2,1,0:T(8,128)(2,1)} %collective-permute-done.8), channel_id=1, source_target_pairs={{2,0},{3,1},{10,8},{11,9},{18,16},{19,17},{26,24},{27,25}} | collective-permute-start | bytes 2359304 | tf_op jit(solution)/shard_map/ppermute | solution.py:240
  77.7 20.0 %collective-permute-start.17 = (bf16[2,128,1536]{2,1,0:T(8,128)(2,1)}, bf16[2,128,1536]{2,1,0:T(8,128)(2,1)}, u32[]{:S(2)}, u32[]{:S(2)}) collective-permute-start(bf16[2,128,1536]{2,1,0:T(8,128)(2,1)} %get-tuple-element.68), channel_id=1, source_target_pairs={{0,16},{8,24},{16,0},{24,8},{1,17},{9,25},{17,1},{25,9},{2,18},{10... | collective-permute-start | bytes 2359304 | tf_op jit(solution)/shard_map/ppermute | solution.py:228
  93.1 17.3 %copy-start.9 = (bf16[2,32,6144]{2,1,0:T(8,128)(2,1)}, bf16[2,32,6144]{2,1,0:T(8,128)(2,1)S(1)}, u32[]{:S(2)}) copy-start(bf16[2,32,6144]{2,1,0:T(8,128)(2,1)S(1)} %collective-permute-done.14.refs_1_) | copy-start | bytes 2359300
  93.1 17.3 %copy-start.10 = (bf16[2,32,6144]{2,1,0:T(8,128)(2,1)}, bf16[2,32,6144]{2,1,0:T(8,128)(2,1)S(1)}, u32[]{:S(2)}) copy-start(bf16[2,32,6144]{2,1,0:T(8,128)(2,1)S(1)} %collective-permute-done.15.refs_2_) | copy-start | bytes 2359300
  97.8 12.7 %collective-permute-start.20 = (bf16[2,32,6144]{2,1,0:T(8,128)(2,1)S(1)}, bf16[2,32,6144]{2,1,0:T(8,128)(2,1)S(1)}, u32[]{:S(2)}, u32[]{:S(2)}) collective-permute-start(bf16[2,32,6144]{2,1,0:T(8,128)(2,1)S(1)} %collective-permute-done.14.refs_1_), channel_id=1, source_target_pairs={{0,8},{8,0},{16,24},{24,16},{1,9},{9,1},{17,25},{25,17},{2,10},{10... | collective-permute-start | bytes 2359304 | tf_op jit(solution)/shard_map/ppermute | solution.py:231
  99.3 20.0 %collective-permute-start.18 = (bf16[2,32,6144]{2,1,0:T(8,128)(2,1)S(1)}, bf16[2,32,6144]{2,1,0:T(8,128)(2,1)S(1)}, u32[]{:S(2)}, u32[]{:S(2)}) collective-permute-start(bf16[2,32,6144]{2,1,0:T(8,128)(2,1)S(1)} %select_select_fusion.refs_0_), channel_id=1, source_target_pairs={{0,1},{1,0},{2,3},{3,2},{4,5},{5,4},{6,7},{7,6},{8,9},{9,8},{10,11... | collective-permute-start | bytes 2359304 | tf_op jit(solution)/shard_map/ppermute | solution.py:234
  100.9 18.4 %collective-permute-start.19 = (bf16[2,32,6144]{2,1,0:T(8,128)(2,1)S(1)}, bf16[2,32,6144]{2,1,0:T(8,128)(2,1)S(1)}, u32[]{:S(2)}, u32[]{:S(2)}) collective-permute-start(bf16[2,32,6144]{2,1,0:T(8,128)(2,1)S(1)} %select_select_fusion.refs_0_), channel_id=1, source_target_pairs={{0,8},{8,0},{16,24},{24,16},{1,9},{9,1},{17,25},{25,17},{2,10},{10... | collective-permute-start | bytes 2359304 | tf_op jit(solution)/shard_map/ppermute | solution.py:231
  101.1 19.7 %collective-permute-start.21 = (bf16[2,128,1536]{2,1,0:T(8,128)(2,1)S(1)}, bf16[2,128,1536]{2,1,0:T(8,128)(2,1)S(1)}, u32[]{:S(2)}, u32[]{:S(2)}) collective-permute-start(bf16[2,128,1536]{2,1,0:T(8,128)(2,1)S(1)} %copy-done.23), channel_id=1, source_target_pairs={{0,16},{8,24},{16,0},{24,8},{1,17},{9,25},{17,1},{25,9},{2,18},{10... | collective-permute-start | bytes 2359304 | tf_op jit(solution)/shard_map/ppermute | solution.py:228
  119.3 14.9 %copy-start.14 = (bf16[2,32,6144]{2,1,0:T(8,128)(2,1)}, bf16[2,32,6144]{2,1,0:T(8,128)(2,1)S(1)}, u32[]{:S(2)}) copy-start(bf16[2,32,6144]{2,1,0:T(8,128)(2,1)S(1)} %collective-permute-done.18.refs_1_) | copy-start | bytes 2359300
  120.8 13.4 %collective-permute-start.22 = (bf16[2,32,6144]{2,1,0:T(8,128)(2,1)S(1)}, bf16[2,32,6144]{2,1,0:T(8,128)(2,1)S(1)}, u32[]{:S(2)}, u32[]{:S(2)}) collective-permute-start(bf16[2,32,6144]{2,1,0:T(8,128)(2,1)S(1)} %collective-permute-done.18.refs_1_), channel_id=1, source_target_pairs={{0,8},{8,0},{16,24},{24,16},{1,9},{9,1},{17,25},{25,17},{2,10},{10... | collective-permute-start | bytes 2359304 | tf_op jit(solution)/shard_map/ppermute | solution.py:231
  120.8 21.5 %collective-permute-start.23 = (bf16[2,128,1536]{2,1,0:T(8,128)(2,1)}, bf16[2,128,1536]{2,1,0:T(8,128)(2,1)S(1)}, u32[]{:S(2)}, u32[]{:S(2)}) collective-permute-start(bf16[2,128,1536]{2,1,0:T(8,128)(2,1)} %get-tuple-element.82), channel_id=1, source_target_pairs={{0,16},{8,24},{16,0},{24,8},{1,17},{9,25},{17,1},{25,9},{2,18},{10... | collective-permute-start | bytes 2359304 | tf_op jit(solution)/shard_map/ppermute | solution.py:228
  142.4 19.9 %collective-permute-start.24 = (bf16[2,128,1536]{2,1,0:T(8,128)(2,1)}, bf16[2,128,1536]{2,1,0:T(8,128)(2,1)S(1)}, u32[]{:S(2)}, u32[]{:S(2)}) collective-permute-start(bf16[2,128,1536]{2,1,0:T(8,128)(2,1)} %get-tuple-element.89), channel_id=1, source_target_pairs={{0,16},{8,24},{16,0},{24,8},{1,17},{9,25},{17,1},{25,9},{2,18},{10... | collective-permute-start | bytes 2359304 | tf_op jit(solution)/shard_map/ppermute | solution.py:228
  173.2 4.7 %collective-permute-start.25 = (bf16[2,384,1536]{2,1,0:T(8,128)(2,1)}, bf16[2,384,1536]{2,1,0:T(8,128)(2,1)S(1)}, u32[]{:S(2)}, u32[]{:S(2)}) collective-permute-start(bf16[2,384,1536]{2,1,0:T(8,128)(2,1)} %get-tuple-element.95), channel_id=1, source_target_pairs={{0,8},{8,0},{16,24},{24,16},{1,9},{9,1},{17,25},{25,17},{2,10},{10... | collective-permute-start | bytes 7077896 | tf_op jit(solution)/shard_map/ppermute | solution.py:231
  (18 other events, 115.7 us)

commit v2 on v0

--- a/solution.py
+++ b/solution.py
@@ -1,11 +1,25 @@
+import functools
+
 import jax
 import jax.numpy as jnp
 from jax import lax
+from jax.experimental import pallas as pl
+from jax.experimental.pallas import tpu as pltpu
 from jax.sharding import PartitionSpec as P
 
 D = 6144
 BLK = 128
 KEEP = 12
+ROWS = 4
+COLS = 8
+LANES = 4
+SCALE = 0.7978845608028654
+CUBIC = 0.044715
+PARTIAL_VMEM = 20 * 1024 * 1024
+GRAD_VMEM = 24 * 1024 * 1024
+TOTAL_VMEM = 12 * 1024 * 1024
+TOTAL_LANES = 6
+COST = pl.CostEstimate(flops=0, bytes_accessed=0, transcendentals=0)
 
 
 def gelu_tanh(values):
@@ -16,7 +30,7 @@
     return jnp.take(matrix, chosen, axis=1)
 
 
-def per_device(inputs, cotangent, w_in, w_out, keep_in, keep_out):
+def general(inputs, cotangent, w_in, w_out, keep_in, keep_out):
     width = w_in.shape[1]
     blocks_here = width // BLK
     kept_rows = w_in.shape[0]
@@ -53,7 +67,237 @@
     return (summed[:, 0].astype(jnp.bfloat16), summed[:, 1].astype(jnp.bfloat16))
 
 
+def picked_rows(table, buffers, side, block, slots):
+    columns = []
+    for slot in range(slots):
+        start = pl.multiple_of(table[(block * 2 + side) * slots + slot] * BLK, BLK)
+        columns.append(jnp.concatenate([buf[side, :, pl.ds(start, BLK)] for buf in buffers], axis=0))
+    return jnp.concatenate(columns, axis=1)
+
+
+def fixed(array):
+    return pl.BlockSpec(array.shape, lambda g, t: (0,) * array.ndim)
+
+
+def partial_kernel(n_buf, slots, base, table, *refs):
+    buffers = refs[:n_buf]
+    own = refs[n_buf : n_buf + 2]
+    sib = refs[n_buf + 2 : n_buf + 4]
+    keep_ref, send_ref = refs[n_buf + 4 :]
+    step = pl.program_id(0)
+    for lane in range(LANES):
+        at = slice(lane * BLK, (lane + 1) * BLK)
+        for side in range(2):
+            left = picked_rows(table, buffers, side, base + step * LANES + lane, slots)
+            right = jnp.concatenate((own[side][:, at], sib[side][:, at]), axis=0)
+            total = jnp.dot(left, right, preferred_element_type=jnp.float32)
+            keep_ref[side, :, at] = total
+            send_ref[side, :, at] = total.astype(jnp.bfloat16)
+
+
+def partial(table, buffers, weights, part=0, parts=1):
+    tokens = sum(b.shape[1] for b in buffers)
+    kept, width = weights[0].shape
+    wide = LANES * BLK
+    steps = width // wide // parts
+    weight = pl.BlockSpec((kept, wide), lambda g, t: (0, part * steps + g))
+    out = pl.BlockSpec((2, tokens, wide), lambda g, t: (0, 0, g))
+    return pl.pallas_call(
+        functools.partial(partial_kernel, len(buffers), 2 * kept // BLK, part * steps * LANES),
+        grid_spec=pltpu.PrefetchScalarGridSpec(
+            num_scalar_prefetch=1,
+            grid=(steps,),
+            in_specs=[fixed(b) for b in buffers] + [weight] * 4,
+            out_specs=[out, out],
+        ),
+        out_shape=[
+            jax.ShapeDtypeStruct((2, tokens, width // parts), dtype) for dtype in (jnp.float32, jnp.bfloat16)
+        ],
+        compiler_params=pltpu.CompilerParams(vmem_limit_bytes=PARTIAL_VMEM),
+        cost_estimate=COST,
+        name="partial",
+    )(table, *buffers, *weights)
+
+
+def grad_kernel(units, n_buf, n_keep, n_got, slots, base, table, *refs):
+    buffers = refs[:n_buf]
+    keeps = refs[n_buf : n_buf + n_keep]
+    gots = refs[n_buf + n_keep : n_buf + n_keep + n_got]
+    own_ref, away_ref = refs[n_buf + n_keep + n_got :]
+    step = pl.program_id(0)
+    kept = slots * BLK // 2
+    rows = 2 * buffers[0].shape[1]
+    for lane in range(LANES):
+        at = slice(lane * BLK, (lane + 1) * BLK)
+
+        def gathered(side):
+            mine, theirs = [], []
+            for keep, keep_at, got, got_at in units:
+                mine.append(keeps[keep][side, keep_at * rows : (keep_at + 1) * rows, at])
+                theirs.append(gots[got][side, got_at * rows : (got_at + 1) * rows, at])
+            return jnp.concatenate(mine, axis=0) + jnp.concatenate(theirs, axis=0).astype(jnp.float32)
+
+        hidden, d_act = gathered(0), gathered(1)
+        square = hidden * hidden
+        tanh = jnp.tanh(SCALE * (hidden + CUBIC * square * hidden))
+        half_up = 0.5 * (1.0 + tanh)
+        act = (hidden * half_up).astype(jnp.bfloat16)
+        slope = half_up + (0.5 * hidden) * (1.0 - tanh * tanh) * (SCALE + (3.0 * CUBIC * SCALE) * square)
+        d_hidden = (d_act * slope).astype(jnp.bfloat16)
+        for side, right in enumerate((d_hidden, act)):
+            left = picked_rows(table, buffers, side, base + step * LANES + lane, slots)
+            total = lax.dot_general(left, right, (((0,), (0,)), ((), ())), preferred_element_type=jnp.float32)
+            total = total.astype(jnp.bfloat16)
+            own_ref[side, :, at] = total[:kept]
+            away_ref[side, :, at] = total[kept:]
+
+
+def grad(table, units, buffers, keeps, gots, kept, part, parts):
+    width = max(keep.shape[2] for keep in keeps)
+    wide = LANES * BLK
+    steps = width // wide // parts
+
+    def spec(array):
+        first = part * steps if array.shape[2] == width else 0
+        return pl.BlockSpec((2, array.shape[1], wide), lambda g, t: (0, 0, first + g))
+
+    out = pl.BlockSpec((2, kept, wide), lambda g, t: (0, 0, g))
+    return pl.pallas_call(
+        functools.partial(
+            grad_kernel, units, len(buffers), len(keeps), len(gots), 2 * kept // BLK, part * steps * LANES
+        ),
+        grid_spec=pltpu.PrefetchScalarGridSpec(
+            num_scalar_prefetch=1,
+            grid=(steps,),
+            in_specs=[fixed(b) for b in buffers] + [spec(v) for v in (*keeps, *gots)],
+            out_specs=[out, out],
+        ),
+        out_shape=[jax.ShapeDtypeStruct((2, kept, width // parts), jnp.bfloat16)] * 2,
+        compiler_params=pltpu.CompilerParams(vmem_limit_bytes=GRAD_VMEM),
+        cost_estimate=COST,
+        name="grad",
+    )(table, *buffers, *keeps, *gots)
+
+
+def total_kernel(own_ref, got_ref, *refs):
+    for side, ref in enumerate(refs[-2:]):
+        ref[...] = (own_ref[side].astype(jnp.float32) + got_ref[side].astype(jnp.float32)).astype(ref.dtype)
+
+
+def total(own, got, before, part, parts):
+    kept, width = own.shape[1:]
+    wide = TOTAL_LANES * BLK
+    steps = width // wide
+    source = pl.BlockSpec((2, kept, wide), lambda g: (0, 0, g))
+    out = pl.BlockSpec((kept, wide), lambda g: (0, part * steps + g))
+    return pl.pallas_call(
+        total_kernel,
+        grid=(steps,),
+        in_specs=[source, source] + [pl.BlockSpec(memory_space=pl.ANY)] * len(before),
+        out_specs=[out, out],
+        out_shape=[jax.ShapeDtypeStruct((kept, width * parts), jnp.bfloat16)] * 2,
+        input_output_aliases={2: 0, 3: 1} if before else {},
+        compiler_params=pltpu.CompilerParams(vmem_limit_bytes=TOTAL_VMEM),
+        cost_estimate=COST,
+        name="total",
+    )(own, got, *before)
+
+
+def fast(inputs, cotangent, w_in, w_out, keep_in, keep_out):
+    kept, width = w_in.shape
+    here = width // BLK
+    mine = kept // BLK
+    row = lax.axis_index("row")
+    col = lax.axis_index("col")
+
+    def swap_x(v):
+        return lax.ppermute(v, "row", [(r, r ^ 2) for r in range(ROWS)])
+
+    def swap_core(v):
+        return lax.ppermute(v, "row", [(r, r ^ 1) for r in range(ROWS)])
+
+    def swap_y(v):
+        return lax.ppermute(v, "col", [(c, c ^ 1) for c in range(COLS)])
+
+    def near(v):
+        return lax.ppermute(v, "col", [(c, c ^ 2) for c in range(COLS)])
+
+    def far(v):
+        return lax.ppermute(v, "col", [(c, c ^ 4) for c in range(COLS)])
+
+    gate = lax.optimization_barrier
+
+    a0 = jnp.stack((inputs, cotangent), 0)
+    b0 = swap_x(a0)
+    ya0 = swap_y(a0)
+    a1 = near(a0)
+    a2 = far(a0)
+    s_in = swap_core(w_in)
+    pieces = []
+    for keep in (keep_in, keep_out):
+        rows = lax.dynamic_slice_in_dim(keep, col * here, here, 0)
+        pieces += [lax.dynamic_slice_in_dim(rows, r * mine, mine, 1) for r in (row, row ^ 1)]
+    table = jnp.concatenate(pieces, axis=1).reshape(-1)
+    b0, ya0, a1, a0, s_in, table, w_late = gate((b0, ya0, a1, a0, s_in, table, w_out))
+    s_out = swap_core(w_late)
+    yb0 = swap_y(b0)
+    b1 = near(b0)
+    b2 = far(b0)
+    s_out, a1 = gate((s_out, a1))
+    weights = (w_in, w_out, s_in, s_out)
+    ya1 = swap_y(a1)
+    keep0, send0 = partial(table, (a0, ya0), weights)
+    yb0, a2, send0, b0 = gate((yb0, a2, send0, b0))
+    got0 = swap_x(send0)
+    ya2 = swap_y(a2)
+    a3 = near(a2)
+    keep1, send1 = partial(table, (b0, yb0), weights)
+    ya1, b1, send1 = gate((ya1, b1, send1))
+    got1 = swap_x(send1)
+    yb1 = swap_y(b1)
+    ya2, b2, a1, a2, ya1 = gate((ya2, b2, a1, a2, ya1))
+    b3 = near(b2)
+    keep2, send2 = partial(table, (a1, ya1, a2, ya2), weights)
+    yb1, a3, send2, got0 = gate((yb1, a3, send2, got0))
+    got2 = swap_x(send2)
+    ya3 = swap_y(a3)
+    yb2 = swap_y(b2)
+    ya3, b3, got1, b1, yb1, a3 = gate((ya3, b3, got1, b1, yb1, a3))
+    yb3 = swap_y(b3)
+    keep3, send3 = partial(table, (b1, yb1, a3, ya3), weights)
+    yb2, send3, b2 = gate((yb2, send3, b2))
+    got3 = swap_x(send3)
+    keep4, send4 = partial(table, (b2, yb2), weights)
+    yb3, send4, got2, b3 = gate((yb3, send4, got2, b3))
+    got4 = swap_x(send4)
+    keep5, send5 = partial(table, (b3, yb3), weights, 0, 2)
+    send5, got3, b3, yb3 = gate((send5, got3, b3, yb3))
+    got5 = swap_x(send5)
+    keep6, send6 = partial(table, (b3, yb3), weights, 1, 2)
+    got6 = swap_x(send6)
+
+    buffers = (a0, ya0, b0, yb0, a1, ya1, a2, ya2, b1, yb1, a3, ya3, b2, yb2, b3, yb3)
+    units = ((0, 0, 1, 0), (1, 0, 0, 0), (2, 0, 3, 0), (2, 1, 4, 0), (3, 0, 2, 0), (3, 1, 5, 0), (4, 0, 2, 1), (5, 0, 3, 1))
+    keeps = (keep0, keep1, keep2, keep3, keep4)
+    gots = (got0, got1, got2, got3, got4)
+    own0, away0 = grad(table, units, buffers, (*keeps, keep5), (*gots, got5), kept, 0, 2)
+    own0, away0, got6 = gate((own0, away0, got6))
+    back0 = swap_core(away0)
+    own1, away1 = grad(table, units, buffers, (*keeps, keep6), (*gots, got6), kept, 1, 2)
+    own1, away1, back0 = gate((own1, away1, back0))
+    back1 = swap_core(away1)
+    outs = total(own0, back0, (), 0, 2)
+    return tuple(total(own1, back1, tuple(outs), 1, 2))
+
+
 def solution(mesh):
+    def per_device(inputs, cotangent, w_in, w_out, keep_in, keep_out):
+        kept, width = w_in.shape
+        fits = kept % BLK == 0 and inputs.shape[0] % 16 == 0
+        fits = fits and all(width % (2 * lanes * BLK) == 0 for lanes in (LANES, TOTAL_LANES))
+        chosen = fast if fits and mesh.shape["row"] == ROWS and mesh.shape["col"] == COLS else general
+        return chosen(inputs, cotangent, w_in, w_out, keep_in, keep_out)
+
     in_specs = (
         P(("row", "col"), None),
         P(("row", "col"), None),

time: 440 us -> 132 us (0.30)
  waiting for transfers between devices: 233 us -> 58.3 us
  local copies, waits for them, and re-layouts: 132 us -> 5.07 us
  Pallas kernels: 0 us -> 40.5 us
  matrix products: 30.5 us -> 0 us
  starting transfers between devices: 0.12 us -> 25.7 us
  other arithmetic: 27 us -> 1.67 us
  between operations: 13.8 us -> 0.8 us
    unnamed x4 -> x0, waiting for transfers between devices: 140 us -> none
    all_gather x2 -> x0, waiting for transfers between devices: 93.8 us -> none  [the longest x1 58 us: per_device(): whole = lax.all_gather(stacked, 'col', axis=1, tiled=True)]
    ppermute x0 -> x26, waiting for transfers between devices: none -> 58.3 us  [the longest x8 17.3 us: swap_x(): return lax.ppermute(v, 'row', [(r, r ^ 2) for r in range(ROWS)])]
    gather x4 -> x0, local copies, waits for them, and re-layouts: 50.3 us -> none  [pick_one(): return jnp.take(matrix, chosen, axis=1)]
    pallas_call x0 -> x11, Pallas kernels: none -> 40.5 us  [the longest x7 24.8 us: partial(): pl.pallas_call(functools.partial(partial_kernel, len(buffers), 2 * kept /...]
    unnamed x8, local copies, waits for them, and re-layouts: 39 us -> 3.34 us
    all_gather x2 -> x0, local copies, waits for them, and re-layouts: 33.4 us -> none  [the longest x1 24.6 us: per_device(): full = lax.all_gather(weights, 'row', axis=0, tiled=True)]
    dot_general x2 -> x0, matrix products: 30.5 us -> none  [the longest x1 16.1 us: per_device(): jnp.einsum('ptck,ptcq->kpcq', picked, paired, preferred_element_type=jnp....]
  transfers between devices with their start and end apart: 3 -> 26, of which waited for: 3 -> 15; matrix products, arithmetic and copies ran while one was open for 20% -> 3% of each run, Pallas kernels for 0% -> 29%
where the time goes in v2:
time: 132 us
  waiting for transfers between devices  58.3 us (44%)
  Pallas kernels  40.5 us (31%)
  starting transfers between devices  25.7 us (19%)
  local copies, waits for them, and re-layouts  5.07 us (4%)
  other arithmetic  1.67 us (1%)
    pallas_call x7, Pallas kernels, partial(): pl.pallas_call(functools.partial(partial_kernel, len(buffers), 2 * kept /...  24.8 us
    ppermute x8, waiting for transfers between devices, swap_x(): return lax.ppermute(v, 'row', [(r, r ^ 2) for r in range(ROWS)])  17.3 us
    ppermute x8, waiting for transfers between devices, swap_y(): return lax.ppermute(v, 'col', [(c, c ^ 1) for c in range(COLS)])  15.6 us
    ppermute x2, waiting for transfers between devices, far(): return lax.ppermute(v, 'col', [(c, c ^ 4) for c in range(COLS)])  14.6 us
    pallas_call x2, Pallas kernels, grad(): pl.pallas_call(functools.partial(grad_kernel, units, len(buffers), len(ke...  11.8 us
    ppermute x8, starting transfers between devices, swap_x(): return lax.ppermute(v, 'row', [(r, r ^ 2) for r in range(ROWS)])  9.34 us
    ppermute x4, waiting for transfers between devices, near(): return lax.ppermute(v, 'col', [(c, c ^ 2) for c in range(COLS)])  7.34 us
    ppermute x8, starting transfers between devices, swap_y(): return lax.ppermute(v, 'col', [(c, c ^ 1) for c in range(COLS)])  7.04 us
  transfers between devices with their start and end apart: 26, of which 15 were waited for; matrix products, arithmetic and copies ran while one was open for 3% of the time, Pallas kernels for 29%

profile of v2, /device:TPU:0, one launch (start us, length us, event | category | flops | bytes accessed | tf_op | source)
XLA Modules:
  0.0 132.0 jit_solution(12791747096983529583)
XLA Ops:
  2.2 2.7 %collective-permute-start.2 = (bf16[2,16,6144]{2,1,0:T(8,128)(2,1)S(1)}, bf16[2,16,6144]{2,1,0:T(8,128)(2,1)S(1)}, u32[]{:S(2)}, u32[]{:S(2)}) collective-permute-start(bf16[2,16,6144]{2,1,0:T(8,128)(2,1)S(1)} %pad_maximum_fusion.refs_0_), channel_id=1, source_target_pairs={{0,2},{1,3},{2,0},{3,1},{4,6},{5,7},{6,4},{7,5},{8,10},{9,11},{10,... | collective-permute-start | bytes 1179656 | tf_op jit(solution)/shard_map/ppermute | solution.py:223
  4.9 1.5 %collective-permute-start.1 = (bf16[2,16,6144]{2,1,0:T(8,128)(2,1)S(1)}, bf16[2,16,6144]{2,1,0:T(8,128)(2,1)S(1)}, u32[]{:S(2)}, u32[]{:S(2)}) collective-permute-start(bf16[2,16,6144]{2,1,0:T(8,128)(2,1)S(1)} %pad_maximum_fusion.refs_0_), channel_id=1, source_target_pairs={{0,1},{1,0},{2,3},{3,2},{4,5},{5,4},{6,7},{7,6},{8,9},{9,8},{10,11... | collective-permute-start | bytes 1179656 | tf_op jit(solution)/shard_map/ppermute | solution.py:220
  10.2 4.4 %collective-permute-done.2.refs_0_.refs_4_ = bf16[2,16,6144]{2,1,0:T(8,128)(2,1)S(1)} collective-permute-done((bf16[2,16,6144]{2,1,0:T(8,128)(2,1)S(1)}, bf16[2,16,6144]{2,1,0:T(8,128)(2,1)S(1)}, u32[]{:S(2)}, u32[]{:S(2)}) %collective-permute-start.2) | collective-permute-done | bytes 393248 | tf_op jit(solution)/shard_map/ppermute | solution.py:223
  17.4 2.6 %collective-permute-start.5 = (bf16[2,16,6144]{2,1,0:T(8,128)(2,1)S(1)}, bf16[2,16,6144]{2,1,0:T(8,128)(2,1)S(1)}, u32[]{:S(2)}, u32[]{:S(2)}) collective-permute-start(bf16[2,16,6144]{2,1,0:T(8,128)(2,1)S(1)} %pad_maximum_fusion.refs_0_), channel_id=1, source_target_pairs={{0,4},{1,5},{2,6},{3,7},{4,0},{5,1},{6,2},{7,3},{8,12},{9,13},{10,... | collective-permute-start | bytes 1179656 | tf_op jit(solution)/shard_map/ppermute | solution.py:226
  22.7 2.6 %collective-permute-start.8 = (bf16[2,16,6144]{2,1,0:T(8,128)(2,1)}, bf16[2,16,6144]{2,1,0:T(8,128)(2,1)S(1)}, u32[]{:S(2)}, u32[]{:S(2)}) collective-permute-start(bf16[2,16,6144]{2,1,0:T(8,128)(2,1)} %collective-permute-done.refs_0_.refs_2_), channel_id=1, source_target_pairs={{0,4},{1,5},{2,6},{3,7},{4,0},{5,1},{6,2},{7,3},{8,12},{9,13},{10,... | collective-permute-start | bytes 1179656 | tf_op jit(solution)/shard_map/ppermute | solution.py:226
  25.3 1.7 %copy-done = bf16[384,3072]{1,0:T(8,128)(2,1)S(1)} copy-done((bf16[384,3072]{1,0:T(8,128)(2,1)S(1)}, bf16[384,3072]{1,0:T(8,128)(2,1)}, u32[]{:S(2)}) %copy-start) | copy-done | bytes 2359320
  27.0 1.7 %copy-done.2 = bf16[384,3072]{1,0:T(8,128)(2,1)S(1)} copy-done((bf16[384,3072]{1,0:T(8,128)(2,1)S(1)}, bf16[384,3072]{1,0:T(8,128)(2,1)}, u32[]{:S(2)}) %copy-start.2) | copy-done | bytes 2359320
  28.6 3.7 %partial.7 = (f32[2,32,3072]{2,1,0:T(8,128)S(1)}, bf16[2,32,3072]{2,1,0:T(8,128)(2,1)S(1)}) custom-call(s32[288]{0:T(512)S(1)} %reshape.7.table, bf16[2,16,6144]{2,1,0:T(8,128)(2,1)S(1)} %pad_maximum_fusion.refs_0_, bf16[2,16,6144]{2,1,0:T(8,128)(2,1)S(1)} %collective-permute-done.1.refs_1_, bf16[384,3072]{1,0:T(8,128)(2,1)S(1)} %copy-done, ...), custom_call_target="tpu_custom_call" | custom-call | tf_op jit(solution)/shard_map/partial/pallas_call | solution.py:105
  32.3 6.4 %collective-permute-done.5.refs_2_.refs_6_ = bf16[2,16,6144]{2,1,0:T(8,128)(2,1)S(1)} collective-permute-done((bf16[2,16,6144]{2,1,0:T(8,128)(2,1)S(1)}, bf16[2,16,6144]{2,1,0:T(8,128)(2,1)S(1)}, u32[]{:S(2)}, u32[]{:S(2)}) %collective-permute-start.5) | collective-permute-done | bytes 393248 | tf_op jit(solution)/shard_map/ppermute | solution.py:226
  39.1 4.6 %partial.8 = (f32[2,32,3072]{2,1,0:T(8,128)S(1)}, bf16[2,32,3072]{2,1,0:T(8,128)(2,1)S(1)}) custom-call(s32[288]{0:T(512)S(1)} %reshape.7.table, bf16[2,16,6144]{2,1,0:T(8,128)(2,1)} %collective-permute-done.refs_0_.refs_2_, bf16[2,16,6144]{2,1,0:T(8,128)(2,1)S(1)} %collective-permute-done.4.refs_1_.refs_3_, bf16[384,3072]{1,0:T(8,128)(2,1)S(1)} %copy-done.1, ...), custom_call_target="tpu_custom_call" | custom-call | tf_op jit(solution)/shard_map/partial/pallas_call | solution.py:105
  43.7 1.7 %collective-permute-start.13 = (bf16[2,32,3072]{2,1,0:T(8,128)(2,1)S(1)}, bf16[2,32,3072]{2,1,0:T(8,128)(2,1)S(1)}, u32[]{:S(2)}, u32[]{:S(2)}) collective-permute-start(bf16[2,32,3072]{2,1,0:T(8,128)(2,1)S(1)} %get-tuple-element.91), channel_id=1, source_target_pairs={{0,16},{8,24},{16,0},{24,8},{1,17},{9,25},{17,1},{25,9},{2,18},{10... | collective-permute-start | bytes 1179656 | tf_op jit(solution)/shard_map/ppermute | solution.py:214
  45.4 1.5 %collective-permute-start.11 = (bf16[2,16,6144]{2,1,0:T(8,128)(2,1)S(1)}, bf16[2,16,6144]{2,1,0:T(8,128)(2,1)S(1)}, u32[]{:S(2)}, u32[]{:S(2)}) collective-permute-start(bf16[2,16,6144]{2,1,0:T(8,128)(2,1)S(1)} %collective-permute-done.10.refs_0_.refs_8_), channel_id=1, source_target_pairs={{0,1},{1,0},{2,3},{3,2},{4,5},{5,4},{6,7},{7,6},{8,9},{9,8},{10,11... | collective-permute-start | bytes 1179656 | tf_op jit(solution)/shard_map/ppermute | solution.py:220
  46.9 8.3 %collective-permute-done.8.refs_0_.refs_12_ = bf16[2,16,6144]{2,1,0:T(8,128)(2,1)S(1)} collective-permute-done((bf16[2,16,6144]{2,1,0:T(8,128)(2,1)}, bf16[2,16,6144]{2,1,0:T(8,128)(2,1)S(1)}, u32[]{:S(2)}, u32[]{:S(2)}) %collective-permute-start.8) | collective-permute-done | bytes 393248 | tf_op jit(solution)/shard_map/ppermute | solution.py:226
  56.7 4.3 %partial.9 = (f32[2,64,3072]{2,1,0:T(8,128)S(1)}, bf16[2,64,3072]{2,1,0:T(8,128)(2,1)S(1)}) custom-call(s32[288]{0:T(512)S(1)} %reshape.7.table, bf16[2,16,6144]{2,1,0:T(8,128)(2,1)S(1)} %collective-permute-done.2.refs_0_.refs_4_, bf16[2,16,6144]{2,1,0:T(8,128)(2,1)S(1)} %collective-permute-done.9.refs_1_.refs_5_, ...), custom_call_target="tpu_custom_call" | custom-call | tf_op jit(solution)/shard_map/partial/pallas_call | solution.py:105
  61.6 1.5 %collective-permute-start.17 = (bf16[2,16,6144]{2,1,0:T(8,128)(2,1)S(1)}, bf16[2,16,6144]{2,1,0:T(8,128)(2,1)S(1)}, u32[]{:S(2)}, u32[]{:S(2)}) collective-permute-start(bf16[2,16,6144]{2,1,0:T(8,128)(2,1)S(1)} %collective-permute-done.8.refs_0_.refs_12_), channel_id=1, source_target_pairs={{0,1},{1,0},{2,3},{3,2},{4,5},{5,4},{6,7},{7,6},{8,9},{9,8},{10,11... | collective-permute-start | bytes 1179656 | tf_op jit(solution)/shard_map/ppermute | solution.py:220
  63.6 2.9 %collective-permute-done.15.refs_0_.refs_14_ = bf16[2,16,6144]{2,1,0:T(8,128)(2,1)S(1)} collective-permute-done((bf16[2,16,6144]{2,1,0:T(8,128)(2,1)S(1)}, bf16[2,16,6144]{2,1,0:T(8,128)(2,1)S(1)}, u32[]{:S(2)}, u32[]{:S(2)}) %collective-permute-start.15) | collective-permute-done | bytes 393248 | tf_op jit(solution)/shard_map/ppermute | solution.py:223
  67.2 5.9 %collective-permute-done.14.refs_3_.refs_11_ = bf16[2,16,6144]{2,1,0:T(8,128)(2,1)S(1)} collective-permute-done((bf16[2,16,6144]{2,1,0:T(8,128)(2,1)S(1)}, bf16[2,16,6144]{2,1,0:T(8,128)(2,1)S(1)}, u32[]{:S(2)}, u32[]{:S(2)}) %collective-permute-start.14) | collective-permute-done | bytes 393248 | tf_op jit(solution)/shard_map/ppermute | solution.py:220
  73.1 4.2 %partial.10 = (f32[2,64,3072]{2,1,0:T(8,128)S(1)}, bf16[2,64,3072]{2,1,0:T(8,128)(2,1)S(1)}) custom-call(s32[288]{0:T(512)S(1)} %reshape.7.table, bf16[2,16,6144]{2,1,0:T(8,128)(2,1)S(1)} %collective-permute-done.10.refs_0_.refs_8_, bf16[2,16,6144]{2,1,0:T(8,128)(2,1)S(1)} %collective-permute-done.11.refs_1_.refs_9_, ...), custom_call_target="tpu_custom_call" | custom-call | tf_op jit(solution)/shard_map/partial/pallas_call | solution.py:105
  77.3 2.9 %collective-permute-done.17.refs_1_.refs_13_ = bf16[2,16,6144]{2,1,0:T(8,128)(2,1)S(1)} collective-permute-done((bf16[2,16,6144]{2,1,0:T(8,128)(2,1)S(1)}, bf16[2,16,6144]{2,1,0:T(8,128)(2,1)S(1)}, u32[]{:S(2)}, u32[]{:S(2)}) %collective-permute-start.17) | collective-permute-done | bytes 393248 | tf_op jit(solution)/shard_map/ppermute | solution.py:220
  81.2 3.7 %partial.11 = (f32[2,32,3072]{2,1,0:T(8,128)S(1)}, bf16[2,32,3072]{2,1,0:T(8,128)(2,1)S(1)}) custom-call(s32[288]{0:T(512)S(1)} %reshape.7.table, bf16[2,16,6144]{2,1,0:T(8,128)(2,1)S(1)} %collective-permute-done.8.refs_0_.refs_12_, bf16[2,16,6144]{2,1,0:T(8,128)(2,1)S(1)} %collective-permute-done.17.refs_1_.refs_13_, bf16[384,3072]{1,0:T(8,128)(2,1)S(1)} %copy-done.1, ...), custom_call_target="tpu_custom_call" | custom-call | tf_op jit(solution)/shard_map/partial/pallas_call | solution.py:105
  84.9 5.3 %collective-permute-done.18.refs_1_.refs_15_ = bf16[2,16,6144]{2,1,0:T(8,128)(2,1)S(1)} collective-permute-done((bf16[2,16,6144]{2,1,0:T(8,128)(2,1)S(1)}, bf16[2,16,6144]{2,1,0:T(8,128)(2,1)S(1)}, u32[]{:S(2)}, u32[]{:S(2)}) %collective-permute-start.18) | collective-permute-done | bytes 393248 | tf_op jit(solution)/shard_map/ppermute | solution.py:220
  90.2 1.6 %collective-permute-start.21 = (bf16[2,32,3072]{2,1,0:T(8,128)(2,1)S(1)}, bf16[2,32,3072]{2,1,0:T(8,128)(2,1)S(1)}, u32[]{:S(2)}, u32[]{:S(2)}) collective-permute-start(bf16[2,32,3072]{2,1,0:T(8,128)(2,1)S(1)} %get-tuple-element.122), channel_id=1, source_target_pairs={{0,16},{8,24},{16,0},{24,8},{1,17},{9,25},{17,1},{25,9},{2,18},{10... | collective-permute-start | bytes 1179656 | tf_op jit(solution)/shard_map/ppermute | solution.py:214
  91.8 2.1 %partial.12 = (f32[2,32,1536]{2,1,0:T(8,128)S(1)}, bf16[2,32,1536]{2,1,0:T(8,128)(2,1)S(1)}) custom-call(s32[288]{0:T(512)S(1)} %reshape.7.table, bf16[2,16,6144]{2,1,0:T(8,128)(2,1)S(1)} %collective-permute-done.15.refs_0_.refs_14_, bf16[2,16,6144]{2,1,0:T(8,128)(2,1)S(1)} %collective-permute-done.18.refs_1_.refs_15_, bf16[384,3072]{1,0:T(8,128)(2,1)S(1)} %copy-done.1, ...), custom_call_target="tpu_custom_call" | custom-call | tf_op jit(solution)/shard_map/partial/pallas_call | solution.py:105
  93.9 6.9 %collective-permute-done.20.refs_25_ = bf16[2,64,3072]{2,1,0:T(8,128)(2,1)S(1)} collective-permute-done((bf16[2,64,3072]{2,1,0:T(8,128)(2,1)S(1)}, bf16[2,64,3072]{2,1,0:T(8,128)(2,1)S(1)}, u32[]{:S(2)}, u32[]{:S(2)}) %collective-permute-start.20) | collective-permute-done | bytes 786464 | tf_op jit(solution)/shard_map/ppermute | solution.py:214
  102.4 2.2 %partial.13 = (f32[2,32,1536]{2,1,0:T(8,128)S(1)}, bf16[2,32,1536]{2,1,0:T(8,128)(2,1)S(1)}) custom-call(s32[288]{0:T(512)S(1)} %reshape.7.table, bf16[2,16,6144]{2,1,0:T(8,128)(2,1)S(1)} %collective-permute-done.15.refs_0_.refs_14_, bf16[2,16,6144]{2,1,0:T(8,128)(2,1)S(1)} %collective-permute-done.18.refs_1_.refs_15_, bf16[384,3072]{1,0:T(8,128)(2,1)S(1)} %copy-done.1, ...), custom_call_target="tpu_custom_call" | custom-call | tf_op jit(solution)/shard_map/partial/pallas_call | solution.py:105
  105.2 4.1 %collective-permute-done.21.refs_26_ = bf16[2,32,3072]{2,1,0:T(8,128)(2,1)S(1)} collective-permute-done((bf16[2,32,3072]{2,1,0:T(8,128)(2,1)S(1)}, bf16[2,32,3072]{2,1,0:T(8,128)(2,1)S(1)}, u32[]{:S(2)}, u32[]{:S(2)}) %collective-permute-start.21) | collective-permute-done | bytes 393248 | tf_op jit(solution)/shard_map/ppermute | solution.py:214
  109.3 4.2 %collective-permute-done.22.refs_27_ = bf16[2,32,1536]{2,1,0:T(8,128)(2,1)S(1)} collective-permute-done((bf16[2,32,1536]{2,1,0:T(8,128)(2,1)S(1)}, bf16[2,32,1536]{2,1,0:T(8,128)(2,1)S(1)}, u32[]{:S(2)}, u32[]{:S(2)}) %collective-permute-start.22) | collective-permute-done | bytes 196640 | tf_op jit(solution)/shard_map/ppermute | solution.py:214
  113.5 5.9 %grad.2 = (bf16[2,384,1536]{2,1,0:T(8,128)(2,1)S(1)}, bf16[2,384,1536]{2,1,0:T(8,128)(2,1)S(1)}) custom-call(s32[288]{0:T(512)S(1)} %reshape.7.table, bf16[2,16,6144]{2,1,0:T(8,128)(2,1)S(1)} %pad_maximum_fusion.refs_0_, bf16[2,16,6144]{2,1,0:T(8,128)(2,1)S(1)} %collective-permute-done.1.refs_1_, bf16[2,16,6144]{2,1,0:T(8,128)(2,1)} %collective-permute-done.refs_0_.refs_2_, ...), custom_call_target="tpu_custom_call" | custom-call | tf_op jit(solution)/shard_map/grad/pallas_call | solution.py:165
  119.5 5.9 %grad.3 = (bf16[2,384,1536]{2,1,0:T(8,128)(2,1)S(1)}, bf16[2,384,1536]{2,1,0:T(8,128)(2,1)S(1)}) custom-call(s32[288]{0:T(512)S(1)} %reshape.7.table, bf16[2,16,6144]{2,1,0:T(8,128)(2,1)S(1)} %pad_maximum_fusion.refs_0_, bf16[2,16,6144]{2,1,0:T(8,128)(2,1)S(1)} %collective-permute-done.1.refs_1_, bf16[2,16,6144]{2,1,0:T(8,128)(2,1)} %collective-permute-done.refs_0_.refs_2_, ...), custom_call_target="tpu_custom_call" | custom-call | tf_op jit(solution)/shard_map/grad/pallas_call | solution.py:165
  125.9 1.9 %total.2 = (bf16[384,3072]{1,0:T(8,128)(2,1)}, bf16[384,3072]{1,0:T(8,128)(2,1)}) custom-call(bf16[2,384,1536]{2,1,0:T(8,128)(2,1)S(1)} %get-tuple-element.134.own_ref, bf16[2,384,1536]{2,1,0:T(8,128)(2,1)S(1)} %collective-permute-done.24.got_ref), custom_call_target="tpu_custom_call" | custom-call | tf_op jit(solution)/shard_map/total/pallas_call | solution.py:193
  127.9 2.2 %collective-permute-done.25.got_ref = bf16[2,384,1536]{2,1,0:T(8,128)(2,1)S(1)} collective-permute-done((bf16[2,384,1536]{2,1,0:T(8,128)(2,1)S(1)}, bf16[2,384,1536]{2,1,0:T(8,128)(2,1)S(1)}, u32[]{:S(2)}, u32[]{:S(2)}) %collective-permute-start.25) | collective-permute-done | bytes 2359328 | tf_op jit(solution)/shard_map/ppermute | solution.py:217
  130.1 1.9 %total.3 = (bf16[384,3072]{1,0:T(8,128)(2,1)}, bf16[384,3072]{1,0:T(8,128)(2,1)}) custom-call(bf16[2,384,1536]{2,1,0:T(8,128)(2,1)S(1)} %get-tuple-element.132.own_ref, bf16[2,384,1536]{2,1,0:T(8,128)(2,1)S(1)} %collective-permute-done.25.got_ref, bf16[384,3072]{1,0:T(8,128)(2,1)} %get-tuple-element.136.refs_0_, ...), custom_call_target="tpu_custom_call", output_to_operand_aliasing={{0}: (2, {}), {1}: (3, {})} | custom-call | tf_op jit(solution)/shard_map/total/pallas_call | solution.py:193
  (44 shorter events, 18.2 us)
Async XLA Ops:
  0.6 16.8 %collective-permute-start.3 = (bf16[384,3072]{1,0:T(8,128)(2,1)}, bf16[384,3072]{1,0:T(8,128)(2,1)S(1)}, u32[]{:S(2)}, u32[]{:S(2)}) collective-permute-start(bf16[384,3072]{1,0:T(8,128)(2,1)} %refs_2_.9), channel_id=1, source_target_pairs={{0,8},{8,0},{16,24},{24,16},{1,9},{9,1},{17,25},{25,17},{2,10},{10... | collective-permute-start | bytes 7077896 | tf_op jit(solution)/shard_map/ppermute | solution.py:217
  2.2 12.4 %collective-permute-start.2 = (bf16[2,16,6144]{2,1,0:T(8,128)(2,1)S(1)}, bf16[2,16,6144]{2,1,0:T(8,128)(2,1)S(1)}, u32[]{:S(2)}, u32[]{:S(2)}) collective-permute-start(bf16[2,16,6144]{2,1,0:T(8,128)(2,1)S(1)} %pad_maximum_fusion.refs_0_), channel_id=1, source_target_pairs={{0,2},{1,3},{2,0},{3,1},{4,6},{5,7},{6,4},{7,5},{8,10},{9,11},{10,... | collective-permute-start | bytes 1179656 | tf_op jit(solution)/shard_map/ppermute | solution.py:223
  4.9 11.2 %collective-permute-start.1 = (bf16[2,16,6144]{2,1,0:T(8,128)(2,1)S(1)}, bf16[2,16,6144]{2,1,0:T(8,128)(2,1)S(1)}, u32[]{:S(2)}, u32[]{:S(2)}) collective-permute-start(bf16[2,16,6144]{2,1,0:T(8,128)(2,1)S(1)} %pad_maximum_fusion.refs_0_), channel_id=1, source_target_pairs={{0,1},{1,0},{2,3},{3,2},{4,5},{5,4},{6,7},{7,6},{8,9},{9,8},{10,11... | collective-permute-start | bytes 1179656 | tf_op jit(solution)/shard_map/ppermute | solution.py:220
  6.4 11.1 %collective-permute-start = (bf16[2,16,6144]{2,1,0:T(8,128)(2,1)S(1)}, bf16[2,16,6144]{2,1,0:T(8,128)(2,1)}, u32[]{:S(2)}, u32[]{:S(2)}) collective-permute-start(bf16[2,16,6144]{2,1,0:T(8,128)(2,1)S(1)} %pad_maximum_fusion.refs_0_), channel_id=1, source_target_pairs={{0,16},{8,24},{16,0},{24,8},{1,17},{9,25},{17,1},{25,9},{2,18},{10... | collective-permute-start | bytes 1179656 | tf_op jit(solution)/shard_map/ppermute | solution.py:214
  17.4 4.7 %collective-permute-start.6 = (bf16[384,3072]{1,0:T(8,128)(2,1)}, bf16[384,3072]{1,0:T(8,128)(2,1)S(1)}, u32[]{:S(2)}, u32[]{:S(2)}) collective-permute-start(bf16[384,3072]{1,0:T(8,128)(2,1)} %refs_3_.9), channel_id=1, source_target_pairs={{0,8},{8,0},{16,24},{24,16},{1,9},{9,1},{17,25},{25,17},{2,10},{10... | collective-permute-start | bytes 7077896 | tf_op jit(solution)/shard_map/ppermute | solution.py:217
  17.4 21.2 %collective-permute-start.5 = (bf16[2,16,6144]{2,1,0:T(8,128)(2,1)S(1)}, bf16[2,16,6144]{2,1,0:T(8,128)(2,1)S(1)}, u32[]{:S(2)}, u32[]{:S(2)}) collective-permute-start(bf16[2,16,6144]{2,1,0:T(8,128)(2,1)S(1)} %pad_maximum_fusion.refs_0_), channel_id=1, source_target_pairs={{0,4},{1,5},{2,6},{3,7},{4,0},{5,1},{6,2},{7,3},{8,12},{9,13},{10,... | collective-permute-start | bytes 1179656 | tf_op jit(solution)/shard_map/ppermute | solution.py:226
  20.0 18.6 %collective-permute-start.4 = (bf16[2,16,6144]{2,1,0:T(8,128)(2,1)}, bf16[2,16,6144]{2,1,0:T(8,128)(2,1)S(1)}, u32[]{:S(2)}, u32[]{:S(2)}) collective-permute-start(bf16[2,16,6144]{2,1,0:T(8,128)(2,1)} %collective-permute-done.refs_0_.refs_2_), channel_id=1, source_target_pairs={{0,1},{1,0},{2,3},{3,2},{4,5},{5,4},{6,7},{7,6},{8,9},{9,8},{10,11... | collective-permute-start | bytes 1179656 | tf_op jit(solution)/shard_map/ppermute | solution.py:220
  20.5 23.2 %collective-permute-start.10 = (bf16[2,16,6144]{2,1,0:T(8,128)(2,1)}, bf16[2,16,6144]{2,1,0:T(8,128)(2,1)S(1)}, u32[]{:S(2)}, u32[]{:S(2)}) collective-permute-start(bf16[2,16,6144]{2,1,0:T(8,128)(2,1)} %collective-permute-done.refs_0_.refs_2_), channel_id=1, source_target_pairs={{0,2},{1,3},{2,0},{3,1},{4,6},{5,7},{6,4},{7,5},{8,10},{9,11},{10,... | collective-permute-start | bytes 1179656 | tf_op jit(solution)/shard_map/ppermute | solution.py:223
  22.2 23.2 %collective-permute-start.9 = (bf16[2,16,6144]{2,1,0:T(8,128)(2,1)S(1)}, bf16[2,16,6144]{2,1,0:T(8,128)(2,1)S(1)}, u32[]{:S(2)}, u32[]{:S(2)}) collective-permute-start(bf16[2,16,6144]{2,1,0:T(8,128)(2,1)S(1)} %collective-permute-done.2.refs_0_.refs_4_), channel_id=1, source_target_pairs={{0,1},{1,0},{2,3},{3,2},{4,5},{5,4},{6,7},{7,6},{8,9},{9,8},{10,11... | collective-permute-start | bytes 1179656 | tf_op jit(solution)/shard_map/ppermute | solution.py:220
  22.7 32.5 %collective-permute-start.8 = (bf16[2,16,6144]{2,1,0:T(8,128)(2,1)}, bf16[2,16,6144]{2,1,0:T(8,128)(2,1)S(1)}, u32[]{:S(2)}, u32[]{:S(2)}) collective-permute-start(bf16[2,16,6144]{2,1,0:T(8,128)(2,1)} %collective-permute-done.refs_0_.refs_2_), channel_id=1, source_target_pairs={{0,4},{1,5},{2,6},{3,7},{4,0},{5,1},{6,2},{7,3},{8,12},{9,13},{10,... | collective-permute-start | bytes 1179656 | tf_op jit(solution)/shard_map/ppermute | solution.py:226
  25.3 1.7 %copy-start = (bf16[384,3072]{1,0:T(8,128)(2,1)S(1)}, bf16[384,3072]{1,0:T(8,128)(2,1)}, u32[]{:S(2)}) copy-start(bf16[384,3072]{1,0:T(8,128)(2,1)} %refs_2_.9) | copy-start | bytes 7077892
  27.0 1.7 %copy-start.2 = (bf16[384,3072]{1,0:T(8,128)(2,1)S(1)}, bf16[384,3072]{1,0:T(8,128)(2,1)}, u32[]{:S(2)}) copy-start(bf16[384,3072]{1,0:T(8,128)(2,1)} %refs_3_.9) | copy-start | bytes 7077892
  28.6 10.5 %copy-start.1 = (bf16[384,3072]{1,0:T(8,128)(2,1)S(1)}, bf16[384,3072]{1,0:T(8,128)(2,1)}, u32[]{:S(2)}) copy-start(bf16[384,3072]{1,0:T(8,128)(2,1)} %refs_2_.9) | copy-start | bytes 7077892
  28.6 10.5 %copy-start.3 = (bf16[384,3072]{1,0:T(8,128)(2,1)S(1)}, bf16[384,3072]{1,0:T(8,128)(2,1)}, u32[]{:S(2)}) copy-start(bf16[384,3072]{1,0:T(8,128)(2,1)} %refs_3_.9) | copy-start | bytes 7077892
  38.7 16.5 %collective-permute-start.7 = (bf16[2,16,6144]{2,1,0:T(8,128)(2,1)S(1)}, bf16[2,16,6144]{2,1,0:T(8,128)(2,1)S(1)}, u32[]{:S(2)}, u32[]{:S(2)}) collective-permute-start(bf16[2,16,6144]{2,1,0:T(8,128)(2,1)S(1)} %collective-permute-done.5.refs_2_.refs_6_), channel_id=1, source_target_pairs={{0,1},{1,0},{2,3},{3,2},{4,5},{5,4},{6,7},{7,6},{8,9},{9,8},{10,11... | collective-permute-start | bytes 1179656 | tf_op jit(solution)/shard_map/ppermute | solution.py:220
  39.1 21.9 %collective-permute-start.12 = (bf16[2,16,6144]{2,1,0:T(8,128)(2,1)S(1)}, bf16[2,16,6144]{2,1,0:T(8,128)(2,1)S(1)}, u32[]{:S(2)}, u32[]{:S(2)}) collective-permute-start(bf16[2,16,6144]{2,1,0:T(8,128)(2,1)S(1)} %collective-permute-done.5.refs_2_.refs_6_), channel_id=1, source_target_pairs={{0,2},{1,3},{2,0},{3,1},{4,6},{5,7},{6,4},{7,5},{8,10},{9,11},{10,... | collective-permute-start | bytes 1179656 | tf_op jit(solution)/shard_map/ppermute | solution.py:223
  43.7 17.2 %collective-permute-start.13 = (bf16[2,32,3072]{2,1,0:T(8,128)(2,1)S(1)}, bf16[2,32,3072]{2,1,0:T(8,128)(2,1)S(1)}, u32[]{:S(2)}, u32[]{:S(2)}) collective-permute-start(bf16[2,32,3072]{2,1,0:T(8,128)(2,1)S(1)} %get-tuple-element.91), channel_id=1, source_target_pairs={{0,16},{8,24},{16,0},{24,8},{1,17},{9,25},{17,1},{25,9},{2,18},{10... | collective-permute-start | bytes 1179656 | tf_op jit(solution)/shard_map/ppermute | solution.py:214
  45.4 15.6 %collective-permute-start.11 = (bf16[2,16,6144]{2,1,0:T(8,128)(2,1)S(1)}, bf16[2,16,6144]{2,1,0:T(8,128)(2,1)S(1)}, u32[]{:S(2)}, u32[]{:S(2)}) collective-permute-start(bf16[2,16,6144]{2,1,0:T(8,128)(2,1)S(1)} %collective-permute-done.10.refs_0_.refs_8_), channel_id=1, source_target_pairs={{0,1},{1,0},{2,3},{3,2},{4,5},{5,4},{6,7},{7,6},{8,9},{9,8},{10,11... | collective-permute-start | bytes 1179656 | tf_op jit(solution)/shard_map/ppermute | solution.py:220
  55.2 11.4 %collective-permute-start.15 = (bf16[2,16,6144]{2,1,0:T(8,128)(2,1)S(1)}, bf16[2,16,6144]{2,1,0:T(8,128)(2,1)S(1)}, u32[]{:S(2)}, u32[]{:S(2)}) collective-permute-start(bf16[2,16,6144]{2,1,0:T(8,128)(2,1)S(1)} %collective-permute-done.8.refs_0_.refs_12_), channel_id=1, source_target_pairs={{0,2},{1,3},{2,0},{3,1},{4,6},{5,7},{6,4},{7,5},{8,10},{9,11},{10,... | collective-permute-start | bytes 1179656 | tf_op jit(solution)/shard_map/ppermute | solution.py:223
  55.2 12.0 %collective-permute-start.16 = (bf16[2,32,3072]{2,1,0:T(8,128)(2,1)S(1)}, bf16[2,32,3072]{2,1,0:T(8,128)(2,1)S(1)}, u32[]{:S(2)}, u32[]{:S(2)}) collective-permute-start(bf16[2,32,3072]{2,1,0:T(8,128)(2,1)S(1)} %get-tuple-element.94), channel_id=1, source_target_pairs={{0,16},{8,24},{16,0},{24,8},{1,17},{9,25},{17,1},{25,9},{2,18},{10... | collective-permute-start | bytes 1179656 | tf_op jit(solution)/shard_map/ppermute | solution.py:214
  61.0 12.1 %collective-permute-start.14 = (bf16[2,16,6144]{2,1,0:T(8,128)(2,1)S(1)}, bf16[2,16,6144]{2,1,0:T(8,128)(2,1)S(1)}, u32[]{:S(2)}, u32[]{:S(2)}) collective-permute-start(bf16[2,16,6144]{2,1,0:T(8,128)(2,1)S(1)} %collective-permute-done.12.refs_2_.refs_10_), channel_id=1, source_target_pairs={{0,1},{1,0},{2,3},{3,2},{4,5},{5,4},{6,7},{7,6},{8,9},{9,8},{10,11... | collective-permute-start | bytes 1179656 | tf_op jit(solution)/shard_map/ppermute | solution.py:220
  61.6 18.7 %collective-permute-start.17 = (bf16[2,16,6144]{2,1,0:T(8,128)(2,1)S(1)}, bf16[2,16,6144]{2,1,0:T(8,128)(2,1)S(1)}, u32[]{:S(2)}, u32[]{:S(2)}) collective-permute-start(bf16[2,16,6144]{2,1,0:T(8,128)(2,1)S(1)} %collective-permute-done.8.refs_0_.refs_12_), channel_id=1, source_target_pairs={{0,1},{1,0},{2,3},{3,2},{4,5},{5,4},{6,7},{7,6},{8,9},{9,8},{10,11... | collective-permute-start | bytes 1179656 | tf_op jit(solution)/shard_map/ppermute | solution.py:220
  63.1 21.8 %collective-permute-start.19 = (bf16[2,64,3072]{2,1,0:T(8,128)(2,1)S(1)}, bf16[2,64,3072]{2,1,0:T(8,128)(2,1)S(1)}, u32[]{:S(2)}, u32[]{:S(2)}) collective-permute-start(bf16[2,64,3072]{2,1,0:T(8,128)(2,1)S(1)} %get-tuple-element.105), channel_id=1, source_target_pairs={{0,16},{8,24},{16,0},{24,8},{1,17},{9,25},{17,1},{25,9},{2,18},{10... | collective-permute-start | bytes 2359304 | tf_op jit(solution)/shard_map/ppermute | solution.py:214
  80.2 20.7 %collective-permute-start.20 = (bf16[2,64,3072]{2,1,0:T(8,128)(2,1)S(1)}, bf16[2,64,3072]{2,1,0:T(8,128)(2,1)S(1)}, u32[]{:S(2)}, u32[]{:S(2)}) collective-permute-start(bf16[2,64,3072]{2,1,0:T(8,128)(2,1)S(1)} %get-tuple-element.109), channel_id=1, source_target_pairs={{0,16},{8,24},{16,0},{24,8},{1,17},{9,25},{17,1},{25,9},{2,18},{10... | collective-permute-start | bytes 2359304 | tf_op jit(solution)/shard_map/ppermute | solution.py:214
  80.7 9.5 %collective-permute-start.18 = (bf16[2,16,6144]{2,1,0:T(8,128)(2,1)S(1)}, bf16[2,16,6144]{2,1,0:T(8,128)(2,1)S(1)}, u32[]{:S(2)}, u32[]{:S(2)}) collective-permute-start(bf16[2,16,6144]{2,1,0:T(8,128)(2,1)S(1)} %collective-permute-done.15.refs_0_.refs_14_), channel_id=1, source_target_pairs={{0,1},{1,0},{2,3},{3,2},{4,5},{5,4},{6,7},{7,6},{8,9},{9,8},{10,11... | collective-permute-start | bytes 1179656 | tf_op jit(solution)/shard_map/ppermute | solution.py:220
  90.2 19.1 %collective-permute-start.21 = (bf16[2,32,3072]{2,1,0:T(8,128)(2,1)S(1)}, bf16[2,32,3072]{2,1,0:T(8,128)(2,1)S(1)}, u32[]{:S(2)}, u32[]{:S(2)}) collective-permute-start(bf16[2,32,3072]{2,1,0:T(8,128)(2,1)S(1)} %get-tuple-element.122), channel_id=1, source_target_pairs={{0,16},{8,24},{16,0},{24,8},{1,17},{9,25},{17,1},{25,9},{2,18},{10... | collective-permute-start | bytes 1179656 | tf_op jit(solution)/shard_map/ppermute | solution.py:214
  100.9 12.6 %collective-permute-start.22 = (bf16[2,32,1536]{2,1,0:T(8,128)(2,1)S(1)}, bf16[2,32,1536]{2,1,0:T(8,128)(2,1)S(1)}, u32[]{:S(2)}, u32[]{:S(2)}) collective-permute-start(bf16[2,32,1536]{2,1,0:T(8,128)(2,1)S(1)} %get-tuple-element.124), channel_id=1, source_target_pairs={{0,16},{8,24},{16,0},{24,8},{1,17},{9,25},{17,1},{25,9},{2,18},{10... | collective-permute-start | bytes 589832 | tf_op jit(solution)/shard_map/ppermute | solution.py:214
  104.6 14.8 %collective-permute-start.23 = (bf16[2,32,1536]{2,1,0:T(8,128)(2,1)S(1)}, bf16[2,32,1536]{2,1,0:T(8,128)(2,1)S(1)}, u32[]{:S(2)}, u32[]{:S(2)}) collective-permute-start(bf16[2,32,1536]{2,1,0:T(8,128)(2,1)S(1)} %get-tuple-element.127), channel_id=1, source_target_pairs={{0,16},{8,24},{16,0},{24,8},{1,17},{9,25},{17,1},{25,9},{2,18},{10... | collective-permute-start | bytes 589832 | tf_op jit(solution)/shard_map/ppermute | solution.py:214
  119.4 6.0 %collective-permute-start.24 = (bf16[2,384,1536]{2,1,0:T(8,128)(2,1)S(1)}, bf16[2,384,1536]{2,1,0:T(8,128)(2,1)S(1)}, u32[]{:S(2)}, u32[]{:S(2)}) collective-permute-start(bf16[2,384,1536]{2,1,0:T(8,128)(2,1)S(1)} %get-tuple-element.131), channel_id=1, source_target_pairs={{0,8},{8,0},{16,24},{24,16},{1,9},{9,1},{17,25},{25,17},{2,10},{10... | collective-permute-start | bytes 7077896 | tf_op jit(solution)/shard_map/ppermute | solution.py:217
  125.4 4.7 %collective-permute-start.25 = (bf16[2,384,1536]{2,1,0:T(8,128)(2,1)S(1)}, bf16[2,384,1536]{2,1,0:T(8,128)(2,1)S(1)}, u32[]{:S(2)}, u32[]{:S(2)}) collective-permute-start(bf16[2,384,1536]{2,1,0:T(8,128)(2,1)S(1)} %get-tuple-element.133), channel_id=1, source_target_pairs={{0,8},{8,0},{16,24},{24,16},{1,9},{9,1},{17,25},{25,17},{2,10},{10... | collective-permute-start | bytes 7077896 | tf_op jit(solution)/shard_map/ppermute | solution.py:217

commit v3 on v2

--- a/solution.py
+++ b/solution.py
@@ -15,9 +15,11 @@
 LANES = 4
 SCALE = 0.7978845608028654
 CUBIC = 0.044715
-PARTIAL_VMEM = 20 * 1024 * 1024
-GRAD_VMEM = 24 * 1024 * 1024
-TOTAL_VMEM = 12 * 1024 * 1024
+PARTIAL_VMEM = 8 * 1024 * 1024
+GRAD_VMEM = 16 * 1024 * 1024
+TOTAL_VMEM = 8 * 1024 * 1024
+PACK_LANES = 4
+PACK_VMEM = 12 * 1024 * 1024
 TOTAL_LANES = 6
 COST = pl.CostEstimate(flops=0, bytes_accessed=0, transcendentals=0)
 
@@ -76,20 +78,38 @@
 
 
 def fixed(array):
-    return pl.BlockSpec(array.shape, lambda g, t: (0,) * array.ndim)
+    return pl.BlockSpec(array.shape, lambda g, t: (0,) * array.ndim, pipeline_mode=pl.Buffered(1))
+
+
+def pack_kernel(*refs):
+    for index, ref in enumerate(refs[:-1]):
+        refs[-1][index] = ref[...]
+
+
+def pack(*weights):
+    kept, width = weights[0].shape
+    wide = PACK_LANES * BLK
+    return pl.pallas_call(
+        pack_kernel,
+        grid=(width // wide,),
+        in_specs=[pl.BlockSpec((kept, wide), lambda g: (0, g))] * len(weights),
+        out_specs=pl.BlockSpec((len(weights), kept, wide), lambda g: (0, 0, g)),
+        out_shape=jax.ShapeDtypeStruct((len(weights), kept, width), weights[0].dtype),
+        compiler_params=pltpu.CompilerParams(vmem_limit_bytes=PACK_VMEM),
+        cost_estimate=COST,
+        name="pack",
+    )(*weights)
 
 
 def partial_kernel(n_buf, slots, base, table, *refs):
     buffers = refs[:n_buf]
-    own = refs[n_buf : n_buf + 2]
-    sib = refs[n_buf + 2 : n_buf + 4]
-    keep_ref, send_ref = refs[n_buf + 4 :]
+    weights, keep_ref, send_ref = refs[n_buf:]
     step = pl.program_id(0)
     for lane in range(LANES):
         at = slice(lane * BLK, (lane + 1) * BLK)
         for side in range(2):
             left = picked_rows(table, buffers, side, base + step * LANES + lane, slots)
-            right = jnp.concatenate((own[side][:, at], sib[side][:, at]), axis=0)
+            right = jnp.concatenate((weights[side, :, at], weights[2 + side, :, at]), axis=0)
             total = jnp.dot(left, right, preferred_element_type=jnp.float32)
             keep_ref[side, :, at] = total
             send_ref[side, :, at] = total.astype(jnp.bfloat16)
@@ -97,17 +117,17 @@
 
 def partial(table, buffers, weights, part=0, parts=1):
     tokens = sum(b.shape[1] for b in buffers)
-    kept, width = weights[0].shape
+    kept, width = weights.shape[1:]
     wide = LANES * BLK
     steps = width // wide // parts
-    weight = pl.BlockSpec((kept, wide), lambda g, t: (0, part * steps + g))
+    weight = pl.BlockSpec((4, kept, wide), lambda g, t: (0, 0, part * steps + g))
     out = pl.BlockSpec((2, tokens, wide), lambda g, t: (0, 0, g))
     return pl.pallas_call(
         functools.partial(partial_kernel, len(buffers), 2 * kept // BLK, part * steps * LANES),
         grid_spec=pltpu.PrefetchScalarGridSpec(
             num_scalar_prefetch=1,
             grid=(steps,),
-            in_specs=[fixed(b) for b in buffers] + [weight] * 4,
+            in_specs=[fixed(b) for b in buffers] + [weight],
             out_specs=[out, out],
         ),
         out_shape=[
@@ -116,7 +136,7 @@
         compiler_params=pltpu.CompilerParams(vmem_limit_bytes=PARTIAL_VMEM),
         cost_estimate=COST,
         name="partial",
-    )(table, *buffers, *weights)
+    )(table, *buffers, weights)
 
 
 def grad_kernel(units, n_buf, n_keep, n_got, slots, base, table, *refs):
@@ -228,62 +248,65 @@
     gate = lax.optimization_barrier
 
     a0 = jnp.stack((inputs, cotangent), 0)
-    b0 = swap_x(a0)
-    ya0 = swap_y(a0)
-    a1 = near(a0)
-    a2 = far(a0)
-    s_in = swap_core(w_in)
+    b0, ya0, a1 = swap_x(a0), swap_y(a0), near(a0)
+    s_in, s_out = swap_core(w_in), swap_core(w_out)
     pieces = []
     for keep in (keep_in, keep_out):
         rows = lax.dynamic_slice_in_dim(keep, col * here, here, 0)
         pieces += [lax.dynamic_slice_in_dim(rows, r * mine, mine, 1) for r in (row, row ^ 1)]
     table = jnp.concatenate(pieces, axis=1).reshape(-1)
-    b0, ya0, a1, a0, s_in, table, w_late = gate((b0, ya0, a1, a0, s_in, table, w_out))
-    s_out = swap_core(w_late)
-    yb0 = swap_y(b0)
-    b1 = near(b0)
+    weights = pack(w_in, w_out, s_in, s_out)
+    table, weights, b0, ya0, a1, a0 = gate((table, weights, b0, ya0, a1, a0))
+    yb0, b1, ya1, a2 = swap_y(b0), near(b0), swap_y(a1), far(a0)
+    keep0, send0 = partial(table, (a0, ya0), weights)
+    table, send0 = gate((table, send0))
+    got0 = swap_x(send0)
+    table, yb0, b0 = gate((table, yb0, b0))
+    keep1, send1 = partial(table, (b0, yb0), weights)
+    table, send1, b1 = gate((table, send1, b1))
+    got1, yb1 = swap_x(send1), swap_y(b1)
+    table, got0, b0 = gate((table, got0, b0))
     b2 = far(b0)
-    s_out, a1 = gate((s_out, a1))
-    weights = (w_in, w_out, s_in, s_out)
-    ya1 = swap_y(a1)
-    keep0, send0 = partial(table, (a0, ya0), weights)
-    yb0, a2, send0, b0 = gate((yb0, a2, send0, b0))
-    got0 = swap_x(send0)
-    ya2 = swap_y(a2)
-    a3 = near(a2)
-    keep1, send1 = partial(table, (b0, yb0), weights)
-    ya1, b1, send1 = gate((ya1, b1, send1))
-    got1 = swap_x(send1)
-    yb1 = swap_y(b1)
-    ya2, b2, a1, a2, ya1 = gate((ya2, b2, a1, a2, ya1))
-    b3 = near(b2)
-    keep2, send2 = partial(table, (a1, ya1, a2, ya2), weights)
-    yb1, a3, send2, got0 = gate((yb1, a3, send2, got0))
-    got2 = swap_x(send2)
+    table, ya1, a1 = gate((table, ya1, a1))
+    keep2, send2 = partial(table, (a1, ya1), weights)
+    table, send2, a2, got1 = gate((table, send2, a2, got1))
+    got2, ya2, a3 = swap_x(send2), swap_y(a2), near(a2)
+    table, yb1, b1 = gate((table, yb1, b1))
+    keep3, send3 = partial(table, (b1, yb1), weights)
+    table, send3 = gate((table, send3))
+    got3 = swap_x(send3)
+    table, a3 = gate((table, a3))
     ya3 = swap_y(a3)
-    yb2 = swap_y(b2)
-    ya3, b3, got1, b1, yb1, a3 = gate((ya3, b3, got1, b1, yb1, a3))
+    table, ya2, got2 = gate((table, ya2, got2))
+    keep4, send4 = partial(table, (a2, ya2), weights)
+    table, send4, b2 = gate((table, send4, b2))
+    got4, yb2, b3 = swap_x(send4), swap_y(b2), near(b2)
+    table, ya3, got3 = gate((table, ya3, got3))
+    keep5, send5 = partial(table, (a3, ya3), weights)
+    table, send5 = gate((table, send5))
+    got5 = swap_x(send5)
+    table, b3 = gate((table, b3))
     yb3 = swap_y(b3)
-    keep3, send3 = partial(table, (b1, yb1, a3, ya3), weights)
-    yb2, send3, b2 = gate((yb2, send3, b2))
-    got3 = swap_x(send3)
-    keep4, send4 = partial(table, (b2, yb2), weights)
-    yb3, send4, got2, b3 = gate((yb3, send4, got2, b3))
-    got4 = swap_x(send4)
-    keep5, send5 = partial(table, (b3, yb3), weights, 0, 2)
-    send5, got3, b3, yb3 = gate((send5, got3, b3, yb3))
-    got5 = swap_x(send5)
-    keep6, send6 = partial(table, (b3, yb3), weights, 1, 2)
+    table, yb2, got4 = gate((table, yb2, got4))
+    keep6, send6 = partial(table, (b2, yb2), weights)
+    table, send6 = gate((table, send6))
     got6 = swap_x(send6)
-
-    buffers = (a0, ya0, b0, yb0, a1, ya1, a2, ya2, b1, yb1, a3, ya3, b2, yb2, b3, yb3)
-    units = ((0, 0, 1, 0), (1, 0, 0, 0), (2, 0, 3, 0), (2, 1, 4, 0), (3, 0, 2, 0), (3, 1, 5, 0), (4, 0, 2, 1), (5, 0, 3, 1))
-    keeps = (keep0, keep1, keep2, keep3, keep4)
-    gots = (got0, got1, got2, got3, got4)
-    own0, away0 = grad(table, units, buffers, (*keeps, keep5), (*gots, got5), kept, 0, 2)
-    own0, away0, got6 = gate((own0, away0, got6))
+    table, yb3, got5 = gate((table, yb3, got5))
+    keep7, send7 = partial(table, (b3, yb3), weights, 0, 2)
+    table, send7 = gate((table, send7))
+    got7 = swap_x(send7)
+    keep8, send8 = partial(table, (b3, yb3), weights, 1, 2)
+    table, send8, got6 = gate((table, send8, got6))
+    got8 = swap_x(send8)
+
+    buffers = (a0, ya0, b0, yb0, a1, ya1, b1, yb1, a2, ya2, a3, ya3, b2, yb2, b3, yb3)
+    units = ((0, 0, 1, 0), (1, 0, 0, 0), (2, 0, 3, 0), (3, 0, 2, 0), (4, 0, 6, 0), (5, 0, 7, 0), (6, 0, 4, 0), (7, 0, 5, 0))
+    keeps = (keep0, keep1, keep2, keep3, keep4, keep5, keep6)
+    gots = (got0, got1, got2, got3, got4, got5, got6)
+    own0, away0 = grad(table, units, buffers, (*keeps, keep7), (*gots, got7), kept, 0, 2)
+    own0, away0, got8 = gate((own0, away0, got8))
     back0 = swap_core(away0)
-    own1, away1 = grad(table, units, buffers, (*keeps, keep6), (*gots, got6), kept, 1, 2)
+    own1, away1 = grad(table, units, buffers, (*keeps, keep8), (*gots, got8), kept, 1, 2)
     own1, away1, back0 = gate((own1, away1, back0))
     back1 = swap_core(away1)
     outs = total(own0, back0, (), 0, 2)

time: 132 us -> 121 us (0.917)
  waiting for transfers between devices: 58.3 us -> 27.2 us
  starting transfers between devices: 25.7 us -> 38.9 us
  Pallas kernels: 40.5 us -> 48 us
    ppermute x2, waiting for transfers between devices: 14.6 us -> 0.63 us  [far(): return lax.ppermute(v, 'col', [(c, c ^ 4) for c in range(COLS)])]
    ppermute x8, waiting for transfers between devices: 15.6 us -> 4.04 us  [swap_y(): return lax.ppermute(v, 'col', [(c, c ^ 1) for c in range(COLS)])]
    ppermute x8 -> x10, starting transfers between devices: 9.34 us -> 19.7 us  [swap_x(): return lax.ppermute(v, 'row', [(r, r ^ 2) for r in range(ROWS)])]
    ppermute x8 -> x10, waiting for transfers between devices: 17.3 us -> 7.98 us  [swap_x(): return lax.ppermute(v, 'row', [(r, r ^ 2) for r in range(ROWS)])]
    ppermute x4, waiting for transfers between devices: 7.34 us -> 12.3 us  [near(): return lax.ppermute(v, 'col', [(c, c ^ 2) for c in range(COLS)])]
    pallas_call x0 -> x1, Pallas kernels: none -> 4.64 us  [pack(): pl.pallas_call(pack_kernel, grid=(width // wide,), in_specs=[pl.BlockSpec...]
    pallas_call x7 -> x9, Pallas kernels: 24.8 us -> 29.2 us  [partial(): pl.pallas_call(functools.partial(partial_kernel, len(buffers), 2 * kept /...]
    pallas_call x2, Pallas kernels: 11.8 us -> 10.2 us  [grad(): pl.pallas_call(functools.partial(grad_kernel, units, len(buffers), len(ke...]
  transfers between devices with their start and end apart: 26 -> 28, of which waited for: 15 -> 9; matrix products, arithmetic and copies ran while one was open for 3% -> 2% of each run, Pallas kernels for 29% -> 38%
where the time goes in v3:
time: 121 us; the launch traced here: 120 us
  Pallas kernels  48 us (40%)
  starting transfers between devices  38.9 us (32%)
  waiting for transfers between devices  27.2 us (22%)
  local copies, waits for them, and re-layouts  4.38 us (4%)
    pallas_call x9, Pallas kernels, partial(): pl.pallas_call(functools.partial(partial_kernel, len(buffers), 2 * kept /...  29.2 us
    ppermute x10, starting transfers between devices, swap_x(): return lax.ppermute(v, 'row', [(r, r ^ 2) for r in range(ROWS)])  19.7 us
    ppermute x4, waiting for transfers between devices, near(): return lax.ppermute(v, 'col', [(c, c ^ 2) for c in range(COLS)])  12.3 us
    pallas_call x2, Pallas kernels, grad(): pl.pallas_call(functools.partial(grad_kernel, units, len(buffers), len(ke...  10.2 us
    ppermute x10, waiting for transfers between devices, swap_x(): return lax.ppermute(v, 'row', [(r, r ^ 2) for r in range(ROWS)])  7.98 us
    ppermute x8, starting transfers between devices, swap_y(): return lax.ppermute(v, 'col', [(c, c ^ 1) for c in range(COLS)])  7.67 us
    ppermute x2, starting transfers between devices, far(): return lax.ppermute(v, 'col', [(c, c ^ 4) for c in range(COLS)])  5.64 us
    ppermute x4, starting transfers between devices, near(): return lax.ppermute(v, 'col', [(c, c ^ 2) for c in range(COLS)])  4.65 us
  transfers between devices with their start and end apart: 28, of which 9 were waited for; matrix products, arithmetic and copies ran while one was open for 2% of the time, Pallas kernels for 38%

profile of v3, /device:TPU:0, one launch (start us, length us, event | category | flops | bytes accessed | tf_op | source)
XLA Modules:
  0.0 120.4 jit_solution(9505777061027076882)
XLA Ops:
  2.3 3.1 %collective-permute-start.4 = (bf16[2,16,6144]{2,1,0:T(8,128)(2,1)S(1)}, bf16[2,16,6144]{2,1,0:T(8,128)(2,1)S(1)}, u32[]{:S(2)}, u32[]{:S(2)}) collective-permute-start(bf16[2,16,6144]{2,1,0:T(8,128)(2,1)S(1)} %pad_maximum_fusion.refs_0_), channel_id=1, source_target_pairs={{0,2},{1,3},{2,0},{3,1},{4,6},{5,7},{6,4},{7,5},{8,10},{9,11},{10,... | collective-permute-start | bytes 1179656 | tf_op jit(solution)/shard_map/ppermute | solution.py:243
  9.5 1.7 %copy-done = bf16[384,3072]{1,0:T(8,128)(2,1)S(1)} copy-done((bf16[384,3072]{1,0:T(8,128)(2,1)S(1)}, bf16[384,3072]{1,0:T(8,128)(2,1)}, u32[]{:S(2)}) %copy-start) | copy-done | bytes 2359320
  11.1 1.7 %copy-done.1 = bf16[384,3072]{1,0:T(8,128)(2,1)S(1)} copy-done((bf16[384,3072]{1,0:T(8,128)(2,1)S(1)}, bf16[384,3072]{1,0:T(8,128)(2,1)}, u32[]{:S(2)}) %copy-start.1) | copy-done | bytes 2359320
  12.8 4.6 %pack.1.refs_2_ = bf16[4,384,3072]{2,1,0:T(8,128)(2,1)S(1)} custom-call(bf16[384,3072]{1,0:T(8,128)(2,1)S(1)} %copy-done, bf16[384,3072]{1,0:T(8,128)(2,1)S(1)} %copy-done.1, bf16[384,3072]{1,0:T(8,128)(2,1)} %collective-permute-done.refs_2_, bf16[384,3072]{1,0:T(8,128)(2,1)} %collective-permute-done.1.refs_3_), custom_call_target="tpu_custom_call" | custom-call | tf_op jit(solution)/shard_map/pack/pallas_call | solution.py:92
  17.5 2.5 %collective-permute-start.5 = (bf16[2,16,6144]{2,1,0:T(8,128)(2,1)S(1)}, bf16[2,16,6144]{2,1,0:T(8,128)(2,1)S(1)}, u32[]{:S(2)}, u32[]{:S(2)}) collective-permute-start(bf16[2,16,6144]{2,1,0:T(8,128)(2,1)S(1)} %collective-permute-done.2.refs_0_.refs_2_), channel_id=1, source_target_pairs={{0,1},{1,0},{2,3},{3,2},{4,5},{5,4},{6,7},{7,6},{8,9},{9,8},{10,11... | collective-permute-start | bytes 1179656 | tf_op jit(solution)/shard_map/ppermute | solution.py:240
  21.6 2.6 %collective-permute-start.9 = (bf16[2,16,6144]{2,1,0:T(8,128)(2,1)S(1)}, bf16[2,16,6144]{2,1,0:T(8,128)(2,1)S(1)}, u32[]{:S(2)}, u32[]{:S(2)}) collective-permute-start(bf16[2,16,6144]{2,1,0:T(8,128)(2,1)S(1)} %pad_maximum_fusion.refs_0_), channel_id=1, source_target_pairs={{0,4},{1,5},{2,6},{3,7},{4,0},{5,1},{6,2},{7,3},{8,12},{9,13},{10,... | collective-permute-start | bytes 1179656 | tf_op jit(solution)/shard_map/ppermute | solution.py:246
  24.2 3.6 %partial.9 = (f32[2,32,3072]{2,1,0:T(8,128)S(1)}, bf16[2,32,3072]{2,1,0:T(8,128)(2,1)S(1)}) custom-call(s32[288]{0:T(512)S(1)} %reshape.7.table, bf16[2,16,6144]{2,1,0:T(8,128)(2,1)S(1)} %pad_maximum_fusion.refs_0_, bf16[2,16,6144]{2,1,0:T(8,128)(2,1)S(1)} %collective-permute-done.3.refs_1_, bf16[4,384,3072]{2,1,0:T(8,128)(2,1)S(1)} %pack.1.refs_2_), custom_call_target="tpu_custom_call" | custom-call | tf_op jit(solution)/shard_map/partial/pallas_call | solution.py:125
  29.8 3.6 %partial.10 = (f32[2,32,3072]{2,1,0:T(8,128)S(1)}, bf16[2,32,3072]{2,1,0:T(8,128)(2,1)S(1)}) custom-call(s32[288]{0:T(512)S(1)} %reshape.7.table, bf16[2,16,6144]{2,1,0:T(8,128)(2,1)S(1)} %collective-permute-done.2.refs_0_.refs_2_, bf16[2,16,6144]{2,1,0:T(8,128)(2,1)S(1)} %collective-permute-done.5.refs_1_.refs_3_, bf16[4,384,3072]{2,1,0:T(8,128)(2,1)S(1)} %pack.1.refs_2_), custom_call_target="tpu_custom_call" | custom-call | tf_op jit(solution)/shard_map/partial/pallas_call | solution.py:125
  33.4 5.7 %collective-permute-done.6.refs_0_.refs_6_ = bf16[2,16,6144]{2,1,0:T(8,128)(2,1)S(1)} collective-permute-done((bf16[2,16,6144]{2,1,0:T(8,128)(2,1)S(1)}, bf16[2,16,6144]{2,1,0:T(8,128)(2,1)S(1)}, u32[]{:S(2)}, u32[]{:S(2)}) %collective-permute-start.6) | collective-permute-done | bytes 393248 | tf_op jit(solution)/shard_map/ppermute | solution.py:243
  41.2 3.6 %partial.11 = (f32[2,32,3072]{2,1,0:T(8,128)S(1)}, bf16[2,32,3072]{2,1,0:T(8,128)(2,1)S(1)}) custom-call(s32[288]{0:T(512)S(1)} %reshape.7.table, bf16[2,16,6144]{2,1,0:T(8,128)(2,1)S(1)} %collective-permute-done.4.refs_0_.refs_4_, bf16[2,16,6144]{2,1,0:T(8,128)(2,1)S(1)} %collective-permute-done.8.refs_1_.refs_5_, bf16[4,384,3072]{2,1,0:T(8,128)(2,1)S(1)} %pack.1.refs_2_), custom_call_target="tpu_custom_call" | custom-call | tf_op jit(solution)/shard_map/partial/pallas_call | solution.py:125
  44.8 4.4 %collective-permute-done.10.refs_25_ = bf16[2,32,3072]{2,1,0:T(8,128)(2,1)S(1)} collective-permute-done((bf16[2,32,3072]{2,1,0:T(8,128)(2,1)S(1)}, bf16[2,32,3072]{2,1,0:T(8,128)(2,1)S(1)}, u32[]{:S(2)}, u32[]{:S(2)}) %collective-permute-start.10) | collective-permute-done | bytes 393248 | tf_op jit(solution)/shard_map/ppermute | solution.py:234
  51.2 3.0 %collective-permute-start.15 = (bf16[2,16,6144]{2,1,0:T(8,128)(2,1)S(1)}, bf16[2,16,6144]{2,1,0:T(8,128)(2,1)S(1)}, u32[]{:S(2)}, u32[]{:S(2)}) collective-permute-start(bf16[2,16,6144]{2,1,0:T(8,128)(2,1)S(1)} %collective-permute-done.2.refs_0_.refs_2_), channel_id=1, source_target_pairs={{0,4},{1,5},{2,6},{3,7},{4,0},{5,1},{6,2},{7,3},{8,12},{9,13},{10,... | collective-permute-start | bytes 1179656 | tf_op jit(solution)/shard_map/ppermute | solution.py:246
  54.2 3.6 %partial.12 = (f32[2,32,3072]{2,1,0:T(8,128)S(1)}, bf16[2,32,3072]{2,1,0:T(8,128)(2,1)S(1)}) custom-call(s32[288]{0:T(512)S(1)} %reshape.7.table, bf16[2,16,6144]{2,1,0:T(8,128)(2,1)S(1)} %collective-permute-done.6.refs_0_.refs_6_, bf16[2,16,6144]{2,1,0:T(8,128)(2,1)S(1)} %collective-permute-done.11.refs_1_.refs_7_, bf16[4,384,3072]{2,1,0:T(8,128)(2,1)S(1)} %pack.1.refs_2_), custom_call_target="tpu_custom_call" | custom-call | tf_op jit(solution)/shard_map/partial/pallas_call | solution.py:125
  58.4 6.6 %collective-permute-done.12.refs_0_.refs_10_ = bf16[2,16,6144]{2,1,0:T(8,128)(2,1)S(1)} collective-permute-done((bf16[2,16,6144]{2,1,0:T(8,128)(2,1)S(1)}, bf16[2,16,6144]{2,1,0:T(8,128)(2,1)S(1)}, u32[]{:S(2)}, u32[]{:S(2)}) %collective-permute-start.12) | collective-permute-done | bytes 393248 | tf_op jit(solution)/shard_map/ppermute | solution.py:243
  65.0 3.6 %partial.13 = (f32[2,32,3072]{2,1,0:T(8,128)S(1)}, bf16[2,32,3072]{2,1,0:T(8,128)(2,1)S(1)}) custom-call(s32[288]{0:T(512)S(1)} %reshape.7.table, bf16[2,16,6144]{2,1,0:T(8,128)(2,1)S(1)} %collective-permute-done.9.refs_0_.refs_8_, bf16[2,16,6144]{2,1,0:T(8,128)(2,1)S(1)} %collective-permute-done.13.refs_1_.refs_9_, bf16[4,384,3072]{2,1,0:T(8,128)(2,1)S(1)} %pack.1.refs_2_), custom_call_target="tpu_custom_call" | custom-call | tf_op jit(solution)/shard_map/partial/pallas_call | solution.py:125
  69.3 1.6 %collective-permute-start.20 = (bf16[2,32,3072]{2,1,0:T(8,128)(2,1)S(1)}, bf16[2,32,3072]{2,1,0:T(8,128)(2,1)S(1)}, u32[]{:S(2)}, u32[]{:S(2)}) collective-permute-start(bf16[2,32,3072]{2,1,0:T(8,128)(2,1)S(1)} %get-tuple-element.132), channel_id=1, source_target_pairs={{0,16},{8,24},{16,0},{24,8},{1,17},{9,25},{17,1},{25,9},{2,18},{10... | collective-permute-start | bytes 1179656 | tf_op jit(solution)/shard_map/ppermute | solution.py:234
  70.9 2.0 %collective-permute-start.19 = (bf16[2,16,6144]{2,1,0:T(8,128)(2,1)S(1)}, bf16[2,16,6144]{2,1,0:T(8,128)(2,1)S(1)}, u32[]{:S(2)}, u32[]{:S(2)}) collective-permute-start(bf16[2,16,6144]{2,1,0:T(8,128)(2,1)S(1)} %collective-permute-done.15.refs_0_.refs_12_), channel_id=1, source_target_pairs={{0,1},{1,0},{2,3},{3,2},{4,5},{5,4},{6,7},{7,6},{8,9},{9,8},{10,11... | collective-permute-start | bytes 1179656 | tf_op jit(solution)/shard_map/ppermute | solution.py:240
  72.9 2.8 %collective-permute-done.16.refs_1_.refs_11_ = bf16[2,16,6144]{2,1,0:T(8,128)(2,1)S(1)} collective-permute-done((bf16[2,16,6144]{2,1,0:T(8,128)(2,1)S(1)}, bf16[2,16,6144]{2,1,0:T(8,128)(2,1)S(1)}, u32[]{:S(2)}, u32[]{:S(2)}) %collective-permute-start.16) | collective-permute-done | bytes 393248 | tf_op jit(solution)/shard_map/ppermute | solution.py:240
  75.7 3.6 %partial.14 = (f32[2,32,3072]{2,1,0:T(8,128)S(1)}, bf16[2,32,3072]{2,1,0:T(8,128)(2,1)S(1)}) custom-call(s32[288]{0:T(512)S(1)} %reshape.7.table, bf16[2,16,6144]{2,1,0:T(8,128)(2,1)S(1)} %collective-permute-done.12.refs_0_.refs_10_, bf16[2,16,6144]{2,1,0:T(8,128)(2,1)S(1)} %collective-permute-done.16.refs_1_.refs_11_, bf16[4,384,3072]{2,1,0:T(8,128)(2,1)S(1)} %pack.1.refs_2_), custom_call_target="tpu_custom_call" | custom-call | tf_op jit(solution)/shard_map/partial/pallas_call | solution.py:125
  79.4 3.5 %collective-permute-start.22 = (bf16[2,32,3072]{2,1,0:T(8,128)(2,1)S(1)}, bf16[2,32,3072]{2,1,0:T(8,128)(2,1)S(1)}, u32[]{:S(2)}, u32[]{:S(2)}) collective-permute-start(bf16[2,32,3072]{2,1,0:T(8,128)(2,1)S(1)} %get-tuple-element.138), channel_id=1, source_target_pairs={{0,16},{8,24},{16,0},{24,8},{1,17},{9,25},{17,1},{25,9},{2,18},{10... | collective-permute-start | bytes 1179656 | tf_op jit(solution)/shard_map/ppermute | solution.py:234
  84.1 3.6 %partial.15 = (f32[2,32,3072]{2,1,0:T(8,128)S(1)}, bf16[2,32,3072]{2,1,0:T(8,128)(2,1)S(1)}) custom-call(s32[288]{0:T(512)S(1)} %reshape.7.table, bf16[2,16,6144]{2,1,0:T(8,128)(2,1)S(1)} %collective-permute-done.15.refs_0_.refs_12_, bf16[2,16,6144]{2,1,0:T(8,128)(2,1)S(1)} %collective-permute-done.19.refs_1_.refs_13_, bf16[4,384,3072]{2,1,0:T(8,128)(2,1)S(1)} %pack.1.refs_2_), custom_call_target="tpu_custom_call" | custom-call | tf_op jit(solution)/shard_map/partial/pallas_call | solution.py:125
  87.7 3.5 %collective-permute-start.23 = (bf16[2,32,3072]{2,1,0:T(8,128)(2,1)S(1)}, bf16[2,32,3072]{2,1,0:T(8,128)(2,1)S(1)}, u32[]{:S(2)}, u32[]{:S(2)}) collective-permute-start(bf16[2,32,3072]{2,1,0:T(8,128)(2,1)S(1)} %get-tuple-element.144), channel_id=1, source_target_pairs={{0,16},{8,24},{16,0},{24,8},{1,17},{9,25},{17,1},{25,9},{2,18},{10... | collective-permute-start | bytes 1179656 | tf_op jit(solution)/shard_map/ppermute | solution.py:234
  91.3 2.1 %partial.16 = (f32[2,32,1536]{2,1,0:T(8,128)S(1)}, bf16[2,32,1536]{2,1,0:T(8,128)(2,1)S(1)}) custom-call(s32[288]{0:T(512)S(1)} %reshape.7.table, bf16[2,16,6144]{2,1,0:T(8,128)(2,1)S(1)} %collective-permute-done.18.refs_0_.refs_14_, bf16[2,16,6144]{2,1,0:T(8,128)(2,1)S(1)} %collective-permute-done.21.refs_1_.refs_15_, bf16[4,384,3072]{2,1,0:T(8,128)(2,1)S(1)} %pack.1.refs_2_), custom_call_target="tpu_custom_call" | custom-call | tf_op jit(solution)/shard_map/partial/pallas_call | solution.py:125
  93.4 2.1 %collective-permute-start.24 = (bf16[2,32,1536]{2,1,0:T(8,128)(2,1)S(1)}, bf16[2,32,1536]{2,1,0:T(8,128)(2,1)S(1)}, u32[]{:S(2)}, u32[]{:S(2)}) collective-permute-start(bf16[2,32,1536]{2,1,0:T(8,128)(2,1)S(1)} %get-tuple-element.162), channel_id=1, source_target_pairs={{0,16},{8,24},{16,0},{24,8},{1,17},{9,25},{17,1},{25,9},{2,18},{10... | collective-permute-start | bytes 589832 | tf_op jit(solution)/shard_map/ppermute | solution.py:234
  95.5 2.1 %partial.17 = (f32[2,32,1536]{2,1,0:T(8,128)S(1)}, bf16[2,32,1536]{2,1,0:T(8,128)(2,1)S(1)}) custom-call(s32[288]{0:T(512)S(1)} %reshape.7.table, bf16[2,16,6144]{2,1,0:T(8,128)(2,1)S(1)} %collective-permute-done.18.refs_0_.refs_14_, bf16[2,16,6144]{2,1,0:T(8,128)(2,1)S(1)} %collective-permute-done.21.refs_1_.refs_15_, bf16[4,384,3072]{2,1,0:T(8,128)(2,1)S(1)} %pack.1.refs_2_), custom_call_target="tpu_custom_call" | custom-call | tf_op jit(solution)/shard_map/partial/pallas_call | solution.py:125
  97.6 3.4 %collective-permute-done.23.refs_30_ = bf16[2,32,3072]{2,1,0:T(8,128)(2,1)S(1)} collective-permute-done((bf16[2,32,3072]{2,1,0:T(8,128)(2,1)S(1)}, bf16[2,32,3072]{2,1,0:T(8,128)(2,1)S(1)}, u32[]{:S(2)}, u32[]{:S(2)}) %collective-permute-start.23) | collective-permute-done | bytes 393248 | tf_op jit(solution)/shard_map/ppermute | solution.py:234
  101.0 2.3 %collective-permute-start.25 = (bf16[2,32,1536]{2,1,0:T(8,128)(2,1)S(1)}, bf16[2,32,1536]{2,1,0:T(8,128)(2,1)S(1)}, u32[]{:S(2)}, u32[]{:S(2)}) collective-permute-start(bf16[2,32,1536]{2,1,0:T(8,128)(2,1)S(1)} %get-tuple-element.165), channel_id=1, source_target_pairs={{0,16},{8,24},{16,0},{24,8},{1,17},{9,25},{17,1},{25,9},{2,18},{10... | collective-permute-start | bytes 589832 | tf_op jit(solution)/shard_map/ppermute | solution.py:234
  103.4 5.1 %grad.2 = (bf16[2,384,1536]{2,1,0:T(8,128)(2,1)S(1)}, bf16[2,384,1536]{2,1,0:T(8,128)(2,1)S(1)}) custom-call(s32[288]{0:T(512)S(1)} %reshape.7.table, bf16[2,16,6144]{2,1,0:T(8,128)(2,1)S(1)} %pad_maximum_fusion.refs_0_, bf16[2,16,6144]{2,1,0:T(8,128)(2,1)S(1)} %collective-permute-done.3.refs_1_, ...), custom_call_target="tpu_custom_call" | custom-call | tf_op jit(solution)/shard_map/grad/pallas_call | solution.py:185
  108.6 5.2 %grad.3 = (bf16[2,384,1536]{2,1,0:T(8,128)(2,1)S(1)}, bf16[2,384,1536]{2,1,0:T(8,128)(2,1)S(1)}) custom-call(s32[288]{0:T(512)S(1)} %reshape.7.table, bf16[2,16,6144]{2,1,0:T(8,128)(2,1)S(1)} %pad_maximum_fusion.refs_0_, bf16[2,16,6144]{2,1,0:T(8,128)(2,1)S(1)} %collective-permute-done.3.refs_1_, ...), custom_call_target="tpu_custom_call" | custom-call | tf_op jit(solution)/shard_map/grad/pallas_call | solution.py:185
  114.3 1.9 %total.2 = (bf16[384,3072]{1,0:T(8,128)(2,1)}, bf16[384,3072]{1,0:T(8,128)(2,1)}) custom-call(bf16[2,384,1536]{2,1,0:T(8,128)(2,1)S(1)} %get-tuple-element.172.own_ref, bf16[2,384,1536]{2,1,0:T(8,128)(2,1)S(1)} %collective-permute-done.26.got_ref), custom_call_target="tpu_custom_call" | custom-call | tf_op jit(solution)/shard_map/total/pallas_call | solution.py:213
  116.2 2.2 %collective-permute-done.27.got_ref = bf16[2,384,1536]{2,1,0:T(8,128)(2,1)S(1)} collective-permute-done((bf16[2,384,1536]{2,1,0:T(8,128)(2,1)S(1)}, bf16[2,384,1536]{2,1,0:T(8,128)(2,1)S(1)}, u32[]{:S(2)}, u32[]{:S(2)}) %collective-permute-start.27) | collective-permute-done | bytes 2359328 | tf_op jit(solution)/shard_map/ppermute | solution.py:237
  118.5 1.9 %total.3 = (bf16[384,3072]{1,0:T(8,128)(2,1)}, bf16[384,3072]{1,0:T(8,128)(2,1)}) custom-call(bf16[2,384,1536]{2,1,0:T(8,128)(2,1)S(1)} %get-tuple-element.170.own_ref, bf16[2,384,1536]{2,1,0:T(8,128)(2,1)S(1)} %collective-permute-done.27.got_ref, bf16[384,3072]{1,0:T(8,128)(2,1)} %get-tuple-element.174.refs_0_, ...), custom_call_target="tpu_custom_call", output_to_operand_aliasing={{0}: (2, {}), {1}: (3, {})} | custom-call | tf_op jit(solution)/shard_map/total/pallas_call | solution.py:213
  (47 shorter events, 16.7 us)
Async XLA Ops:
  0.6 8.8 %collective-permute-start = (bf16[384,3072]{1,0:T(8,128)(2,1)}, bf16[384,3072]{1,0:T(8,128)(2,1)}, u32[]{:S(2)}, u32[]{:S(2)}) collective-permute-start(bf16[384,3072]{1,0:T(8,128)(2,1)} %refs_0_.1), channel_id=1, source_target_pairs={{0,8},{8,0},{16,24},{24,16},{1,9},{9,1},{17,25},{25,17},{2,10},{10... | collective-permute-start | bytes 7077896 | tf_op jit(solution)/shard_map/ppermute | solution.py:237
  1.1 8.3 %collective-permute-start.1 = (bf16[384,3072]{1,0:T(8,128)(2,1)}, bf16[384,3072]{1,0:T(8,128)(2,1)}, u32[]{:S(2)}, u32[]{:S(2)}) collective-permute-start(bf16[384,3072]{1,0:T(8,128)(2,1)} %refs_1_.1), channel_id=1, source_target_pairs={{0,8},{8,0},{16,24},{24,16},{1,9},{9,1},{17,25},{25,17},{2,10},{10... | collective-permute-start | bytes 7077896 | tf_op jit(solution)/shard_map/ppermute | solution.py:237
  2.3 15.2 %collective-permute-start.4 = (bf16[2,16,6144]{2,1,0:T(8,128)(2,1)S(1)}, bf16[2,16,6144]{2,1,0:T(8,128)(2,1)S(1)}, u32[]{:S(2)}, u32[]{:S(2)}) collective-permute-start(bf16[2,16,6144]{2,1,0:T(8,128)(2,1)S(1)} %pad_maximum_fusion.refs_0_), channel_id=1, source_target_pairs={{0,2},{1,3},{2,0},{3,1},{4,6},{5,7},{6,4},{7,5},{8,10},{9,11},{10,... | collective-permute-start | bytes 1179656 | tf_op jit(solution)/shard_map/ppermute | solution.py:243
  5.4 12.1 %collective-permute-start.3 = (bf16[2,16,6144]{2,1,0:T(8,128)(2,1)S(1)}, bf16[2,16,6144]{2,1,0:T(8,128)(2,1)S(1)}, u32[]{:S(2)}, u32[]{:S(2)}) collective-permute-start(bf16[2,16,6144]{2,1,0:T(8,128)(2,1)S(1)} %pad_maximum_fusion.refs_0_), channel_id=1, source_target_pairs={{0,1},{1,0},{2,3},{3,2},{4,5},{5,4},{6,7},{7,6},{8,9},{9,8},{10,11... | collective-permute-start | bytes 1179656 | tf_op jit(solution)/shard_map/ppermute | solution.py:240
  6.9 10.6 %collective-permute-start.2 = (bf16[2,16,6144]{2,1,0:T(8,128)(2,1)S(1)}, bf16[2,16,6144]{2,1,0:T(8,128)(2,1)S(1)}, u32[]{:S(2)}, u32[]{:S(2)}) collective-permute-start(bf16[2,16,6144]{2,1,0:T(8,128)(2,1)S(1)} %pad_maximum_fusion.refs_0_), channel_id=1, source_target_pairs={{0,16},{8,24},{16,0},{24,8},{1,17},{9,25},{17,1},{25,9},{2,18},{10... | collective-permute-start | bytes 1179656 | tf_op jit(solution)/shard_map/ppermute | solution.py:234
  9.5 1.7 %copy-start = (bf16[384,3072]{1,0:T(8,128)(2,1)S(1)}, bf16[384,3072]{1,0:T(8,128)(2,1)}, u32[]{:S(2)}) copy-start(bf16[384,3072]{1,0:T(8,128)(2,1)} %refs_0_.1) | copy-start | bytes 7077892
  11.1 1.7 %copy-start.1 = (bf16[384,3072]{1,0:T(8,128)(2,1)S(1)}, bf16[384,3072]{1,0:T(8,128)(2,1)}, u32[]{:S(2)}) copy-start(bf16[384,3072]{1,0:T(8,128)(2,1)} %refs_1_.1) | copy-start | bytes 7077892
  17.5 12.4 %collective-permute-start.5 = (bf16[2,16,6144]{2,1,0:T(8,128)(2,1)S(1)}, bf16[2,16,6144]{2,1,0:T(8,128)(2,1)S(1)}, u32[]{:S(2)}, u32[]{:S(2)}) collective-permute-start(bf16[2,16,6144]{2,1,0:T(8,128)(2,1)S(1)} %collective-permute-done.2.refs_0_.refs_2_), channel_id=1, source_target_pairs={{0,1},{1,0},{2,3},{3,2},{4,5},{5,4},{6,7},{7,6},{8,9},{9,8},{10,11... | collective-permute-start | bytes 1179656 | tf_op jit(solution)/shard_map/ppermute | solution.py:240
  20.0 19.2 %collective-permute-start.6 = (bf16[2,16,6144]{2,1,0:T(8,128)(2,1)S(1)}, bf16[2,16,6144]{2,1,0:T(8,128)(2,1)S(1)}, u32[]{:S(2)}, u32[]{:S(2)}) collective-permute-start(bf16[2,16,6144]{2,1,0:T(8,128)(2,1)S(1)} %collective-permute-done.2.refs_0_.refs_2_), channel_id=1, source_target_pairs={{0,2},{1,3},{2,0},{3,1},{4,6},{5,7},{6,4},{7,5},{8,10},{9,11},{10,... | collective-permute-start | bytes 1179656 | tf_op jit(solution)/shard_map/ppermute | solution.py:243
  21.6 23.2 %collective-permute-start.9 = (bf16[2,16,6144]{2,1,0:T(8,128)(2,1)S(1)}, bf16[2,16,6144]{2,1,0:T(8,128)(2,1)S(1)}, u32[]{:S(2)}, u32[]{:S(2)}) collective-permute-start(bf16[2,16,6144]{2,1,0:T(8,128)(2,1)S(1)} %pad_maximum_fusion.refs_0_), channel_id=1, source_target_pairs={{0,4},{1,5},{2,6},{3,7},{4,0},{5,1},{6,2},{7,3},{8,12},{9,13},{10,... | collective-permute-start | bytes 1179656 | tf_op jit(solution)/shard_map/ppermute | solution.py:246
  27.8 12.9 %collective-permute-start.7 = (bf16[2,32,3072]{2,1,0:T(8,128)(2,1)S(1)}, bf16[2,32,3072]{2,1,0:T(8,128)(2,1)S(1)}, u32[]{:S(2)}, u32[]{:S(2)}) collective-permute-start(bf16[2,32,3072]{2,1,0:T(8,128)(2,1)S(1)} %get-tuple-element.101), channel_id=1, source_target_pairs={{0,16},{8,24},{16,0},{24,8},{1,17},{9,25},{17,1},{25,9},{2,18},{10... | collective-permute-start | bytes 1179656 | tf_op jit(solution)/shard_map/ppermute | solution.py:234
  29.3 11.9 %collective-permute-start.8 = (bf16[2,16,6144]{2,1,0:T(8,128)(2,1)S(1)}, bf16[2,16,6144]{2,1,0:T(8,128)(2,1)S(1)}, u32[]{:S(2)}, u32[]{:S(2)}) collective-permute-start(bf16[2,16,6144]{2,1,0:T(8,128)(2,1)S(1)} %collective-permute-done.4.refs_0_.refs_4_), channel_id=1, source_target_pairs={{0,1},{1,0},{2,3},{3,2},{4,5},{5,4},{6,7},{7,6},{8,9},{9,8},{10,11... | collective-permute-start | bytes 1179656 | tf_op jit(solution)/shard_map/ppermute | solution.py:240
  39.2 10.0 %collective-permute-start.10 = (bf16[2,32,3072]{2,1,0:T(8,128)(2,1)S(1)}, bf16[2,32,3072]{2,1,0:T(8,128)(2,1)S(1)}, u32[]{:S(2)}, u32[]{:S(2)}) collective-permute-start(bf16[2,32,3072]{2,1,0:T(8,128)(2,1)S(1)} %get-tuple-element.108), channel_id=1, source_target_pairs={{0,16},{8,24},{16,0},{24,8},{1,17},{9,25},{17,1},{25,9},{2,18},{10... | collective-permute-start | bytes 1179656 | tf_op jit(solution)/shard_map/ppermute | solution.py:234
  40.7 13.6 %collective-permute-start.11 = (bf16[2,16,6144]{2,1,0:T(8,128)(2,1)S(1)}, bf16[2,16,6144]{2,1,0:T(8,128)(2,1)S(1)}, u32[]{:S(2)}, u32[]{:S(2)}) collective-permute-start(bf16[2,16,6144]{2,1,0:T(8,128)(2,1)S(1)} %collective-permute-done.6.refs_0_.refs_6_), channel_id=1, source_target_pairs={{0,1},{1,0},{2,3},{3,2},{4,5},{5,4},{6,7},{7,6},{8,9},{9,8},{10,11... | collective-permute-start | bytes 1179656 | tf_op jit(solution)/shard_map/ppermute | solution.py:240
  49.2 15.8 %collective-permute-start.12 = (bf16[2,16,6144]{2,1,0:T(8,128)(2,1)S(1)}, bf16[2,16,6144]{2,1,0:T(8,128)(2,1)S(1)}, u32[]{:S(2)}, u32[]{:S(2)}) collective-permute-start(bf16[2,16,6144]{2,1,0:T(8,128)(2,1)S(1)} %collective-permute-done.9.refs_0_.refs_8_), channel_id=1, source_target_pairs={{0,2},{1,3},{2,0},{3,1},{4,6},{5,7},{6,4},{7,5},{8,10},{9,11},{10,... | collective-permute-start | bytes 1179656 | tf_op jit(solution)/shard_map/ppermute | solution.py:243
  49.2 15.8 %collective-permute-start.14 = (bf16[2,32,3072]{2,1,0:T(8,128)(2,1)S(1)}, bf16[2,32,3072]{2,1,0:T(8,128)(2,1)S(1)}, u32[]{:S(2)}, u32[]{:S(2)}) collective-permute-start(bf16[2,32,3072]{2,1,0:T(8,128)(2,1)S(1)} %get-tuple-element.118), channel_id=1, source_target_pairs={{0,16},{8,24},{16,0},{24,8},{1,17},{9,25},{17,1},{25,9},{2,18},{10... | collective-permute-start | bytes 1179656 | tf_op jit(solution)/shard_map/ppermute | solution.py:234
  50.7 14.4 %collective-permute-start.13 = (bf16[2,16,6144]{2,1,0:T(8,128)(2,1)S(1)}, bf16[2,16,6144]{2,1,0:T(8,128)(2,1)S(1)}, u32[]{:S(2)}, u32[]{:S(2)}) collective-permute-start(bf16[2,16,6144]{2,1,0:T(8,128)(2,1)S(1)} %collective-permute-done.9.refs_0_.refs_8_), channel_id=1, source_target_pairs={{0,1},{1,0},{2,3},{3,2},{4,5},{5,4},{6,7},{7,6},{8,9},{9,8},{10,11... | collective-permute-start | bytes 1179656 | tf_op jit(solution)/shard_map/ppermute | solution.py:240
  51.2 18.1 %collective-permute-start.15 = (bf16[2,16,6144]{2,1,0:T(8,128)(2,1)S(1)}, bf16[2,16,6144]{2,1,0:T(8,128)(2,1)S(1)}, u32[]{:S(2)}, u32[]{:S(2)}) collective-permute-start(bf16[2,16,6144]{2,1,0:T(8,128)(2,1)S(1)} %collective-permute-done.2.refs_0_.refs_2_), channel_id=1, source_target_pairs={{0,4},{1,5},{2,6},{3,7},{4,0},{5,1},{6,2},{7,3},{8,12},{9,13},{10,... | collective-permute-start | bytes 1179656 | tf_op jit(solution)/shard_map/ppermute | solution.py:246
  57.8 15.1 %collective-permute-start.17 = (bf16[2,32,3072]{2,1,0:T(8,128)(2,1)S(1)}, bf16[2,32,3072]{2,1,0:T(8,128)(2,1)S(1)}, u32[]{:S(2)}, u32[]{:S(2)}) collective-permute-start(bf16[2,32,3072]{2,1,0:T(8,128)(2,1)S(1)} %get-tuple-element.125), channel_id=1, source_target_pairs={{0,16},{8,24},{16,0},{24,8},{1,17},{9,25},{17,1},{25,9},{2,18},{10... | collective-permute-start | bytes 1179656 | tf_op jit(solution)/shard_map/ppermute | solution.py:234
  65.0 10.7 %collective-permute-start.16 = (bf16[2,16,6144]{2,1,0:T(8,128)(2,1)S(1)}, bf16[2,16,6144]{2,1,0:T(8,128)(2,1)S(1)}, u32[]{:S(2)}, u32[]{:S(2)}) collective-permute-start(bf16[2,16,6144]{2,1,0:T(8,128)(2,1)S(1)} %collective-permute-done.12.refs_0_.refs_10_), channel_id=1, source_target_pairs={{0,1},{1,0},{2,3},{3,2},{4,5},{5,4},{6,7},{7,6},{8,9},{9,8},{10,11... | collective-permute-start | bytes 1179656 | tf_op jit(solution)/shard_map/ppermute | solution.py:240
  69.3 10.0 %collective-permute-start.18 = (bf16[2,16,6144]{2,1,0:T(8,128)(2,1)S(1)}, bf16[2,16,6144]{2,1,0:T(8,128)(2,1)S(1)}, u32[]{:S(2)}, u32[]{:S(2)}) collective-permute-start(bf16[2,16,6144]{2,1,0:T(8,128)(2,1)S(1)} %collective-permute-done.15.refs_0_.refs_12_), channel_id=1, source_target_pairs={{0,2},{1,3},{2,0},{3,1},{4,6},{5,7},{6,4},{7,5},{8,10},{9,11},{10,... | collective-permute-start | bytes 1179656 | tf_op jit(solution)/shard_map/ppermute | solution.py:243
  69.3 13.7 %collective-permute-start.20 = (bf16[2,32,3072]{2,1,0:T(8,128)(2,1)S(1)}, bf16[2,32,3072]{2,1,0:T(8,128)(2,1)S(1)}, u32[]{:S(2)}, u32[]{:S(2)}) collective-permute-start(bf16[2,32,3072]{2,1,0:T(8,128)(2,1)S(1)} %get-tuple-element.132), channel_id=1, source_target_pairs={{0,16},{8,24},{16,0},{24,8},{1,17},{9,25},{17,1},{25,9},{2,18},{10... | collective-permute-start | bytes 1179656 | tf_op jit(solution)/shard_map/ppermute | solution.py:234
  70.9 13.3 %collective-permute-start.19 = (bf16[2,16,6144]{2,1,0:T(8,128)(2,1)S(1)}, bf16[2,16,6144]{2,1,0:T(8,128)(2,1)S(1)}, u32[]{:S(2)}, u32[]{:S(2)}) collective-permute-start(bf16[2,16,6144]{2,1,0:T(8,128)(2,1)S(1)} %collective-permute-done.15.refs_0_.refs_12_), channel_id=1, source_target_pairs={{0,1},{1,0},{2,3},{3,2},{4,5},{5,4},{6,7},{7,6},{8,9},{9,8},{10,11... | collective-permute-start | bytes 1179656 | tf_op jit(solution)/shard_map/ppermute | solution.py:240
  79.3 12.0 %collective-permute-start.21 = (bf16[2,16,6144]{2,1,0:T(8,128)(2,1)S(1)}, bf16[2,16,6144]{2,1,0:T(8,128)(2,1)S(1)}, u32[]{:S(2)}, u32[]{:S(2)}) collective-permute-start(bf16[2,16,6144]{2,1,0:T(8,128)(2,1)S(1)} %collective-permute-done.18.refs_0_.refs_14_), channel_id=1, source_target_pairs={{0,1},{1,0},{2,3},{3,2},{4,5},{5,4},{6,7},{7,6},{8,9},{9,8},{10,11... | collective-permute-start | bytes 1179656 | tf_op jit(solution)/shard_map/ppermute | solution.py:240
  79.4 11.9 %collective-permute-start.22 = (bf16[2,32,3072]{2,1,0:T(8,128)(2,1)S(1)}, bf16[2,32,3072]{2,1,0:T(8,128)(2,1)S(1)}, u32[]{:S(2)}, u32[]{:S(2)}) collective-permute-start(bf16[2,32,3072]{2,1,0:T(8,128)(2,1)S(1)} %get-tuple-element.138), channel_id=1, source_target_pairs={{0,16},{8,24},{16,0},{24,8},{1,17},{9,25},{17,1},{25,9},{2,18},{10... | collective-permute-start | bytes 1179656 | tf_op jit(solution)/shard_map/ppermute | solution.py:234
  87.7 13.3 %collective-permute-start.23 = (bf16[2,32,3072]{2,1,0:T(8,128)(2,1)S(1)}, bf16[2,32,3072]{2,1,0:T(8,128)(2,1)S(1)}, u32[]{:S(2)}, u32[]{:S(2)}) collective-permute-start(bf16[2,32,3072]{2,1,0:T(8,128)(2,1)S(1)} %get-tuple-element.144), channel_id=1, source_target_pairs={{0,16},{8,24},{16,0},{24,8},{1,17},{9,25},{17,1},{25,9},{2,18},{10... | collective-permute-start | bytes 1179656 | tf_op jit(solution)/shard_map/ppermute | solution.py:234
  93.4 10.1 %collective-permute-start.24 = (bf16[2,32,1536]{2,1,0:T(8,128)(2,1)S(1)}, bf16[2,32,1536]{2,1,0:T(8,128)(2,1)S(1)}, u32[]{:S(2)}, u32[]{:S(2)}) collective-permute-start(bf16[2,32,1536]{2,1,0:T(8,128)(2,1)S(1)} %get-tuple-element.162), channel_id=1, source_target_pairs={{0,16},{8,24},{16,0},{24,8},{1,17},{9,25},{17,1},{25,9},{2,18},{10... | collective-permute-start | bytes 589832 | tf_op jit(solution)/shard_map/ppermute | solution.py:234
  101.0 7.5 %collective-permute-start.25 = (bf16[2,32,1536]{2,1,0:T(8,128)(2,1)S(1)}, bf16[2,32,1536]{2,1,0:T(8,128)(2,1)S(1)}, u32[]{:S(2)}, u32[]{:S(2)}) collective-permute-start(bf16[2,32,1536]{2,1,0:T(8,128)(2,1)S(1)} %get-tuple-element.165), channel_id=1, source_target_pairs={{0,16},{8,24},{16,0},{24,8},{1,17},{9,25},{17,1},{25,9},{2,18},{10... | collective-permute-start | bytes 589832 | tf_op jit(solution)/shard_map/ppermute | solution.py:234
  108.5 5.2 %collective-permute-start.26 = (bf16[2,384,1536]{2,1,0:T(8,128)(2,1)S(1)}, bf16[2,384,1536]{2,1,0:T(8,128)(2,1)S(1)}, u32[]{:S(2)}, u32[]{:S(2)}) collective-permute-start(bf16[2,384,1536]{2,1,0:T(8,128)(2,1)S(1)} %get-tuple-element.169), channel_id=1, source_target_pairs={{0,8},{8,0},{16,24},{24,16},{1,9},{9,1},{17,25},{25,17},{2,10},{10... | collective-permute-start | bytes 7077896 | tf_op jit(solution)/shard_map/ppermute | solution.py:237
  113.8 4.7 %collective-permute-start.27 = (bf16[2,384,1536]{2,1,0:T(8,128)(2,1)S(1)}, bf16[2,384,1536]{2,1,0:T(8,128)(2,1)S(1)}, u32[]{:S(2)}, u32[]{:S(2)}) collective-permute-start(bf16[2,384,1536]{2,1,0:T(8,128)(2,1)S(1)} %get-tuple-element.171), channel_id=1, source_target_pairs={{0,8},{8,0},{16,24},{24,16},{1,9},{9,1},{17,25},{25,17},{2,10},{10... | collective-permute-start | bytes 7077896 | tf_op jit(solution)/shard_map/ppermute | solution.py:237

commit v4 on v3

--- a/solution.py
+++ b/solution.py
@@ -20,7 +20,8 @@
 TOTAL_VMEM = 8 * 1024 * 1024
 PACK_LANES = 4
 PACK_VMEM = 12 * 1024 * 1024
-TOTAL_LANES = 6
+TOTAL_LANES = 8
+PARTS = 3
 COST = pl.CostEstimate(flops=0, bytes_accessed=0, transcendentals=0)
 
 
@@ -255,7 +256,8 @@
         rows = lax.dynamic_slice_in_dim(keep, col * here, here, 0)
         pieces += [lax.dynamic_slice_in_dim(rows, r * mine, mine, 1) for r in (row, row ^ 1)]
     table = jnp.concatenate(pieces, axis=1).reshape(-1)
-    weights = pack(w_in, w_out, s_in, s_out)
+    held = [pltpu.with_memory_space_constraint(w, pltpu.HBM) for w in (w_in, w_out)]
+    weights = pack(*held, s_in, s_out)
     table, weights, b0, ya0, a1, a0 = gate((table, weights, b0, ya0, a1, a0))
     yb0, b1, ya1, a2 = swap_y(b0), near(b0), swap_y(a1), far(a0)
     keep0, send0 = partial(table, (a0, ya0), weights)
@@ -263,8 +265,10 @@
     got0 = swap_x(send0)
     table, yb0, b0 = gate((table, yb0, b0))
     keep1, send1 = partial(table, (b0, yb0), weights)
-    table, send1, b1 = gate((table, send1, b1))
-    got1, yb1 = swap_x(send1), swap_y(b1)
+    table, send1 = gate((table, send1))
+    got1 = swap_x(send1)
+    table, b1 = gate((table, b1))
+    yb1 = swap_y(b1)
     table, got0, b0 = gate((table, got0, b0))
     b2 = far(b0)
     table, ya1, a1 = gate((table, ya1, a1))
@@ -292,32 +296,35 @@
     table, send6 = gate((table, send6))
     got6 = swap_x(send6)
     table, yb3, got5 = gate((table, yb3, got5))
-    keep7, send7 = partial(table, (b3, yb3), weights, 0, 2)
-    table, send7 = gate((table, send7))
-    got7 = swap_x(send7)
-    keep8, send8 = partial(table, (b3, yb3), weights, 1, 2)
-    table, send8, got6 = gate((table, send8, got6))
-    got8 = swap_x(send8)
+    keep7, got7 = [], []
+    for part in range(PARTS):
+        keep, send = partial(table, (b3, yb3), weights, part, PARTS)
+        table, send = gate((table, send))
+        keep7.append(keep)
+        got7.append(swap_x(send))
+    table, got6, got7[0] = gate((table, got6, got7[0]))
 
     buffers = (a0, ya0, b0, yb0, a1, ya1, b1, yb1, a2, ya2, a3, ya3, b2, yb2, b3, yb3)
     units = ((0, 0, 1, 0), (1, 0, 0, 0), (2, 0, 3, 0), (3, 0, 2, 0), (4, 0, 6, 0), (5, 0, 7, 0), (6, 0, 4, 0), (7, 0, 5, 0))
     keeps = (keep0, keep1, keep2, keep3, keep4, keep5, keep6)
     gots = (got0, got1, got2, got3, got4, got5, got6)
-    own0, away0 = grad(table, units, buffers, (*keeps, keep7), (*gots, got7), kept, 0, 2)
-    own0, away0, got8 = gate((own0, away0, got8))
-    back0 = swap_core(away0)
-    own1, away1 = grad(table, units, buffers, (*keeps, keep8), (*gots, got8), kept, 1, 2)
-    own1, away1, back0 = gate((own1, away1, back0))
-    back1 = swap_core(away1)
-    outs = total(own0, back0, (), 0, 2)
-    return tuple(total(own1, back1, tuple(outs), 1, 2))
+    outs, waiting = (), None
+    for part in range(PARTS):
+        own, away = grad(table, units, buffers, (*keeps, keep7[part]), (*gots, got7[part]), kept, part, PARTS)
+        if part < PARTS - 1:
+            table, own, away, got7[part + 1] = gate((table, own, away, got7[part + 1]))
+        back = swap_core(away)
+        if waiting is not None:
+            outs = total(*waiting, outs, part - 1, PARTS)
+        waiting = (own, back)
+    return tuple(total(*waiting, tuple(outs), PARTS - 1, PARTS))
 
 
 def solution(mesh):
     def per_device(inputs, cotangent, w_in, w_out, keep_in, keep_out):
         kept, width = w_in.shape
         fits = kept % BLK == 0 and inputs.shape[0] % 16 == 0
-        fits = fits and all(width % (2 * lanes * BLK) == 0 for lanes in (LANES, TOTAL_LANES))
+        fits = fits and all(width % (PARTS * lanes * BLK) == 0 for lanes in (LANES, PACK_LANES, TOTAL_LANES))
         chosen = fast if fits and mesh.shape["row"] == ROWS and mesh.shape["col"] == COLS else general
         return chosen(inputs, cotangent, w_in, w_out, keep_in, keep_out)
 

time: 121 us -> 114 us (0.942)
  waiting for transfers between devices: 27.2 us -> 22.9 us
  local copies, waits for them, and re-layouts: 4.38 us -> 1.05 us
  Pallas kernels: 48 us -> 50.8 us
  starting transfers between devices: 38.9 us -> 37.3 us
    unnamed x4 -> x0, local copies, waits for them, and re-layouts: 3.33 us -> none
    ppermute x10 -> x11, waiting for transfers between devices: 7.98 us -> 5.89 us  [swap_x(): return lax.ppermute(v, 'row', [(r, r ^ 2) for r in range(ROWS)])]
    ppermute x2, waiting for transfers between devices: 0.63 us -> 2.23 us  [far(): return lax.ppermute(v, 'col', [(c, c ^ 4) for c in range(COLS)])]
    ppermute x8, waiting for transfers between devices: 4.04 us -> 2.49 us  [swap_y(): return lax.ppermute(v, 'col', [(c, c ^ 1) for c in range(COLS)])]
    ppermute x4 -> x5, waiting for transfers between devices: 2.24 us -> 0.74 us  [swap_core(): return lax.ppermute(v, 'row', [(r, r ^ 1) for r in range(ROWS)])]
    ppermute x2, starting transfers between devices: 5.64 us -> 4.38 us  [far(): return lax.ppermute(v, 'col', [(c, c ^ 4) for c in range(COLS)])]
    ppermute x10 -> x11, starting transfers between devices: 19.7 us -> 20.5 us  [swap_x(): return lax.ppermute(v, 'row', [(r, r ^ 2) for r in range(ROWS)])]
    pallas_call x9 -> x10, Pallas kernels: 29.2 us -> 30 us  [partial(): pl.pallas_call(functools.partial(partial_kernel, len(buffers), 2 * kept /...]
  transfers between devices with their start and end apart: 28 -> 30, of which waited for: 9 -> 12; matrix products, arithmetic and copies ran while one was open for 2% -> 2% of each run, Pallas kernels for 38% -> 43%
where the time goes in v4:
time: 114 us
  Pallas kernels  50.8 us (45%)
  starting transfers between devices  37.3 us (33%)
  waiting for transfers between devices  22.9 us (20%)
    pallas_call x10, Pallas kernels, partial(): pl.pallas_call(functools.partial(partial_kernel, len(buffers), 2 * kept /...  30 us
    ppermute x11, starting transfers between devices, swap_x(): return lax.ppermute(v, 'row', [(r, r ^ 2) for r in range(ROWS)])  20.5 us
    ppermute x4, waiting for transfers between devices, near(): return lax.ppermute(v, 'col', [(c, c ^ 2) for c in range(COLS)])  11.5 us
    pallas_call x3, Pallas kernels, grad(): pl.pallas_call(functools.partial(grad_kernel, units, len(buffers), len(ke...  11 us
    ppermute x8, starting transfers between devices, swap_y(): return lax.ppermute(v, 'col', [(c, c ^ 1) for c in range(COLS)])  7.47 us
    ppermute x11, waiting for transfers between devices, swap_x(): return lax.ppermute(v, 'row', [(r, r ^ 2) for r in range(ROWS)])  5.89 us
    pallas_call x1, Pallas kernels, pack(): pl.pallas_call(pack_kernel, grid=(width // wide,), in_specs=[pl.BlockSpec...  5.52 us
    ppermute x2, starting transfers between devices, far(): return lax.ppermute(v, 'col', [(c, c ^ 4) for c in range(COLS)])  4.38 us
  transfers between devices with their start and end apart: 30, of which 12 were waited for; matrix products, arithmetic and copies ran while one was open for 2% of the time, Pallas kernels for 43%

profile of v4, /device:TPU:0, one launch (start us, length us, event | category | flops | bytes accessed | tf_op | source)
XLA Modules:
  0.0 113.9 jit_solution(16576253153796048583)
XLA Ops:
  2.3 3.0 %collective-permute-start.2 = (bf16[2,16,6144]{2,1,0:T(8,128)(2,1)S(1)}, bf16[2,16,6144]{2,1,0:T(8,128)(2,1)S(1)}, u32[]{:S(2)}, u32[]{:S(2)}) collective-permute-start(bf16[2,16,6144]{2,1,0:T(8,128)(2,1)S(1)} %pad_maximum_fusion.refs_0_), channel_id=1, source_target_pairs={{0,16},{8,24},{16,0},{24,8},{1,17},{9,25},{17,1},{25,9},{2,18},{10... | collective-permute-start | bytes 1179656 | tf_op jit(solution)/shard_map/ppermute | solution.py:235
  5.3 1.5 %collective-permute-start.3 = (bf16[2,16,6144]{2,1,0:T(8,128)(2,1)S(1)}, bf16[2,16,6144]{2,1,0:T(8,128)(2,1)S(1)}, u32[]{:S(2)}, u32[]{:S(2)}) collective-permute-start(bf16[2,16,6144]{2,1,0:T(8,128)(2,1)S(1)} %pad_maximum_fusion.refs_0_), channel_id=1, source_target_pairs={{0,1},{1,0},{2,3},{3,2},{4,5},{5,4},{6,7},{7,6},{8,9},{9,8},{10,11... | collective-permute-start | bytes 1179656 | tf_op jit(solution)/shard_map/ppermute | solution.py:241
  6.8 1.6 %collective-permute-start.4 = (bf16[2,16,6144]{2,1,0:T(8,128)(2,1)S(1)}, bf16[2,16,6144]{2,1,0:T(8,128)(2,1)S(1)}, u32[]{:S(2)}, u32[]{:S(2)}) collective-permute-start(bf16[2,16,6144]{2,1,0:T(8,128)(2,1)S(1)} %pad_maximum_fusion.refs_0_), channel_id=1, source_target_pairs={{0,2},{1,3},{2,0},{3,1},{4,6},{5,7},{6,4},{7,5},{8,10},{9,11},{10,... | collective-permute-start | bytes 1179656 | tf_op jit(solution)/shard_map/ppermute | solution.py:244
  9.5 5.5 %pack.1.refs_2_ = bf16[4,384,3072]{2,1,0:T(8,128)(2,1)S(1)} custom-call(bf16[384,3072]{1,0:T(8,128)(2,1)} %refs_0_.1, bf16[384,3072]{1,0:T(8,128)(2,1)} %refs_1_.1, bf16[384,3072]{1,0:T(8,128)(2,1)} %collective-permute-done.refs_2_, bf16[384,3072]{1,0:T(8,128)(2,1)} %collective-permute-done.1.refs_3_), custom_call_target="tpu_custom_call" | custom-call | tf_op jit(solution)/shard_map/pack/pallas_call | solution.py:93
  17.8 1.6 %collective-permute-start.6 = (bf16[2,16,6144]{2,1,0:T(8,128)(2,1)S(1)}, bf16[2,16,6144]{2,1,0:T(8,128)(2,1)S(1)}, u32[]{:S(2)}, u32[]{:S(2)}) collective-permute-start(bf16[2,16,6144]{2,1,0:T(8,128)(2,1)S(1)} %collective-permute-done.2.refs_0_.refs_2_), channel_id=1, source_target_pairs={{0,2},{1,3},{2,0},{3,1},{4,6},{5,7},{6,4},{7,5},{8,10},{9,11},{10,... | collective-permute-start | bytes 1179656 | tf_op jit(solution)/shard_map/ppermute | solution.py:244
  19.4 2.6 %collective-permute-start.9 = (bf16[2,16,6144]{2,1,0:T(8,128)(2,1)S(1)}, bf16[2,16,6144]{2,1,0:T(8,128)(2,1)S(1)}, u32[]{:S(2)}, u32[]{:S(2)}) collective-permute-start(bf16[2,16,6144]{2,1,0:T(8,128)(2,1)S(1)} %pad_maximum_fusion.refs_0_), channel_id=1, source_target_pairs={{0,4},{1,5},{2,6},{3,7},{4,0},{5,1},{6,2},{7,3},{8,12},{9,13},{10,... | collective-permute-start | bytes 1179656 | tf_op jit(solution)/shard_map/ppermute | solution.py:247
  22.0 3.6 %partial.10 = (f32[2,32,3072]{2,1,0:T(8,128)S(1)}, bf16[2,32,3072]{2,1,0:T(8,128)(2,1)S(1)}) custom-call(s32[288]{0:T(512)S(1)} %reshape.7.table, bf16[2,16,6144]{2,1,0:T(8,128)(2,1)S(1)} %pad_maximum_fusion.refs_0_, bf16[2,16,6144]{2,1,0:T(8,128)(2,1)S(1)} %collective-permute-done.3.refs_1_, bf16[4,384,3072]{2,1,0:T(8,128)(2,1)S(1)} %pack.1.refs_2_), custom_call_target="tpu_custom_call" | custom-call | tf_op jit(solution)/shard_map/partial/pallas_call | solution.py:126
  27.7 3.6 %partial.11 = (f32[2,32,3072]{2,1,0:T(8,128)S(1)}, bf16[2,32,3072]{2,1,0:T(8,128)(2,1)S(1)}) custom-call(s32[288]{0:T(512)S(1)} %reshape.7.table, bf16[2,16,6144]{2,1,0:T(8,128)(2,1)S(1)} %collective-permute-done.2.refs_0_.refs_2_, bf16[2,16,6144]{2,1,0:T(8,128)(2,1)S(1)} %collective-permute-done.5.refs_1_.refs_3_, bf16[4,384,3072]{2,1,0:T(8,128)(2,1)S(1)} %pack.1.refs_2_), custom_call_target="tpu_custom_call" | custom-call | tf_op jit(solution)/shard_map/partial/pallas_call | solution.py:126
  31.3 1.6 %collective-permute-start.10 = (bf16[2,32,3072]{2,1,0:T(8,128)(2,1)S(1)}, bf16[2,32,3072]{2,1,0:T(8,128)(2,1)S(1)}, u32[]{:S(2)}, u32[]{:S(2)}) collective-permute-start(bf16[2,32,3072]{2,1,0:T(8,128)(2,1)S(1)} %get-tuple-element.122), channel_id=1, source_target_pairs={{0,16},{8,24},{16,0},{24,8},{1,17},{9,25},{17,1},{25,9},{2,18},{10... | collective-permute-start | bytes 1179656 | tf_op jit(solution)/shard_map/ppermute | solution.py:235
  32.9 3.8 %collective-permute-done.6.refs_0_.refs_6_ = bf16[2,16,6144]{2,1,0:T(8,128)(2,1)S(1)} collective-permute-done((bf16[2,16,6144]{2,1,0:T(8,128)(2,1)S(1)}, bf16[2,16,6144]{2,1,0:T(8,128)(2,1)S(1)}, u32[]{:S(2)}, u32[]{:S(2)}) %collective-permute-start.6) | collective-permute-done | bytes 393248 | tf_op jit(solution)/shard_map/ppermute | solution.py:244
  38.3 3.6 %partial.12 = (f32[2,32,3072]{2,1,0:T(8,128)S(1)}, bf16[2,32,3072]{2,1,0:T(8,128)(2,1)S(1)}) custom-call(s32[288]{0:T(512)S(1)} %reshape.7.table, bf16[2,16,6144]{2,1,0:T(8,128)(2,1)S(1)} %collective-permute-done.4.refs_0_.refs_4_, bf16[2,16,6144]{2,1,0:T(8,128)(2,1)S(1)} %collective-permute-done.8.refs_1_.refs_5_, bf16[4,384,3072]{2,1,0:T(8,128)(2,1)S(1)} %pack.1.refs_2_), custom_call_target="tpu_custom_call" | custom-call | tf_op jit(solution)/shard_map/partial/pallas_call | solution.py:126
  42.0 2.1 %collective-permute-done.10.refs_25_ = bf16[2,32,3072]{2,1,0:T(8,128)(2,1)S(1)} collective-permute-done((bf16[2,32,3072]{2,1,0:T(8,128)(2,1)S(1)}, bf16[2,32,3072]{2,1,0:T(8,128)(2,1)S(1)}, u32[]{:S(2)}, u32[]{:S(2)}) %collective-permute-start.10) | collective-permute-done | bytes 393248 | tf_op jit(solution)/shard_map/ppermute | solution.py:235
  45.1 1.5 %collective-permute-start.14 = (bf16[2,32,3072]{2,1,0:T(8,128)(2,1)S(1)}, bf16[2,32,3072]{2,1,0:T(8,128)(2,1)S(1)}, u32[]{:S(2)}, u32[]{:S(2)}) collective-permute-start(bf16[2,32,3072]{2,1,0:T(8,128)(2,1)S(1)} %get-tuple-element.132), channel_id=1, source_target_pairs={{0,16},{8,24},{16,0},{24,8},{1,17},{9,25},{17,1},{25,9},{2,18},{10... | collective-permute-start | bytes 1179656 | tf_op jit(solution)/shard_map/ppermute | solution.py:235
  46.5 1.8 %collective-permute-start.15 = (bf16[2,16,6144]{2,1,0:T(8,128)(2,1)S(1)}, bf16[2,16,6144]{2,1,0:T(8,128)(2,1)S(1)}, u32[]{:S(2)}, u32[]{:S(2)}) collective-permute-start(bf16[2,16,6144]{2,1,0:T(8,128)(2,1)S(1)} %collective-permute-done.2.refs_0_.refs_2_), channel_id=1, source_target_pairs={{0,4},{1,5},{2,6},{3,7},{4,0},{5,1},{6,2},{7,3},{8,12},{9,13},{10,... | collective-permute-start | bytes 1179656 | tf_op jit(solution)/shard_map/ppermute | solution.py:247
  48.3 3.6 %partial.13 = (f32[2,32,3072]{2,1,0:T(8,128)S(1)}, bf16[2,32,3072]{2,1,0:T(8,128)(2,1)S(1)}) custom-call(s32[288]{0:T(512)S(1)} %reshape.7.table, bf16[2,16,6144]{2,1,0:T(8,128)(2,1)S(1)} %collective-permute-done.6.refs_0_.refs_6_, bf16[2,16,6144]{2,1,0:T(8,128)(2,1)S(1)} %collective-permute-done.11.refs_1_.refs_7_, bf16[4,384,3072]{2,1,0:T(8,128)(2,1)S(1)} %pack.1.refs_2_), custom_call_target="tpu_custom_call" | custom-call | tf_op jit(solution)/shard_map/partial/pallas_call | solution.py:126
  53.3 5.5 %collective-permute-done.12.refs_0_.refs_10_ = bf16[2,16,6144]{2,1,0:T(8,128)(2,1)S(1)} collective-permute-done((bf16[2,16,6144]{2,1,0:T(8,128)(2,1)S(1)}, bf16[2,16,6144]{2,1,0:T(8,128)(2,1)S(1)}, u32[]{:S(2)}, u32[]{:S(2)}) %collective-permute-start.12) | collective-permute-done | bytes 393248 | tf_op jit(solution)/shard_map/ppermute | solution.py:244
  58.7 3.6 %partial.14 = (f32[2,32,3072]{2,1,0:T(8,128)S(1)}, bf16[2,32,3072]{2,1,0:T(8,128)(2,1)S(1)}) custom-call(s32[288]{0:T(512)S(1)} %reshape.7.table, bf16[2,16,6144]{2,1,0:T(8,128)(2,1)S(1)} %collective-permute-done.9.refs_0_.refs_8_, bf16[2,16,6144]{2,1,0:T(8,128)(2,1)S(1)} %collective-permute-done.13.refs_1_.refs_9_, bf16[4,384,3072]{2,1,0:T(8,128)(2,1)S(1)} %pack.1.refs_2_), custom_call_target="tpu_custom_call" | custom-call | tf_op jit(solution)/shard_map/partial/pallas_call | solution.py:126
  62.3 2.2 %collective-permute-done.15.refs_0_.refs_12_ = bf16[2,16,6144]{2,1,0:T(8,128)(2,1)S(1)} collective-permute-done((bf16[2,16,6144]{2,1,0:T(8,128)(2,1)S(1)}, bf16[2,16,6144]{2,1,0:T(8,128)(2,1)S(1)}, u32[]{:S(2)}, u32[]{:S(2)}) %collective-permute-start.15) | collective-permute-done | bytes 393248 | tf_op jit(solution)/shard_map/ppermute | solution.py:247
  68.3 3.6 %partial.15 = (f32[2,32,3072]{2,1,0:T(8,128)S(1)}, bf16[2,32,3072]{2,1,0:T(8,128)(2,1)S(1)}) custom-call(s32[288]{0:T(512)S(1)} %reshape.7.table, bf16[2,16,6144]{2,1,0:T(8,128)(2,1)S(1)} %collective-permute-done.12.refs_0_.refs_10_, bf16[2,16,6144]{2,1,0:T(8,128)(2,1)S(1)} %collective-permute-done.16.refs_1_.refs_11_, bf16[4,384,3072]{2,1,0:T(8,128)(2,1)S(1)} %pack.1.refs_2_), custom_call_target="tpu_custom_call" | custom-call | tf_op jit(solution)/shard_map/partial/pallas_call | solution.py:126
  72.9 2.0 %collective-permute-start.21 = (bf16[2,16,6144]{2,1,0:T(8,128)(2,1)S(1)}, bf16[2,16,6144]{2,1,0:T(8,128)(2,1)S(1)}, u32[]{:S(2)}, u32[]{:S(2)}) collective-permute-start(bf16[2,16,6144]{2,1,0:T(8,128)(2,1)S(1)} %collective-permute-done.18.refs_0_.refs_14_), channel_id=1, source_target_pairs={{0,1},{1,0},{2,3},{3,2},{4,5},{5,4},{6,7},{7,6},{8,9},{9,8},{10,11... | collective-permute-start | bytes 1179656 | tf_op jit(solution)/shard_map/ppermute | solution.py:241
  74.9 2.0 %collective-permute-start.22 = (bf16[2,32,3072]{2,1,0:T(8,128)(2,1)S(1)}, bf16[2,32,3072]{2,1,0:T(8,128)(2,1)S(1)}, u32[]{:S(2)}, u32[]{:S(2)}) collective-permute-start(bf16[2,32,3072]{2,1,0:T(8,128)(2,1)S(1)} %get-tuple-element.152), channel_id=1, source_target_pairs={{0,16},{8,24},{16,0},{24,8},{1,17},{9,25},{17,1},{25,9},{2,18},{10... | collective-permute-start | bytes 1179656 | tf_op jit(solution)/shard_map/ppermute | solution.py:235
  76.9 3.6 %partial.16 = (f32[2,32,3072]{2,1,0:T(8,128)S(1)}, bf16[2,32,3072]{2,1,0:T(8,128)(2,1)S(1)}) custom-call(s32[288]{0:T(512)S(1)} %reshape.7.table, bf16[2,16,6144]{2,1,0:T(8,128)(2,1)S(1)} %collective-permute-done.15.refs_0_.refs_12_, bf16[2,16,6144]{2,1,0:T(8,128)(2,1)S(1)} %collective-permute-done.19.refs_1_.refs_13_, bf16[4,384,3072]{2,1,0:T(8,128)(2,1)S(1)} %pack.1.refs_2_), custom_call_target="tpu_custom_call" | custom-call | tf_op jit(solution)/shard_map/partial/pallas_call | solution.py:126
  80.5 4.7 %collective-permute-start.23 = (bf16[2,32,3072]{2,1,0:T(8,128)(2,1)S(1)}, bf16[2,32,3072]{2,1,0:T(8,128)(2,1)S(1)}, u32[]{:S(2)}, u32[]{:S(2)}) collective-permute-start(bf16[2,32,3072]{2,1,0:T(8,128)(2,1)S(1)} %get-tuple-element.161), channel_id=1, source_target_pairs={{0,16},{8,24},{16,0},{24,8},{1,17},{9,25},{17,1},{25,9},{2,18},{10... | collective-permute-start | bytes 1179656 | tf_op jit(solution)/shard_map/ppermute | solution.py:235
  85.3 1.6 %partial.17 = (f32[2,32,1024]{2,1,0:T(8,128)S(1)}, bf16[2,32,1024]{2,1,0:T(8,128)(2,1)S(1)}) custom-call(s32[288]{0:T(512)S(1)} %reshape.7.table, bf16[2,16,6144]{2,1,0:T(8,128)(2,1)S(1)} %collective-permute-done.18.refs_0_.refs_14_, bf16[2,16,6144]{2,1,0:T(8,128)(2,1)S(1)} %collective-permute-done.21.refs_1_.refs_15_, bf16[4,384,3072]{2,1,0:T(8,128)(2,1)S(1)} %pack.1.refs_2_), custom_call_target="tpu_custom_call" | custom-call | tf_op jit(solution)/shard_map/partial/pallas_call | solution.py:126
  86.9 2.1 %collective-permute-start.24 = (bf16[2,32,1024]{2,1,0:T(8,128)(2,1)S(1)}, bf16[2,32,1024]{2,1,0:T(8,128)(2,1)S(1)}, u32[]{:S(2)}, u32[]{:S(2)}) collective-permute-start(bf16[2,32,1024]{2,1,0:T(8,128)(2,1)S(1)} %get-tuple-element.162), channel_id=1, source_target_pairs={{0,16},{8,24},{16,0},{24,8},{1,17},{9,25},{17,1},{25,9},{2,18},{10... | collective-permute-start | bytes 393224 | tf_op jit(solution)/shard_map/ppermute | solution.py:235
  89.0 1.6 %partial.18 = (f32[2,32,1024]{2,1,0:T(8,128)S(1)}, bf16[2,32,1024]{2,1,0:T(8,128)(2,1)S(1)}) custom-call(s32[288]{0:T(512)S(1)} %reshape.7.table, bf16[2,16,6144]{2,1,0:T(8,128)(2,1)S(1)} %collective-permute-done.18.refs_0_.refs_14_, bf16[2,16,6144]{2,1,0:T(8,128)(2,1)S(1)} %collective-permute-done.21.refs_1_.refs_15_, bf16[4,384,3072]{2,1,0:T(8,128)(2,1)S(1)} %pack.1.refs_2_), custom_call_target="tpu_custom_call" | custom-call | tf_op jit(solution)/shard_map/partial/pallas_call | solution.py:126
  90.7 1.6 %partial.19 = (f32[2,32,1024]{2,1,0:T(8,128)S(1)}, bf16[2,32,1024]{2,1,0:T(8,128)(2,1)S(1)}) custom-call(s32[288]{0:T(512)S(1)} %reshape.7.table, bf16[2,16,6144]{2,1,0:T(8,128)(2,1)S(1)} %collective-permute-done.18.refs_0_.refs_14_, bf16[2,16,6144]{2,1,0:T(8,128)(2,1)S(1)} %collective-permute-done.21.refs_1_.refs_15_, bf16[4,384,3072]{2,1,0:T(8,128)(2,1)S(1)} %pack.1.refs_2_), custom_call_target="tpu_custom_call" | custom-call | tf_op jit(solution)/shard_map/partial/pallas_call | solution.py:126
  92.3 2.1 %collective-permute-start.26 = (bf16[2,32,1024]{2,1,0:T(8,128)(2,1)S(1)}, bf16[2,32,1024]{2,1,0:T(8,128)(2,1)S(1)}, u32[]{:S(2)}, u32[]{:S(2)}) collective-permute-start(bf16[2,32,1024]{2,1,0:T(8,128)(2,1)S(1)} %get-tuple-element.188), channel_id=1, source_target_pairs={{0,16},{8,24},{16,0},{24,8},{1,17},{9,25},{17,1},{25,9},{2,18},{10... | collective-permute-start | bytes 393224 | tf_op jit(solution)/shard_map/ppermute | solution.py:235
  95.3 1.8 %collective-permute-done.24.refs_31_ = bf16[2,32,1024]{2,1,0:T(8,128)(2,1)S(1)} collective-permute-done((bf16[2,32,1024]{2,1,0:T(8,128)(2,1)S(1)}, bf16[2,32,1024]{2,1,0:T(8,128)(2,1)S(1)}, u32[]{:S(2)}, u32[]{:S(2)}) %collective-permute-start.24) | collective-permute-done | bytes 131104 | tf_op jit(solution)/shard_map/ppermute | solution.py:235
  97.1 3.6 %grad.3 = (bf16[2,384,1024]{2,1,0:T(8,128)(2,1)S(1)}, bf16[2,384,1024]{2,1,0:T(8,128)(2,1)S(1)}) custom-call(s32[288]{0:T(512)S(1)} %reshape.7.table, bf16[2,16,6144]{2,1,0:T(8,128)(2,1)S(1)} %pad_maximum_fusion.refs_0_, bf16[2,16,6144]{2,1,0:T(8,128)(2,1)S(1)} %collective-permute-done.3.refs_1_, ...), custom_call_target="tpu_custom_call" | custom-call | tf_op jit(solution)/shard_map/grad/pallas_call | solution.py:186
  100.7 3.7 %grad.4 = (bf16[2,384,1024]{2,1,0:T(8,128)(2,1)S(1)}, bf16[2,384,1024]{2,1,0:T(8,128)(2,1)S(1)}) custom-call(s32[288]{0:T(512)S(1)} %reshape.7.table, bf16[2,16,6144]{2,1,0:T(8,128)(2,1)S(1)} %pad_maximum_fusion.refs_0_, bf16[2,16,6144]{2,1,0:T(8,128)(2,1)S(1)} %collective-permute-done.3.refs_1_, ...), custom_call_target="tpu_custom_call" | custom-call | tf_op jit(solution)/shard_map/grad/pallas_call | solution.py:186
  105.1 3.6 %grad.5 = (bf16[2,384,1024]{2,1,0:T(8,128)(2,1)S(1)}, bf16[2,384,1024]{2,1,0:T(8,128)(2,1)S(1)}) custom-call(s32[288]{0:T(512)S(1)} %reshape.7.table, bf16[2,16,6144]{2,1,0:T(8,128)(2,1)S(1)} %pad_maximum_fusion.refs_0_, bf16[2,16,6144]{2,1,0:T(8,128)(2,1)S(1)} %collective-permute-done.3.refs_1_, ...), custom_call_target="tpu_custom_call" | custom-call | tf_op jit(solution)/shard_map/grad/pallas_call | solution.py:186
  (50 shorter events, 23.1 us)
Async XLA Ops:
  0.6 8.8 %collective-permute-start = (bf16[384,3072]{1,0:T(8,128)(2,1)}, bf16[384,3072]{1,0:T(8,128)(2,1)}, u32[]{:S(2)}, u32[]{:S(2)}) collective-permute-start(bf16[384,3072]{1,0:T(8,128)(2,1)} %refs_0_.1), channel_id=1, source_target_pairs={{0,8},{8,0},{16,24},{24,16},{1,9},{9,1},{17,25},{25,17},{2,10},{10... | collective-permute-start | bytes 7077896 | tf_op jit(solution)/shard_map/ppermute | solution.py:238
  1.1 8.3 %collective-permute-start.1 = (bf16[384,3072]{1,0:T(8,128)(2,1)}, bf16[384,3072]{1,0:T(8,128)(2,1)}, u32[]{:S(2)}, u32[]{:S(2)}) collective-permute-start(bf16[384,3072]{1,0:T(8,128)(2,1)} %refs_1_.1), channel_id=1, source_target_pairs={{0,8},{8,0},{16,24},{24,16},{1,9},{9,1},{17,25},{25,17},{2,10},{10... | collective-permute-start | bytes 7077896 | tf_op jit(solution)/shard_map/ppermute | solution.py:238
  2.3 12.7 %collective-permute-start.2 = (bf16[2,16,6144]{2,1,0:T(8,128)(2,1)S(1)}, bf16[2,16,6144]{2,1,0:T(8,128)(2,1)S(1)}, u32[]{:S(2)}, u32[]{:S(2)}) collective-permute-start(bf16[2,16,6144]{2,1,0:T(8,128)(2,1)S(1)} %pad_maximum_fusion.refs_0_), channel_id=1, source_target_pairs={{0,16},{8,24},{16,0},{24,8},{1,17},{9,25},{17,1},{25,9},{2,18},{10... | collective-permute-start | bytes 1179656 | tf_op jit(solution)/shard_map/ppermute | solution.py:235
  5.3 10.8 %collective-permute-start.3 = (bf16[2,16,6144]{2,1,0:T(8,128)(2,1)S(1)}, bf16[2,16,6144]{2,1,0:T(8,128)(2,1)S(1)}, u32[]{:S(2)}, u32[]{:S(2)}) collective-permute-start(bf16[2,16,6144]{2,1,0:T(8,128)(2,1)S(1)} %pad_maximum_fusion.refs_0_), channel_id=1, source_target_pairs={{0,1},{1,0},{2,3},{3,2},{4,5},{5,4},{6,7},{7,6},{8,9},{9,8},{10,11... | collective-permute-start | bytes 1179656 | tf_op jit(solution)/shard_map/ppermute | solution.py:241
  6.8 10.5 %collective-permute-start.4 = (bf16[2,16,6144]{2,1,0:T(8,128)(2,1)S(1)}, bf16[2,16,6144]{2,1,0:T(8,128)(2,1)S(1)}, u32[]{:S(2)}, u32[]{:S(2)}) collective-permute-start(bf16[2,16,6144]{2,1,0:T(8,128)(2,1)S(1)} %pad_maximum_fusion.refs_0_), channel_id=1, source_target_pairs={{0,2},{1,3},{2,0},{3,1},{4,6},{5,7},{6,4},{7,5},{8,10},{9,11},{10,... | collective-permute-start | bytes 1179656 | tf_op jit(solution)/shard_map/ppermute | solution.py:244
  17.3 10.4 %collective-permute-start.5 = (bf16[2,16,6144]{2,1,0:T(8,128)(2,1)S(1)}, bf16[2,16,6144]{2,1,0:T(8,128)(2,1)S(1)}, u32[]{:S(2)}, u32[]{:S(2)}) collective-permute-start(bf16[2,16,6144]{2,1,0:T(8,128)(2,1)S(1)} %collective-permute-done.2.refs_0_.refs_2_), channel_id=1, source_target_pairs={{0,1},{1,0},{2,3},{3,2},{4,5},{5,4},{6,7},{7,6},{8,9},{9,8},{10,11... | collective-permute-start | bytes 1179656 | tf_op jit(solution)/shard_map/ppermute | solution.py:241
  17.8 18.9 %collective-permute-start.6 = (bf16[2,16,6144]{2,1,0:T(8,128)(2,1)S(1)}, bf16[2,16,6144]{2,1,0:T(8,128)(2,1)S(1)}, u32[]{:S(2)}, u32[]{:S(2)}) collective-permute-start(bf16[2,16,6144]{2,1,0:T(8,128)(2,1)S(1)} %collective-permute-done.2.refs_0_.refs_2_), channel_id=1, source_target_pairs={{0,2},{1,3},{2,0},{3,1},{4,6},{5,7},{6,4},{7,5},{8,10},{9,11},{10,... | collective-permute-start | bytes 1179656 | tf_op jit(solution)/shard_map/ppermute | solution.py:244
  19.4 22.5 %collective-permute-start.9 = (bf16[2,16,6144]{2,1,0:T(8,128)(2,1)S(1)}, bf16[2,16,6144]{2,1,0:T(8,128)(2,1)S(1)}, u32[]{:S(2)}, u32[]{:S(2)}) collective-permute-start(bf16[2,16,6144]{2,1,0:T(8,128)(2,1)S(1)} %pad_maximum_fusion.refs_0_), channel_id=1, source_target_pairs={{0,4},{1,5},{2,6},{3,7},{4,0},{5,1},{6,2},{7,3},{8,12},{9,13},{10,... | collective-permute-start | bytes 1179656 | tf_op jit(solution)/shard_map/ppermute | solution.py:247
  25.6 12.1 %collective-permute-start.7 = (bf16[2,32,3072]{2,1,0:T(8,128)(2,1)S(1)}, bf16[2,32,3072]{2,1,0:T(8,128)(2,1)S(1)}, u32[]{:S(2)}, u32[]{:S(2)}) collective-permute-start(bf16[2,32,3072]{2,1,0:T(8,128)(2,1)S(1)} %get-tuple-element.115), channel_id=1, source_target_pairs={{0,16},{8,24},{16,0},{24,8},{1,17},{9,25},{17,1},{25,9},{2,18},{10... | collective-permute-start | bytes 1179656 | tf_op jit(solution)/shard_map/ppermute | solution.py:235
  26.8 11.5 %collective-permute-start.8 = (bf16[2,16,6144]{2,1,0:T(8,128)(2,1)S(1)}, bf16[2,16,6144]{2,1,0:T(8,128)(2,1)S(1)}, u32[]{:S(2)}, u32[]{:S(2)}) collective-permute-start(bf16[2,16,6144]{2,1,0:T(8,128)(2,1)S(1)} %collective-permute-done.4.refs_0_.refs_4_), channel_id=1, source_target_pairs={{0,1},{1,0},{2,3},{3,2},{4,5},{5,4},{6,7},{7,6},{8,9},{9,8},{10,11... | collective-permute-start | bytes 1179656 | tf_op jit(solution)/shard_map/ppermute | solution.py:241
  31.3 12.8 %collective-permute-start.10 = (bf16[2,32,3072]{2,1,0:T(8,128)(2,1)S(1)}, bf16[2,32,3072]{2,1,0:T(8,128)(2,1)S(1)}, u32[]{:S(2)}, u32[]{:S(2)}) collective-permute-start(bf16[2,32,3072]{2,1,0:T(8,128)(2,1)S(1)} %get-tuple-element.122), channel_id=1, source_target_pairs={{0,16},{8,24},{16,0},{24,8},{1,17},{9,25},{17,1},{25,9},{2,18},{10... | collective-permute-start | bytes 1179656 | tf_op jit(solution)/shard_map/ppermute | solution.py:235
  37.7 10.6 %collective-permute-start.11 = (bf16[2,16,6144]{2,1,0:T(8,128)(2,1)S(1)}, bf16[2,16,6144]{2,1,0:T(8,128)(2,1)S(1)}, u32[]{:S(2)}, u32[]{:S(2)}) collective-permute-start(bf16[2,16,6144]{2,1,0:T(8,128)(2,1)S(1)} %collective-permute-done.6.refs_0_.refs_6_), channel_id=1, source_target_pairs={{0,1},{1,0},{2,3},{3,2},{4,5},{5,4},{6,7},{7,6},{8,9},{9,8},{10,11... | collective-permute-start | bytes 1179656 | tf_op jit(solution)/shard_map/ppermute | solution.py:241
  44.1 14.6 %collective-permute-start.12 = (bf16[2,16,6144]{2,1,0:T(8,128)(2,1)S(1)}, bf16[2,16,6144]{2,1,0:T(8,128)(2,1)S(1)}, u32[]{:S(2)}, u32[]{:S(2)}) collective-permute-start(bf16[2,16,6144]{2,1,0:T(8,128)(2,1)S(1)} %collective-permute-done.9.refs_0_.refs_8_), channel_id=1, source_target_pairs={{0,2},{1,3},{2,0},{3,1},{4,6},{5,7},{6,4},{7,5},{8,10},{9,11},{10,... | collective-permute-start | bytes 1179656 | tf_op jit(solution)/shard_map/ppermute | solution.py:244
  44.5 14.2 %collective-permute-start.13 = (bf16[2,16,6144]{2,1,0:T(8,128)(2,1)S(1)}, bf16[2,16,6144]{2,1,0:T(8,128)(2,1)S(1)}, u32[]{:S(2)}, u32[]{:S(2)}) collective-permute-start(bf16[2,16,6144]{2,1,0:T(8,128)(2,1)S(1)} %collective-permute-done.9.refs_0_.refs_8_), channel_id=1, source_target_pairs={{0,1},{1,0},{2,3},{3,2},{4,5},{5,4},{6,7},{7,6},{8,9},{9,8},{10,11... | collective-permute-start | bytes 1179656 | tf_op jit(solution)/shard_map/ppermute | solution.py:241
  45.1 13.7 %collective-permute-start.14 = (bf16[2,32,3072]{2,1,0:T(8,128)(2,1)S(1)}, bf16[2,32,3072]{2,1,0:T(8,128)(2,1)S(1)}, u32[]{:S(2)}, u32[]{:S(2)}) collective-permute-start(bf16[2,32,3072]{2,1,0:T(8,128)(2,1)S(1)} %get-tuple-element.132), channel_id=1, source_target_pairs={{0,16},{8,24},{16,0},{24,8},{1,17},{9,25},{17,1},{25,9},{2,18},{10... | collective-permute-start | bytes 1179656 | tf_op jit(solution)/shard_map/ppermute | solution.py:235
  46.5 18.0 %collective-permute-start.15 = (bf16[2,16,6144]{2,1,0:T(8,128)(2,1)S(1)}, bf16[2,16,6144]{2,1,0:T(8,128)(2,1)S(1)}, u32[]{:S(2)}, u32[]{:S(2)}) collective-permute-start(bf16[2,16,6144]{2,1,0:T(8,128)(2,1)S(1)} %collective-permute-done.2.refs_0_.refs_2_), channel_id=1, source_target_pairs={{0,4},{1,5},{2,6},{3,7},{4,0},{5,1},{6,2},{7,3},{8,12},{9,13},{10,... | collective-permute-start | bytes 1179656 | tf_op jit(solution)/shard_map/ppermute | solution.py:247
  51.9 15.0 %collective-permute-start.17 = (bf16[2,32,3072]{2,1,0:T(8,128)(2,1)S(1)}, bf16[2,32,3072]{2,1,0:T(8,128)(2,1)S(1)}, u32[]{:S(2)}, u32[]{:S(2)}) collective-permute-start(bf16[2,32,3072]{2,1,0:T(8,128)(2,1)S(1)} %get-tuple-element.139), channel_id=1, source_target_pairs={{0,16},{8,24},{16,0},{24,8},{1,17},{9,25},{17,1},{25,9},{2,18},{10... | collective-permute-start | bytes 1179656 | tf_op jit(solution)/shard_map/ppermute | solution.py:235
  58.7 9.5 %collective-permute-start.16 = (bf16[2,16,6144]{2,1,0:T(8,128)(2,1)S(1)}, bf16[2,16,6144]{2,1,0:T(8,128)(2,1)S(1)}, u32[]{:S(2)}, u32[]{:S(2)}) collective-permute-start(bf16[2,16,6144]{2,1,0:T(8,128)(2,1)S(1)} %collective-permute-done.12.refs_0_.refs_10_), channel_id=1, source_target_pairs={{0,1},{1,0},{2,3},{3,2},{4,5},{5,4},{6,7},{7,6},{8,9},{9,8},{10,11... | collective-permute-start | bytes 1179656 | tf_op jit(solution)/shard_map/ppermute | solution.py:241
  64.6 8.3 %collective-permute-start.18 = (bf16[2,16,6144]{2,1,0:T(8,128)(2,1)S(1)}, bf16[2,16,6144]{2,1,0:T(8,128)(2,1)S(1)}, u32[]{:S(2)}, u32[]{:S(2)}) collective-permute-start(bf16[2,16,6144]{2,1,0:T(8,128)(2,1)S(1)} %collective-permute-done.15.refs_0_.refs_12_), channel_id=1, source_target_pairs={{0,2},{1,3},{2,0},{3,1},{4,6},{5,7},{6,4},{7,5},{8,10},{9,11},{10,... | collective-permute-start | bytes 1179656 | tf_op jit(solution)/shard_map/ppermute | solution.py:244
  64.6 12.4 %collective-permute-start.19 = (bf16[2,16,6144]{2,1,0:T(8,128)(2,1)S(1)}, bf16[2,16,6144]{2,1,0:T(8,128)(2,1)S(1)}, u32[]{:S(2)}, u32[]{:S(2)}) collective-permute-start(bf16[2,16,6144]{2,1,0:T(8,128)(2,1)S(1)} %collective-permute-done.15.refs_0_.refs_12_), channel_id=1, source_target_pairs={{0,1},{1,0},{2,3},{3,2},{4,5},{5,4},{6,7},{7,6},{8,9},{9,8},{10,11... | collective-permute-start | bytes 1179656 | tf_op jit(solution)/shard_map/ppermute | solution.py:241
  66.0 10.9 %collective-permute-start.20 = (bf16[2,32,3072]{2,1,0:T(8,128)(2,1)S(1)}, bf16[2,32,3072]{2,1,0:T(8,128)(2,1)S(1)}, u32[]{:S(2)}, u32[]{:S(2)}) collective-permute-start(bf16[2,32,3072]{2,1,0:T(8,128)(2,1)S(1)} %get-tuple-element.146), channel_id=1, source_target_pairs={{0,16},{8,24},{16,0},{24,8},{1,17},{9,25},{17,1},{25,9},{2,18},{10... | collective-permute-start | bytes 1179656 | tf_op jit(solution)/shard_map/ppermute | solution.py:235
  72.9 12.4 %collective-permute-start.21 = (bf16[2,16,6144]{2,1,0:T(8,128)(2,1)S(1)}, bf16[2,16,6144]{2,1,0:T(8,128)(2,1)S(1)}, u32[]{:S(2)}, u32[]{:S(2)}) collective-permute-start(bf16[2,16,6144]{2,1,0:T(8,128)(2,1)S(1)} %collective-permute-done.18.refs_0_.refs_14_), channel_id=1, source_target_pairs={{0,1},{1,0},{2,3},{3,2},{4,5},{5,4},{6,7},{7,6},{8,9},{9,8},{10,11... | collective-permute-start | bytes 1179656 | tf_op jit(solution)/shard_map/ppermute | solution.py:241
  74.9 10.4 %collective-permute-start.22 = (bf16[2,32,3072]{2,1,0:T(8,128)(2,1)S(1)}, bf16[2,32,3072]{2,1,0:T(8,128)(2,1)S(1)}, u32[]{:S(2)}, u32[]{:S(2)}) collective-permute-start(bf16[2,32,3072]{2,1,0:T(8,128)(2,1)S(1)} %get-tuple-element.152), channel_id=1, source_target_pairs={{0,16},{8,24},{16,0},{24,8},{1,17},{9,25},{17,1},{25,9},{2,18},{10... | collective-permute-start | bytes 1179656 | tf_op jit(solution)/shard_map/ppermute | solution.py:235
  80.5 14.8 %collective-permute-start.23 = (bf16[2,32,3072]{2,1,0:T(8,128)(2,1)S(1)}, bf16[2,32,3072]{2,1,0:T(8,128)(2,1)S(1)}, u32[]{:S(2)}, u32[]{:S(2)}) collective-permute-start(bf16[2,32,3072]{2,1,0:T(8,128)(2,1)S(1)} %get-tuple-element.161), channel_id=1, source_target_pairs={{0,16},{8,24},{16,0},{24,8},{1,17},{9,25},{17,1},{25,9},{2,18},{10... | collective-permute-start | bytes 1179656 | tf_op jit(solution)/shard_map/ppermute | solution.py:235
  86.9 10.2 %collective-permute-start.24 = (bf16[2,32,1024]{2,1,0:T(8,128)(2,1)S(1)}, bf16[2,32,1024]{2,1,0:T(8,128)(2,1)S(1)}, u32[]{:S(2)}, u32[]{:S(2)}) collective-permute-start(bf16[2,32,1024]{2,1,0:T(8,128)(2,1)S(1)} %get-tuple-element.162), channel_id=1, source_target_pairs={{0,16},{8,24},{16,0},{24,8},{1,17},{9,25},{17,1},{25,9},{2,18},{10... | collective-permute-start | bytes 393224 | tf_op jit(solution)/shard_map/ppermute | solution.py:235
  90.6 10.1 %collective-permute-start.25 = (bf16[2,32,1024]{2,1,0:T(8,128)(2,1)S(1)}, bf16[2,32,1024]{2,1,0:T(8,128)(2,1)S(1)}, u32[]{:S(2)}, u32[]{:S(2)}) collective-permute-start(bf16[2,32,1024]{2,1,0:T(8,128)(2,1)S(1)} %get-tuple-element.182), channel_id=1, source_target_pairs={{0,16},{8,24},{16,0},{24,8},{1,17},{9,25},{17,1},{25,9},{2,18},{10... | collective-permute-start | bytes 393224 | tf_op jit(solution)/shard_map/ppermute | solution.py:235
  92.3 12.1 %collective-permute-start.26 = (bf16[2,32,1024]{2,1,0:T(8,128)(2,1)S(1)}, bf16[2,32,1024]{2,1,0:T(8,128)(2,1)S(1)}, u32[]{:S(2)}, u32[]{:S(2)}) collective-permute-start(bf16[2,32,1024]{2,1,0:T(8,128)(2,1)S(1)} %get-tuple-element.188), channel_id=1, source_target_pairs={{0,16},{8,24},{16,0},{24,8},{1,17},{9,25},{17,1},{25,9},{2,18},{10... | collective-permute-start | bytes 393224 | tf_op jit(solution)/shard_map/ppermute | solution.py:235
  104.5 4.4 %collective-permute-start.29 = (bf16[2,384,1024]{2,1,0:T(8,128)(2,1)S(1)}, bf16[2,384,1024]{2,1,0:T(8,128)(2,1)S(1)}, u32[]{:S(2)}, u32[]{:S(2)}) collective-permute-start(bf16[2,384,1024]{2,1,0:T(8,128)(2,1)S(1)} %get-tuple-element.197), channel_id=1, source_target_pairs={{0,8},{8,0},{16,24},{24,16},{1,9},{9,1},{17,25},{25,17},{2,10},{10... | collective-permute-start | bytes 4718600 | tf_op jit(solution)/shard_map/ppermute | solution.py:238
  104.6 5.7 %collective-permute-start.28 = (bf16[2,384,1024]{2,1,0:T(8,128)(2,1)S(1)}, bf16[2,384,1024]{2,1,0:T(8,128)(2,1)S(1)}, u32[]{:S(2)}, u32[]{:S(2)}) collective-permute-start(bf16[2,384,1024]{2,1,0:T(8,128)(2,1)S(1)} %get-tuple-element.195), channel_id=1, source_target_pairs={{0,8},{8,0},{16,24},{24,16},{1,9},{9,1},{17,25},{25,17},{2,10},{10... | collective-permute-start | bytes 4718600 | tf_op jit(solution)/shard_map/ppermute | solution.py:238
  108.7 3.8 %collective-permute-start.27 = (bf16[2,384,1024]{2,1,0:T(8,128)(2,1)S(1)}, bf16[2,384,1024]{2,1,0:T(8,128)(2,1)S(1)}, u32[]{:S(2)}, u32[]{:S(2)}) collective-permute-start(bf16[2,384,1024]{2,1,0:T(8,128)(2,1)S(1)} %get-tuple-element.193), channel_id=1, source_target_pairs={{0,8},{8,0},{16,24},{24,16},{1,9},{9,1},{17,25},{25,17},{2,10},{10... | collective-permute-start | bytes 4718600 | tf_op jit(solution)/shard_map/ppermute | solution.py:238

commit v5 on v4

--- a/solution.py
+++ b/solution.py
@@ -19,6 +19,7 @@
 GRAD_VMEM = 16 * 1024 * 1024
 TOTAL_VMEM = 8 * 1024 * 1024
 PACK_LANES = 4
+TICK_VMEM = 1024 * 1024
 PACK_VMEM = 12 * 1024 * 1024
 TOTAL_LANES = 8
 PARTS = 3
@@ -140,6 +141,24 @@
     )(table, *buffers, weights)
 
 
+def tick_kernel(table_ref, out_ref):
+    pass
+
+
+def tick(table):
+    anywhere = pl.BlockSpec(memory_space=pl.ANY)
+    return pl.pallas_call(
+        tick_kernel,
+        in_specs=[anywhere],
+        out_specs=anywhere,
+        out_shape=jax.ShapeDtypeStruct(table.shape, table.dtype),
+        input_output_aliases={0: 0},
+        compiler_params=pltpu.CompilerParams(vmem_limit_bytes=TICK_VMEM),
+        cost_estimate=COST,
+        name="tick",
+    )(table)
+
+
 def grad_kernel(units, n_buf, n_keep, n_got, slots, base, table, *refs):
     buffers = refs[:n_buf]
     keeps = refs[n_buf : n_buf + n_keep]
@@ -258,11 +277,17 @@
     table = jnp.concatenate(pieces, axis=1).reshape(-1)
     held = [pltpu.with_memory_space_constraint(w, pltpu.HBM) for w in (w_in, w_out)]
     weights = pack(*held, s_in, s_out)
-    table, weights, b0, ya0, a1, a0 = gate((table, weights, b0, ya0, a1, a0))
-    yb0, b1, ya1, a2 = swap_y(b0), near(b0), swap_y(a1), far(a0)
+    table, weights, b0, ya0 = gate((table, weights, b0, ya0))
+    yb0, b1, a2 = swap_y(b0), near(b0), far(a0)
     keep0, send0 = partial(table, (a0, ya0), weights)
     table, send0 = gate((table, send0))
     got0 = swap_x(send0)
+    table, a1 = gate((table, a1))
+    ya1 = swap_y(a1)
+    table = tick(table)
+    table, a2 = gate((table, a2))
+    a3 = near(a2)
+    table = tick(table)
     table, yb0, b0 = gate((table, yb0, b0))
     keep1, send1 = partial(table, (b0, yb0), weights)
     table, send1 = gate((table, send1))
@@ -273,18 +298,23 @@
     b2 = far(b0)
     table, ya1, a1 = gate((table, ya1, a1))
     keep2, send2 = partial(table, (a1, ya1), weights)
-    table, send2, a2, got1 = gate((table, send2, a2, got1))
-    got2, ya2, a3 = swap_x(send2), swap_y(a2), near(a2)
+    table, send2 = gate((table, send2))
+    got2 = swap_x(send2)
+    table, got1, a2 = gate((table, got1, a2))
+    ya2 = swap_y(a2)
     table, yb1, b1 = gate((table, yb1, b1))
     keep3, send3 = partial(table, (b1, yb1), weights)
     table, send3 = gate((table, send3))
     got3 = swap_x(send3)
     table, a3 = gate((table, a3))
     ya3 = swap_y(a3)
+    table, b2 = gate((table, b2))
+    yb2, b3 = swap_y(b2), near(b2)
+    table = tick(table)
     table, ya2, got2 = gate((table, ya2, got2))
     keep4, send4 = partial(table, (a2, ya2), weights)
-    table, send4, b2 = gate((table, send4, b2))
-    got4, yb2, b3 = swap_x(send4), swap_y(b2), near(b2)
+    table, send4 = gate((table, send4))
+    got4 = swap_x(send4)
     table, ya3, got3 = gate((table, ya3, got3))
     keep5, send5 = partial(table, (a3, ya3), weights)
     table, send5 = gate((table, send5))
@@ -295,11 +325,13 @@
     keep6, send6 = partial(table, (b2, yb2), weights)
     table, send6 = gate((table, send6))
     got6 = swap_x(send6)
-    table, yb3, got5 = gate((table, yb3, got5))
+    table, yb3, b3 = gate((table, yb3, b3))
     keep7, got7 = [], []
     for part in range(PARTS):
         keep, send = partial(table, (b3, yb3), weights, part, PARTS)
         table, send = gate((table, send))
+        if part == 0:
+            table, got5 = gate((table, got5))
         keep7.append(keep)
         got7.append(swap_x(send))
     table, got6, got7[0] = gate((table, got6, got7[0]))

time: 114 us -> 110 us (0.965)
  starting transfers between devices: 37.3 us -> 32.8 us
    ppermute x11, starting transfers between devices: 20.5 us -> 12.6 us  [swap_x(): return lax.ppermute(v, 'row', [(r, r ^ 2) for r in range(ROWS)])]
    ppermute x4, waiting for transfers between devices: 11.5 us -> 4.11 us  [near(): return lax.ppermute(v, 'col', [(c, c ^ 2) for c in range(COLS)])]
    ppermute x8, waiting for transfers between devices: 2.49 us -> 8.7 us  [swap_y(): return lax.ppermute(v, 'col', [(c, c ^ 1) for c in range(COLS)])]
    ppermute x8, starting transfers between devices: 7.47 us -> 9.19 us  [swap_y(): return lax.ppermute(v, 'col', [(c, c ^ 1) for c in range(COLS)])]
    ppermute x2, waiting for transfers between devices: 2.23 us -> 3.39 us  [far(): return lax.ppermute(v, 'col', [(c, c ^ 4) for c in range(COLS)])]
  transfers between devices with their start and end apart: 30 -> 30, of which waited for: 12 -> 11; matrix products, arithmetic and copies ran while one was open for 2% -> 2% of each run, Pallas kernels for 43% -> 45%
where the time goes in v5:
time: 110 us
  Pallas kernels  50.7 us (46%)
  starting transfers between devices  32.8 us (30%)
  waiting for transfers between devices  23.1 us (21%)
    pallas_call x10, Pallas kernels, partial(): pl.pallas_call(functools.partial(partial_kernel, len(buffers), 2 * kept /...  29.9 us
    ppermute x11, starting transfers between devices, swap_x(): return lax.ppermute(v, 'row', [(r, r ^ 2) for r in range(ROWS)])  12.6 us
    pallas_call x3, Pallas kernels, grad(): pl.pallas_call(functools.partial(grad_kernel, units, len(buffers), len(ke...  10.9 us
    ppermute x8, starting transfers between devices, swap_y(): return lax.ppermute(v, 'col', [(c, c ^ 1) for c in range(COLS)])  9.19 us
    ppermute x8, waiting for transfers between devices, swap_y(): return lax.ppermute(v, 'col', [(c, c ^ 1) for c in range(COLS)])  8.7 us
    ppermute x11, waiting for transfers between devices, swap_x(): return lax.ppermute(v, 'row', [(r, r ^ 2) for r in range(ROWS)])  6.16 us
    pallas_call x1, Pallas kernels, pack(): pl.pallas_call(pack_kernel, grid=(width // wide,), in_specs=[pl.BlockSpec...  5.5 us
    ppermute x2, starting transfers between devices, far(): return lax.ppermute(v, 'col', [(c, c ^ 4) for c in range(COLS)])  5.36 us
  transfers between devices with their start and end apart: 30, of which 11 were waited for; matrix products, arithmetic and copies ran while one was open for 2% of the time, Pallas kernels for 45%

profile of v5, /device:TPU:0, one launch (start us, length us, event | category | flops | bytes accessed | tf_op | source)
XLA Modules:
  0.0 109.5 jit_solution(9757113062714549392)
XLA Ops:
  2.3 3.0 %collective-permute-start.2 = (bf16[2,16,6144]{2,1,0:T(8,128)(2,1)S(1)}, bf16[2,16,6144]{2,1,0:T(8,128)(2,1)S(1)}, u32[]{:S(2)}, u32[]{:S(2)}) collective-permute-start(bf16[2,16,6144]{2,1,0:T(8,128)(2,1)S(1)} %pad_maximum_fusion.refs_0_), channel_id=1, source_target_pairs={{0,16},{8,24},{16,0},{24,8},{1,17},{9,25},{17,1},{25,9},{2,18},{10... | collective-permute-start | bytes 1179656 | tf_op jit(solution)/shard_map/ppermute | solution.py:254
  5.3 1.5 %collective-permute-start.3 = (bf16[2,16,6144]{2,1,0:T(8,128)(2,1)S(1)}, bf16[2,16,6144]{2,1,0:T(8,128)(2,1)S(1)}, u32[]{:S(2)}, u32[]{:S(2)}) collective-permute-start(bf16[2,16,6144]{2,1,0:T(8,128)(2,1)S(1)} %pad_maximum_fusion.refs_0_), channel_id=1, source_target_pairs={{0,1},{1,0},{2,3},{3,2},{4,5},{5,4},{6,7},{7,6},{8,9},{9,8},{10,11... | collective-permute-start | bytes 1179656 | tf_op jit(solution)/shard_map/ppermute | solution.py:260
  6.8 1.6 %collective-permute-start.4 = (bf16[2,16,6144]{2,1,0:T(8,128)(2,1)S(1)}, bf16[2,16,6144]{2,1,0:T(8,128)(2,1)S(1)}, u32[]{:S(2)}, u32[]{:S(2)}) collective-permute-start(bf16[2,16,6144]{2,1,0:T(8,128)(2,1)S(1)} %pad_maximum_fusion.refs_0_), channel_id=1, source_target_pairs={{0,2},{1,3},{2,0},{3,1},{4,6},{5,7},{6,4},{7,5},{8,10},{9,11},{10,... | collective-permute-start | bytes 1179656 | tf_op jit(solution)/shard_map/ppermute | solution.py:263
  9.4 2.7 %collective-permute-start.5 = (bf16[2,16,6144]{2,1,0:T(8,128)(2,1)S(1)}, bf16[2,16,6144]{2,1,0:T(8,128)(2,1)S(1)}, u32[]{:S(2)}, u32[]{:S(2)}) collective-permute-start(bf16[2,16,6144]{2,1,0:T(8,128)(2,1)S(1)} %pad_maximum_fusion.refs_0_), channel_id=1, source_target_pairs={{0,4},{1,5},{2,6},{3,7},{4,0},{5,1},{6,2},{7,3},{8,12},{9,13},{10,... | collective-permute-start | bytes 1179656 | tf_op jit(solution)/shard_map/ppermute | solution.py:266
  12.1 5.5 %pack.1.refs_2_ = bf16[4,384,3072]{2,1,0:T(8,128)(2,1)S(1)} custom-call(bf16[384,3072]{1,0:T(8,128)(2,1)} %refs_0_.1, bf16[384,3072]{1,0:T(8,128)(2,1)} %refs_1_.1, bf16[384,3072]{1,0:T(8,128)(2,1)} %collective-permute-done.refs_2_, bf16[384,3072]{1,0:T(8,128)(2,1)} %collective-permute-done.1.refs_3_), custom_call_target="tpu_custom_call" | custom-call | tf_op jit(solution)/shard_map/pack/pallas_call | solution.py:94
  19.2 3.6 %partial.10 = (f32[2,32,3072]{2,1,0:T(8,128)S(1)}, bf16[2,32,3072]{2,1,0:T(8,128)(2,1)S(1)}) custom-call(s32[288]{0:T(512)S(1)} %reshape.7.table.table_ref, bf16[2,16,6144]{2,1,0:T(8,128)(2,1)S(1)} %pad_maximum_fusion.refs_0_, bf16[2,16,6144]{2,1,0:T(8,128)(2,1)S(1)} %collective-permute-done.3.refs_1_, bf16[4,384,3072]{2,1,0:T(8,128)(2,1)S(1)} %pack.1.refs_2_), custom_call_target="tpu_custom_call" | custom-call | tf_op jit(solution)/shard_map/partial/pallas_call | solution.py:127
  22.8 1.4 %collective-permute-start.8 = (bf16[2,32,3072]{2,1,0:T(8,128)(2,1)S(1)}, bf16[2,32,3072]{2,1,0:T(8,128)(2,1)S(1)}, u32[]{:S(2)}, u32[]{:S(2)}) collective-permute-start(bf16[2,32,3072]{2,1,0:T(8,128)(2,1)S(1)} %get-tuple-element.122), channel_id=1, source_target_pairs={{0,16},{8,24},{16,0},{24,8},{1,17},{9,25},{17,1},{25,9},{2,18},{10... | collective-permute-start | bytes 1179656 | tf_op jit(solution)/shard_map/ppermute | solution.py:254
  24.2 1.8 %collective-permute-done.4.refs_0_.refs_4_ = bf16[2,16,6144]{2,1,0:T(8,128)(2,1)S(1)} collective-permute-done((bf16[2,16,6144]{2,1,0:T(8,128)(2,1)S(1)}, bf16[2,16,6144]{2,1,0:T(8,128)(2,1)S(1)}, u32[]{:S(2)}, u32[]{:S(2)}) %collective-permute-start.4) | collective-permute-done | bytes 393248 | tf_op jit(solution)/shard_map/ppermute | solution.py:263
  26.0 2.9 %collective-permute-done.5.refs_0_.refs_8_ = bf16[2,16,6144]{2,1,0:T(8,128)(2,1)S(1)} collective-permute-done((bf16[2,16,6144]{2,1,0:T(8,128)(2,1)S(1)}, bf16[2,16,6144]{2,1,0:T(8,128)(2,1)S(1)}, u32[]{:S(2)}, u32[]{:S(2)}) %collective-permute-start.5) | collective-permute-done | bytes 393248 | tf_op jit(solution)/shard_map/ppermute | solution.py:266
  29.5 3.6 %partial.11 = (f32[2,32,3072]{2,1,0:T(8,128)S(1)}, bf16[2,32,3072]{2,1,0:T(8,128)(2,1)S(1)}) custom-call(s32[288]{0:T(512)S(1)} %tick.4.table.table_ref, bf16[2,16,6144]{2,1,0:T(8,128)(2,1)S(1)} %collective-permute-done.2.refs_0_.refs_2_, bf16[2,16,6144]{2,1,0:T(8,128)(2,1)S(1)} %collective-permute-done.6.refs_1_.refs_3_, bf16[4,384,3072]{2,1,0:T(8,128)(2,1)S(1)} %pack.1.refs_2_), custom_call_target="tpu_custom_call" | custom-call | tf_op jit(solution)/shard_map/partial/pallas_call | solution.py:127
  36.3 2.7 %collective-permute-start.13 = (bf16[2,16,6144]{2,1,0:T(8,128)(2,1)S(1)}, bf16[2,16,6144]{2,1,0:T(8,128)(2,1)S(1)}, u32[]{:S(2)}, u32[]{:S(2)}) collective-permute-start(bf16[2,16,6144]{2,1,0:T(8,128)(2,1)S(1)} %collective-permute-done.2.refs_0_.refs_2_), channel_id=1, source_target_pairs={{0,4},{1,5},{2,6},{3,7},{4,0},{5,1},{6,2},{7,3},{8,12},{9,13},{10,... | collective-permute-start | bytes 1179656 | tf_op jit(solution)/shard_map/ppermute | solution.py:266
  39.0 3.6 %partial.12 = (f32[2,32,3072]{2,1,0:T(8,128)S(1)}, bf16[2,32,3072]{2,1,0:T(8,128)(2,1)S(1)}) custom-call(s32[288]{0:T(512)S(1)} %tick.4.table.table_ref, bf16[2,16,6144]{2,1,0:T(8,128)(2,1)S(1)} %collective-permute-done.4.refs_0_.refs_4_, bf16[2,16,6144]{2,1,0:T(8,128)(2,1)S(1)} %collective-permute-done.9.refs_1_.refs_5_, bf16[4,384,3072]{2,1,0:T(8,128)(2,1)S(1)} %pack.1.refs_2_), custom_call_target="tpu_custom_call" | custom-call | tf_op jit(solution)/shard_map/partial/pallas_call | solution.py:127
  43.7 1.7 %collective-permute-start.14 = (bf16[2,16,6144]{2,1,0:T(8,128)(2,1)S(1)}, bf16[2,16,6144]{2,1,0:T(8,128)(2,1)S(1)}, u32[]{:S(2)}, u32[]{:S(2)}) collective-permute-start(bf16[2,16,6144]{2,1,0:T(8,128)(2,1)S(1)} %collective-permute-done.5.refs_0_.refs_8_), channel_id=1, source_target_pairs={{0,1},{1,0},{2,3},{3,2},{4,5},{5,4},{6,7},{7,6},{8,9},{9,8},{10,11... | collective-permute-start | bytes 1179656 | tf_op jit(solution)/shard_map/ppermute | solution.py:260
  46.4 3.6 %partial.13 = (f32[2,32,3072]{2,1,0:T(8,128)S(1)}, bf16[2,32,3072]{2,1,0:T(8,128)(2,1)S(1)}) custom-call(s32[288]{0:T(512)S(1)} %tick.4.table.table_ref, bf16[2,16,6144]{2,1,0:T(8,128)(2,1)S(1)} %collective-permute-done.7.refs_0_.refs_6_, bf16[2,16,6144]{2,1,0:T(8,128)(2,1)S(1)} %collective-permute-done.11.refs_1_.refs_7_, bf16[4,384,3072]{2,1,0:T(8,128)(2,1)S(1)} %pack.1.refs_2_), custom_call_target="tpu_custom_call" | custom-call | tf_op jit(solution)/shard_map/partial/pallas_call | solution.py:127
  50.0 2.3 %collective-permute-done.12.refs_0_.refs_10_ = bf16[2,16,6144]{2,1,0:T(8,128)(2,1)S(1)} collective-permute-done((bf16[2,16,6144]{2,1,0:T(8,128)(2,1)S(1)}, bf16[2,16,6144]{2,1,0:T(8,128)(2,1)S(1)}, u32[]{:S(2)}, u32[]{:S(2)}) %collective-permute-start.12) | collective-permute-done | bytes 393248 | tf_op jit(solution)/shard_map/ppermute | solution.py:263
  56.8 3.6 %partial.14 = (f32[2,32,3072]{2,1,0:T(8,128)S(1)}, bf16[2,32,3072]{2,1,0:T(8,128)(2,1)S(1)}) custom-call(s32[288]{0:T(512)S(1)} %tick.5.table, bf16[2,16,6144]{2,1,0:T(8,128)(2,1)S(1)} %collective-permute-done.5.refs_0_.refs_8_, bf16[2,16,6144]{2,1,0:T(8,128)(2,1)S(1)} %collective-permute-done.14.refs_1_.refs_9_, bf16[4,384,3072]{2,1,0:T(8,128)(2,1)S(1)} %pack.1.refs_2_), custom_call_target="tpu_custom_call" | custom-call | tf_op jit(solution)/shard_map/partial/pallas_call | solution.py:127
  60.9 3.5 %collective-permute-done.16.refs_1_.refs_11_ = bf16[2,16,6144]{2,1,0:T(8,128)(2,1)S(1)} collective-permute-done((bf16[2,16,6144]{2,1,0:T(8,128)(2,1)S(1)}, bf16[2,16,6144]{2,1,0:T(8,128)(2,1)S(1)}, u32[]{:S(2)}, u32[]{:S(2)}) %collective-permute-start.16) | collective-permute-done | bytes 393248 | tf_op jit(solution)/shard_map/ppermute | solution.py:260
  64.4 3.6 %partial.15 = (f32[2,32,3072]{2,1,0:T(8,128)S(1)}, bf16[2,32,3072]{2,1,0:T(8,128)(2,1)S(1)}) custom-call(s32[288]{0:T(512)S(1)} %tick.5.table, bf16[2,16,6144]{2,1,0:T(8,128)(2,1)S(1)} %collective-permute-done.12.refs_0_.refs_10_, bf16[2,16,6144]{2,1,0:T(8,128)(2,1)S(1)} %collective-permute-done.16.refs_1_.refs_11_, bf16[4,384,3072]{2,1,0:T(8,128)(2,1)S(1)} %pack.1.refs_2_), custom_call_target="tpu_custom_call" | custom-call | tf_op jit(solution)/shard_map/partial/pallas_call | solution.py:127
  68.0 1.5 %collective-permute-start.21 = (bf16[2,16,6144]{2,1,0:T(8,128)(2,1)S(1)}, bf16[2,16,6144]{2,1,0:T(8,128)(2,1)S(1)}, u32[]{:S(2)}, u32[]{:S(2)}) collective-permute-start(bf16[2,16,6144]{2,1,0:T(8,128)(2,1)S(1)} %collective-permute-done.18.refs_0_.refs_14_), channel_id=1, source_target_pairs={{0,1},{1,0},{2,3},{3,2},{4,5},{5,4},{6,7},{7,6},{8,9},{9,8},{10,11... | collective-permute-start | bytes 1179656 | tf_op jit(solution)/shard_map/ppermute | solution.py:260
  70.1 2.7 %collective-permute-done.19.refs_1_.refs_13_ = bf16[2,16,6144]{2,1,0:T(8,128)(2,1)S(1)} collective-permute-done((bf16[2,16,6144]{2,1,0:T(8,128)(2,1)S(1)}, bf16[2,16,6144]{2,1,0:T(8,128)(2,1)S(1)}, u32[]{:S(2)}, u32[]{:S(2)}) %collective-permute-start.19) | collective-permute-done | bytes 393248 | tf_op jit(solution)/shard_map/ppermute | solution.py:260
  72.8 3.6 %partial.16 = (f32[2,32,3072]{2,1,0:T(8,128)S(1)}, bf16[2,32,3072]{2,1,0:T(8,128)(2,1)S(1)}) custom-call(s32[288]{0:T(512)S(1)} %tick.5.table, bf16[2,16,6144]{2,1,0:T(8,128)(2,1)S(1)} %collective-permute-done.13.refs_0_.refs_12_, bf16[2,16,6144]{2,1,0:T(8,128)(2,1)S(1)} %collective-permute-done.19.refs_1_.refs_13_, bf16[4,384,3072]{2,1,0:T(8,128)(2,1)S(1)} %pack.1.refs_2_), custom_call_target="tpu_custom_call" | custom-call | tf_op jit(solution)/shard_map/partial/pallas_call | solution.py:127
  77.4 1.5 %collective-permute-done.21.refs_1_.refs_15_ = bf16[2,16,6144]{2,1,0:T(8,128)(2,1)S(1)} collective-permute-done((bf16[2,16,6144]{2,1,0:T(8,128)(2,1)S(1)}, bf16[2,16,6144]{2,1,0:T(8,128)(2,1)S(1)}, u32[]{:S(2)}, u32[]{:S(2)}) %collective-permute-start.21) | collective-permute-done | bytes 393248 | tf_op jit(solution)/shard_map/ppermute | solution.py:260
  78.9 1.6 %partial.17 = (f32[2,32,1024]{2,1,0:T(8,128)S(1)}, bf16[2,32,1024]{2,1,0:T(8,128)(2,1)S(1)}) custom-call(s32[288]{0:T(512)S(1)} %tick.5.table, bf16[2,16,6144]{2,1,0:T(8,128)(2,1)S(1)} %collective-permute-done.18.refs_0_.refs_14_, bf16[2,16,6144]{2,1,0:T(8,128)(2,1)S(1)} %collective-permute-done.21.refs_1_.refs_15_, bf16[4,384,3072]{2,1,0:T(8,128)(2,1)S(1)} %pack.1.refs_2_), custom_call_target="tpu_custom_call" | custom-call | tf_op jit(solution)/shard_map/partial/pallas_call | solution.py:127
  81.5 1.6 %partial.18 = (f32[2,32,1024]{2,1,0:T(8,128)S(1)}, bf16[2,32,1024]{2,1,0:T(8,128)(2,1)S(1)}) custom-call(s32[288]{0:T(512)S(1)} %tick.5.table, bf16[2,16,6144]{2,1,0:T(8,128)(2,1)S(1)} %collective-permute-done.18.refs_0_.refs_14_, bf16[2,16,6144]{2,1,0:T(8,128)(2,1)S(1)} %collective-permute-done.21.refs_1_.refs_15_, bf16[4,384,3072]{2,1,0:T(8,128)(2,1)S(1)} %pack.1.refs_2_), custom_call_target="tpu_custom_call" | custom-call | tf_op jit(solution)/shard_map/partial/pallas_call | solution.py:127
  84.2 1.6 %partial.19 = (f32[2,32,1024]{2,1,0:T(8,128)S(1)}, bf16[2,32,1024]{2,1,0:T(8,128)(2,1)S(1)}) custom-call(s32[288]{0:T(512)S(1)} %tick.5.table, bf16[2,16,6144]{2,1,0:T(8,128)(2,1)S(1)} %collective-permute-done.18.refs_0_.refs_14_, bf16[2,16,6144]{2,1,0:T(8,128)(2,1)S(1)} %collective-permute-done.21.refs_1_.refs_15_, bf16[4,384,3072]{2,1,0:T(8,128)(2,1)S(1)} %pack.1.refs_2_), custom_call_target="tpu_custom_call" | custom-call | tf_op jit(solution)/shard_map/partial/pallas_call | solution.py:127
  86.9 5.8 %collective-permute-done.24.refs_31_ = bf16[2,32,1024]{2,1,0:T(8,128)(2,1)S(1)} collective-permute-done((bf16[2,32,1024]{2,1,0:T(8,128)(2,1)S(1)}, bf16[2,32,1024]{2,1,0:T(8,128)(2,1)S(1)}, u32[]{:S(2)}, u32[]{:S(2)}) %collective-permute-start.24) | collective-permute-done | bytes 131104 | tf_op jit(solution)/shard_map/ppermute | solution.py:254
  92.8 3.6 %grad.3 = (bf16[2,384,1024]{2,1,0:T(8,128)(2,1)S(1)}, bf16[2,384,1024]{2,1,0:T(8,128)(2,1)S(1)}) custom-call(s32[288]{0:T(512)S(1)} %tick.5.table, bf16[2,16,6144]{2,1,0:T(8,128)(2,1)S(1)} %pad_maximum_fusion.refs_0_, bf16[2,16,6144]{2,1,0:T(8,128)(2,1)S(1)} %collective-permute-done.3.refs_1_, ...), custom_call_target="tpu_custom_call" | custom-call | tf_op jit(solution)/shard_map/grad/pallas_call | solution.py:205
  96.4 3.7 %grad.4 = (bf16[2,384,1024]{2,1,0:T(8,128)(2,1)S(1)}, bf16[2,384,1024]{2,1,0:T(8,128)(2,1)S(1)}) custom-call(s32[288]{0:T(512)S(1)} %tick.5.table, bf16[2,16,6144]{2,1,0:T(8,128)(2,1)S(1)} %pad_maximum_fusion.refs_0_, bf16[2,16,6144]{2,1,0:T(8,128)(2,1)S(1)} %collective-permute-done.3.refs_1_, ...), custom_call_target="tpu_custom_call" | custom-call | tf_op jit(solution)/shard_map/grad/pallas_call | solution.py:205
  100.7 3.6 %grad.5 = (bf16[2,384,1024]{2,1,0:T(8,128)(2,1)S(1)}, bf16[2,384,1024]{2,1,0:T(8,128)(2,1)S(1)}) custom-call(s32[288]{0:T(512)S(1)} %tick.5.table, bf16[2,16,6144]{2,1,0:T(8,128)(2,1)S(1)} %pad_maximum_fusion.refs_0_, bf16[2,16,6144]{2,1,0:T(8,128)(2,1)S(1)} %collective-permute-done.3.refs_1_, ...), custom_call_target="tpu_custom_call" | custom-call | tf_op jit(solution)/shard_map/grad/pallas_call | solution.py:205
  104.5 1.4 %total.3 = (bf16[384,3072]{1,0:T(8,128)(2,1)}, bf16[384,3072]{1,0:T(8,128)(2,1)}) custom-call(bf16[2,384,1024]{2,1,0:T(8,128)(2,1)S(1)} %get-tuple-element.208.own_ref, bf16[2,384,1024]{2,1,0:T(8,128)(2,1)S(1)} %collective-permute-done.29.got_ref), custom_call_target="tpu_custom_call" | custom-call | tf_op jit(solution)/shard_map/total/pallas_call | solution.py:233
  105.9 1.4 %total.4 = (bf16[384,3072]{1,0:T(8,128)(2,1)}, bf16[384,3072]{1,0:T(8,128)(2,1)}) custom-call(bf16[2,384,1024]{2,1,0:T(8,128)(2,1)S(1)} %get-tuple-element.206.own_ref, bf16[2,384,1024]{2,1,0:T(8,128)(2,1)S(1)} %collective-permute-done.28.got_ref, bf16[384,3072]{1,0:T(8,128)(2,1)} %get-tuple-element.210.refs_0_, ...), custom_call_target="tpu_custom_call", output_to_operand_aliasing={{0}: (2, {}), {1}: (3, {})} | custom-call | tf_op jit(solution)/shard_map/total/pallas_call | solution.py:233
  108.1 1.4 %total.5 = (bf16[384,3072]{1,0:T(8,128)(2,1)}, bf16[384,3072]{1,0:T(8,128)(2,1)}) custom-call(bf16[2,384,1024]{2,1,0:T(8,128)(2,1)S(1)} %get-tuple-element.204.own_ref, bf16[2,384,1024]{2,1,0:T(8,128)(2,1)S(1)} %collective-permute-done.27.got_ref, bf16[384,3072]{1,0:T(8,128)(2,1)} %get-tuple-element.212.refs_0_, ...), custom_call_target="tpu_custom_call", output_to_operand_aliasing={{0}: (2, {}), {1}: (3, {})} | custom-call | tf_op jit(solution)/shard_map/total/pallas_call | solution.py:233
  (53 shorter events, 21.6 us)
Async XLA Ops:
  0.6 8.8 %collective-permute-start = (bf16[384,3072]{1,0:T(8,128)(2,1)}, bf16[384,3072]{1,0:T(8,128)(2,1)}, u32[]{:S(2)}, u32[]{:S(2)}) collective-permute-start(bf16[384,3072]{1,0:T(8,128)(2,1)} %refs_0_.1), channel_id=1, source_target_pairs={{0,8},{8,0},{16,24},{24,16},{1,9},{9,1},{17,25},{25,17},{2,10},{10... | collective-permute-start | bytes 7077896 | tf_op jit(solution)/shard_map/ppermute | solution.py:257
  1.1 11.0 %collective-permute-start.1 = (bf16[384,3072]{1,0:T(8,128)(2,1)}, bf16[384,3072]{1,0:T(8,128)(2,1)}, u32[]{:S(2)}, u32[]{:S(2)}) collective-permute-start(bf16[384,3072]{1,0:T(8,128)(2,1)} %refs_1_.1), channel_id=1, source_target_pairs={{0,8},{8,0},{16,24},{24,16},{1,9},{9,1},{17,25},{25,17},{2,10},{10... | collective-permute-start | bytes 7077896 | tf_op jit(solution)/shard_map/ppermute | solution.py:257
  2.3 15.3 %collective-permute-start.2 = (bf16[2,16,6144]{2,1,0:T(8,128)(2,1)S(1)}, bf16[2,16,6144]{2,1,0:T(8,128)(2,1)S(1)}, u32[]{:S(2)}, u32[]{:S(2)}) collective-permute-start(bf16[2,16,6144]{2,1,0:T(8,128)(2,1)S(1)} %pad_maximum_fusion.refs_0_), channel_id=1, source_target_pairs={{0,16},{8,24},{16,0},{24,8},{1,17},{9,25},{17,1},{25,9},{2,18},{10... | collective-permute-start | bytes 1179656 | tf_op jit(solution)/shard_map/ppermute | solution.py:254
  5.3 12.4 %collective-permute-start.3 = (bf16[2,16,6144]{2,1,0:T(8,128)(2,1)S(1)}, bf16[2,16,6144]{2,1,0:T(8,128)(2,1)S(1)}, u32[]{:S(2)}, u32[]{:S(2)}) collective-permute-start(bf16[2,16,6144]{2,1,0:T(8,128)(2,1)S(1)} %pad_maximum_fusion.refs_0_), channel_id=1, source_target_pairs={{0,1},{1,0},{2,3},{3,2},{4,5},{5,4},{6,7},{7,6},{8,9},{9,8},{10,11... | collective-permute-start | bytes 1179656 | tf_op jit(solution)/shard_map/ppermute | solution.py:260
  6.8 19.2 %collective-permute-start.4 = (bf16[2,16,6144]{2,1,0:T(8,128)(2,1)S(1)}, bf16[2,16,6144]{2,1,0:T(8,128)(2,1)S(1)}, u32[]{:S(2)}, u32[]{:S(2)}) collective-permute-start(bf16[2,16,6144]{2,1,0:T(8,128)(2,1)S(1)} %pad_maximum_fusion.refs_0_), channel_id=1, source_target_pairs={{0,2},{1,3},{2,0},{3,1},{4,6},{5,7},{6,4},{7,5},{8,10},{9,11},{10,... | collective-permute-start | bytes 1179656 | tf_op jit(solution)/shard_map/ppermute | solution.py:263
  9.4 19.5 %collective-permute-start.5 = (bf16[2,16,6144]{2,1,0:T(8,128)(2,1)S(1)}, bf16[2,16,6144]{2,1,0:T(8,128)(2,1)S(1)}, u32[]{:S(2)}, u32[]{:S(2)}) collective-permute-start(bf16[2,16,6144]{2,1,0:T(8,128)(2,1)S(1)} %pad_maximum_fusion.refs_0_), channel_id=1, source_target_pairs={{0,4},{1,5},{2,6},{3,7},{4,0},{5,1},{6,2},{7,3},{8,12},{9,13},{10,... | collective-permute-start | bytes 1179656 | tf_op jit(solution)/shard_map/ppermute | solution.py:266
  17.6 11.8 %collective-permute-start.6 = (bf16[2,16,6144]{2,1,0:T(8,128)(2,1)S(1)}, bf16[2,16,6144]{2,1,0:T(8,128)(2,1)S(1)}, u32[]{:S(2)}, u32[]{:S(2)}) collective-permute-start(bf16[2,16,6144]{2,1,0:T(8,128)(2,1)S(1)} %collective-permute-done.2.refs_0_.refs_2_), channel_id=1, source_target_pairs={{0,1},{1,0},{2,3},{3,2},{4,5},{5,4},{6,7},{7,6},{8,9},{9,8},{10,11... | collective-permute-start | bytes 1179656 | tf_op jit(solution)/shard_map/ppermute | solution.py:260
  18.2 16.1 %collective-permute-start.7 = (bf16[2,16,6144]{2,1,0:T(8,128)(2,1)S(1)}, bf16[2,16,6144]{2,1,0:T(8,128)(2,1)S(1)}, u32[]{:S(2)}, u32[]{:S(2)}) collective-permute-start(bf16[2,16,6144]{2,1,0:T(8,128)(2,1)S(1)} %collective-permute-done.2.refs_0_.refs_2_), channel_id=1, source_target_pairs={{0,2},{1,3},{2,0},{3,1},{4,6},{5,7},{6,4},{7,5},{8,10},{9,11},{10,... | collective-permute-start | bytes 1179656 | tf_op jit(solution)/shard_map/ppermute | solution.py:263
  22.8 13.5 %collective-permute-start.8 = (bf16[2,32,3072]{2,1,0:T(8,128)(2,1)S(1)}, bf16[2,32,3072]{2,1,0:T(8,128)(2,1)S(1)}, u32[]{:S(2)}, u32[]{:S(2)}) collective-permute-start(bf16[2,32,3072]{2,1,0:T(8,128)(2,1)S(1)} %get-tuple-element.122), channel_id=1, source_target_pairs={{0,16},{8,24},{16,0},{24,8},{1,17},{9,25},{17,1},{25,9},{2,18},{10... | collective-permute-start | bytes 1179656 | tf_op jit(solution)/shard_map/ppermute | solution.py:254
  28.9 10.1 %collective-permute-start.9 = (bf16[2,16,6144]{2,1,0:T(8,128)(2,1)S(1)}, bf16[2,16,6144]{2,1,0:T(8,128)(2,1)S(1)}, u32[]{:S(2)}, u32[]{:S(2)}) collective-permute-start(bf16[2,16,6144]{2,1,0:T(8,128)(2,1)S(1)} %collective-permute-done.4.refs_0_.refs_4_), channel_id=1, source_target_pairs={{0,1},{1,0},{2,3},{3,2},{4,5},{5,4},{6,7},{7,6},{8,9},{9,8},{10,11... | collective-permute-start | bytes 1179656 | tf_op jit(solution)/shard_map/ppermute | solution.py:260
  33.1 10.6 %collective-permute-start.10 = (bf16[2,32,3072]{2,1,0:T(8,128)(2,1)S(1)}, bf16[2,32,3072]{2,1,0:T(8,128)(2,1)S(1)}, u32[]{:S(2)}, u32[]{:S(2)}) collective-permute-start(bf16[2,32,3072]{2,1,0:T(8,128)(2,1)S(1)} %get-tuple-element.130), channel_id=1, source_target_pairs={{0,16},{8,24},{16,0},{24,8},{1,17},{9,25},{17,1},{25,9},{2,18},{10... | collective-permute-start | bytes 1179656 | tf_op jit(solution)/shard_map/ppermute | solution.py:254
  34.3 12.1 %collective-permute-start.11 = (bf16[2,16,6144]{2,1,0:T(8,128)(2,1)S(1)}, bf16[2,16,6144]{2,1,0:T(8,128)(2,1)S(1)}, u32[]{:S(2)}, u32[]{:S(2)}) collective-permute-start(bf16[2,16,6144]{2,1,0:T(8,128)(2,1)S(1)} %collective-permute-done.7.refs_0_.refs_6_), channel_id=1, source_target_pairs={{0,1},{1,0},{2,3},{3,2},{4,5},{5,4},{6,7},{7,6},{8,9},{9,8},{10,11... | collective-permute-start | bytes 1179656 | tf_op jit(solution)/shard_map/ppermute | solution.py:260
  35.2 17.2 %collective-permute-start.12 = (bf16[2,16,6144]{2,1,0:T(8,128)(2,1)S(1)}, bf16[2,16,6144]{2,1,0:T(8,128)(2,1)S(1)}, u32[]{:S(2)}, u32[]{:S(2)}) collective-permute-start(bf16[2,16,6144]{2,1,0:T(8,128)(2,1)S(1)} %collective-permute-done.5.refs_0_.refs_8_), channel_id=1, source_target_pairs={{0,2},{1,3},{2,0},{3,1},{4,6},{5,7},{6,4},{7,5},{8,10},{9,11},{10,... | collective-permute-start | bytes 1179656 | tf_op jit(solution)/shard_map/ppermute | solution.py:263
  36.3 18.5 %collective-permute-start.13 = (bf16[2,16,6144]{2,1,0:T(8,128)(2,1)S(1)}, bf16[2,16,6144]{2,1,0:T(8,128)(2,1)S(1)}, u32[]{:S(2)}, u32[]{:S(2)}) collective-permute-start(bf16[2,16,6144]{2,1,0:T(8,128)(2,1)S(1)} %collective-permute-done.2.refs_0_.refs_2_), channel_id=1, source_target_pairs={{0,4},{1,5},{2,6},{3,7},{4,0},{5,1},{6,2},{7,3},{8,12},{9,13},{10,... | collective-permute-start | bytes 1179656 | tf_op jit(solution)/shard_map/ppermute | solution.py:266
  42.6 12.9 %collective-permute-start.15 = (bf16[2,32,3072]{2,1,0:T(8,128)(2,1)S(1)}, bf16[2,32,3072]{2,1,0:T(8,128)(2,1)S(1)}, u32[]{:S(2)}, u32[]{:S(2)}) collective-permute-start(bf16[2,32,3072]{2,1,0:T(8,128)(2,1)S(1)} %get-tuple-element.143), channel_id=1, source_target_pairs={{0,16},{8,24},{16,0},{24,8},{1,17},{9,25},{17,1},{25,9},{2,18},{10... | collective-permute-start | bytes 1179656 | tf_op jit(solution)/shard_map/ppermute | solution.py:254
  43.7 13.1 %collective-permute-start.14 = (bf16[2,16,6144]{2,1,0:T(8,128)(2,1)S(1)}, bf16[2,16,6144]{2,1,0:T(8,128)(2,1)S(1)}, u32[]{:S(2)}, u32[]{:S(2)}) collective-permute-start(bf16[2,16,6144]{2,1,0:T(8,128)(2,1)S(1)} %collective-permute-done.5.refs_0_.refs_8_), channel_id=1, source_target_pairs={{0,1},{1,0},{2,3},{3,2},{4,5},{5,4},{6,7},{7,6},{8,9},{9,8},{10,11... | collective-permute-start | bytes 1179656 | tf_op jit(solution)/shard_map/ppermute | solution.py:260
  52.3 12.1 %collective-permute-start.16 = (bf16[2,16,6144]{2,1,0:T(8,128)(2,1)S(1)}, bf16[2,16,6144]{2,1,0:T(8,128)(2,1)S(1)}, u32[]{:S(2)}, u32[]{:S(2)}) collective-permute-start(bf16[2,16,6144]{2,1,0:T(8,128)(2,1)S(1)} %collective-permute-done.12.refs_0_.refs_10_), channel_id=1, source_target_pairs={{0,1},{1,0},{2,3},{3,2},{4,5},{5,4},{6,7},{7,6},{8,9},{9,8},{10,11... | collective-permute-start | bytes 1179656 | tf_op jit(solution)/shard_map/ppermute | solution.py:260
  53.7 10.7 %collective-permute-start.17 = (bf16[2,32,3072]{2,1,0:T(8,128)(2,1)S(1)}, bf16[2,32,3072]{2,1,0:T(8,128)(2,1)S(1)}, u32[]{:S(2)}, u32[]{:S(2)}) collective-permute-start(bf16[2,32,3072]{2,1,0:T(8,128)(2,1)S(1)} %get-tuple-element.149), channel_id=1, source_target_pairs={{0,16},{8,24},{16,0},{24,8},{1,17},{9,25},{17,1},{25,9},{2,18},{10... | collective-permute-start | bytes 1179656 | tf_op jit(solution)/shard_map/ppermute | solution.py:254
  54.9 13.1 %collective-permute-start.18 = (bf16[2,16,6144]{2,1,0:T(8,128)(2,1)S(1)}, bf16[2,16,6144]{2,1,0:T(8,128)(2,1)S(1)}, u32[]{:S(2)}, u32[]{:S(2)}) collective-permute-start(bf16[2,16,6144]{2,1,0:T(8,128)(2,1)S(1)} %collective-permute-done.13.refs_0_.refs_12_), channel_id=1, source_target_pairs={{0,2},{1,3},{2,0},{3,1},{4,6},{5,7},{6,4},{7,5},{8,10},{9,11},{10,... | collective-permute-start | bytes 1179656 | tf_op jit(solution)/shard_map/ppermute | solution.py:263
  55.5 17.3 %collective-permute-start.19 = (bf16[2,16,6144]{2,1,0:T(8,128)(2,1)S(1)}, bf16[2,16,6144]{2,1,0:T(8,128)(2,1)S(1)}, u32[]{:S(2)}, u32[]{:S(2)}) collective-permute-start(bf16[2,16,6144]{2,1,0:T(8,128)(2,1)S(1)} %collective-permute-done.13.refs_0_.refs_12_), channel_id=1, source_target_pairs={{0,1},{1,0},{2,3},{3,2},{4,5},{5,4},{6,7},{7,6},{8,9},{9,8},{10,11... | collective-permute-start | bytes 1179656 | tf_op jit(solution)/shard_map/ppermute | solution.py:260
  60.4 12.5 %collective-permute-start.20 = (bf16[2,32,3072]{2,1,0:T(8,128)(2,1)S(1)}, bf16[2,32,3072]{2,1,0:T(8,128)(2,1)S(1)}, u32[]{:S(2)}, u32[]{:S(2)}) collective-permute-start(bf16[2,32,3072]{2,1,0:T(8,128)(2,1)S(1)} %get-tuple-element.156), channel_id=1, source_target_pairs={{0,16},{8,24},{16,0},{24,8},{1,17},{9,25},{17,1},{25,9},{2,18},{10... | collective-permute-start | bytes 1179656 | tf_op jit(solution)/shard_map/ppermute | solution.py:254
  68.0 10.8 %collective-permute-start.21 = (bf16[2,16,6144]{2,1,0:T(8,128)(2,1)S(1)}, bf16[2,16,6144]{2,1,0:T(8,128)(2,1)S(1)}, u32[]{:S(2)}, u32[]{:S(2)}) collective-permute-start(bf16[2,16,6144]{2,1,0:T(8,128)(2,1)S(1)} %collective-permute-done.18.refs_0_.refs_14_), channel_id=1, source_target_pairs={{0,1},{1,0},{2,3},{3,2},{4,5},{5,4},{6,7},{7,6},{8,9},{9,8},{10,11... | collective-permute-start | bytes 1179656 | tf_op jit(solution)/shard_map/ppermute | solution.py:260
  69.5 12.1 %collective-permute-start.22 = (bf16[2,32,3072]{2,1,0:T(8,128)(2,1)S(1)}, bf16[2,32,3072]{2,1,0:T(8,128)(2,1)S(1)}, u32[]{:S(2)}, u32[]{:S(2)}) collective-permute-start(bf16[2,32,3072]{2,1,0:T(8,128)(2,1)S(1)} %get-tuple-element.167), channel_id=1, source_target_pairs={{0,16},{8,24},{16,0},{24,8},{1,17},{9,25},{17,1},{25,9},{2,18},{10... | collective-permute-start | bytes 1179656 | tf_op jit(solution)/shard_map/ppermute | solution.py:254
  76.4 16.3 %collective-permute-start.23 = (bf16[2,32,3072]{2,1,0:T(8,128)(2,1)S(1)}, bf16[2,32,3072]{2,1,0:T(8,128)(2,1)S(1)}, u32[]{:S(2)}, u32[]{:S(2)}) collective-permute-start(bf16[2,32,3072]{2,1,0:T(8,128)(2,1)S(1)} %get-tuple-element.173), channel_id=1, source_target_pairs={{0,16},{8,24},{16,0},{24,8},{1,17},{9,25},{17,1},{25,9},{2,18},{10... | collective-permute-start | bytes 1179656 | tf_op jit(solution)/shard_map/ppermute | solution.py:254
  80.5 12.3 %collective-permute-start.24 = (bf16[2,32,1024]{2,1,0:T(8,128)(2,1)S(1)}, bf16[2,32,1024]{2,1,0:T(8,128)(2,1)S(1)}, u32[]{:S(2)}, u32[]{:S(2)}) collective-permute-start(bf16[2,32,1024]{2,1,0:T(8,128)(2,1)S(1)} %get-tuple-element.174), channel_id=1, source_target_pairs={{0,16},{8,24},{16,0},{24,8},{1,17},{9,25},{17,1},{25,9},{2,18},{10... | collective-permute-start | bytes 393224 | tf_op jit(solution)/shard_map/ppermute | solution.py:254
  83.1 13.3 %collective-permute-start.25 = (bf16[2,32,1024]{2,1,0:T(8,128)(2,1)S(1)}, bf16[2,32,1024]{2,1,0:T(8,128)(2,1)S(1)}, u32[]{:S(2)}, u32[]{:S(2)}) collective-permute-start(bf16[2,32,1024]{2,1,0:T(8,128)(2,1)S(1)} %get-tuple-element.194), channel_id=1, source_target_pairs={{0,16},{8,24},{16,0},{24,8},{1,17},{9,25},{17,1},{25,9},{2,18},{10... | collective-permute-start | bytes 393224 | tf_op jit(solution)/shard_map/ppermute | solution.py:254
  85.8 14.3 %collective-permute-start.26 = (bf16[2,32,1024]{2,1,0:T(8,128)(2,1)S(1)}, bf16[2,32,1024]{2,1,0:T(8,128)(2,1)S(1)}, u32[]{:S(2)}, u32[]{:S(2)}) collective-permute-start(bf16[2,32,1024]{2,1,0:T(8,128)(2,1)S(1)} %get-tuple-element.200), channel_id=1, source_target_pairs={{0,16},{8,24},{16,0},{24,8},{1,17},{9,25},{17,1},{25,9},{2,18},{10... | collective-permute-start | bytes 393224 | tf_op jit(solution)/shard_map/ppermute | solution.py:254
  100.1 4.4 %collective-permute-start.29 = (bf16[2,384,1024]{2,1,0:T(8,128)(2,1)S(1)}, bf16[2,384,1024]{2,1,0:T(8,128)(2,1)S(1)}, u32[]{:S(2)}, u32[]{:S(2)}) collective-permute-start(bf16[2,384,1024]{2,1,0:T(8,128)(2,1)S(1)} %get-tuple-element.209), channel_id=1, source_target_pairs={{0,8},{8,0},{16,24},{24,16},{1,9},{9,1},{17,25},{25,17},{2,10},{10... | collective-permute-start | bytes 4718600 | tf_op jit(solution)/shard_map/ppermute | solution.py:257
  100.2 5.7 %collective-permute-start.28 = (bf16[2,384,1024]{2,1,0:T(8,128)(2,1)S(1)}, bf16[2,384,1024]{2,1,0:T(8,128)(2,1)S(1)}, u32[]{:S(2)}, u32[]{:S(2)}) collective-permute-start(bf16[2,384,1024]{2,1,0:T(8,128)(2,1)S(1)} %get-tuple-element.207), channel_id=1, source_target_pairs={{0,8},{8,0},{16,24},{24,16},{1,9},{9,1},{17,25},{25,17},{2,10},{10... | collective-permute-start | bytes 4718600 | tf_op jit(solution)/shard_map/ppermute | solution.py:257
  104.3 3.8 %collective-permute-start.27 = (bf16[2,384,1024]{2,1,0:T(8,128)(2,1)S(1)}, bf16[2,384,1024]{2,1,0:T(8,128)(2,1)S(1)}, u32[]{:S(2)}, u32[]{:S(2)}) collective-permute-start(bf16[2,384,1024]{2,1,0:T(8,128)(2,1)S(1)} %get-tuple-element.205), channel_id=1, source_target_pairs={{0,8},{8,0},{16,24},{24,16},{1,9},{9,1},{17,25},{25,17},{2,10},{10... | collective-permute-start | bytes 4718600 | tf_op jit(solution)/shard_map/ppermute | solution.py:257

commit v6 on v5

--- a/solution.py
+++ b/solution.py
@@ -18,11 +18,11 @@
 PARTIAL_VMEM = 8 * 1024 * 1024
 GRAD_VMEM = 16 * 1024 * 1024
 TOTAL_VMEM = 8 * 1024 * 1024
-PACK_LANES = 4
+PACK_ROWS = 64
 TICK_VMEM = 1024 * 1024
 PACK_VMEM = 12 * 1024 * 1024
-TOTAL_LANES = 8
-PARTS = 3
+PARTS = ((0, 2), (2, 2), (4, 2))
+EARLY_VMEM = 8 * 1024 * 1024
 COST = pl.CostEstimate(flops=0, bytes_accessed=0, transcendentals=0)
 
 
@@ -90,12 +90,11 @@
 
 def pack(*weights):
     kept, width = weights[0].shape
-    wide = PACK_LANES * BLK
     return pl.pallas_call(
         pack_kernel,
-        grid=(width // wide,),
-        in_specs=[pl.BlockSpec((kept, wide), lambda g: (0, g))] * len(weights),
-        out_specs=pl.BlockSpec((len(weights), kept, wide), lambda g: (0, 0, g)),
+        grid=(kept // PACK_ROWS,),
+        in_specs=[pl.BlockSpec((PACK_ROWS, width), lambda g: (g, 0))] * len(weights),
+        out_specs=pl.BlockSpec((len(weights), PACK_ROWS, width), lambda g: (0, g, 0)),
         out_shape=jax.ShapeDtypeStruct((len(weights), kept, width), weights[0].dtype),
         compiler_params=pltpu.CompilerParams(vmem_limit_bytes=PACK_VMEM),
         cost_estimate=COST,
@@ -117,15 +116,15 @@
             send_ref[side, :, at] = total.astype(jnp.bfloat16)
 
 
-def partial(table, buffers, weights, part=0, parts=1):
+def partial(table, buffers, weights, first=0, steps=None):
     tokens = sum(b.shape[1] for b in buffers)
     kept, width = weights.shape[1:]
     wide = LANES * BLK
-    steps = width // wide // parts
-    weight = pl.BlockSpec((4, kept, wide), lambda g, t: (0, 0, part * steps + g))
+    steps = width // wide if steps is None else steps
+    weight = pl.BlockSpec((4, kept, wide), lambda g, t: (0, 0, first + g))
     out = pl.BlockSpec((2, tokens, wide), lambda g, t: (0, 0, g))
     return pl.pallas_call(
-        functools.partial(partial_kernel, len(buffers), 2 * kept // BLK, part * steps * LANES),
+        functools.partial(partial_kernel, len(buffers), 2 * kept // BLK, first * LANES),
         grid_spec=pltpu.PrefetchScalarGridSpec(
             num_scalar_prefetch=1,
             grid=(steps,),
@@ -133,7 +132,7 @@
             out_specs=[out, out],
         ),
         out_shape=[
-            jax.ShapeDtypeStruct((2, tokens, width // parts), dtype) for dtype in (jnp.float32, jnp.bfloat16)
+            jax.ShapeDtypeStruct((2, tokens, steps * wide), dtype) for dtype in (jnp.float32, jnp.bfloat16)
         ],
         compiler_params=pltpu.CompilerParams(vmem_limit_bytes=PARTIAL_VMEM),
         cost_estimate=COST,
@@ -159,32 +158,54 @@
     )(table)
 
 
-def grad_kernel(units, n_buf, n_keep, n_got, slots, base, table, *refs):
-    buffers = refs[:n_buf]
-    keeps = refs[n_buf : n_buf + n_keep]
-    gots = refs[n_buf + n_keep : n_buf + n_keep + n_got]
-    own_ref, away_ref = refs[n_buf + n_keep + n_got :]
+def activations(keeps, gots, at):
+    def summed(side):
+        mine = jnp.concatenate([ref[side, :, at] for ref in keeps], axis=0)
+        return mine + jnp.concatenate([ref[side, :, at] for ref in gots], axis=0).astype(jnp.float32)
+
+    hidden, d_act = summed(0), summed(1)
+    square = hidden * hidden
+    tanh = jnp.tanh(SCALE * (hidden + CUBIC * square * hidden))
+    half_up = 0.5 * (1.0 + tanh)
+    slope = half_up + (0.5 * hidden) * (1.0 - tanh * tanh) * (SCALE + (3.0 * CUBIC * SCALE) * square)
+    return (d_act * slope).astype(jnp.bfloat16), (hidden * half_up).astype(jnp.bfloat16)
+
+
+def early_kernel(*refs):
+    n = len(refs) // 2
+    for lane in range(LANES):
+        at = slice(lane * BLK, (lane + 1) * BLK)
+        for side, value in enumerate(activations(refs[:n], refs[n : 2 * n], at)):
+            refs[2 * n][side, :, at] = value
+
+
+def early(keeps, gots):
+    tokens = sum(v.shape[1] for v in keeps)
+    width = keeps[0].shape[2]
+    wide = LANES * BLK
+    return pl.pallas_call(
+        early_kernel,
+        grid=(width // wide,),
+        in_specs=[pl.BlockSpec((2, v.shape[1], wide), lambda g: (0, 0, g)) for v in (*keeps, *gots)],
+        out_specs=pl.BlockSpec((2, tokens, wide), lambda g: (0, 0, g)),
+        out_shape=jax.ShapeDtypeStruct((2, tokens, width), jnp.bfloat16),
+        compiler_params=pltpu.CompilerParams(vmem_limit_bytes=EARLY_VMEM),
+        cost_estimate=COST,
+        name="early",
+    )(*keeps, *gots)
+
+
+def grad_kernel(n_buf, n_late, slots, base, table, *refs):
+    buffers, done = refs[:n_buf], refs[n_buf]
+    keeps = refs[n_buf + 1 : n_buf + 1 + n_late]
+    gots = refs[n_buf + 1 + n_late : n_buf + 1 + 2 * n_late]
+    own_ref, away_ref = refs[n_buf + 1 + 2 * n_late :]
     step = pl.program_id(0)
     kept = slots * BLK // 2
-    rows = 2 * buffers[0].shape[1]
     for lane in range(LANES):
         at = slice(lane * BLK, (lane + 1) * BLK)
-
-        def gathered(side):
-            mine, theirs = [], []
-            for keep, keep_at, got, got_at in units:
-                mine.append(keeps[keep][side, keep_at * rows : (keep_at + 1) * rows, at])
-                theirs.append(gots[got][side, got_at * rows : (got_at + 1) * rows, at])
-            return jnp.concatenate(mine, axis=0) + jnp.concatenate(theirs, axis=0).astype(jnp.float32)
-
-        hidden, d_act = gathered(0), gathered(1)
-        square = hidden * hidden
-        tanh = jnp.tanh(SCALE * (hidden + CUBIC * square * hidden))
-        half_up = 0.5 * (1.0 + tanh)
-        act = (hidden * half_up).astype(jnp.bfloat16)
-        slope = half_up + (0.5 * hidden) * (1.0 - tanh * tanh) * (SCALE + (3.0 * CUBIC * SCALE) * square)
-        d_hidden = (d_act * slope).astype(jnp.bfloat16)
-        for side, right in enumerate((d_hidden, act)):
+        for side, late in enumerate(activations(keeps, gots, at)):
+            right = jnp.concatenate((done[side, :, at], late), axis=0)
             left = picked_rows(table, buffers, side, base + step * LANES + lane, slots)
             total = lax.dot_general(left, right, (((0,), (0,)), ((), ())), preferred_element_type=jnp.float32)
             total = total.astype(jnp.bfloat16)
@@ -192,31 +213,28 @@
             away_ref[side, :, at] = total[kept:]
 
 
-def grad(table, units, buffers, keeps, gots, kept, part, parts):
-    width = max(keep.shape[2] for keep in keeps)
+def grad(table, buffers, done, keeps, gots, kept, first, steps):
+    width = done.shape[2]
     wide = LANES * BLK
-    steps = width // wide // parts
 
     def spec(array):
-        first = part * steps if array.shape[2] == width else 0
-        return pl.BlockSpec((2, array.shape[1], wide), lambda g, t: (0, 0, first + g))
+        start = first if array.shape[2] == width else 0
+        return pl.BlockSpec((2, array.shape[1], wide), lambda g, t: (0, 0, start + g))
 
     out = pl.BlockSpec((2, kept, wide), lambda g, t: (0, 0, g))
     return pl.pallas_call(
-        functools.partial(
-            grad_kernel, units, len(buffers), len(keeps), len(gots), 2 * kept // BLK, part * steps * LANES
-        ),
+        functools.partial(grad_kernel, len(buffers), len(keeps), 2 * kept // BLK, first * LANES),
         grid_spec=pltpu.PrefetchScalarGridSpec(
             num_scalar_prefetch=1,
             grid=(steps,),
-            in_specs=[fixed(b) for b in buffers] + [spec(v) for v in (*keeps, *gots)],
+            in_specs=[fixed(b) for b in buffers] + [spec(v) for v in (done, *keeps, *gots)],
             out_specs=[out, out],
         ),
-        out_shape=[jax.ShapeDtypeStruct((2, kept, width // parts), jnp.bfloat16)] * 2,
+        out_shape=[jax.ShapeDtypeStruct((2, kept, steps * wide), jnp.bfloat16)] * 2,
         compiler_params=pltpu.CompilerParams(vmem_limit_bytes=GRAD_VMEM),
         cost_estimate=COST,
         name="grad",
-    )(table, *buffers, *keeps, *gots)
+    )(table, *buffers, done, *keeps, *gots)
 
 
 def total_kernel(own_ref, got_ref, *refs):
@@ -224,18 +242,17 @@
         ref[...] = (own_ref[side].astype(jnp.float32) + got_ref[side].astype(jnp.float32)).astype(ref.dtype)
 
 
-def total(own, got, before, part, parts):
-    kept, width = own.shape[1:]
-    wide = TOTAL_LANES * BLK
-    steps = width // wide
+def total(own, got, before, first, width):
+    kept, here = own.shape[1:]
+    wide = LANES * BLK
     source = pl.BlockSpec((2, kept, wide), lambda g: (0, 0, g))
-    out = pl.BlockSpec((kept, wide), lambda g: (0, part * steps + g))
+    out = pl.BlockSpec((kept, wide), lambda g: (0, first + g))
     return pl.pallas_call(
         total_kernel,
-        grid=(steps,),
+        grid=(here // wide,),
         in_specs=[source, source] + [pl.BlockSpec(memory_space=pl.ANY)] * len(before),
         out_specs=[out, out],
-        out_shape=[jax.ShapeDtypeStruct((kept, width * parts), jnp.bfloat16)] * 2,
+        out_shape=[jax.ShapeDtypeStruct((kept, width), jnp.bfloat16)] * 2,
         input_output_aliases={2: 0, 3: 1} if before else {},
         compiler_params=pltpu.CompilerParams(vmem_limit_bytes=TOTAL_VMEM),
         cost_estimate=COST,
@@ -325,38 +342,38 @@
     keep6, send6 = partial(table, (b2, yb2), weights)
     table, send6 = gate((table, send6))
     got6 = swap_x(send6)
+    done = early((keep0, keep1, keep2, keep3, keep6), (got1, got0, got3, got2, got4))
+    table, done = gate((table, done))
     table, yb3, b3 = gate((table, yb3, b3))
     keep7, got7 = [], []
-    for part in range(PARTS):
-        keep, send = partial(table, (b3, yb3), weights, part, PARTS)
+    for part, (first, steps) in enumerate(PARTS):
+        keep, send = partial(table, (b3, yb3), weights, first, steps)
         table, send = gate((table, send))
         if part == 0:
             table, got5 = gate((table, got5))
         keep7.append(keep)
         got7.append(swap_x(send))
-    table, got6, got7[0] = gate((table, got6, got7[0]))
-
-    buffers = (a0, ya0, b0, yb0, a1, ya1, b1, yb1, a2, ya2, a3, ya3, b2, yb2, b3, yb3)
-    units = ((0, 0, 1, 0), (1, 0, 0, 0), (2, 0, 3, 0), (3, 0, 2, 0), (4, 0, 6, 0), (5, 0, 7, 0), (6, 0, 4, 0), (7, 0, 5, 0))
-    keeps = (keep0, keep1, keep2, keep3, keep4, keep5, keep6)
-    gots = (got0, got1, got2, got3, got4, got5, got6)
-    outs, waiting = (), None
-    for part in range(PARTS):
-        own, away = grad(table, units, buffers, (*keeps, keep7[part]), (*gots, got7[part]), kept, part, PARTS)
-        if part < PARTS - 1:
+    buffers = (a0, ya0, b0, yb0, a1, ya1, b1, yb1, b2, yb2, a2, ya2, a3, ya3, b3, yb3)
+    table, got7[0] = gate((table, got7[0]))
+    table, got6 = gate((table, got6))
+    outs = ()
+    for part, (first, steps) in enumerate(PARTS):
+        keeps, gots = (keep4, keep5, keep7[part]), (got6, got7[part], got5)
+        own, away = grad(table, buffers, done, keeps, gots, kept, first, steps)
+        if part < len(PARTS) - 1:
             table, own, away, got7[part + 1] = gate((table, own, away, got7[part + 1]))
         back = swap_core(away)
-        if waiting is not None:
-            outs = total(*waiting, outs, part - 1, PARTS)
-        waiting = (own, back)
-    return tuple(total(*waiting, tuple(outs), PARTS - 1, PARTS))
+        if part > 0:
+            outs = total(*before, outs, PARTS[part - 1][0], width)
+        before = [own, back]
+    return tuple(total(*before, outs, PARTS[-1][0], width))
 
 
 def solution(mesh):
     def per_device(inputs, cotangent, w_in, w_out, keep_in, keep_out):
         kept, width = w_in.shape
         fits = kept % BLK == 0 and inputs.shape[0] % 16 == 0
-        fits = fits and all(width % (PARTS * lanes * BLK) == 0 for lanes in (LANES, PACK_LANES, TOTAL_LANES))
+        fits = fits and kept % PACK_ROWS == 0 and width == sum(steps for _, steps in PARTS) * LANES * BLK
         chosen = fast if fits and mesh.shape["row"] == ROWS and mesh.shape["col"] == COLS else general
         return chosen(inputs, cotangent, w_in, w_out, keep_in, keep_out)
 

time: 110 us -> 109 us (level)
  waiting for transfers between devices: 23.1 us -> 20.2 us
  Pallas kernels: 50.7 us -> 52 us
    ppermute x8, waiting for transfers between devices: 8.7 us -> 7.27 us  [swap_y(): return lax.ppermute(v, 'col', [(c, c ^ 1) for c in range(COLS)])]
    ppermute x11, waiting for transfers between devices: 6.16 us -> 4.9 us  [swap_x(): return lax.ppermute(v, 'row', [(r, r ^ 2) for r in range(ROWS)])]
    pallas_call x7 -> x8, Pallas kernels: 20.7 us -> 21.9 us  [the longest x3 9.81 us: grad(): pl.pallas_call(functools.partial(grad_kernel, len(buffers), len(keeps), 2...]
  transfers between devices with their start and end apart: 30 -> 30, of which waited for: 11 -> 9; matrix products, arithmetic and copies ran while one was open for 2% -> 2% of each run, Pallas kernels for 45% -> 47%
where the time goes in v6:
time: 109 us; the launch traced here: 108 us
  Pallas kernels  52 us (48%)
  starting transfers between devices  33 us (30%)
  waiting for transfers between devices  20.2 us (19%)
    pallas_call x10, Pallas kernels, partial(): pl.pallas_call(functools.partial(partial_kernel, len(buffers), 2 * kept /...  30.1 us
    ppermute x11, starting transfers between devices, swap_x(): return lax.ppermute(v, 'row', [(r, r ^ 2) for r in range(ROWS)])  12.7 us
    pallas_call x3, Pallas kernels, grad(): pl.pallas_call(functools.partial(grad_kernel, len(buffers), len(keeps), 2...  9.81 us
    ppermute x8, starting transfers between devices, swap_y(): return lax.ppermute(v, 'col', [(c, c ^ 1) for c in range(COLS)])  9.18 us
    ppermute x8, waiting for transfers between devices, swap_y(): return lax.ppermute(v, 'col', [(c, c ^ 1) for c in range(COLS)])  7.27 us
    pallas_call x1, Pallas kernels, pack(): pl.pallas_call(pack_kernel, grid=(kept // PACK_ROWS,), in_specs=[pl.Block...  5.39 us
    ppermute x2, starting transfers between devices, far(): return lax.ppermute(v, 'col', [(c, c ^ 4) for c in range(COLS)])  5.34 us
    ppermute x11, waiting for transfers between devices, swap_x(): return lax.ppermute(v, 'row', [(r, r ^ 2) for r in range(ROWS)])  4.9 us
  transfers between devices with their start and end apart: 30, of which 9 were waited for; matrix products, arithmetic and copies ran while one was open for 2% of the time, Pallas kernels for 47%

profile of v6, /device:TPU:0, one launch (start us, length us, event | category | flops | bytes accessed | tf_op | source)
XLA Modules:
  0.0 108.2 jit_solution(15280039145998093326)
XLA Ops:
  2.3 3.0 %collective-permute-start.2 = (bf16[2,16,6144]{2,1,0:T(8,128)(2,1)S(1)}, bf16[2,16,6144]{2,1,0:T(8,128)(2,1)S(1)}, u32[]{:S(2)}, u32[]{:S(2)}) collective-permute-start(bf16[2,16,6144]{2,1,0:T(8,128)(2,1)S(1)} %pad_maximum_fusion.refs_0_), channel_id=1, source_target_pairs={{0,16},{8,24},{16,0},{24,8},{1,17},{9,25},{17,1},{25,9},{2,18},{10... | collective-permute-start | bytes 1179656 | tf_op jit(solution)/shard_map/ppermute | solution.py:271
  5.3 1.5 %collective-permute-start.3 = (bf16[2,16,6144]{2,1,0:T(8,128)(2,1)S(1)}, bf16[2,16,6144]{2,1,0:T(8,128)(2,1)S(1)}, u32[]{:S(2)}, u32[]{:S(2)}) collective-permute-start(bf16[2,16,6144]{2,1,0:T(8,128)(2,1)S(1)} %pad_maximum_fusion.refs_0_), channel_id=1, source_target_pairs={{0,1},{1,0},{2,3},{3,2},{4,5},{5,4},{6,7},{7,6},{8,9},{9,8},{10,11... | collective-permute-start | bytes 1179656 | tf_op jit(solution)/shard_map/ppermute | solution.py:277
  6.8 1.6 %collective-permute-start.4 = (bf16[2,16,6144]{2,1,0:T(8,128)(2,1)S(1)}, bf16[2,16,6144]{2,1,0:T(8,128)(2,1)S(1)}, u32[]{:S(2)}, u32[]{:S(2)}) collective-permute-start(bf16[2,16,6144]{2,1,0:T(8,128)(2,1)S(1)} %pad_maximum_fusion.refs_0_), channel_id=1, source_target_pairs={{0,2},{1,3},{2,0},{3,1},{4,6},{5,7},{6,4},{7,5},{8,10},{9,11},{10,... | collective-permute-start | bytes 1179656 | tf_op jit(solution)/shard_map/ppermute | solution.py:280
  9.4 2.7 %collective-permute-start.5 = (bf16[2,16,6144]{2,1,0:T(8,128)(2,1)S(1)}, bf16[2,16,6144]{2,1,0:T(8,128)(2,1)S(1)}, u32[]{:S(2)}, u32[]{:S(2)}) collective-permute-start(bf16[2,16,6144]{2,1,0:T(8,128)(2,1)S(1)} %pad_maximum_fusion.refs_0_), channel_id=1, source_target_pairs={{0,4},{1,5},{2,6},{3,7},{4,0},{5,1},{6,2},{7,3},{8,12},{9,13},{10,... | collective-permute-start | bytes 1179656 | tf_op jit(solution)/shard_map/ppermute | solution.py:283
  12.1 5.4 %pack.1.refs_2_ = bf16[4,384,3072]{2,1,0:T(8,128)(2,1)S(1)} custom-call(bf16[384,3072]{1,0:T(8,128)(2,1)} %refs_0_.1, bf16[384,3072]{1,0:T(8,128)(2,1)} %refs_1_.1, bf16[384,3072]{1,0:T(8,128)(2,1)} %collective-permute-done.refs_2_, bf16[384,3072]{1,0:T(8,128)(2,1)} %collective-permute-done.1.refs_3_), custom_call_target="tpu_custom_call" | custom-call | tf_op jit(solution)/shard_map/pack/pallas_call | solution.py:93
  19.2 3.6 %partial.10 = (f32[2,32,3072]{2,1,0:T(8,128)S(1)}, bf16[2,32,3072]{2,1,0:T(8,128)(2,1)S(1)}) custom-call(s32[288]{0:T(512)S(1)} %reshape.7.table.table_ref, bf16[2,16,6144]{2,1,0:T(8,128)(2,1)S(1)} %pad_maximum_fusion.refs_0_, bf16[2,16,6144]{2,1,0:T(8,128)(2,1)S(1)} %collective-permute-done.3.refs_1_, bf16[4,384,3072]{2,1,0:T(8,128)(2,1)S(1)} %pack.1.refs_2_), custom_call_target="tpu_custom_call" | custom-call | tf_op jit(solution)/shard_map/partial/pallas_call | solution.py:126
  24.1 1.9 %collective-permute-done.4.refs_0_.refs_4_ = bf16[2,16,6144]{2,1,0:T(8,128)(2,1)S(1)} collective-permute-done((bf16[2,16,6144]{2,1,0:T(8,128)(2,1)S(1)}, bf16[2,16,6144]{2,1,0:T(8,128)(2,1)S(1)}, u32[]{:S(2)}, u32[]{:S(2)}) %collective-permute-start.4) | collective-permute-done | bytes 393248 | tf_op jit(solution)/shard_map/ppermute | solution.py:280
  26.0 2.9 %collective-permute-done.5.refs_0_.refs_10_ = bf16[2,16,6144]{2,1,0:T(8,128)(2,1)S(1)} collective-permute-done((bf16[2,16,6144]{2,1,0:T(8,128)(2,1)S(1)}, bf16[2,16,6144]{2,1,0:T(8,128)(2,1)S(1)}, u32[]{:S(2)}, u32[]{:S(2)}) %collective-permute-start.5) | collective-permute-done | bytes 393248 | tf_op jit(solution)/shard_map/ppermute | solution.py:283
  29.5 3.6 %partial.11 = (f32[2,32,3072]{2,1,0:T(8,128)S(1)}, bf16[2,32,3072]{2,1,0:T(8,128)(2,1)S(1)}) custom-call(s32[288]{0:T(512)S(1)} %tick.4.table.table_ref, bf16[2,16,6144]{2,1,0:T(8,128)(2,1)S(1)} %collective-permute-done.2.refs_0_.refs_2_, bf16[2,16,6144]{2,1,0:T(8,128)(2,1)S(1)} %collective-permute-done.6.refs_1_.refs_3_, bf16[4,384,3072]{2,1,0:T(8,128)(2,1)S(1)} %pack.1.refs_2_), custom_call_target="tpu_custom_call" | custom-call | tf_op jit(solution)/shard_map/partial/pallas_call | solution.py:126
  36.3 2.7 %collective-permute-start.13 = (bf16[2,16,6144]{2,1,0:T(8,128)(2,1)S(1)}, bf16[2,16,6144]{2,1,0:T(8,128)(2,1)S(1)}, u32[]{:S(2)}, u32[]{:S(2)}) collective-permute-start(bf16[2,16,6144]{2,1,0:T(8,128)(2,1)S(1)} %collective-permute-done.2.refs_0_.refs_2_), channel_id=1, source_target_pairs={{0,4},{1,5},{2,6},{3,7},{4,0},{5,1},{6,2},{7,3},{8,12},{9,13},{10,... | collective-permute-start | bytes 1179656 | tf_op jit(solution)/shard_map/ppermute | solution.py:283
  39.0 3.6 %partial.12 = (f32[2,32,3072]{2,1,0:T(8,128)S(1)}, bf16[2,32,3072]{2,1,0:T(8,128)(2,1)S(1)}) custom-call(s32[288]{0:T(512)S(1)} %tick.4.table.table_ref, bf16[2,16,6144]{2,1,0:T(8,128)(2,1)S(1)} %collective-permute-done.4.refs_0_.refs_4_, bf16[2,16,6144]{2,1,0:T(8,128)(2,1)S(1)} %collective-permute-done.9.refs_1_.refs_5_, bf16[4,384,3072]{2,1,0:T(8,128)(2,1)S(1)} %pack.1.refs_2_), custom_call_target="tpu_custom_call" | custom-call | tf_op jit(solution)/shard_map/partial/pallas_call | solution.py:126
  43.7 1.7 %collective-permute-start.14 = (bf16[2,16,6144]{2,1,0:T(8,128)(2,1)S(1)}, bf16[2,16,6144]{2,1,0:T(8,128)(2,1)S(1)}, u32[]{:S(2)}, u32[]{:S(2)}) collective-permute-start(bf16[2,16,6144]{2,1,0:T(8,128)(2,1)S(1)} %collective-permute-done.5.refs_0_.refs_10_), channel_id=1, source_target_pairs={{0,1},{1,0},{2,3},{3,2},{4,5},{5,4},{6,7},{7,6},{8,9},{9,8},{10,11... | collective-permute-start | bytes 1179656 | tf_op jit(solution)/shard_map/ppermute | solution.py:277
  46.4 3.6 %partial.13 = (f32[2,32,3072]{2,1,0:T(8,128)S(1)}, bf16[2,32,3072]{2,1,0:T(8,128)(2,1)S(1)}) custom-call(s32[288]{0:T(512)S(1)} %tick.4.table.table_ref, bf16[2,16,6144]{2,1,0:T(8,128)(2,1)S(1)} %collective-permute-done.7.refs_0_.refs_6_, bf16[2,16,6144]{2,1,0:T(8,128)(2,1)S(1)} %collective-permute-done.11.refs_1_.refs_7_, bf16[4,384,3072]{2,1,0:T(8,128)(2,1)S(1)} %pack.1.refs_2_), custom_call_target="tpu_custom_call" | custom-call | tf_op jit(solution)/shard_map/partial/pallas_call | solution.py:126
  50.0 2.3 %collective-permute-done.12.refs_0_.refs_12_ = bf16[2,16,6144]{2,1,0:T(8,128)(2,1)S(1)} collective-permute-done((bf16[2,16,6144]{2,1,0:T(8,128)(2,1)S(1)}, bf16[2,16,6144]{2,1,0:T(8,128)(2,1)S(1)}, u32[]{:S(2)}, u32[]{:S(2)}) %collective-permute-start.12) | collective-permute-done | bytes 393248 | tf_op jit(solution)/shard_map/ppermute | solution.py:280
  52.3 1.4 %collective-permute-start.16 = (bf16[2,16,6144]{2,1,0:T(8,128)(2,1)S(1)}, bf16[2,16,6144]{2,1,0:T(8,128)(2,1)S(1)}, u32[]{:S(2)}, u32[]{:S(2)}) collective-permute-start(bf16[2,16,6144]{2,1,0:T(8,128)(2,1)S(1)} %collective-permute-done.12.refs_0_.refs_12_), channel_id=1, source_target_pairs={{0,1},{1,0},{2,3},{3,2},{4,5},{5,4},{6,7},{7,6},{8,9},{9,8},{10,11... | collective-permute-start | bytes 1179656 | tf_op jit(solution)/shard_map/ppermute | solution.py:277
  56.8 3.6 %partial.14 = (f32[2,32,3072]{2,1,0:T(8,128)S(1)}, bf16[2,32,3072]{2,1,0:T(8,128)(2,1)S(1)}) custom-call(s32[288]{0:T(512)S(1)} %tick.5.table, bf16[2,16,6144]{2,1,0:T(8,128)(2,1)S(1)} %collective-permute-done.5.refs_0_.refs_10_, bf16[2,16,6144]{2,1,0:T(8,128)(2,1)S(1)} %collective-permute-done.14.refs_1_.refs_11_, bf16[4,384,3072]{2,1,0:T(8,128)(2,1)S(1)} %pack.1.refs_2_), custom_call_target="tpu_custom_call" | custom-call | tf_op jit(solution)/shard_map/partial/pallas_call | solution.py:126
  60.9 3.5 %collective-permute-done.16.refs_1_.refs_13_ = bf16[2,16,6144]{2,1,0:T(8,128)(2,1)S(1)} collective-permute-done((bf16[2,16,6144]{2,1,0:T(8,128)(2,1)S(1)}, bf16[2,16,6144]{2,1,0:T(8,128)(2,1)S(1)}, u32[]{:S(2)}, u32[]{:S(2)}) %collective-permute-start.16) | collective-permute-done | bytes 393248 | tf_op jit(solution)/shard_map/ppermute | solution.py:277
  64.4 3.6 %partial.15 = (f32[2,32,3072]{2,1,0:T(8,128)S(1)}, bf16[2,32,3072]{2,1,0:T(8,128)(2,1)S(1)}) custom-call(s32[288]{0:T(512)S(1)} %tick.5.table, bf16[2,16,6144]{2,1,0:T(8,128)(2,1)S(1)} %collective-permute-done.12.refs_0_.refs_12_, bf16[2,16,6144]{2,1,0:T(8,128)(2,1)S(1)} %collective-permute-done.16.refs_1_.refs_13_, bf16[4,384,3072]{2,1,0:T(8,128)(2,1)S(1)} %pack.1.refs_2_), custom_call_target="tpu_custom_call" | custom-call | tf_op jit(solution)/shard_map/partial/pallas_call | solution.py:126
  68.0 1.4 %collective-permute-start.21 = (bf16[2,16,6144]{2,1,0:T(8,128)(2,1)S(1)}, bf16[2,16,6144]{2,1,0:T(8,128)(2,1)S(1)}, u32[]{:S(2)}, u32[]{:S(2)}) collective-permute-start(bf16[2,16,6144]{2,1,0:T(8,128)(2,1)S(1)} %collective-permute-done.18.refs_0_.refs_14_), channel_id=1, source_target_pairs={{0,1},{1,0},{2,3},{3,2},{4,5},{5,4},{6,7},{7,6},{8,9},{9,8},{10,11... | collective-permute-start | bytes 1179656 | tf_op jit(solution)/shard_map/ppermute | solution.py:277
  70.1 2.7 %collective-permute-done.19.refs_1_.refs_9_ = bf16[2,16,6144]{2,1,0:T(8,128)(2,1)S(1)} collective-permute-done((bf16[2,16,6144]{2,1,0:T(8,128)(2,1)S(1)}, bf16[2,16,6144]{2,1,0:T(8,128)(2,1)S(1)}, u32[]{:S(2)}, u32[]{:S(2)}) %collective-permute-start.19) | collective-permute-done | bytes 393248 | tf_op jit(solution)/shard_map/ppermute | solution.py:277
  72.8 3.6 %partial.16 = (f32[2,32,3072]{2,1,0:T(8,128)S(1)}, bf16[2,32,3072]{2,1,0:T(8,128)(2,1)S(1)}) custom-call(s32[288]{0:T(512)S(1)} %tick.5.table, bf16[2,16,6144]{2,1,0:T(8,128)(2,1)S(1)} %collective-permute-done.13.refs_0_.refs_8_, bf16[2,16,6144]{2,1,0:T(8,128)(2,1)S(1)} %collective-permute-done.19.refs_1_.refs_9_, bf16[4,384,3072]{2,1,0:T(8,128)(2,1)S(1)} %pack.1.refs_2_), custom_call_target="tpu_custom_call" | custom-call | tf_op jit(solution)/shard_map/partial/pallas_call | solution.py:126
  77.4 2.3 %early.1.refs_16_ = bf16[2,160,3072]{2,1,0:T(8,128)(2,1)S(1)} custom-call(f32[2,32,3072]{2,1,0:T(8,128)S(1)} %get-tuple-element.164.refs_0_, f32[2,32,3072]{2,1,0:T(8,128)S(1)} %get-tuple-element.165.refs_1_, f32[2,32,3072]{2,1,0:T(8,128)S(1)} %get-tuple-element.166.refs_2_, f32[2,32,3072]{2,1,0:T(8,128)S(1)} %get-tuple-element.167.refs_3_, ...), custom_call_target="tpu_custom_call" | custom-call | tf_op jit(solution)/shard_map/early/pallas_call | solution.py:186
  79.7 1.6 %partial.17 = (f32[2,32,1024]{2,1,0:T(8,128)S(1)}, bf16[2,32,1024]{2,1,0:T(8,128)(2,1)S(1)}) custom-call(s32[288]{0:T(512)S(1)} %tick.5.table, bf16[2,16,6144]{2,1,0:T(8,128)(2,1)S(1)} %collective-permute-done.18.refs_0_.refs_14_, bf16[2,16,6144]{2,1,0:T(8,128)(2,1)S(1)} %collective-permute-done.21.refs_1_.refs_15_, bf16[4,384,3072]{2,1,0:T(8,128)(2,1)S(1)} %pack.1.refs_2_), custom_call_target="tpu_custom_call" | custom-call | tf_op jit(solution)/shard_map/partial/pallas_call | solution.py:126
  82.5 1.6 %partial.18 = (f32[2,32,1024]{2,1,0:T(8,128)S(1)}, bf16[2,32,1024]{2,1,0:T(8,128)(2,1)S(1)}) custom-call(s32[288]{0:T(512)S(1)} %tick.5.table, bf16[2,16,6144]{2,1,0:T(8,128)(2,1)S(1)} %collective-permute-done.18.refs_0_.refs_14_, bf16[2,16,6144]{2,1,0:T(8,128)(2,1)S(1)} %collective-permute-done.21.refs_1_.refs_15_, bf16[4,384,3072]{2,1,0:T(8,128)(2,1)S(1)} %pack.1.refs_2_), custom_call_target="tpu_custom_call" | custom-call | tf_op jit(solution)/shard_map/partial/pallas_call | solution.py:126
  85.1 1.6 %partial.19 = (f32[2,32,1024]{2,1,0:T(8,128)S(1)}, bf16[2,32,1024]{2,1,0:T(8,128)(2,1)S(1)}) custom-call(s32[288]{0:T(512)S(1)} %tick.5.table, bf16[2,16,6144]{2,1,0:T(8,128)(2,1)S(1)} %collective-permute-done.18.refs_0_.refs_14_, bf16[2,16,6144]{2,1,0:T(8,128)(2,1)S(1)} %collective-permute-done.21.refs_1_.refs_15_, bf16[4,384,3072]{2,1,0:T(8,128)(2,1)S(1)} %pack.1.refs_2_), custom_call_target="tpu_custom_call" | custom-call | tf_op jit(solution)/shard_map/partial/pallas_call | solution.py:126
  87.9 4.9 %collective-permute-done.23.refs_21_ = bf16[2,32,1024]{2,1,0:T(8,128)(2,1)S(1)} collective-permute-done((bf16[2,32,1024]{2,1,0:T(8,128)(2,1)S(1)}, bf16[2,32,1024]{2,1,0:T(8,128)(2,1)S(1)}, u32[]{:S(2)}, u32[]{:S(2)}) %collective-permute-start.23) | collective-permute-done | bytes 131104 | tf_op jit(solution)/shard_map/ppermute | solution.py:271
  92.8 3.3 %grad.3 = (bf16[2,384,1024]{2,1,0:T(8,128)(2,1)S(1)}, bf16[2,384,1024]{2,1,0:T(8,128)(2,1)S(1)}) custom-call(s32[288]{0:T(512)S(1)} %tick.5.table, bf16[2,16,6144]{2,1,0:T(8,128)(2,1)S(1)} %pad_maximum_fusion.refs_0_, bf16[2,16,6144]{2,1,0:T(8,128)(2,1)S(1)} %collective-permute-done.3.refs_1_, ...), custom_call_target="tpu_custom_call" | custom-call | tf_op jit(solution)/shard_map/grad/pallas_call | solution.py:225
  96.1 3.3 %grad.4 = (bf16[2,384,1024]{2,1,0:T(8,128)(2,1)S(1)}, bf16[2,384,1024]{2,1,0:T(8,128)(2,1)S(1)}) custom-call(s32[288]{0:T(512)S(1)} %tick.5.table, bf16[2,16,6144]{2,1,0:T(8,128)(2,1)S(1)} %pad_maximum_fusion.refs_0_, bf16[2,16,6144]{2,1,0:T(8,128)(2,1)S(1)} %collective-permute-done.3.refs_1_, ...), custom_call_target="tpu_custom_call" | custom-call | tf_op jit(solution)/shard_map/grad/pallas_call | solution.py:225
  100.0 3.3 %grad.5 = (bf16[2,384,1024]{2,1,0:T(8,128)(2,1)S(1)}, bf16[2,384,1024]{2,1,0:T(8,128)(2,1)S(1)}) custom-call(s32[288]{0:T(512)S(1)} %tick.5.table, bf16[2,16,6144]{2,1,0:T(8,128)(2,1)S(1)} %pad_maximum_fusion.refs_0_, bf16[2,16,6144]{2,1,0:T(8,128)(2,1)S(1)} %collective-permute-done.3.refs_1_, ...), custom_call_target="tpu_custom_call" | custom-call | tf_op jit(solution)/shard_map/grad/pallas_call | solution.py:225
  103.3 1.5 %total.3 = (bf16[384,3072]{1,0:T(8,128)(2,1)}, bf16[384,3072]{1,0:T(8,128)(2,1)}) custom-call(bf16[2,384,1024]{2,1,0:T(8,128)(2,1)S(1)} %get-tuple-element.214.own_ref, bf16[2,384,1024]{2,1,0:T(8,128)(2,1)S(1)} %collective-permute-done.29.got_ref), custom_call_target="tpu_custom_call" | custom-call | tf_op jit(solution)/shard_map/total/pallas_call | solution.py:250
  104.8 1.5 %total.4 = (bf16[384,3072]{1,0:T(8,128)(2,1)}, bf16[384,3072]{1,0:T(8,128)(2,1)}) custom-call(bf16[2,384,1024]{2,1,0:T(8,128)(2,1)S(1)} %get-tuple-element.212.own_ref, bf16[2,384,1024]{2,1,0:T(8,128)(2,1)S(1)} %collective-permute-done.28.got_ref, bf16[384,3072]{1,0:T(8,128)(2,1)} %get-tuple-element.216.refs_0_, ...), custom_call_target="tpu_custom_call", output_to_operand_aliasing={{0}: (2, {}), {1}: (3, {})} | custom-call | tf_op jit(solution)/shard_map/total/pallas_call | solution.py:250
  106.7 1.5 %total.5 = (bf16[384,3072]{1,0:T(8,128)(2,1)}, bf16[384,3072]{1,0:T(8,128)(2,1)}) custom-call(bf16[2,384,1024]{2,1,0:T(8,128)(2,1)S(1)} %get-tuple-element.210.own_ref, bf16[2,384,1024]{2,1,0:T(8,128)(2,1)S(1)} %collective-permute-done.27.got_ref, bf16[384,3072]{1,0:T(8,128)(2,1)} %get-tuple-element.218.refs_0_, ...), custom_call_target="tpu_custom_call", output_to_operand_aliasing={{0}: (2, {}), {1}: (3, {})} | custom-call | tf_op jit(solution)/shard_map/total/pallas_call | solution.py:250
  (54 shorter events, 21.2 us)
Async XLA Ops:
  0.6 8.8 %collective-permute-start = (bf16[384,3072]{1,0:T(8,128)(2,1)}, bf16[384,3072]{1,0:T(8,128)(2,1)}, u32[]{:S(2)}, u32[]{:S(2)}) collective-permute-start(bf16[384,3072]{1,0:T(8,128)(2,1)} %refs_0_.1), channel_id=1, source_target_pairs={{0,8},{8,0},{16,24},{24,16},{1,9},{9,1},{17,25},{25,17},{2,10},{10... | collective-permute-start | bytes 7077896 | tf_op jit(solution)/shard_map/ppermute | solution.py:274
  1.1 11.0 %collective-permute-start.1 = (bf16[384,3072]{1,0:T(8,128)(2,1)}, bf16[384,3072]{1,0:T(8,128)(2,1)}, u32[]{:S(2)}, u32[]{:S(2)}) collective-permute-start(bf16[384,3072]{1,0:T(8,128)(2,1)} %refs_1_.1), channel_id=1, source_target_pairs={{0,8},{8,0},{16,24},{24,16},{1,9},{9,1},{17,25},{25,17},{2,10},{10... | collective-permute-start | bytes 7077896 | tf_op jit(solution)/shard_map/ppermute | solution.py:274
  2.3 15.2 %collective-permute-start.2 = (bf16[2,16,6144]{2,1,0:T(8,128)(2,1)S(1)}, bf16[2,16,6144]{2,1,0:T(8,128)(2,1)S(1)}, u32[]{:S(2)}, u32[]{:S(2)}) collective-permute-start(bf16[2,16,6144]{2,1,0:T(8,128)(2,1)S(1)} %pad_maximum_fusion.refs_0_), channel_id=1, source_target_pairs={{0,16},{8,24},{16,0},{24,8},{1,17},{9,25},{17,1},{25,9},{2,18},{10... | collective-permute-start | bytes 1179656 | tf_op jit(solution)/shard_map/ppermute | solution.py:271
  5.3 12.2 %collective-permute-start.3 = (bf16[2,16,6144]{2,1,0:T(8,128)(2,1)S(1)}, bf16[2,16,6144]{2,1,0:T(8,128)(2,1)S(1)}, u32[]{:S(2)}, u32[]{:S(2)}) collective-permute-start(bf16[2,16,6144]{2,1,0:T(8,128)(2,1)S(1)} %pad_maximum_fusion.refs_0_), channel_id=1, source_target_pairs={{0,1},{1,0},{2,3},{3,2},{4,5},{5,4},{6,7},{7,6},{8,9},{9,8},{10,11... | collective-permute-start | bytes 1179656 | tf_op jit(solution)/shard_map/ppermute | solution.py:277
  6.8 19.2 %collective-permute-start.4 = (bf16[2,16,6144]{2,1,0:T(8,128)(2,1)S(1)}, bf16[2,16,6144]{2,1,0:T(8,128)(2,1)S(1)}, u32[]{:S(2)}, u32[]{:S(2)}) collective-permute-start(bf16[2,16,6144]{2,1,0:T(8,128)(2,1)S(1)} %pad_maximum_fusion.refs_0_), channel_id=1, source_target_pairs={{0,2},{1,3},{2,0},{3,1},{4,6},{5,7},{6,4},{7,5},{8,10},{9,11},{10,... | collective-permute-start | bytes 1179656 | tf_op jit(solution)/shard_map/ppermute | solution.py:280
  9.4 19.5 %collective-permute-start.5 = (bf16[2,16,6144]{2,1,0:T(8,128)(2,1)S(1)}, bf16[2,16,6144]{2,1,0:T(8,128)(2,1)S(1)}, u32[]{:S(2)}, u32[]{:S(2)}) collective-permute-start(bf16[2,16,6144]{2,1,0:T(8,128)(2,1)S(1)} %pad_maximum_fusion.refs_0_), channel_id=1, source_target_pairs={{0,4},{1,5},{2,6},{3,7},{4,0},{5,1},{6,2},{7,3},{8,12},{9,13},{10,... | collective-permute-start | bytes 1179656 | tf_op jit(solution)/shard_map/ppermute | solution.py:283
  17.5 11.9 %collective-permute-start.6 = (bf16[2,16,6144]{2,1,0:T(8,128)(2,1)S(1)}, bf16[2,16,6144]{2,1,0:T(8,128)(2,1)S(1)}, u32[]{:S(2)}, u32[]{:S(2)}) collective-permute-start(bf16[2,16,6144]{2,1,0:T(8,128)(2,1)S(1)} %collective-permute-done.2.refs_0_.refs_2_), channel_id=1, source_target_pairs={{0,1},{1,0},{2,3},{3,2},{4,5},{5,4},{6,7},{7,6},{8,9},{9,8},{10,11... | collective-permute-start | bytes 1179656 | tf_op jit(solution)/shard_map/ppermute | solution.py:277
  18.1 16.2 %collective-permute-start.7 = (bf16[2,16,6144]{2,1,0:T(8,128)(2,1)S(1)}, bf16[2,16,6144]{2,1,0:T(8,128)(2,1)S(1)}, u32[]{:S(2)}, u32[]{:S(2)}) collective-permute-start(bf16[2,16,6144]{2,1,0:T(8,128)(2,1)S(1)} %collective-permute-done.2.refs_0_.refs_2_), channel_id=1, source_target_pairs={{0,2},{1,3},{2,0},{3,1},{4,6},{5,7},{6,4},{7,5},{8,10},{9,11},{10,... | collective-permute-start | bytes 1179656 | tf_op jit(solution)/shard_map/ppermute | solution.py:280
  22.8 13.5 %collective-permute-start.8 = (bf16[2,32,3072]{2,1,0:T(8,128)(2,1)S(1)}, bf16[2,32,3072]{2,1,0:T(8,128)(2,1)S(1)}, u32[]{:S(2)}, u32[]{:S(2)}) collective-permute-start(bf16[2,32,3072]{2,1,0:T(8,128)(2,1)S(1)} %get-tuple-element.125), channel_id=1, source_target_pairs={{0,16},{8,24},{16,0},{24,8},{1,17},{9,25},{17,1},{25,9},{2,18},{10... | collective-permute-start | bytes 1179656 | tf_op jit(solution)/shard_map/ppermute | solution.py:271
  28.9 10.1 %collective-permute-start.9 = (bf16[2,16,6144]{2,1,0:T(8,128)(2,1)S(1)}, bf16[2,16,6144]{2,1,0:T(8,128)(2,1)S(1)}, u32[]{:S(2)}, u32[]{:S(2)}) collective-permute-start(bf16[2,16,6144]{2,1,0:T(8,128)(2,1)S(1)} %collective-permute-done.4.refs_0_.refs_4_), channel_id=1, source_target_pairs={{0,1},{1,0},{2,3},{3,2},{4,5},{5,4},{6,7},{7,6},{8,9},{9,8},{10,11... | collective-permute-start | bytes 1179656 | tf_op jit(solution)/shard_map/ppermute | solution.py:277
  33.1 10.6 %collective-permute-start.10 = (bf16[2,32,3072]{2,1,0:T(8,128)(2,1)S(1)}, bf16[2,32,3072]{2,1,0:T(8,128)(2,1)S(1)}, u32[]{:S(2)}, u32[]{:S(2)}) collective-permute-start(bf16[2,32,3072]{2,1,0:T(8,128)(2,1)S(1)} %get-tuple-element.133), channel_id=1, source_target_pairs={{0,16},{8,24},{16,0},{24,8},{1,17},{9,25},{17,1},{25,9},{2,18},{10... | collective-permute-start | bytes 1179656 | tf_op jit(solution)/shard_map/ppermute | solution.py:271
  34.3 12.1 %collective-permute-start.11 = (bf16[2,16,6144]{2,1,0:T(8,128)(2,1)S(1)}, bf16[2,16,6144]{2,1,0:T(8,128)(2,1)S(1)}, u32[]{:S(2)}, u32[]{:S(2)}) collective-permute-start(bf16[2,16,6144]{2,1,0:T(8,128)(2,1)S(1)} %collective-permute-done.7.refs_0_.refs_6_), channel_id=1, source_target_pairs={{0,1},{1,0},{2,3},{3,2},{4,5},{5,4},{6,7},{7,6},{8,9},{9,8},{10,11... | collective-permute-start | bytes 1179656 | tf_op jit(solution)/shard_map/ppermute | solution.py:277
  35.2 17.2 %collective-permute-start.12 = (bf16[2,16,6144]{2,1,0:T(8,128)(2,1)S(1)}, bf16[2,16,6144]{2,1,0:T(8,128)(2,1)S(1)}, u32[]{:S(2)}, u32[]{:S(2)}) collective-permute-start(bf16[2,16,6144]{2,1,0:T(8,128)(2,1)S(1)} %collective-permute-done.5.refs_0_.refs_10_), channel_id=1, source_target_pairs={{0,2},{1,3},{2,0},{3,1},{4,6},{5,7},{6,4},{7,5},{8,10},{9,11},{10,... | collective-permute-start | bytes 1179656 | tf_op jit(solution)/shard_map/ppermute | solution.py:280
  36.3 18.5 %collective-permute-start.13 = (bf16[2,16,6144]{2,1,0:T(8,128)(2,1)S(1)}, bf16[2,16,6144]{2,1,0:T(8,128)(2,1)S(1)}, u32[]{:S(2)}, u32[]{:S(2)}) collective-permute-start(bf16[2,16,6144]{2,1,0:T(8,128)(2,1)S(1)} %collective-permute-done.2.refs_0_.refs_2_), channel_id=1, source_target_pairs={{0,4},{1,5},{2,6},{3,7},{4,0},{5,1},{6,2},{7,3},{8,12},{9,13},{10,... | collective-permute-start | bytes 1179656 | tf_op jit(solution)/shard_map/ppermute | solution.py:283
  42.6 12.9 %collective-permute-start.15 = (bf16[2,32,3072]{2,1,0:T(8,128)(2,1)S(1)}, bf16[2,32,3072]{2,1,0:T(8,128)(2,1)S(1)}, u32[]{:S(2)}, u32[]{:S(2)}) collective-permute-start(bf16[2,32,3072]{2,1,0:T(8,128)(2,1)S(1)} %get-tuple-element.146), channel_id=1, source_target_pairs={{0,16},{8,24},{16,0},{24,8},{1,17},{9,25},{17,1},{25,9},{2,18},{10... | collective-permute-start | bytes 1179656 | tf_op jit(solution)/shard_map/ppermute | solution.py:271
  43.7 13.1 %collective-permute-start.14 = (bf16[2,16,6144]{2,1,0:T(8,128)(2,1)S(1)}, bf16[2,16,6144]{2,1,0:T(8,128)(2,1)S(1)}, u32[]{:S(2)}, u32[]{:S(2)}) collective-permute-start(bf16[2,16,6144]{2,1,0:T(8,128)(2,1)S(1)} %collective-permute-done.5.refs_0_.refs_10_), channel_id=1, source_target_pairs={{0,1},{1,0},{2,3},{3,2},{4,5},{5,4},{6,7},{7,6},{8,9},{9,8},{10,11... | collective-permute-start | bytes 1179656 | tf_op jit(solution)/shard_map/ppermute | solution.py:277
  52.3 12.1 %collective-permute-start.16 = (bf16[2,16,6144]{2,1,0:T(8,128)(2,1)S(1)}, bf16[2,16,6144]{2,1,0:T(8,128)(2,1)S(1)}, u32[]{:S(2)}, u32[]{:S(2)}) collective-permute-start(bf16[2,16,6144]{2,1,0:T(8,128)(2,1)S(1)} %collective-permute-done.12.refs_0_.refs_12_), channel_id=1, source_target_pairs={{0,1},{1,0},{2,3},{3,2},{4,5},{5,4},{6,7},{7,6},{8,9},{9,8},{10,11... | collective-permute-start | bytes 1179656 | tf_op jit(solution)/shard_map/ppermute | solution.py:277
  53.8 10.6 %collective-permute-start.17 = (bf16[2,32,3072]{2,1,0:T(8,128)(2,1)S(1)}, bf16[2,32,3072]{2,1,0:T(8,128)(2,1)S(1)}, u32[]{:S(2)}, u32[]{:S(2)}) collective-permute-start(bf16[2,32,3072]{2,1,0:T(8,128)(2,1)S(1)} %get-tuple-element.152), channel_id=1, source_target_pairs={{0,16},{8,24},{16,0},{24,8},{1,17},{9,25},{17,1},{25,9},{2,18},{10... | collective-permute-start | bytes 1179656 | tf_op jit(solution)/shard_map/ppermute | solution.py:271
  54.9 13.2 %collective-permute-start.18 = (bf16[2,16,6144]{2,1,0:T(8,128)(2,1)S(1)}, bf16[2,16,6144]{2,1,0:T(8,128)(2,1)S(1)}, u32[]{:S(2)}, u32[]{:S(2)}) collective-permute-start(bf16[2,16,6144]{2,1,0:T(8,128)(2,1)S(1)} %collective-permute-done.13.refs_0_.refs_8_), channel_id=1, source_target_pairs={{0,2},{1,3},{2,0},{3,1},{4,6},{5,7},{6,4},{7,5},{8,10},{9,11},{10,... | collective-permute-start | bytes 1179656 | tf_op jit(solution)/shard_map/ppermute | solution.py:280
  55.5 17.3 %collective-permute-start.19 = (bf16[2,16,6144]{2,1,0:T(8,128)(2,1)S(1)}, bf16[2,16,6144]{2,1,0:T(8,128)(2,1)S(1)}, u32[]{:S(2)}, u32[]{:S(2)}) collective-permute-start(bf16[2,16,6144]{2,1,0:T(8,128)(2,1)S(1)} %collective-permute-done.13.refs_0_.refs_8_), channel_id=1, source_target_pairs={{0,1},{1,0},{2,3},{3,2},{4,5},{5,4},{6,7},{7,6},{8,9},{9,8},{10,11... | collective-permute-start | bytes 1179656 | tf_op jit(solution)/shard_map/ppermute | solution.py:277
  60.4 12.4 %collective-permute-start.20 = (bf16[2,32,3072]{2,1,0:T(8,128)(2,1)S(1)}, bf16[2,32,3072]{2,1,0:T(8,128)(2,1)S(1)}, u32[]{:S(2)}, u32[]{:S(2)}) collective-permute-start(bf16[2,32,3072]{2,1,0:T(8,128)(2,1)S(1)} %get-tuple-element.159), channel_id=1, source_target_pairs={{0,16},{8,24},{16,0},{24,8},{1,17},{9,25},{17,1},{25,9},{2,18},{10... | collective-permute-start | bytes 1179656 | tf_op jit(solution)/shard_map/ppermute | solution.py:271
  68.0 11.7 %collective-permute-start.21 = (bf16[2,16,6144]{2,1,0:T(8,128)(2,1)S(1)}, bf16[2,16,6144]{2,1,0:T(8,128)(2,1)S(1)}, u32[]{:S(2)}, u32[]{:S(2)}) collective-permute-start(bf16[2,16,6144]{2,1,0:T(8,128)(2,1)S(1)} %collective-permute-done.18.refs_0_.refs_14_), channel_id=1, source_target_pairs={{0,1},{1,0},{2,3},{3,2},{4,5},{5,4},{6,7},{7,6},{8,9},{9,8},{10,11... | collective-permute-start | bytes 1179656 | tf_op jit(solution)/shard_map/ppermute | solution.py:277
  69.5 13.0 %collective-permute-start.22 = (bf16[2,32,3072]{2,1,0:T(8,128)(2,1)S(1)}, bf16[2,32,3072]{2,1,0:T(8,128)(2,1)S(1)}, u32[]{:S(2)}, u32[]{:S(2)}) collective-permute-start(bf16[2,32,3072]{2,1,0:T(8,128)(2,1)S(1)} %get-tuple-element.181), channel_id=1, source_target_pairs={{0,16},{8,24},{16,0},{24,8},{1,17},{9,25},{17,1},{25,9},{2,18},{10... | collective-permute-start | bytes 1179656 | tf_op jit(solution)/shard_map/ppermute | solution.py:271
  76.4 16.3 %collective-permute-start.24 = (bf16[2,32,3072]{2,1,0:T(8,128)(2,1)S(1)}, bf16[2,32,3072]{2,1,0:T(8,128)(2,1)S(1)}, u32[]{:S(2)}, u32[]{:S(2)}) collective-permute-start(bf16[2,32,3072]{2,1,0:T(8,128)(2,1)S(1)} %get-tuple-element.189), channel_id=1, source_target_pairs={{0,16},{8,24},{16,0},{24,8},{1,17},{9,25},{17,1},{25,9},{2,18},{10... | collective-permute-start | bytes 1179656 | tf_op jit(solution)/shard_map/ppermute | solution.py:271
  81.3 11.5 %collective-permute-start.23 = (bf16[2,32,1024]{2,1,0:T(8,128)(2,1)S(1)}, bf16[2,32,1024]{2,1,0:T(8,128)(2,1)S(1)}, u32[]{:S(2)}, u32[]{:S(2)}) collective-permute-start(bf16[2,32,1024]{2,1,0:T(8,128)(2,1)S(1)} %get-tuple-element.187), channel_id=1, source_target_pairs={{0,16},{8,24},{16,0},{24,8},{1,17},{9,25},{17,1},{25,9},{2,18},{10... | collective-permute-start | bytes 393224 | tf_op jit(solution)/shard_map/ppermute | solution.py:271
  84.1 11.9 %collective-permute-start.25 = (bf16[2,32,1024]{2,1,0:T(8,128)(2,1)S(1)}, bf16[2,32,1024]{2,1,0:T(8,128)(2,1)S(1)}, u32[]{:S(2)}, u32[]{:S(2)}) collective-permute-start(bf16[2,32,1024]{2,1,0:T(8,128)(2,1)S(1)} %get-tuple-element.200), channel_id=1, source_target_pairs={{0,16},{8,24},{16,0},{24,8},{1,17},{9,25},{17,1},{25,9},{2,18},{10... | collective-permute-start | bytes 393224 | tf_op jit(solution)/shard_map/ppermute | solution.py:271
  86.7 12.7 %collective-permute-start.26 = (bf16[2,32,1024]{2,1,0:T(8,128)(2,1)S(1)}, bf16[2,32,1024]{2,1,0:T(8,128)(2,1)S(1)}, u32[]{:S(2)}, u32[]{:S(2)}) collective-permute-start(bf16[2,32,1024]{2,1,0:T(8,128)(2,1)S(1)} %get-tuple-element.206), channel_id=1, source_target_pairs={{0,16},{8,24},{16,0},{24,8},{1,17},{9,25},{17,1},{25,9},{2,18},{10... | collective-permute-start | bytes 393224 | tf_op jit(solution)/shard_map/ppermute | solution.py:271
  96.0 7.3 %collective-permute-start.29 = (bf16[2,384,1024]{2,1,0:T(8,128)(2,1)S(1)}, bf16[2,384,1024]{2,1,0:T(8,128)(2,1)S(1)}, u32[]{:S(2)}, u32[]{:S(2)}) collective-permute-start(bf16[2,384,1024]{2,1,0:T(8,128)(2,1)S(1)} %get-tuple-element.215), channel_id=1, source_target_pairs={{0,8},{8,0},{16,24},{24,16},{1,9},{9,1},{17,25},{25,17},{2,10},{10... | collective-permute-start | bytes 4718600 | tf_op jit(solution)/shard_map/ppermute | solution.py:274
  99.4 5.4 %collective-permute-start.28 = (bf16[2,384,1024]{2,1,0:T(8,128)(2,1)S(1)}, bf16[2,384,1024]{2,1,0:T(8,128)(2,1)S(1)}, u32[]{:S(2)}, u32[]{:S(2)}) collective-permute-start(bf16[2,384,1024]{2,1,0:T(8,128)(2,1)S(1)} %get-tuple-element.213), channel_id=1, source_target_pairs={{0,8},{8,0},{16,24},{24,16},{1,9},{9,1},{17,25},{25,17},{2,10},{10... | collective-permute-start | bytes 4718600 | tf_op jit(solution)/shard_map/ppermute | solution.py:274
  103.2 3.5 %collective-permute-start.27 = (bf16[2,384,1024]{2,1,0:T(8,128)(2,1)S(1)}, bf16[2,384,1024]{2,1,0:T(8,128)(2,1)S(1)}, u32[]{:S(2)}, u32[]{:S(2)}) collective-permute-start(bf16[2,384,1024]{2,1,0:T(8,128)(2,1)S(1)} %get-tuple-element.211), channel_id=1, source_target_pairs={{0,8},{8,0},{16,24},{24,16},{1,9},{9,1},{17,25},{25,17},{2,10},{10... | collective-permute-start | bytes 4718600 | tf_op jit(solution)/shard_map/ppermute | solution.py:274

commit v7 on v6

--- a/solution.py
+++ b/solution.py
@@ -13,14 +13,14 @@
 ROWS = 4
 COLS = 8
 LANES = 4
+GRAD_LANES = 8
 SCALE = 0.7978845608028654
 CUBIC = 0.044715
 PARTIAL_VMEM = 8 * 1024 * 1024
-GRAD_VMEM = 16 * 1024 * 1024
-TOTAL_VMEM = 8 * 1024 * 1024
-PACK_ROWS = 64
+GRAD_VMEM = 20 * 1024 * 1024
+TOTAL_VMEM = 14 * 1024 * 1024
 TICK_VMEM = 1024 * 1024
-PACK_VMEM = 12 * 1024 * 1024
+PACK_VMEM = 1024 * 1024
 PARTS = ((0, 2), (2, 2), (4, 2))
 EARLY_VMEM = 8 * 1024 * 1024
 COST = pl.CostEstimate(flops=0, bytes_accessed=0, transcendentals=0)
@@ -84,18 +84,23 @@
 
 
 def pack_kernel(*refs):
-    for index, ref in enumerate(refs[:-1]):
-        refs[-1][index] = ref[...]
+    sources, packed, sems = refs[:-2], refs[-2], refs[-1]
+    copies = [pltpu.make_async_copy(ref, packed.at[i], sems.at[i]) for i, ref in enumerate(sources)]
+    for copy in copies:
+        copy.start()
+    for copy in copies:
+        copy.wait()
 
 
 def pack(*weights):
     kept, width = weights[0].shape
+    anywhere = pl.BlockSpec(memory_space=pl.ANY)
     return pl.pallas_call(
         pack_kernel,
-        grid=(kept // PACK_ROWS,),
-        in_specs=[pl.BlockSpec((PACK_ROWS, width), lambda g: (g, 0))] * len(weights),
-        out_specs=pl.BlockSpec((len(weights), PACK_ROWS, width), lambda g: (0, g, 0)),
+        in_specs=[anywhere] * len(weights),
+        out_specs=anywhere,
         out_shape=jax.ShapeDtypeStruct((len(weights), kept, width), weights[0].dtype),
+        scratch_shapes=[pltpu.SemaphoreType.DMA((len(weights),))],
         compiler_params=pltpu.CompilerParams(vmem_limit_bytes=PACK_VMEM),
         cost_estimate=COST,
         name="pack",
@@ -202,11 +207,11 @@
     own_ref, away_ref = refs[n_buf + 1 + 2 * n_late :]
     step = pl.program_id(0)
     kept = slots * BLK // 2
-    for lane in range(LANES):
+    for lane in range(GRAD_LANES):
         at = slice(lane * BLK, (lane + 1) * BLK)
         for side, late in enumerate(activations(keeps, gots, at)):
             right = jnp.concatenate((done[side, :, at], late), axis=0)
-            left = picked_rows(table, buffers, side, base + step * LANES + lane, slots)
+            left = picked_rows(table, buffers, side, base + step * GRAD_LANES + lane, slots)
             total = lax.dot_general(left, right, (((0,), (0,)), ((), ())), preferred_element_type=jnp.float32)
             total = total.astype(jnp.bfloat16)
             own_ref[side, :, at] = total[:kept]
@@ -215,10 +220,11 @@
 
 def grad(table, buffers, done, keeps, gots, kept, first, steps):
     width = done.shape[2]
-    wide = LANES * BLK
+    wide = GRAD_LANES * BLK
+    begin, steps = first * LANES // GRAD_LANES, steps * LANES // GRAD_LANES
 
     def spec(array):
-        start = first if array.shape[2] == width else 0
+        start = begin if array.shape[2] == width else 0
         return pl.BlockSpec((2, array.shape[1], wide), lambda g, t: (0, 0, start + g))
 
     out = pl.BlockSpec((2, kept, wide), lambda g, t: (0, 0, g))
@@ -244,9 +250,10 @@
 
 def total(own, got, before, first, width):
     kept, here = own.shape[1:]
-    wide = LANES * BLK
+    wide = GRAD_LANES * BLK
+    begin = first * LANES // GRAD_LANES
     source = pl.BlockSpec((2, kept, wide), lambda g: (0, 0, g))
-    out = pl.BlockSpec((kept, wide), lambda g: (0, first + g))
+    out = pl.BlockSpec((kept, wide), lambda g: (0, begin + g))
     return pl.pallas_call(
         total_kernel,
         grid=(here // wide,),
@@ -373,7 +380,8 @@
     def per_device(inputs, cotangent, w_in, w_out, keep_in, keep_out):
         kept, width = w_in.shape
         fits = kept % BLK == 0 and inputs.shape[0] % 16 == 0
-        fits = fits and kept % PACK_ROWS == 0 and width == sum(steps for _, steps in PARTS) * LANES * BLK
+        fits = fits and all(v * LANES % GRAD_LANES == 0 for part in PARTS for v in part)
+        fits = fits and width == sum(steps for _, steps in PARTS) * LANES * BLK
         chosen = fast if fits and mesh.shape["row"] == ROWS and mesh.shape["col"] == COLS else general
         return chosen(inputs, cotangent, w_in, w_out, keep_in, keep_out)
 

time: 109 us -> 107 us (0.982)
  Pallas kernels: 52 us -> 48.4 us
    pallas_call x3, Pallas kernels: 9.81 us -> 7.92 us  [grad(): pl.pallas_call(functools.partial(grad_kernel, len(buffers), len(keeps), 2...]
    pallas_call x1, Pallas kernels: 5.39 us -> 3.8 us  [pack(): pl.pallas_call(pack_kernel, in_specs=[anywhere] * len(weights), out_specs...]
  transfers between devices with their start and end apart: 30 -> 30, of which waited for: 9 -> 10; matrix products, arithmetic and copies ran while one was open for 2% -> 2% of each run, Pallas kernels for 47% -> 44%
where the time goes in v7:
time: 107 us; the launch traced here: 106 us
  Pallas kernels  48.4 us (45%)
  starting transfers between devices  33.8 us (32%)
  waiting for transfers between devices  21 us (20%)
  other arithmetic  1.07 us (1%)
    pallas_call x10, Pallas kernels, partial(): pl.pallas_call(functools.partial(partial_kernel, len(buffers), 2 * kept /...  30.1 us
    ppermute x11, starting transfers between devices, swap_x(): return lax.ppermute(v, 'row', [(r, r ^ 2) for r in range(ROWS)])  12.1 us
    ppermute x8, starting transfers between devices, swap_y(): return lax.ppermute(v, 'col', [(c, c ^ 1) for c in range(COLS)])  10.1 us
    pallas_call x3, Pallas kernels, grad(): pl.pallas_call(functools.partial(grad_kernel, len(buffers), len(keeps), 2...  7.92 us
    ppermute x8, waiting for transfers between devices, swap_y(): return lax.ppermute(v, 'col', [(c, c ^ 1) for c in range(COLS)])  7.46 us
    ppermute x2, starting transfers between devices, far(): return lax.ppermute(v, 'col', [(c, c ^ 4) for c in range(COLS)])  5.36 us
    ppermute x4, starting transfers between devices, near(): return lax.ppermute(v, 'col', [(c, c ^ 2) for c in range(COLS)])  4.97 us
    ppermute x4, waiting for transfers between devices, near(): return lax.ppermute(v, 'col', [(c, c ^ 2) for c in range(COLS)])  4.93 us
  transfers between devices with their start and end apart: 30, of which 10 were waited for; matrix products, arithmetic and copies ran while one was open for 2% of the time, Pallas kernels for 44%

profile of v7, /device:TPU:0, one launch (start us, length us, event | category | flops | bytes accessed | tf_op | source)
XLA Modules:
  0.0 106.2 jit_solution(9538226487882695767)
XLA Ops:
  2.3 3.0 %collective-permute-start.2 = (bf16[2,16,6144]{2,1,0:T(8,128)(2,1)S(1)}, bf16[2,16,6144]{2,1,0:T(8,128)(2,1)S(1)}, u32[]{:S(2)}, u32[]{:S(2)}) collective-permute-start(bf16[2,16,6144]{2,1,0:T(8,128)(2,1)S(1)} %pad_maximum_fusion.refs_0_), channel_id=1, source_target_pairs={{0,16},{8,24},{16,0},{24,8},{1,17},{9,25},{17,1},{25,9},{2,18},{10... | collective-permute-start | bytes 1179656 | tf_op jit(solution)/shard_map/ppermute | solution.py:278
  5.3 1.5 %collective-permute-start.3 = (bf16[2,16,6144]{2,1,0:T(8,128)(2,1)S(1)}, bf16[2,16,6144]{2,1,0:T(8,128)(2,1)S(1)}, u32[]{:S(2)}, u32[]{:S(2)}) collective-permute-start(bf16[2,16,6144]{2,1,0:T(8,128)(2,1)S(1)} %pad_maximum_fusion.refs_0_), channel_id=1, source_target_pairs={{0,1},{1,0},{2,3},{3,2},{4,5},{5,4},{6,7},{7,6},{8,9},{9,8},{10,11... | collective-permute-start | bytes 1179656 | tf_op jit(solution)/shard_map/ppermute | solution.py:284
  6.8 1.6 %collective-permute-start.4 = (bf16[2,16,6144]{2,1,0:T(8,128)(2,1)S(1)}, bf16[2,16,6144]{2,1,0:T(8,128)(2,1)S(1)}, u32[]{:S(2)}, u32[]{:S(2)}) collective-permute-start(bf16[2,16,6144]{2,1,0:T(8,128)(2,1)S(1)} %pad_maximum_fusion.refs_0_), channel_id=1, source_target_pairs={{0,2},{1,3},{2,0},{3,1},{4,6},{5,7},{6,4},{7,5},{8,10},{9,11},{10,... | collective-permute-start | bytes 1179656 | tf_op jit(solution)/shard_map/ppermute | solution.py:287
  9.4 2.7 %collective-permute-start.5 = (bf16[2,16,6144]{2,1,0:T(8,128)(2,1)S(1)}, bf16[2,16,6144]{2,1,0:T(8,128)(2,1)S(1)}, u32[]{:S(2)}, u32[]{:S(2)}) collective-permute-start(bf16[2,16,6144]{2,1,0:T(8,128)(2,1)S(1)} %pad_maximum_fusion.refs_0_), channel_id=1, source_target_pairs={{0,4},{1,5},{2,6},{3,7},{4,0},{5,1},{6,2},{7,3},{8,12},{9,13},{10,... | collective-permute-start | bytes 1179656 | tf_op jit(solution)/shard_map/ppermute | solution.py:290
  12.1 3.8 %pack.1.refs_2_ = bf16[4,384,3072]{2,1,0:T(8,128)(2,1)S(1)} custom-call(bf16[384,3072]{1,0:T(8,128)(2,1)} %refs_0_.1, bf16[384,3072]{1,0:T(8,128)(2,1)} %refs_1_.1, bf16[384,3072]{1,0:T(8,128)(2,1)} %collective-permute-done.refs_2_, bf16[384,3072]{1,0:T(8,128)(2,1)} %collective-permute-done.1.refs_3_), custom_call_target="tpu_custom_call" | custom-call | tf_op jit(solution)/shard_map/pack/pallas_call | solution.py:98
  16.1 1.5 %collective-permute-start.6 = (bf16[2,16,6144]{2,1,0:T(8,128)(2,1)S(1)}, bf16[2,16,6144]{2,1,0:T(8,128)(2,1)S(1)}, u32[]{:S(2)}, u32[]{:S(2)}) collective-permute-start(bf16[2,16,6144]{2,1,0:T(8,128)(2,1)S(1)} %collective-permute-done.2.refs_0_.refs_2_), channel_id=1, source_target_pairs={{0,1},{1,0},{2,3},{3,2},{4,5},{5,4},{6,7},{7,6},{8,9},{9,8},{10,11... | collective-permute-start | bytes 1179656 | tf_op jit(solution)/shard_map/ppermute | solution.py:284
  17.6 1.6 %collective-permute-start.7 = (bf16[2,16,6144]{2,1,0:T(8,128)(2,1)S(1)}, bf16[2,16,6144]{2,1,0:T(8,128)(2,1)S(1)}, u32[]{:S(2)}, u32[]{:S(2)}) collective-permute-start(bf16[2,16,6144]{2,1,0:T(8,128)(2,1)S(1)} %collective-permute-done.2.refs_0_.refs_2_), channel_id=1, source_target_pairs={{0,2},{1,3},{2,0},{3,1},{4,6},{5,7},{6,4},{7,5},{8,10},{9,11},{10,... | collective-permute-start | bytes 1179656 | tf_op jit(solution)/shard_map/ppermute | solution.py:287
  19.2 3.6 %partial.10 = (f32[2,32,3072]{2,1,0:T(8,128)S(1)}, bf16[2,32,3072]{2,1,0:T(8,128)(2,1)S(1)}) custom-call(s32[288]{0:T(512)S(1)} %reshape.7.table.table_ref, bf16[2,16,6144]{2,1,0:T(8,128)(2,1)S(1)} %pad_maximum_fusion.refs_0_, bf16[2,16,6144]{2,1,0:T(8,128)(2,1)S(1)} %collective-permute-done.3.refs_1_, bf16[4,384,3072]{2,1,0:T(8,128)(2,1)S(1)} %pack.1.refs_2_), custom_call_target="tpu_custom_call" | custom-call | tf_op jit(solution)/shard_map/partial/pallas_call | solution.py:131
  23.4 2.6 %collective-permute-done.4.refs_0_.refs_4_ = bf16[2,16,6144]{2,1,0:T(8,128)(2,1)S(1)} collective-permute-done((bf16[2,16,6144]{2,1,0:T(8,128)(2,1)S(1)}, bf16[2,16,6144]{2,1,0:T(8,128)(2,1)S(1)}, u32[]{:S(2)}, u32[]{:S(2)}) %collective-permute-start.4) | collective-permute-done | bytes 393248 | tf_op jit(solution)/shard_map/ppermute | solution.py:287
  26.0 2.9 %collective-permute-done.5.refs_0_.refs_10_ = bf16[2,16,6144]{2,1,0:T(8,128)(2,1)S(1)} collective-permute-done((bf16[2,16,6144]{2,1,0:T(8,128)(2,1)S(1)}, bf16[2,16,6144]{2,1,0:T(8,128)(2,1)S(1)}, u32[]{:S(2)}, u32[]{:S(2)}) %collective-permute-start.5) | collective-permute-done | bytes 393248 | tf_op jit(solution)/shard_map/ppermute | solution.py:290
  29.5 3.6 %partial.11 = (f32[2,32,3072]{2,1,0:T(8,128)S(1)}, bf16[2,32,3072]{2,1,0:T(8,128)(2,1)S(1)}) custom-call(s32[288]{0:T(512)S(1)} %tick.4.table.table_ref, bf16[2,16,6144]{2,1,0:T(8,128)(2,1)S(1)} %collective-permute-done.2.refs_0_.refs_2_, bf16[2,16,6144]{2,1,0:T(8,128)(2,1)S(1)} %collective-permute-done.6.refs_1_.refs_3_, bf16[4,384,3072]{2,1,0:T(8,128)(2,1)S(1)} %pack.1.refs_2_), custom_call_target="tpu_custom_call" | custom-call | tf_op jit(solution)/shard_map/partial/pallas_call | solution.py:131
  36.3 2.7 %collective-permute-start.13 = (bf16[2,16,6144]{2,1,0:T(8,128)(2,1)S(1)}, bf16[2,16,6144]{2,1,0:T(8,128)(2,1)S(1)}, u32[]{:S(2)}, u32[]{:S(2)}) collective-permute-start(bf16[2,16,6144]{2,1,0:T(8,128)(2,1)S(1)} %collective-permute-done.2.refs_0_.refs_2_), channel_id=1, source_target_pairs={{0,4},{1,5},{2,6},{3,7},{4,0},{5,1},{6,2},{7,3},{8,12},{9,13},{10,... | collective-permute-start | bytes 1179656 | tf_op jit(solution)/shard_map/ppermute | solution.py:290
  39.0 3.6 %partial.12 = (f32[2,32,3072]{2,1,0:T(8,128)S(1)}, bf16[2,32,3072]{2,1,0:T(8,128)(2,1)S(1)}) custom-call(s32[288]{0:T(512)S(1)} %tick.4.table.table_ref, bf16[2,16,6144]{2,1,0:T(8,128)(2,1)S(1)} %collective-permute-done.4.refs_0_.refs_4_, bf16[2,16,6144]{2,1,0:T(8,128)(2,1)S(1)} %collective-permute-done.9.refs_1_.refs_5_, bf16[4,384,3072]{2,1,0:T(8,128)(2,1)S(1)} %pack.1.refs_2_), custom_call_target="tpu_custom_call" | custom-call | tf_op jit(solution)/shard_map/partial/pallas_call | solution.py:131
  43.7 1.7 %collective-permute-start.14 = (bf16[2,16,6144]{2,1,0:T(8,128)(2,1)S(1)}, bf16[2,16,6144]{2,1,0:T(8,128)(2,1)S(1)}, u32[]{:S(2)}, u32[]{:S(2)}) collective-permute-start(bf16[2,16,6144]{2,1,0:T(8,128)(2,1)S(1)} %collective-permute-done.5.refs_0_.refs_10_), channel_id=1, source_target_pairs={{0,1},{1,0},{2,3},{3,2},{4,5},{5,4},{6,7},{7,6},{8,9},{9,8},{10,11... | collective-permute-start | bytes 1179656 | tf_op jit(solution)/shard_map/ppermute | solution.py:284
  46.4 3.6 %partial.13 = (f32[2,32,3072]{2,1,0:T(8,128)S(1)}, bf16[2,32,3072]{2,1,0:T(8,128)(2,1)S(1)}) custom-call(s32[288]{0:T(512)S(1)} %tick.4.table.table_ref, bf16[2,16,6144]{2,1,0:T(8,128)(2,1)S(1)} %collective-permute-done.7.refs_0_.refs_6_, bf16[2,16,6144]{2,1,0:T(8,128)(2,1)S(1)} %collective-permute-done.11.refs_1_.refs_7_, bf16[4,384,3072]{2,1,0:T(8,128)(2,1)S(1)} %pack.1.refs_2_), custom_call_target="tpu_custom_call" | custom-call | tf_op jit(solution)/shard_map/partial/pallas_call | solution.py:131
  50.0 2.3 %collective-permute-done.12.refs_0_.refs_12_ = bf16[2,16,6144]{2,1,0:T(8,128)(2,1)S(1)} collective-permute-done((bf16[2,16,6144]{2,1,0:T(8,128)(2,1)S(1)}, bf16[2,16,6144]{2,1,0:T(8,128)(2,1)S(1)}, u32[]{:S(2)}, u32[]{:S(2)}) %collective-permute-start.12) | collective-permute-done | bytes 393248 | tf_op jit(solution)/shard_map/ppermute | solution.py:287
  56.7 3.6 %partial.14 = (f32[2,32,3072]{2,1,0:T(8,128)S(1)}, bf16[2,32,3072]{2,1,0:T(8,128)(2,1)S(1)}) custom-call(s32[288]{0:T(512)S(1)} %tick.5.table, bf16[2,16,6144]{2,1,0:T(8,128)(2,1)S(1)} %collective-permute-done.5.refs_0_.refs_10_, bf16[2,16,6144]{2,1,0:T(8,128)(2,1)S(1)} %collective-permute-done.14.refs_1_.refs_11_, bf16[4,384,3072]{2,1,0:T(8,128)(2,1)S(1)} %pack.1.refs_2_), custom_call_target="tpu_custom_call" | custom-call | tf_op jit(solution)/shard_map/partial/pallas_call | solution.py:131
  60.9 3.5 %collective-permute-done.16.refs_1_.refs_13_ = bf16[2,16,6144]{2,1,0:T(8,128)(2,1)S(1)} collective-permute-done((bf16[2,16,6144]{2,1,0:T(8,128)(2,1)S(1)}, bf16[2,16,6144]{2,1,0:T(8,128)(2,1)S(1)}, u32[]{:S(2)}, u32[]{:S(2)}) %collective-permute-start.16) | collective-permute-done | bytes 393248 | tf_op jit(solution)/shard_map/ppermute | solution.py:284
  64.4 3.6 %partial.15 = (f32[2,32,3072]{2,1,0:T(8,128)S(1)}, bf16[2,32,3072]{2,1,0:T(8,128)(2,1)S(1)}) custom-call(s32[288]{0:T(512)S(1)} %tick.5.table, bf16[2,16,6144]{2,1,0:T(8,128)(2,1)S(1)} %collective-permute-done.12.refs_0_.refs_12_, bf16[2,16,6144]{2,1,0:T(8,128)(2,1)S(1)} %collective-permute-done.16.refs_1_.refs_13_, bf16[4,384,3072]{2,1,0:T(8,128)(2,1)S(1)} %pack.1.refs_2_), custom_call_target="tpu_custom_call" | custom-call | tf_op jit(solution)/shard_map/partial/pallas_call | solution.py:131
  68.0 1.5 %collective-permute-start.21 = (bf16[2,16,6144]{2,1,0:T(8,128)(2,1)S(1)}, bf16[2,16,6144]{2,1,0:T(8,128)(2,1)S(1)}, u32[]{:S(2)}, u32[]{:S(2)}) collective-permute-start(bf16[2,16,6144]{2,1,0:T(8,128)(2,1)S(1)} %collective-permute-done.18.refs_0_.refs_14_), channel_id=1, source_target_pairs={{0,1},{1,0},{2,3},{3,2},{4,5},{5,4},{6,7},{7,6},{8,9},{9,8},{10,11... | collective-permute-start | bytes 1179656 | tf_op jit(solution)/shard_map/ppermute | solution.py:284
  70.1 2.7 %collective-permute-done.19.refs_1_.refs_9_ = bf16[2,16,6144]{2,1,0:T(8,128)(2,1)S(1)} collective-permute-done((bf16[2,16,6144]{2,1,0:T(8,128)(2,1)S(1)}, bf16[2,16,6144]{2,1,0:T(8,128)(2,1)S(1)}, u32[]{:S(2)}, u32[]{:S(2)}) %collective-permute-start.19) | collective-permute-done | bytes 393248 | tf_op jit(solution)/shard_map/ppermute | solution.py:284
  72.8 3.6 %partial.16 = (f32[2,32,3072]{2,1,0:T(8,128)S(1)}, bf16[2,32,3072]{2,1,0:T(8,128)(2,1)S(1)}) custom-call(s32[288]{0:T(512)S(1)} %tick.5.table, bf16[2,16,6144]{2,1,0:T(8,128)(2,1)S(1)} %collective-permute-done.13.refs_0_.refs_8_, bf16[2,16,6144]{2,1,0:T(8,128)(2,1)S(1)} %collective-permute-done.19.refs_1_.refs_9_, bf16[4,384,3072]{2,1,0:T(8,128)(2,1)S(1)} %pack.1.refs_2_), custom_call_target="tpu_custom_call" | custom-call | tf_op jit(solution)/shard_map/partial/pallas_call | solution.py:131
  77.4 2.3 %early.1.refs_16_ = bf16[2,160,3072]{2,1,0:T(8,128)(2,1)S(1)} custom-call(f32[2,32,3072]{2,1,0:T(8,128)S(1)} %get-tuple-element.164.refs_0_, f32[2,32,3072]{2,1,0:T(8,128)S(1)} %get-tuple-element.165.refs_1_, f32[2,32,3072]{2,1,0:T(8,128)S(1)} %get-tuple-element.166.refs_2_, f32[2,32,3072]{2,1,0:T(8,128)S(1)} %get-tuple-element.167.refs_3_, ...), custom_call_target="tpu_custom_call" | custom-call | tf_op jit(solution)/shard_map/early/pallas_call | solution.py:191
  79.7 1.6 %partial.17 = (f32[2,32,1024]{2,1,0:T(8,128)S(1)}, bf16[2,32,1024]{2,1,0:T(8,128)(2,1)S(1)}) custom-call(s32[288]{0:T(512)S(1)} %tick.5.table, bf16[2,16,6144]{2,1,0:T(8,128)(2,1)S(1)} %collective-permute-done.18.refs_0_.refs_14_, bf16[2,16,6144]{2,1,0:T(8,128)(2,1)S(1)} %collective-permute-done.21.refs_1_.refs_15_, bf16[4,384,3072]{2,1,0:T(8,128)(2,1)S(1)} %pack.1.refs_2_), custom_call_target="tpu_custom_call" | custom-call | tf_op jit(solution)/shard_map/partial/pallas_call | solution.py:131
  82.5 1.6 %partial.18 = (f32[2,32,1024]{2,1,0:T(8,128)S(1)}, bf16[2,32,1024]{2,1,0:T(8,128)(2,1)S(1)}) custom-call(s32[288]{0:T(512)S(1)} %tick.5.table, bf16[2,16,6144]{2,1,0:T(8,128)(2,1)S(1)} %collective-permute-done.18.refs_0_.refs_14_, bf16[2,16,6144]{2,1,0:T(8,128)(2,1)S(1)} %collective-permute-done.21.refs_1_.refs_15_, bf16[4,384,3072]{2,1,0:T(8,128)(2,1)S(1)} %pack.1.refs_2_), custom_call_target="tpu_custom_call" | custom-call | tf_op jit(solution)/shard_map/partial/pallas_call | solution.py:131
  85.0 1.8 %partial.19 = (f32[2,32,1024]{2,1,0:T(8,128)S(1)}, bf16[2,32,1024]{2,1,0:T(8,128)(2,1)S(1)}) custom-call(s32[288]{0:T(512)S(1)} %tick.5.table, bf16[2,16,6144]{2,1,0:T(8,128)(2,1)S(1)} %collective-permute-done.18.refs_0_.refs_14_, bf16[2,16,6144]{2,1,0:T(8,128)(2,1)S(1)} %collective-permute-done.21.refs_1_.refs_15_, bf16[4,384,3072]{2,1,0:T(8,128)(2,1)S(1)} %pack.1.refs_2_), custom_call_target="tpu_custom_call" | custom-call | tf_op jit(solution)/shard_map/partial/pallas_call | solution.py:131
  88.0 4.7 %collective-permute-done.23.refs_21_ = bf16[2,32,1024]{2,1,0:T(8,128)(2,1)S(1)} collective-permute-done((bf16[2,32,1024]{2,1,0:T(8,128)(2,1)S(1)}, bf16[2,32,1024]{2,1,0:T(8,128)(2,1)S(1)}, u32[]{:S(2)}, u32[]{:S(2)}) %collective-permute-start.23) | collective-permute-done | bytes 131104 | tf_op jit(solution)/shard_map/ppermute | solution.py:278
  92.8 2.6 %grad.3 = (bf16[2,384,1024]{2,1,0:T(8,128)(2,1)S(1)}, bf16[2,384,1024]{2,1,0:T(8,128)(2,1)S(1)}) custom-call(s32[288]{0:T(512)S(1)} %tick.5.table, bf16[2,16,6144]{2,1,0:T(8,128)(2,1)S(1)} %pad_maximum_fusion.refs_0_, bf16[2,16,6144]{2,1,0:T(8,128)(2,1)S(1)} %collective-permute-done.3.refs_1_, ...), custom_call_target="tpu_custom_call" | custom-call | tf_op jit(solution)/shard_map/grad/pallas_call | solution.py:231
  95.5 2.7 %grad.4 = (bf16[2,384,1024]{2,1,0:T(8,128)(2,1)S(1)}, bf16[2,384,1024]{2,1,0:T(8,128)(2,1)S(1)}) custom-call(s32[288]{0:T(512)S(1)} %tick.5.table, bf16[2,16,6144]{2,1,0:T(8,128)(2,1)S(1)} %pad_maximum_fusion.refs_0_, bf16[2,16,6144]{2,1,0:T(8,128)(2,1)S(1)} %collective-permute-done.3.refs_1_, ...), custom_call_target="tpu_custom_call" | custom-call | tf_op jit(solution)/shard_map/grad/pallas_call | solution.py:231
  98.7 2.6 %grad.5 = (bf16[2,384,1024]{2,1,0:T(8,128)(2,1)S(1)}, bf16[2,384,1024]{2,1,0:T(8,128)(2,1)S(1)}) custom-call(s32[288]{0:T(512)S(1)} %tick.5.table, bf16[2,16,6144]{2,1,0:T(8,128)(2,1)S(1)} %pad_maximum_fusion.refs_0_, bf16[2,16,6144]{2,1,0:T(8,128)(2,1)S(1)} %collective-permute-done.3.refs_1_, ...), custom_call_target="tpu_custom_call" | custom-call | tf_op jit(solution)/shard_map/grad/pallas_call | solution.py:231
  101.5 1.4 %total.3 = (bf16[384,3072]{1,0:T(8,128)(2,1)}, bf16[384,3072]{1,0:T(8,128)(2,1)}) custom-call(bf16[2,384,1024]{2,1,0:T(8,128)(2,1)S(1)} %get-tuple-element.214.own_ref, bf16[2,384,1024]{2,1,0:T(8,128)(2,1)S(1)} %collective-permute-done.29.got_ref), custom_call_target="tpu_custom_call" | custom-call | tf_op jit(solution)/shard_map/total/pallas_call | solution.py:257
  102.9 1.4 %total.4 = (bf16[384,3072]{1,0:T(8,128)(2,1)}, bf16[384,3072]{1,0:T(8,128)(2,1)}) custom-call(bf16[2,384,1024]{2,1,0:T(8,128)(2,1)S(1)} %get-tuple-element.212.own_ref, bf16[2,384,1024]{2,1,0:T(8,128)(2,1)S(1)} %collective-permute-done.28.got_ref, bf16[384,3072]{1,0:T(8,128)(2,1)} %get-tuple-element.216.refs_0_, ...), custom_call_target="tpu_custom_call", output_to_operand_aliasing={{0}: (2, {}), {1}: (3, {})} | custom-call | tf_op jit(solution)/shard_map/total/pallas_call | solution.py:257
  (54 shorter events, 22.0 us)
Async XLA Ops:
  0.6 8.8 %collective-permute-start = (bf16[384,3072]{1,0:T(8,128)(2,1)}, bf16[384,3072]{1,0:T(8,128)(2,1)}, u32[]{:S(2)}, u32[]{:S(2)}) collective-permute-start(bf16[384,3072]{1,0:T(8,128)(2,1)} %refs_0_.1), channel_id=1, source_target_pairs={{0,8},{8,0},{16,24},{24,16},{1,9},{9,1},{17,25},{25,17},{2,10},{10... | collective-permute-start | bytes 7077896 | tf_op jit(solution)/shard_map/ppermute | solution.py:281
  1.1 11.0 %collective-permute-start.1 = (bf16[384,3072]{1,0:T(8,128)(2,1)}, bf16[384,3072]{1,0:T(8,128)(2,1)}, u32[]{:S(2)}, u32[]{:S(2)}) collective-permute-start(bf16[384,3072]{1,0:T(8,128)(2,1)} %refs_1_.1), channel_id=1, source_target_pairs={{0,8},{8,0},{16,24},{24,16},{1,9},{9,1},{17,25},{25,17},{2,10},{10... | collective-permute-start | bytes 7077896 | tf_op jit(solution)/shard_map/ppermute | solution.py:281
  2.3 13.6 %collective-permute-start.2 = (bf16[2,16,6144]{2,1,0:T(8,128)(2,1)S(1)}, bf16[2,16,6144]{2,1,0:T(8,128)(2,1)S(1)}, u32[]{:S(2)}, u32[]{:S(2)}) collective-permute-start(bf16[2,16,6144]{2,1,0:T(8,128)(2,1)S(1)} %pad_maximum_fusion.refs_0_), channel_id=1, source_target_pairs={{0,16},{8,24},{16,0},{24,8},{1,17},{9,25},{17,1},{25,9},{2,18},{10... | collective-permute-start | bytes 1179656 | tf_op jit(solution)/shard_map/ppermute | solution.py:278
  5.3 10.8 %collective-permute-start.3 = (bf16[2,16,6144]{2,1,0:T(8,128)(2,1)S(1)}, bf16[2,16,6144]{2,1,0:T(8,128)(2,1)S(1)}, u32[]{:S(2)}, u32[]{:S(2)}) collective-permute-start(bf16[2,16,6144]{2,1,0:T(8,128)(2,1)S(1)} %pad_maximum_fusion.refs_0_), channel_id=1, source_target_pairs={{0,1},{1,0},{2,3},{3,2},{4,5},{5,4},{6,7},{7,6},{8,9},{9,8},{10,11... | collective-permute-start | bytes 1179656 | tf_op jit(solution)/shard_map/ppermute | solution.py:284
  6.8 19.2 %collective-permute-start.4 = (bf16[2,16,6144]{2,1,0:T(8,128)(2,1)S(1)}, bf16[2,16,6144]{2,1,0:T(8,128)(2,1)S(1)}, u32[]{:S(2)}, u32[]{:S(2)}) collective-permute-start(bf16[2,16,6144]{2,1,0:T(8,128)(2,1)S(1)} %pad_maximum_fusion.refs_0_), channel_id=1, source_target_pairs={{0,2},{1,3},{2,0},{3,1},{4,6},{5,7},{6,4},{7,5},{8,10},{9,11},{10,... | collective-permute-start | bytes 1179656 | tf_op jit(solution)/shard_map/ppermute | solution.py:287
  9.4 19.5 %collective-permute-start.5 = (bf16[2,16,6144]{2,1,0:T(8,128)(2,1)S(1)}, bf16[2,16,6144]{2,1,0:T(8,128)(2,1)S(1)}, u32[]{:S(2)}, u32[]{:S(2)}) collective-permute-start(bf16[2,16,6144]{2,1,0:T(8,128)(2,1)S(1)} %pad_maximum_fusion.refs_0_), channel_id=1, source_target_pairs={{0,4},{1,5},{2,6},{3,7},{4,0},{5,1},{6,2},{7,3},{8,12},{9,13},{10,... | collective-permute-start | bytes 1179656 | tf_op jit(solution)/shard_map/ppermute | solution.py:290
  16.1 13.4 %collective-permute-start.6 = (bf16[2,16,6144]{2,1,0:T(8,128)(2,1)S(1)}, bf16[2,16,6144]{2,1,0:T(8,128)(2,1)S(1)}, u32[]{:S(2)}, u32[]{:S(2)}) collective-permute-start(bf16[2,16,6144]{2,1,0:T(8,128)(2,1)S(1)} %collective-permute-done.2.refs_0_.refs_2_), channel_id=1, source_target_pairs={{0,1},{1,0},{2,3},{3,2},{4,5},{5,4},{6,7},{7,6},{8,9},{9,8},{10,11... | collective-permute-start | bytes 1179656 | tf_op jit(solution)/shard_map/ppermute | solution.py:284
  17.6 16.7 %collective-permute-start.7 = (bf16[2,16,6144]{2,1,0:T(8,128)(2,1)S(1)}, bf16[2,16,6144]{2,1,0:T(8,128)(2,1)S(1)}, u32[]{:S(2)}, u32[]{:S(2)}) collective-permute-start(bf16[2,16,6144]{2,1,0:T(8,128)(2,1)S(1)} %collective-permute-done.2.refs_0_.refs_2_), channel_id=1, source_target_pairs={{0,2},{1,3},{2,0},{3,1},{4,6},{5,7},{6,4},{7,5},{8,10},{9,11},{10,... | collective-permute-start | bytes 1179656 | tf_op jit(solution)/shard_map/ppermute | solution.py:287
  22.8 13.5 %collective-permute-start.8 = (bf16[2,32,3072]{2,1,0:T(8,128)(2,1)S(1)}, bf16[2,32,3072]{2,1,0:T(8,128)(2,1)S(1)}, u32[]{:S(2)}, u32[]{:S(2)}) collective-permute-start(bf16[2,32,3072]{2,1,0:T(8,128)(2,1)S(1)} %get-tuple-element.125), channel_id=1, source_target_pairs={{0,16},{8,24},{16,0},{24,8},{1,17},{9,25},{17,1},{25,9},{2,18},{10... | collective-permute-start | bytes 1179656 | tf_op jit(solution)/shard_map/ppermute | solution.py:278
  28.9 10.1 %collective-permute-start.9 = (bf16[2,16,6144]{2,1,0:T(8,128)(2,1)S(1)}, bf16[2,16,6144]{2,1,0:T(8,128)(2,1)S(1)}, u32[]{:S(2)}, u32[]{:S(2)}) collective-permute-start(bf16[2,16,6144]{2,1,0:T(8,128)(2,1)S(1)} %collective-permute-done.4.refs_0_.refs_4_), channel_id=1, source_target_pairs={{0,1},{1,0},{2,3},{3,2},{4,5},{5,4},{6,7},{7,6},{8,9},{9,8},{10,11... | collective-permute-start | bytes 1179656 | tf_op jit(solution)/shard_map/ppermute | solution.py:284
  33.1 10.6 %collective-permute-start.10 = (bf16[2,32,3072]{2,1,0:T(8,128)(2,1)S(1)}, bf16[2,32,3072]{2,1,0:T(8,128)(2,1)S(1)}, u32[]{:S(2)}, u32[]{:S(2)}) collective-permute-start(bf16[2,32,3072]{2,1,0:T(8,128)(2,1)S(1)} %get-tuple-element.133), channel_id=1, source_target_pairs={{0,16},{8,24},{16,0},{24,8},{1,17},{9,25},{17,1},{25,9},{2,18},{10... | collective-permute-start | bytes 1179656 | tf_op jit(solution)/shard_map/ppermute | solution.py:278
  34.3 12.1 %collective-permute-start.11 = (bf16[2,16,6144]{2,1,0:T(8,128)(2,1)S(1)}, bf16[2,16,6144]{2,1,0:T(8,128)(2,1)S(1)}, u32[]{:S(2)}, u32[]{:S(2)}) collective-permute-start(bf16[2,16,6144]{2,1,0:T(8,128)(2,1)S(1)} %collective-permute-done.7.refs_0_.refs_6_), channel_id=1, source_target_pairs={{0,1},{1,0},{2,3},{3,2},{4,5},{5,4},{6,7},{7,6},{8,9},{9,8},{10,11... | collective-permute-start | bytes 1179656 | tf_op jit(solution)/shard_map/ppermute | solution.py:284
  35.2 17.2 %collective-permute-start.12 = (bf16[2,16,6144]{2,1,0:T(8,128)(2,1)S(1)}, bf16[2,16,6144]{2,1,0:T(8,128)(2,1)S(1)}, u32[]{:S(2)}, u32[]{:S(2)}) collective-permute-start(bf16[2,16,6144]{2,1,0:T(8,128)(2,1)S(1)} %collective-permute-done.5.refs_0_.refs_10_), channel_id=1, source_target_pairs={{0,2},{1,3},{2,0},{3,1},{4,6},{5,7},{6,4},{7,5},{8,10},{9,11},{10,... | collective-permute-start | bytes 1179656 | tf_op jit(solution)/shard_map/ppermute | solution.py:287
  36.3 18.5 %collective-permute-start.13 = (bf16[2,16,6144]{2,1,0:T(8,128)(2,1)S(1)}, bf16[2,16,6144]{2,1,0:T(8,128)(2,1)S(1)}, u32[]{:S(2)}, u32[]{:S(2)}) collective-permute-start(bf16[2,16,6144]{2,1,0:T(8,128)(2,1)S(1)} %collective-permute-done.2.refs_0_.refs_2_), channel_id=1, source_target_pairs={{0,4},{1,5},{2,6},{3,7},{4,0},{5,1},{6,2},{7,3},{8,12},{9,13},{10,... | collective-permute-start | bytes 1179656 | tf_op jit(solution)/shard_map/ppermute | solution.py:290
  42.6 12.9 %collective-permute-start.15 = (bf16[2,32,3072]{2,1,0:T(8,128)(2,1)S(1)}, bf16[2,32,3072]{2,1,0:T(8,128)(2,1)S(1)}, u32[]{:S(2)}, u32[]{:S(2)}) collective-permute-start(bf16[2,32,3072]{2,1,0:T(8,128)(2,1)S(1)} %get-tuple-element.146), channel_id=1, source_target_pairs={{0,16},{8,24},{16,0},{24,8},{1,17},{9,25},{17,1},{25,9},{2,18},{10... | collective-permute-start | bytes 1179656 | tf_op jit(solution)/shard_map/ppermute | solution.py:278
  43.7 13.1 %collective-permute-start.14 = (bf16[2,16,6144]{2,1,0:T(8,128)(2,1)S(1)}, bf16[2,16,6144]{2,1,0:T(8,128)(2,1)S(1)}, u32[]{:S(2)}, u32[]{:S(2)}) collective-permute-start(bf16[2,16,6144]{2,1,0:T(8,128)(2,1)S(1)} %collective-permute-done.5.refs_0_.refs_10_), channel_id=1, source_target_pairs={{0,1},{1,0},{2,3},{3,2},{4,5},{5,4},{6,7},{7,6},{8,9},{9,8},{10,11... | collective-permute-start | bytes 1179656 | tf_op jit(solution)/shard_map/ppermute | solution.py:284
  52.3 12.1 %collective-permute-start.16 = (bf16[2,16,6144]{2,1,0:T(8,128)(2,1)S(1)}, bf16[2,16,6144]{2,1,0:T(8,128)(2,1)S(1)}, u32[]{:S(2)}, u32[]{:S(2)}) collective-permute-start(bf16[2,16,6144]{2,1,0:T(8,128)(2,1)S(1)} %collective-permute-done.12.refs_0_.refs_12_), channel_id=1, source_target_pairs={{0,1},{1,0},{2,3},{3,2},{4,5},{5,4},{6,7},{7,6},{8,9},{9,8},{10,11... | collective-permute-start | bytes 1179656 | tf_op jit(solution)/shard_map/ppermute | solution.py:284
  53.8 10.6 %collective-permute-start.17 = (bf16[2,32,3072]{2,1,0:T(8,128)(2,1)S(1)}, bf16[2,32,3072]{2,1,0:T(8,128)(2,1)S(1)}, u32[]{:S(2)}, u32[]{:S(2)}) collective-permute-start(bf16[2,32,3072]{2,1,0:T(8,128)(2,1)S(1)} %get-tuple-element.152), channel_id=1, source_target_pairs={{0,16},{8,24},{16,0},{24,8},{1,17},{9,25},{17,1},{25,9},{2,18},{10... | collective-permute-start | bytes 1179656 | tf_op jit(solution)/shard_map/ppermute | solution.py:278
  54.9 13.1 %collective-permute-start.18 = (bf16[2,16,6144]{2,1,0:T(8,128)(2,1)S(1)}, bf16[2,16,6144]{2,1,0:T(8,128)(2,1)S(1)}, u32[]{:S(2)}, u32[]{:S(2)}) collective-permute-start(bf16[2,16,6144]{2,1,0:T(8,128)(2,1)S(1)} %collective-permute-done.13.refs_0_.refs_8_), channel_id=1, source_target_pairs={{0,2},{1,3},{2,0},{3,1},{4,6},{5,7},{6,4},{7,5},{8,10},{9,11},{10,... | collective-permute-start | bytes 1179656 | tf_op jit(solution)/shard_map/ppermute | solution.py:287
  55.5 17.3 %collective-permute-start.19 = (bf16[2,16,6144]{2,1,0:T(8,128)(2,1)S(1)}, bf16[2,16,6144]{2,1,0:T(8,128)(2,1)S(1)}, u32[]{:S(2)}, u32[]{:S(2)}) collective-permute-start(bf16[2,16,6144]{2,1,0:T(8,128)(2,1)S(1)} %collective-permute-done.13.refs_0_.refs_8_), channel_id=1, source_target_pairs={{0,1},{1,0},{2,3},{3,2},{4,5},{5,4},{6,7},{7,6},{8,9},{9,8},{10,11... | collective-permute-start | bytes 1179656 | tf_op jit(solution)/shard_map/ppermute | solution.py:284
  60.4 12.5 %collective-permute-start.20 = (bf16[2,32,3072]{2,1,0:T(8,128)(2,1)S(1)}, bf16[2,32,3072]{2,1,0:T(8,128)(2,1)S(1)}, u32[]{:S(2)}, u32[]{:S(2)}) collective-permute-start(bf16[2,32,3072]{2,1,0:T(8,128)(2,1)S(1)} %get-tuple-element.159), channel_id=1, source_target_pairs={{0,16},{8,24},{16,0},{24,8},{1,17},{9,25},{17,1},{25,9},{2,18},{10... | collective-permute-start | bytes 1179656 | tf_op jit(solution)/shard_map/ppermute | solution.py:278
  68.0 11.7 %collective-permute-start.21 = (bf16[2,16,6144]{2,1,0:T(8,128)(2,1)S(1)}, bf16[2,16,6144]{2,1,0:T(8,128)(2,1)S(1)}, u32[]{:S(2)}, u32[]{:S(2)}) collective-permute-start(bf16[2,16,6144]{2,1,0:T(8,128)(2,1)S(1)} %collective-permute-done.18.refs_0_.refs_14_), channel_id=1, source_target_pairs={{0,1},{1,0},{2,3},{3,2},{4,5},{5,4},{6,7},{7,6},{8,9},{9,8},{10,11... | collective-permute-start | bytes 1179656 | tf_op jit(solution)/shard_map/ppermute | solution.py:284
  69.5 13.0 %collective-permute-start.22 = (bf16[2,32,3072]{2,1,0:T(8,128)(2,1)S(1)}, bf16[2,32,3072]{2,1,0:T(8,128)(2,1)S(1)}, u32[]{:S(2)}, u32[]{:S(2)}) collective-permute-start(bf16[2,32,3072]{2,1,0:T(8,128)(2,1)S(1)} %get-tuple-element.181), channel_id=1, source_target_pairs={{0,16},{8,24},{16,0},{24,8},{1,17},{9,25},{17,1},{25,9},{2,18},{10... | collective-permute-start | bytes 1179656 | tf_op jit(solution)/shard_map/ppermute | solution.py:278
  76.4 16.3 %collective-permute-start.24 = (bf16[2,32,3072]{2,1,0:T(8,128)(2,1)S(1)}, bf16[2,32,3072]{2,1,0:T(8,128)(2,1)S(1)}, u32[]{:S(2)}, u32[]{:S(2)}) collective-permute-start(bf16[2,32,3072]{2,1,0:T(8,128)(2,1)S(1)} %get-tuple-element.189), channel_id=1, source_target_pairs={{0,16},{8,24},{16,0},{24,8},{1,17},{9,25},{17,1},{25,9},{2,18},{10... | collective-permute-start | bytes 1179656 | tf_op jit(solution)/shard_map/ppermute | solution.py:278
  81.3 11.5 %collective-permute-start.23 = (bf16[2,32,1024]{2,1,0:T(8,128)(2,1)S(1)}, bf16[2,32,1024]{2,1,0:T(8,128)(2,1)S(1)}, u32[]{:S(2)}, u32[]{:S(2)}) collective-permute-start(bf16[2,32,1024]{2,1,0:T(8,128)(2,1)S(1)} %get-tuple-element.187), channel_id=1, source_target_pairs={{0,16},{8,24},{16,0},{24,8},{1,17},{9,25},{17,1},{25,9},{2,18},{10... | collective-permute-start | bytes 393224 | tf_op jit(solution)/shard_map/ppermute | solution.py:278
  84.1 11.3 %collective-permute-start.25 = (bf16[2,32,1024]{2,1,0:T(8,128)(2,1)S(1)}, bf16[2,32,1024]{2,1,0:T(8,128)(2,1)S(1)}, u32[]{:S(2)}, u32[]{:S(2)}) collective-permute-start(bf16[2,32,1024]{2,1,0:T(8,128)(2,1)S(1)} %get-tuple-element.200), channel_id=1, source_target_pairs={{0,16},{8,24},{16,0},{24,8},{1,17},{9,25},{17,1},{25,9},{2,18},{10... | collective-permute-start | bytes 393224 | tf_op jit(solution)/shard_map/ppermute | solution.py:278
  86.8 11.3 %collective-permute-start.26 = (bf16[2,32,1024]{2,1,0:T(8,128)(2,1)S(1)}, bf16[2,32,1024]{2,1,0:T(8,128)(2,1)S(1)}, u32[]{:S(2)}, u32[]{:S(2)}) collective-permute-start(bf16[2,32,1024]{2,1,0:T(8,128)(2,1)S(1)} %get-tuple-element.206), channel_id=1, source_target_pairs={{0,16},{8,24},{16,0},{24,8},{1,17},{9,25},{17,1},{25,9},{2,18},{10... | collective-permute-start | bytes 393224 | tf_op jit(solution)/shard_map/ppermute | solution.py:278
  95.4 6.0 %collective-permute-start.29 = (bf16[2,384,1024]{2,1,0:T(8,128)(2,1)S(1)}, bf16[2,384,1024]{2,1,0:T(8,128)(2,1)S(1)}, u32[]{:S(2)}, u32[]{:S(2)}) collective-permute-start(bf16[2,384,1024]{2,1,0:T(8,128)(2,1)S(1)} %get-tuple-element.215), channel_id=1, source_target_pairs={{0,8},{8,0},{16,24},{24,16},{1,9},{9,1},{17,25},{25,17},{2,10},{10... | collective-permute-start | bytes 4718600 | tf_op jit(solution)/shard_map/ppermute | solution.py:281
  98.2 4.7 %collective-permute-start.28 = (bf16[2,384,1024]{2,1,0:T(8,128)(2,1)S(1)}, bf16[2,384,1024]{2,1,0:T(8,128)(2,1)S(1)}, u32[]{:S(2)}, u32[]{:S(2)}) collective-permute-start(bf16[2,384,1024]{2,1,0:T(8,128)(2,1)S(1)} %get-tuple-element.213), channel_id=1, source_target_pairs={{0,8},{8,0},{16,24},{24,16},{1,9},{9,1},{17,25},{25,17},{2,10},{10... | collective-permute-start | bytes 4718600 | tf_op jit(solution)/shard_map/ppermute | solution.py:281
  101.3 3.5 %collective-permute-start.27 = (bf16[2,384,1024]{2,1,0:T(8,128)(2,1)S(1)}, bf16[2,384,1024]{2,1,0:T(8,128)(2,1)S(1)}, u32[]{:S(2)}, u32[]{:S(2)}) collective-permute-start(bf16[2,384,1024]{2,1,0:T(8,128)(2,1)S(1)} %get-tuple-element.211), channel_id=1, source_target_pairs={{0,8},{8,0},{16,24},{24,16},{1,9},{9,1},{17,25},{25,17},{2,10},{10... | collective-permute-start | bytes 4718600 | tf_op jit(solution)/shard_map/ppermute | solution.py:281

commit v8 on v7

--- a/solution.py
+++ b/solution.py
@@ -13,10 +13,11 @@
 ROWS = 4
 COLS = 8
 LANES = 4
+FULL_LANES = 6
 GRAD_LANES = 8
 SCALE = 0.7978845608028654
 CUBIC = 0.044715
-PARTIAL_VMEM = 8 * 1024 * 1024
+PARTIAL_VMEM = 10 * 1024 * 1024
 GRAD_VMEM = 20 * 1024 * 1024
 TOTAL_VMEM = 14 * 1024 * 1024
 TICK_VMEM = 1024 * 1024
@@ -107,14 +108,14 @@
     )(*weights)
 
 
-def partial_kernel(n_buf, slots, base, table, *refs):
+def partial_kernel(n_buf, slots, base, lanes, table, *refs):
     buffers = refs[:n_buf]
     weights, keep_ref, send_ref = refs[n_buf:]
     step = pl.program_id(0)
-    for lane in range(LANES):
+    for lane in range(lanes):
         at = slice(lane * BLK, (lane + 1) * BLK)
         for side in range(2):
-            left = picked_rows(table, buffers, side, base + step * LANES + lane, slots)
+            left = picked_rows(table, buffers, side, base + step * lanes + lane, slots)
             right = jnp.concatenate((weights[side, :, at], weights[2 + side, :, at]), axis=0)
             total = jnp.dot(left, right, preferred_element_type=jnp.float32)
             keep_ref[side, :, at] = total
@@ -124,12 +125,13 @@
 def partial(table, buffers, weights, first=0, steps=None):
     tokens = sum(b.shape[1] for b in buffers)
     kept, width = weights.shape[1:]
-    wide = LANES * BLK
+    lanes = FULL_LANES if steps is None else LANES
+    wide = lanes * BLK
     steps = width // wide if steps is None else steps
     weight = pl.BlockSpec((4, kept, wide), lambda g, t: (0, 0, first + g))
     out = pl.BlockSpec((2, tokens, wide), lambda g, t: (0, 0, g))
     return pl.pallas_call(
-        functools.partial(partial_kernel, len(buffers), 2 * kept // BLK, first * LANES),
+        functools.partial(partial_kernel, len(buffers), 2 * kept // BLK, first * lanes, lanes),
         grid_spec=pltpu.PrefetchScalarGridSpec(
             num_scalar_prefetch=1,
             grid=(steps,),
@@ -381,6 +383,7 @@
         kept, width = w_in.shape
         fits = kept % BLK == 0 and inputs.shape[0] % 16 == 0
         fits = fits and all(v * LANES % GRAD_LANES == 0 for part in PARTS for v in part)
+        fits = fits and width % (FULL_LANES * BLK) == 0
         fits = fits and width == sum(steps for _, steps in PARTS) * LANES * BLK
         chosen = fast if fits and mesh.shape["row"] == ROWS and mesh.shape["col"] == COLS else general
         return chosen(inputs, cotangent, w_in, w_out, keep_in, keep_out)

time: 107 us -> 107 us (level)
  waiting for transfers between devices: 21 us -> 24.4 us
  Pallas kernels: 48.4 us -> 46 us
    pallas_call x10, Pallas kernels: 30.1 us -> 27.8 us  [partial(): pl.pallas_call(functools.partial(partial_kernel, len(buffers), 2 * kept /...]
    ppermute x11, waiting for transfers between devices: 4.75 us -> 6.21 us  [swap_x(): return lax.ppermute(v, 'row', [(r, r ^ 2) for r in range(ROWS)])]
  transfers between devices with their start and end apart: 30 -> 30, of which waited for: 10 -> 13; matrix products, arithmetic and copies ran while one was open for 2% -> 2% of each run, Pallas kernels for 44% -> 42%
where the time goes in v8:
time: 107 us
  Pallas kernels  46 us (43%)
  starting transfers between devices  33.3 us (31%)
  waiting for transfers between devices  24.4 us (23%)
  other arithmetic  1.07 us (1%)
    pallas_call x10, Pallas kernels, partial(): pl.pallas_call(functools.partial(partial_kernel, len(buffers), 2 * kept /...  27.8 us
    ppermute x11, starting transfers between devices, swap_x(): return lax.ppermute(v, 'row', [(r, r ^ 2) for r in range(ROWS)])  11.8 us
    ppermute x8, starting transfers between devices, swap_y(): return lax.ppermute(v, 'col', [(c, c ^ 1) for c in range(COLS)])  10.1 us
    ppermute x8, waiting for transfers between devices, swap_y(): return lax.ppermute(v, 'col', [(c, c ^ 1) for c in range(COLS)])  8.44 us
    pallas_call x3, Pallas kernels, grad(): pl.pallas_call(functools.partial(grad_kernel, len(buffers), len(keeps), 2...  7.89 us
    ppermute x11, waiting for transfers between devices, swap_x(): return lax.ppermute(v, 'row', [(r, r ^ 2) for r in range(ROWS)])  6.21 us
    ppermute x4, waiting for transfers between devices, near(): return lax.ppermute(v, 'col', [(c, c ^ 2) for c in range(COLS)])  5.81 us
    ppermute x2, starting transfers between devices, far(): return lax.ppermute(v, 'col', [(c, c ^ 4) for c in range(COLS)])  5.2 us
  transfers between devices with their start and end apart: 30, of which 13 were waited for; matrix products, arithmetic and copies ran while one was open for 2% of the time, Pallas kernels for 42%

profile of v8, /device:TPU:0, one launch (start us, length us, event | category | flops | bytes accessed | tf_op | source)
XLA Modules:
  0.0 106.7 jit_solution(16654754473474137463)
XLA Ops:
  2.3 3.0 %collective-permute-start.2 = (bf16[2,16,6144]{2,1,0:T(8,128)(2,1)S(1)}, bf16[2,16,6144]{2,1,0:T(8,128)(2,1)S(1)}, u32[]{:S(2)}, u32[]{:S(2)}) collective-permute-start(bf16[2,16,6144]{2,1,0:T(8,128)(2,1)S(1)} %pad_maximum_fusion.refs_0_), channel_id=1, source_target_pairs={{0,16},{8,24},{16,0},{24,8},{1,17},{9,25},{17,1},{25,9},{2,18},{10... | collective-permute-start | bytes 1179656 | tf_op jit(solution)/shard_map/ppermute | solution.py:280
  5.3 1.5 %collective-permute-start.3 = (bf16[2,16,6144]{2,1,0:T(8,128)(2,1)S(1)}, bf16[2,16,6144]{2,1,0:T(8,128)(2,1)S(1)}, u32[]{:S(2)}, u32[]{:S(2)}) collective-permute-start(bf16[2,16,6144]{2,1,0:T(8,128)(2,1)S(1)} %pad_maximum_fusion.refs_0_), channel_id=1, source_target_pairs={{0,1},{1,0},{2,3},{3,2},{4,5},{5,4},{6,7},{7,6},{8,9},{9,8},{10,11... | collective-permute-start | bytes 1179656 | tf_op jit(solution)/shard_map/ppermute | solution.py:286
  6.8 1.6 %collective-permute-start.4 = (bf16[2,16,6144]{2,1,0:T(8,128)(2,1)S(1)}, bf16[2,16,6144]{2,1,0:T(8,128)(2,1)S(1)}, u32[]{:S(2)}, u32[]{:S(2)}) collective-permute-start(bf16[2,16,6144]{2,1,0:T(8,128)(2,1)S(1)} %pad_maximum_fusion.refs_0_), channel_id=1, source_target_pairs={{0,2},{1,3},{2,0},{3,1},{4,6},{5,7},{6,4},{7,5},{8,10},{9,11},{10,... | collective-permute-start | bytes 1179656 | tf_op jit(solution)/shard_map/ppermute | solution.py:289
  9.4 2.7 %collective-permute-start.5 = (bf16[2,16,6144]{2,1,0:T(8,128)(2,1)S(1)}, bf16[2,16,6144]{2,1,0:T(8,128)(2,1)S(1)}, u32[]{:S(2)}, u32[]{:S(2)}) collective-permute-start(bf16[2,16,6144]{2,1,0:T(8,128)(2,1)S(1)} %pad_maximum_fusion.refs_0_), channel_id=1, source_target_pairs={{0,4},{1,5},{2,6},{3,7},{4,0},{5,1},{6,2},{7,3},{8,12},{9,13},{10,... | collective-permute-start | bytes 1179656 | tf_op jit(solution)/shard_map/ppermute | solution.py:292
  12.1 3.8 %pack.1.refs_2_ = bf16[4,384,3072]{2,1,0:T(8,128)(2,1)S(1)} custom-call(bf16[384,3072]{1,0:T(8,128)(2,1)} %refs_0_.1, bf16[384,3072]{1,0:T(8,128)(2,1)} %refs_1_.1, bf16[384,3072]{1,0:T(8,128)(2,1)} %collective-permute-done.refs_2_, bf16[384,3072]{1,0:T(8,128)(2,1)} %collective-permute-done.1.refs_3_), custom_call_target="tpu_custom_call" | custom-call | tf_op jit(solution)/shard_map/pack/pallas_call | solution.py:99
  16.1 1.5 %collective-permute-start.6 = (bf16[2,16,6144]{2,1,0:T(8,128)(2,1)S(1)}, bf16[2,16,6144]{2,1,0:T(8,128)(2,1)S(1)}, u32[]{:S(2)}, u32[]{:S(2)}) collective-permute-start(bf16[2,16,6144]{2,1,0:T(8,128)(2,1)S(1)} %collective-permute-done.2.refs_0_.refs_2_), channel_id=1, source_target_pairs={{0,1},{1,0},{2,3},{3,2},{4,5},{5,4},{6,7},{7,6},{8,9},{9,8},{10,11... | collective-permute-start | bytes 1179656 | tf_op jit(solution)/shard_map/ppermute | solution.py:286
  17.6 1.6 %collective-permute-start.7 = (bf16[2,16,6144]{2,1,0:T(8,128)(2,1)S(1)}, bf16[2,16,6144]{2,1,0:T(8,128)(2,1)S(1)}, u32[]{:S(2)}, u32[]{:S(2)}) collective-permute-start(bf16[2,16,6144]{2,1,0:T(8,128)(2,1)S(1)} %collective-permute-done.2.refs_0_.refs_2_), channel_id=1, source_target_pairs={{0,2},{1,3},{2,0},{3,1},{4,6},{5,7},{6,4},{7,5},{8,10},{9,11},{10,... | collective-permute-start | bytes 1179656 | tf_op jit(solution)/shard_map/ppermute | solution.py:289
  19.2 3.2 %partial.10 = (f32[2,32,3072]{2,1,0:T(8,128)S(1)}, bf16[2,32,3072]{2,1,0:T(8,128)(2,1)S(1)}) custom-call(s32[288]{0:T(512)S(1)} %reshape.7.table.table_ref, bf16[2,16,6144]{2,1,0:T(8,128)(2,1)S(1)} %pad_maximum_fusion.refs_0_, bf16[2,16,6144]{2,1,0:T(8,128)(2,1)S(1)} %collective-permute-done.3.refs_1_, bf16[4,384,3072]{2,1,0:T(8,128)(2,1)S(1)} %pack.1.refs_2_), custom_call_target="tpu_custom_call" | custom-call | tf_op jit(solution)/shard_map/partial/pallas_call | solution.py:133
  23.1 3.0 %collective-permute-done.4.refs_0_.refs_4_ = bf16[2,16,6144]{2,1,0:T(8,128)(2,1)S(1)} collective-permute-done((bf16[2,16,6144]{2,1,0:T(8,128)(2,1)S(1)}, bf16[2,16,6144]{2,1,0:T(8,128)(2,1)S(1)}, u32[]{:S(2)}, u32[]{:S(2)}) %collective-permute-start.4) | collective-permute-done | bytes 393248 | tf_op jit(solution)/shard_map/ppermute | solution.py:289
  26.0 2.9 %collective-permute-done.5.refs_0_.refs_10_ = bf16[2,16,6144]{2,1,0:T(8,128)(2,1)S(1)} collective-permute-done((bf16[2,16,6144]{2,1,0:T(8,128)(2,1)S(1)}, bf16[2,16,6144]{2,1,0:T(8,128)(2,1)S(1)}, u32[]{:S(2)}, u32[]{:S(2)}) %collective-permute-start.5) | collective-permute-done | bytes 393248 | tf_op jit(solution)/shard_map/ppermute | solution.py:292
  29.5 3.3 %partial.11 = (f32[2,32,3072]{2,1,0:T(8,128)S(1)}, bf16[2,32,3072]{2,1,0:T(8,128)(2,1)S(1)}) custom-call(s32[288]{0:T(512)S(1)} %tick.4.table.table_ref, bf16[2,16,6144]{2,1,0:T(8,128)(2,1)S(1)} %collective-permute-done.2.refs_0_.refs_2_, bf16[2,16,6144]{2,1,0:T(8,128)(2,1)S(1)} %collective-permute-done.6.refs_1_.refs_3_, bf16[4,384,3072]{2,1,0:T(8,128)(2,1)S(1)} %pack.1.refs_2_), custom_call_target="tpu_custom_call" | custom-call | tf_op jit(solution)/shard_map/partial/pallas_call | solution.py:133
  36.3 2.5 %collective-permute-start.13 = (bf16[2,16,6144]{2,1,0:T(8,128)(2,1)S(1)}, bf16[2,16,6144]{2,1,0:T(8,128)(2,1)S(1)}, u32[]{:S(2)}, u32[]{:S(2)}) collective-permute-start(bf16[2,16,6144]{2,1,0:T(8,128)(2,1)S(1)} %collective-permute-done.2.refs_0_.refs_2_), channel_id=1, source_target_pairs={{0,4},{1,5},{2,6},{3,7},{4,0},{5,1},{6,2},{7,3},{8,12},{9,13},{10,... | collective-permute-start | bytes 1179656 | tf_op jit(solution)/shard_map/ppermute | solution.py:292
  38.9 3.2 %partial.12 = (f32[2,32,3072]{2,1,0:T(8,128)S(1)}, bf16[2,32,3072]{2,1,0:T(8,128)(2,1)S(1)}) custom-call(s32[288]{0:T(512)S(1)} %tick.4.table.table_ref, bf16[2,16,6144]{2,1,0:T(8,128)(2,1)S(1)} %collective-permute-done.4.refs_0_.refs_4_, bf16[2,16,6144]{2,1,0:T(8,128)(2,1)S(1)} %collective-permute-done.9.refs_1_.refs_5_, bf16[4,384,3072]{2,1,0:T(8,128)(2,1)S(1)} %pack.1.refs_2_), custom_call_target="tpu_custom_call" | custom-call | tf_op jit(solution)/shard_map/partial/pallas_call | solution.py:133
  43.0 2.0 %collective-permute-start.14 = (bf16[2,16,6144]{2,1,0:T(8,128)(2,1)S(1)}, bf16[2,16,6144]{2,1,0:T(8,128)(2,1)S(1)}, u32[]{:S(2)}, u32[]{:S(2)}) collective-permute-start(bf16[2,16,6144]{2,1,0:T(8,128)(2,1)S(1)} %collective-permute-done.5.refs_0_.refs_10_), channel_id=1, source_target_pairs={{0,1},{1,0},{2,3},{3,2},{4,5},{5,4},{6,7},{7,6},{8,9},{9,8},{10,11... | collective-permute-start | bytes 1179656 | tf_op jit(solution)/shard_map/ppermute | solution.py:286
  46.4 3.3 %partial.13 = (f32[2,32,3072]{2,1,0:T(8,128)S(1)}, bf16[2,32,3072]{2,1,0:T(8,128)(2,1)S(1)}) custom-call(s32[288]{0:T(512)S(1)} %tick.4.table.table_ref, bf16[2,16,6144]{2,1,0:T(8,128)(2,1)S(1)} %collective-permute-done.7.refs_0_.refs_6_, bf16[2,16,6144]{2,1,0:T(8,128)(2,1)S(1)} %collective-permute-done.11.refs_1_.refs_7_, bf16[4,384,3072]{2,1,0:T(8,128)(2,1)S(1)} %pack.1.refs_2_), custom_call_target="tpu_custom_call" | custom-call | tf_op jit(solution)/shard_map/partial/pallas_call | solution.py:133
  49.7 2.7 %collective-permute-done.12.refs_0_.refs_12_ = bf16[2,16,6144]{2,1,0:T(8,128)(2,1)S(1)} collective-permute-done((bf16[2,16,6144]{2,1,0:T(8,128)(2,1)S(1)}, bf16[2,16,6144]{2,1,0:T(8,128)(2,1)S(1)}, u32[]{:S(2)}, u32[]{:S(2)}) %collective-permute-start.12) | collective-permute-done | bytes 393248 | tf_op jit(solution)/shard_map/ppermute | solution.py:289
  52.3 1.5 %collective-permute-start.16 = (bf16[2,16,6144]{2,1,0:T(8,128)(2,1)S(1)}, bf16[2,16,6144]{2,1,0:T(8,128)(2,1)S(1)}, u32[]{:S(2)}, u32[]{:S(2)}) collective-permute-start(bf16[2,16,6144]{2,1,0:T(8,128)(2,1)S(1)} %collective-permute-done.12.refs_0_.refs_12_), channel_id=1, source_target_pairs={{0,1},{1,0},{2,3},{3,2},{4,5},{5,4},{6,7},{7,6},{8,9},{9,8},{10,11... | collective-permute-start | bytes 1179656 | tf_op jit(solution)/shard_map/ppermute | solution.py:286
  56.7 3.3 %partial.14 = (f32[2,32,3072]{2,1,0:T(8,128)S(1)}, bf16[2,32,3072]{2,1,0:T(8,128)(2,1)S(1)}) custom-call(s32[288]{0:T(512)S(1)} %tick.5.table, bf16[2,16,6144]{2,1,0:T(8,128)(2,1)S(1)} %collective-permute-done.5.refs_0_.refs_10_, bf16[2,16,6144]{2,1,0:T(8,128)(2,1)S(1)} %collective-permute-done.14.refs_1_.refs_11_, bf16[4,384,3072]{2,1,0:T(8,128)(2,1)S(1)} %pack.1.refs_2_), custom_call_target="tpu_custom_call" | custom-call | tf_op jit(solution)/shard_map/partial/pallas_call | solution.py:133
  60.6 3.8 %collective-permute-done.16.refs_1_.refs_13_ = bf16[2,16,6144]{2,1,0:T(8,128)(2,1)S(1)} collective-permute-done((bf16[2,16,6144]{2,1,0:T(8,128)(2,1)S(1)}, bf16[2,16,6144]{2,1,0:T(8,128)(2,1)S(1)}, u32[]{:S(2)}, u32[]{:S(2)}) %collective-permute-start.16) | collective-permute-done | bytes 393248 | tf_op jit(solution)/shard_map/ppermute | solution.py:286
  65.1 3.3 %partial.15 = (f32[2,32,3072]{2,1,0:T(8,128)S(1)}, bf16[2,32,3072]{2,1,0:T(8,128)(2,1)S(1)}) custom-call(s32[288]{0:T(512)S(1)} %tick.5.table, bf16[2,16,6144]{2,1,0:T(8,128)(2,1)S(1)} %collective-permute-done.12.refs_0_.refs_12_, bf16[2,16,6144]{2,1,0:T(8,128)(2,1)S(1)} %collective-permute-done.16.refs_1_.refs_13_, bf16[4,384,3072]{2,1,0:T(8,128)(2,1)S(1)} %pack.1.refs_2_), custom_call_target="tpu_custom_call" | custom-call | tf_op jit(solution)/shard_map/partial/pallas_call | solution.py:133
  69.8 3.0 %collective-permute-done.19.refs_1_.refs_9_ = bf16[2,16,6144]{2,1,0:T(8,128)(2,1)S(1)} collective-permute-done((bf16[2,16,6144]{2,1,0:T(8,128)(2,1)S(1)}, bf16[2,16,6144]{2,1,0:T(8,128)(2,1)S(1)}, u32[]{:S(2)}, u32[]{:S(2)}) %collective-permute-start.19) | collective-permute-done | bytes 393248 | tf_op jit(solution)/shard_map/ppermute | solution.py:286
  73.5 3.3 %partial.16 = (f32[2,32,3072]{2,1,0:T(8,128)S(1)}, bf16[2,32,3072]{2,1,0:T(8,128)(2,1)S(1)}) custom-call(s32[288]{0:T(512)S(1)} %tick.5.table, bf16[2,16,6144]{2,1,0:T(8,128)(2,1)S(1)} %collective-permute-done.13.refs_0_.refs_8_, bf16[2,16,6144]{2,1,0:T(8,128)(2,1)S(1)} %collective-permute-done.19.refs_1_.refs_9_, bf16[4,384,3072]{2,1,0:T(8,128)(2,1)S(1)} %pack.1.refs_2_), custom_call_target="tpu_custom_call" | custom-call | tf_op jit(solution)/shard_map/partial/pallas_call | solution.py:133
  77.4 2.3 %early.1.refs_16_ = bf16[2,160,3072]{2,1,0:T(8,128)(2,1)S(1)} custom-call(f32[2,32,3072]{2,1,0:T(8,128)S(1)} %get-tuple-element.164.refs_0_, f32[2,32,3072]{2,1,0:T(8,128)S(1)} %get-tuple-element.165.refs_1_, f32[2,32,3072]{2,1,0:T(8,128)S(1)} %get-tuple-element.166.refs_2_, f32[2,32,3072]{2,1,0:T(8,128)S(1)} %get-tuple-element.167.refs_3_, ...), custom_call_target="tpu_custom_call" | custom-call | tf_op jit(solution)/shard_map/early/pallas_call | solution.py:193
  79.7 1.6 %partial.17 = (f32[2,32,1024]{2,1,0:T(8,128)S(1)}, bf16[2,32,1024]{2,1,0:T(8,128)(2,1)S(1)}) custom-call(s32[288]{0:T(512)S(1)} %tick.5.table, bf16[2,16,6144]{2,1,0:T(8,128)(2,1)S(1)} %collective-permute-done.18.refs_0_.refs_14_, bf16[2,16,6144]{2,1,0:T(8,128)(2,1)S(1)} %collective-permute-done.21.refs_1_.refs_15_, bf16[4,384,3072]{2,1,0:T(8,128)(2,1)S(1)} %pack.1.refs_2_), custom_call_target="tpu_custom_call" | custom-call | tf_op jit(solution)/shard_map/partial/pallas_call | solution.py:133
  81.3 1.6 %collective-permute-start.23 = (bf16[2,32,1024]{2,1,0:T(8,128)(2,1)S(1)}, bf16[2,32,1024]{2,1,0:T(8,128)(2,1)S(1)}, u32[]{:S(2)}, u32[]{:S(2)}) collective-permute-start(bf16[2,32,1024]{2,1,0:T(8,128)(2,1)S(1)} %get-tuple-element.187), channel_id=1, source_target_pairs={{0,16},{8,24},{16,0},{24,8},{1,17},{9,25},{17,1},{25,9},{2,18},{10... | collective-permute-start | bytes 393224 | tf_op jit(solution)/shard_map/ppermute | solution.py:280
  82.9 1.6 %partial.18 = (f32[2,32,1024]{2,1,0:T(8,128)S(1)}, bf16[2,32,1024]{2,1,0:T(8,128)(2,1)S(1)}) custom-call(s32[288]{0:T(512)S(1)} %tick.5.table, bf16[2,16,6144]{2,1,0:T(8,128)(2,1)S(1)} %collective-permute-done.18.refs_0_.refs_14_, bf16[2,16,6144]{2,1,0:T(8,128)(2,1)S(1)} %collective-permute-done.21.refs_1_.refs_15_, bf16[4,384,3072]{2,1,0:T(8,128)(2,1)S(1)} %pack.1.refs_2_), custom_call_target="tpu_custom_call" | custom-call | tf_op jit(solution)/shard_map/partial/pallas_call | solution.py:133
  85.0 1.8 %partial.19 = (f32[2,32,1024]{2,1,0:T(8,128)S(1)}, bf16[2,32,1024]{2,1,0:T(8,128)(2,1)S(1)}) custom-call(s32[288]{0:T(512)S(1)} %tick.5.table, bf16[2,16,6144]{2,1,0:T(8,128)(2,1)S(1)} %collective-permute-done.18.refs_0_.refs_14_, bf16[2,16,6144]{2,1,0:T(8,128)(2,1)S(1)} %collective-permute-done.21.refs_1_.refs_15_, bf16[4,384,3072]{2,1,0:T(8,128)(2,1)S(1)} %pack.1.refs_2_), custom_call_target="tpu_custom_call" | custom-call | tf_op jit(solution)/shard_map/partial/pallas_call | solution.py:133
  86.9 1.6 %collective-permute-start.26 = (bf16[2,32,1024]{2,1,0:T(8,128)(2,1)S(1)}, bf16[2,32,1024]{2,1,0:T(8,128)(2,1)S(1)}, u32[]{:S(2)}, u32[]{:S(2)}) collective-permute-start(bf16[2,32,1024]{2,1,0:T(8,128)(2,1)S(1)} %get-tuple-element.206), channel_id=1, source_target_pairs={{0,16},{8,24},{16,0},{24,8},{1,17},{9,25},{17,1},{25,9},{2,18},{10... | collective-permute-start | bytes 393224 | tf_op jit(solution)/shard_map/ppermute | solution.py:280
  88.4 4.8 %collective-permute-done.23.refs_21_ = bf16[2,32,1024]{2,1,0:T(8,128)(2,1)S(1)} collective-permute-done((bf16[2,32,1024]{2,1,0:T(8,128)(2,1)S(1)}, bf16[2,32,1024]{2,1,0:T(8,128)(2,1)S(1)}, u32[]{:S(2)}, u32[]{:S(2)}) %collective-permute-start.23) | collective-permute-done | bytes 131104 | tf_op jit(solution)/shard_map/ppermute | solution.py:280
  93.2 2.6 %grad.3 = (bf16[2,384,1024]{2,1,0:T(8,128)(2,1)S(1)}, bf16[2,384,1024]{2,1,0:T(8,128)(2,1)S(1)}) custom-call(s32[288]{0:T(512)S(1)} %tick.5.table, bf16[2,16,6144]{2,1,0:T(8,128)(2,1)S(1)} %pad_maximum_fusion.refs_0_, bf16[2,16,6144]{2,1,0:T(8,128)(2,1)S(1)} %collective-permute-done.3.refs_1_, ...), custom_call_target="tpu_custom_call" | custom-call | tf_op jit(solution)/shard_map/grad/pallas_call | solution.py:233
  95.9 2.6 %grad.4 = (bf16[2,384,1024]{2,1,0:T(8,128)(2,1)S(1)}, bf16[2,384,1024]{2,1,0:T(8,128)(2,1)S(1)}) custom-call(s32[288]{0:T(512)S(1)} %tick.5.table, bf16[2,16,6144]{2,1,0:T(8,128)(2,1)S(1)} %pad_maximum_fusion.refs_0_, bf16[2,16,6144]{2,1,0:T(8,128)(2,1)S(1)} %collective-permute-done.3.refs_1_, ...), custom_call_target="tpu_custom_call" | custom-call | tf_op jit(solution)/shard_map/grad/pallas_call | solution.py:233
  99.1 2.6 %grad.5 = (bf16[2,384,1024]{2,1,0:T(8,128)(2,1)S(1)}, bf16[2,384,1024]{2,1,0:T(8,128)(2,1)S(1)}) custom-call(s32[288]{0:T(512)S(1)} %tick.5.table, bf16[2,16,6144]{2,1,0:T(8,128)(2,1)S(1)} %pad_maximum_fusion.refs_0_, bf16[2,16,6144]{2,1,0:T(8,128)(2,1)S(1)} %collective-permute-done.3.refs_1_, ...), custom_call_target="tpu_custom_call" | custom-call | tf_op jit(solution)/shard_map/grad/pallas_call | solution.py:233
  (54 shorter events, 22.9 us)
Async XLA Ops:
  0.6 8.8 %collective-permute-start = (bf16[384,3072]{1,0:T(8,128)(2,1)}, bf16[384,3072]{1,0:T(8,128)(2,1)}, u32[]{:S(2)}, u32[]{:S(2)}) collective-permute-start(bf16[384,3072]{1,0:T(8,128)(2,1)} %refs_0_.1), channel_id=1, source_target_pairs={{0,8},{8,0},{16,24},{24,16},{1,9},{9,1},{17,25},{25,17},{2,10},{10... | collective-permute-start | bytes 7077896 | tf_op jit(solution)/shard_map/ppermute | solution.py:283
  1.1 11.0 %collective-permute-start.1 = (bf16[384,3072]{1,0:T(8,128)(2,1)}, bf16[384,3072]{1,0:T(8,128)(2,1)}, u32[]{:S(2)}, u32[]{:S(2)}) collective-permute-start(bf16[384,3072]{1,0:T(8,128)(2,1)} %refs_1_.1), channel_id=1, source_target_pairs={{0,8},{8,0},{16,24},{24,16},{1,9},{9,1},{17,25},{25,17},{2,10},{10... | collective-permute-start | bytes 7077896 | tf_op jit(solution)/shard_map/ppermute | solution.py:283
  2.3 13.6 %collective-permute-start.2 = (bf16[2,16,6144]{2,1,0:T(8,128)(2,1)S(1)}, bf16[2,16,6144]{2,1,0:T(8,128)(2,1)S(1)}, u32[]{:S(2)}, u32[]{:S(2)}) collective-permute-start(bf16[2,16,6144]{2,1,0:T(8,128)(2,1)S(1)} %pad_maximum_fusion.refs_0_), channel_id=1, source_target_pairs={{0,16},{8,24},{16,0},{24,8},{1,17},{9,25},{17,1},{25,9},{2,18},{10... | collective-permute-start | bytes 1179656 | tf_op jit(solution)/shard_map/ppermute | solution.py:280
  5.3 10.8 %collective-permute-start.3 = (bf16[2,16,6144]{2,1,0:T(8,128)(2,1)S(1)}, bf16[2,16,6144]{2,1,0:T(8,128)(2,1)S(1)}, u32[]{:S(2)}, u32[]{:S(2)}) collective-permute-start(bf16[2,16,6144]{2,1,0:T(8,128)(2,1)S(1)} %pad_maximum_fusion.refs_0_), channel_id=1, source_target_pairs={{0,1},{1,0},{2,3},{3,2},{4,5},{5,4},{6,7},{7,6},{8,9},{9,8},{10,11... | collective-permute-start | bytes 1179656 | tf_op jit(solution)/shard_map/ppermute | solution.py:286
  6.8 19.2 %collective-permute-start.4 = (bf16[2,16,6144]{2,1,0:T(8,128)(2,1)S(1)}, bf16[2,16,6144]{2,1,0:T(8,128)(2,1)S(1)}, u32[]{:S(2)}, u32[]{:S(2)}) collective-permute-start(bf16[2,16,6144]{2,1,0:T(8,128)(2,1)S(1)} %pad_maximum_fusion.refs_0_), channel_id=1, source_target_pairs={{0,2},{1,3},{2,0},{3,1},{4,6},{5,7},{6,4},{7,5},{8,10},{9,11},{10,... | collective-permute-start | bytes 1179656 | tf_op jit(solution)/shard_map/ppermute | solution.py:289
  9.4 19.5 %collective-permute-start.5 = (bf16[2,16,6144]{2,1,0:T(8,128)(2,1)S(1)}, bf16[2,16,6144]{2,1,0:T(8,128)(2,1)S(1)}, u32[]{:S(2)}, u32[]{:S(2)}) collective-permute-start(bf16[2,16,6144]{2,1,0:T(8,128)(2,1)S(1)} %pad_maximum_fusion.refs_0_), channel_id=1, source_target_pairs={{0,4},{1,5},{2,6},{3,7},{4,0},{5,1},{6,2},{7,3},{8,12},{9,13},{10,... | collective-permute-start | bytes 1179656 | tf_op jit(solution)/shard_map/ppermute | solution.py:292
  16.1 13.4 %collective-permute-start.6 = (bf16[2,16,6144]{2,1,0:T(8,128)(2,1)S(1)}, bf16[2,16,6144]{2,1,0:T(8,128)(2,1)S(1)}, u32[]{:S(2)}, u32[]{:S(2)}) collective-permute-start(bf16[2,16,6144]{2,1,0:T(8,128)(2,1)S(1)} %collective-permute-done.2.refs_0_.refs_2_), channel_id=1, source_target_pairs={{0,1},{1,0},{2,3},{3,2},{4,5},{5,4},{6,7},{7,6},{8,9},{9,8},{10,11... | collective-permute-start | bytes 1179656 | tf_op jit(solution)/shard_map/ppermute | solution.py:286
  17.6 16.6 %collective-permute-start.7 = (bf16[2,16,6144]{2,1,0:T(8,128)(2,1)S(1)}, bf16[2,16,6144]{2,1,0:T(8,128)(2,1)S(1)}, u32[]{:S(2)}, u32[]{:S(2)}) collective-permute-start(bf16[2,16,6144]{2,1,0:T(8,128)(2,1)S(1)} %collective-permute-done.2.refs_0_.refs_2_), channel_id=1, source_target_pairs={{0,2},{1,3},{2,0},{3,1},{4,6},{5,7},{6,4},{7,5},{8,10},{9,11},{10,... | collective-permute-start | bytes 1179656 | tf_op jit(solution)/shard_map/ppermute | solution.py:289
  22.4 13.9 %collective-permute-start.8 = (bf16[2,32,3072]{2,1,0:T(8,128)(2,1)S(1)}, bf16[2,32,3072]{2,1,0:T(8,128)(2,1)S(1)}, u32[]{:S(2)}, u32[]{:S(2)}) collective-permute-start(bf16[2,32,3072]{2,1,0:T(8,128)(2,1)S(1)} %get-tuple-element.125), channel_id=1, source_target_pairs={{0,16},{8,24},{16,0},{24,8},{1,17},{9,25},{17,1},{25,9},{2,18},{10... | collective-permute-start | bytes 1179656 | tf_op jit(solution)/shard_map/ppermute | solution.py:280
  28.9 9.9 %collective-permute-start.9 = (bf16[2,16,6144]{2,1,0:T(8,128)(2,1)S(1)}, bf16[2,16,6144]{2,1,0:T(8,128)(2,1)S(1)}, u32[]{:S(2)}, u32[]{:S(2)}) collective-permute-start(bf16[2,16,6144]{2,1,0:T(8,128)(2,1)S(1)} %collective-permute-done.4.refs_0_.refs_4_), channel_id=1, source_target_pairs={{0,1},{1,0},{2,3},{3,2},{4,5},{5,4},{6,7},{7,6},{8,9},{9,8},{10,11... | collective-permute-start | bytes 1179656 | tf_op jit(solution)/shard_map/ppermute | solution.py:286
  32.7 10.3 %collective-permute-start.10 = (bf16[2,32,3072]{2,1,0:T(8,128)(2,1)S(1)}, bf16[2,32,3072]{2,1,0:T(8,128)(2,1)S(1)}, u32[]{:S(2)}, u32[]{:S(2)}) collective-permute-start(bf16[2,32,3072]{2,1,0:T(8,128)(2,1)S(1)} %get-tuple-element.133), channel_id=1, source_target_pairs={{0,16},{8,24},{16,0},{24,8},{1,17},{9,25},{17,1},{25,9},{2,18},{10... | collective-permute-start | bytes 1179656 | tf_op jit(solution)/shard_map/ppermute | solution.py:280
  34.2 12.2 %collective-permute-start.11 = (bf16[2,16,6144]{2,1,0:T(8,128)(2,1)S(1)}, bf16[2,16,6144]{2,1,0:T(8,128)(2,1)S(1)}, u32[]{:S(2)}, u32[]{:S(2)}) collective-permute-start(bf16[2,16,6144]{2,1,0:T(8,128)(2,1)S(1)} %collective-permute-done.7.refs_0_.refs_6_), channel_id=1, source_target_pairs={{0,1},{1,0},{2,3},{3,2},{4,5},{5,4},{6,7},{7,6},{8,9},{9,8},{10,11... | collective-permute-start | bytes 1179656 | tf_op jit(solution)/shard_map/ppermute | solution.py:286
  34.8 17.5 %collective-permute-start.12 = (bf16[2,16,6144]{2,1,0:T(8,128)(2,1)S(1)}, bf16[2,16,6144]{2,1,0:T(8,128)(2,1)S(1)}, u32[]{:S(2)}, u32[]{:S(2)}) collective-permute-start(bf16[2,16,6144]{2,1,0:T(8,128)(2,1)S(1)} %collective-permute-done.5.refs_0_.refs_10_), channel_id=1, source_target_pairs={{0,2},{1,3},{2,0},{3,1},{4,6},{5,7},{6,4},{7,5},{8,10},{9,11},{10,... | collective-permute-start | bytes 1179656 | tf_op jit(solution)/shard_map/ppermute | solution.py:289
  36.3 18.5 %collective-permute-start.13 = (bf16[2,16,6144]{2,1,0:T(8,128)(2,1)S(1)}, bf16[2,16,6144]{2,1,0:T(8,128)(2,1)S(1)}, u32[]{:S(2)}, u32[]{:S(2)}) collective-permute-start(bf16[2,16,6144]{2,1,0:T(8,128)(2,1)S(1)} %collective-permute-done.2.refs_0_.refs_2_), channel_id=1, source_target_pairs={{0,4},{1,5},{2,6},{3,7},{4,0},{5,1},{6,2},{7,3},{8,12},{9,13},{10,... | collective-permute-start | bytes 1179656 | tf_op jit(solution)/shard_map/ppermute | solution.py:292
  42.1 13.1 %collective-permute-start.15 = (bf16[2,32,3072]{2,1,0:T(8,128)(2,1)S(1)}, bf16[2,32,3072]{2,1,0:T(8,128)(2,1)S(1)}, u32[]{:S(2)}, u32[]{:S(2)}) collective-permute-start(bf16[2,32,3072]{2,1,0:T(8,128)(2,1)S(1)} %get-tuple-element.146), channel_id=1, source_target_pairs={{0,16},{8,24},{16,0},{24,8},{1,17},{9,25},{17,1},{25,9},{2,18},{10... | collective-permute-start | bytes 1179656 | tf_op jit(solution)/shard_map/ppermute | solution.py:280
  43.0 13.7 %collective-permute-start.14 = (bf16[2,16,6144]{2,1,0:T(8,128)(2,1)S(1)}, bf16[2,16,6144]{2,1,0:T(8,128)(2,1)S(1)}, u32[]{:S(2)}, u32[]{:S(2)}) collective-permute-start(bf16[2,16,6144]{2,1,0:T(8,128)(2,1)S(1)} %collective-permute-done.5.refs_0_.refs_10_), channel_id=1, source_target_pairs={{0,1},{1,0},{2,3},{3,2},{4,5},{5,4},{6,7},{7,6},{8,9},{9,8},{10,11... | collective-permute-start | bytes 1179656 | tf_op jit(solution)/shard_map/ppermute | solution.py:286
  52.3 12.1 %collective-permute-start.16 = (bf16[2,16,6144]{2,1,0:T(8,128)(2,1)S(1)}, bf16[2,16,6144]{2,1,0:T(8,128)(2,1)S(1)}, u32[]{:S(2)}, u32[]{:S(2)}) collective-permute-start(bf16[2,16,6144]{2,1,0:T(8,128)(2,1)S(1)} %collective-permute-done.12.refs_0_.refs_12_), channel_id=1, source_target_pairs={{0,1},{1,0},{2,3},{3,2},{4,5},{5,4},{6,7},{7,6},{8,9},{9,8},{10,11... | collective-permute-start | bytes 1179656 | tf_op jit(solution)/shard_map/ppermute | solution.py:286
  53.9 11.2 %collective-permute-start.17 = (bf16[2,32,3072]{2,1,0:T(8,128)(2,1)S(1)}, bf16[2,32,3072]{2,1,0:T(8,128)(2,1)S(1)}, u32[]{:S(2)}, u32[]{:S(2)}) collective-permute-start(bf16[2,32,3072]{2,1,0:T(8,128)(2,1)S(1)} %get-tuple-element.152), channel_id=1, source_target_pairs={{0,16},{8,24},{16,0},{24,8},{1,17},{9,25},{17,1},{25,9},{2,18},{10... | collective-permute-start | bytes 1179656 | tf_op jit(solution)/shard_map/ppermute | solution.py:280
  54.9 13.5 %collective-permute-start.18 = (bf16[2,16,6144]{2,1,0:T(8,128)(2,1)S(1)}, bf16[2,16,6144]{2,1,0:T(8,128)(2,1)S(1)}, u32[]{:S(2)}, u32[]{:S(2)}) collective-permute-start(bf16[2,16,6144]{2,1,0:T(8,128)(2,1)S(1)} %collective-permute-done.13.refs_0_.refs_8_), channel_id=1, source_target_pairs={{0,2},{1,3},{2,0},{3,1},{4,6},{5,7},{6,4},{7,5},{8,10},{9,11},{10,... | collective-permute-start | bytes 1179656 | tf_op jit(solution)/shard_map/ppermute | solution.py:289
  55.2 17.6 %collective-permute-start.19 = (bf16[2,16,6144]{2,1,0:T(8,128)(2,1)S(1)}, bf16[2,16,6144]{2,1,0:T(8,128)(2,1)S(1)}, u32[]{:S(2)}, u32[]{:S(2)}) collective-permute-start(bf16[2,16,6144]{2,1,0:T(8,128)(2,1)S(1)} %collective-permute-done.13.refs_0_.refs_8_), channel_id=1, source_target_pairs={{0,1},{1,0},{2,3},{3,2},{4,5},{5,4},{6,7},{7,6},{8,9},{9,8},{10,11... | collective-permute-start | bytes 1179656 | tf_op jit(solution)/shard_map/ppermute | solution.py:286
  60.0 13.5 %collective-permute-start.20 = (bf16[2,32,3072]{2,1,0:T(8,128)(2,1)S(1)}, bf16[2,32,3072]{2,1,0:T(8,128)(2,1)S(1)}, u32[]{:S(2)}, u32[]{:S(2)}) collective-permute-start(bf16[2,32,3072]{2,1,0:T(8,128)(2,1)S(1)} %get-tuple-element.159), channel_id=1, source_target_pairs={{0,16},{8,24},{16,0},{24,8},{1,17},{9,25},{17,1},{25,9},{2,18},{10... | collective-permute-start | bytes 1179656 | tf_op jit(solution)/shard_map/ppermute | solution.py:280
  68.4 11.3 %collective-permute-start.21 = (bf16[2,16,6144]{2,1,0:T(8,128)(2,1)S(1)}, bf16[2,16,6144]{2,1,0:T(8,128)(2,1)S(1)}, u32[]{:S(2)}, u32[]{:S(2)}) collective-permute-start(bf16[2,16,6144]{2,1,0:T(8,128)(2,1)S(1)} %collective-permute-done.18.refs_0_.refs_14_), channel_id=1, source_target_pairs={{0,1},{1,0},{2,3},{3,2},{4,5},{5,4},{6,7},{7,6},{8,9},{9,8},{10,11... | collective-permute-start | bytes 1179656 | tf_op jit(solution)/shard_map/ppermute | solution.py:286
  69.3 13.6 %collective-permute-start.22 = (bf16[2,32,3072]{2,1,0:T(8,128)(2,1)S(1)}, bf16[2,32,3072]{2,1,0:T(8,128)(2,1)S(1)}, u32[]{:S(2)}, u32[]{:S(2)}) collective-permute-start(bf16[2,32,3072]{2,1,0:T(8,128)(2,1)S(1)} %get-tuple-element.181), channel_id=1, source_target_pairs={{0,16},{8,24},{16,0},{24,8},{1,17},{9,25},{17,1},{25,9},{2,18},{10... | collective-permute-start | bytes 1179656 | tf_op jit(solution)/shard_map/ppermute | solution.py:280
  76.8 16.4 %collective-permute-start.24 = (bf16[2,32,3072]{2,1,0:T(8,128)(2,1)S(1)}, bf16[2,32,3072]{2,1,0:T(8,128)(2,1)S(1)}, u32[]{:S(2)}, u32[]{:S(2)}) collective-permute-start(bf16[2,32,3072]{2,1,0:T(8,128)(2,1)S(1)} %get-tuple-element.189), channel_id=1, source_target_pairs={{0,16},{8,24},{16,0},{24,8},{1,17},{9,25},{17,1},{25,9},{2,18},{10... | collective-permute-start | bytes 1179656 | tf_op jit(solution)/shard_map/ppermute | solution.py:280
  81.3 11.9 %collective-permute-start.23 = (bf16[2,32,1024]{2,1,0:T(8,128)(2,1)S(1)}, bf16[2,32,1024]{2,1,0:T(8,128)(2,1)S(1)}, u32[]{:S(2)}, u32[]{:S(2)}) collective-permute-start(bf16[2,32,1024]{2,1,0:T(8,128)(2,1)S(1)} %get-tuple-element.187), channel_id=1, source_target_pairs={{0,16},{8,24},{16,0},{24,8},{1,17},{9,25},{17,1},{25,9},{2,18},{10... | collective-permute-start | bytes 393224 | tf_op jit(solution)/shard_map/ppermute | solution.py:280
  84.5 11.4 %collective-permute-start.25 = (bf16[2,32,1024]{2,1,0:T(8,128)(2,1)S(1)}, bf16[2,32,1024]{2,1,0:T(8,128)(2,1)S(1)}, u32[]{:S(2)}, u32[]{:S(2)}) collective-permute-start(bf16[2,32,1024]{2,1,0:T(8,128)(2,1)S(1)} %get-tuple-element.200), channel_id=1, source_target_pairs={{0,16},{8,24},{16,0},{24,8},{1,17},{9,25},{17,1},{25,9},{2,18},{10... | collective-permute-start | bytes 393224 | tf_op jit(solution)/shard_map/ppermute | solution.py:280
  86.9 11.7 %collective-permute-start.26 = (bf16[2,32,1024]{2,1,0:T(8,128)(2,1)S(1)}, bf16[2,32,1024]{2,1,0:T(8,128)(2,1)S(1)}, u32[]{:S(2)}, u32[]{:S(2)}) collective-permute-start(bf16[2,32,1024]{2,1,0:T(8,128)(2,1)S(1)} %get-tuple-element.206), channel_id=1, source_target_pairs={{0,16},{8,24},{16,0},{24,8},{1,17},{9,25},{17,1},{25,9},{2,18},{10... | collective-permute-start | bytes 393224 | tf_op jit(solution)/shard_map/ppermute | solution.py:280
  95.8 6.0 %collective-permute-start.29 = (bf16[2,384,1024]{2,1,0:T(8,128)(2,1)S(1)}, bf16[2,384,1024]{2,1,0:T(8,128)(2,1)S(1)}, u32[]{:S(2)}, u32[]{:S(2)}) collective-permute-start(bf16[2,384,1024]{2,1,0:T(8,128)(2,1)S(1)} %get-tuple-element.215), channel_id=1, source_target_pairs={{0,8},{8,0},{16,24},{24,16},{1,9},{9,1},{17,25},{25,17},{2,10},{10... | collective-permute-start | bytes 4718600 | tf_op jit(solution)/shard_map/ppermute | solution.py:283
  98.6 4.7 %collective-permute-start.28 = (bf16[2,384,1024]{2,1,0:T(8,128)(2,1)S(1)}, bf16[2,384,1024]{2,1,0:T(8,128)(2,1)S(1)}, u32[]{:S(2)}, u32[]{:S(2)}) collective-permute-start(bf16[2,384,1024]{2,1,0:T(8,128)(2,1)S(1)} %get-tuple-element.213), channel_id=1, source_target_pairs={{0,8},{8,0},{16,24},{24,16},{1,9},{9,1},{17,25},{25,17},{2,10},{10... | collective-permute-start | bytes 4718600 | tf_op jit(solution)/shard_map/ppermute | solution.py:283
  101.7 3.5 %collective-permute-start.27 = (bf16[2,384,1024]{2,1,0:T(8,128)(2,1)S(1)}, bf16[2,384,1024]{2,1,0:T(8,128)(2,1)S(1)}, u32[]{:S(2)}, u32[]{:S(2)}) collective-permute-start(bf16[2,384,1024]{2,1,0:T(8,128)(2,1)S(1)} %get-tuple-element.211), channel_id=1, source_target_pairs={{0,8},{8,0},{16,24},{24,16},{1,9},{9,1},{17,25},{25,17},{2,10},{10... | collective-permute-start | bytes 4718600 | tf_op jit(solution)/shard_map/ppermute | solution.py:283
